TPU v7x, 512 devices: a whole 4x4x16 slice. The times are simulated.
512 devices in a mesh: dp: 16 (over x, z_hi, core), fsdp: 32 (over y, z_lo).
Axes of the slice: x: 4, y: 4, z: 16 (z_hi: 2, z_lo: 8; z = z_hi * 8 + z_lo), core: 2. Of those that a mesh axis runs over, the one named last changes fastest.
Arguments:
- hidden_in: bfloat16 [131072, 4096], P(('dp', 'fsdp')), may hold values from -400 to 400, as said below
- key_grad: bfloat16 [131072, 512], P(('dp', 'fsdp')), may hold values from -6 to 6
- key_weight: bfloat16 [4096, 512], P('fsdp'), may hold values from -0.25 to 0.25
- norm_gain: float32 [4096], replicated, may hold values from 0.5 to 1.5
- head_order: int32 [512], replicated, may hold values from 0 to 511, each once
Outputs:
- fisher_served: bfloat16 [4096, 512], P(('dp', 'fsdp'))
- input_grad: bfloat16 [131072, 4096], P(('dp', 'fsdp'))
Inputs may be any that keep to these rules, and one draw needn't show every extreme that they name: `hidden_in`: each row's magnitude and each feature's magnitude vary over about a factor of ten. `head_order`: a permutation of the key projection's output columns.
All inputs are finite; a program needn't handle non-finite values.
Results may differ from a plain program's by a relative error of at most 0.0095.
Values may be sent and summed in bfloat16 or wider, within the bound.
No kernel may reach another device: no remote copies, remote signals or barrier semaphores. Data moves between devices by JAX's collectives and lax.ppermute only.
A program may use at most 64 MiB of HBM per device.

v0:
```python
import jax
import jax.numpy as jnp
from jax import lax
from jax.sharding import PartitionSpec as P


def body(hidden_in, key_grad, key_weight, norm_gain, head_order):
    seq_tokens = hidden_in.shape[0]
    width_in = hidden_in.shape[1]
    width_out = key_grad.shape[1]
    groups_count = lax.axis_size("dp")
    group_width = lax.axis_size("fsdp")
    row_count = width_in // (groups_count * group_width)
    values = hidden_in.astype(jnp.float32)
    square_mean = jnp.mean(values * values, axis=-1, keepdims=True)
    inverse_rms = lax.rsqrt(square_mean + 1e-06)
    unit_rows = values * inverse_rms
    normed = (unit_rows * norm_gain).astype(jnp.bfloat16)
    reordered = normed.reshape(seq_tokens, groups_count, group_width, row_count)
    reordered = reordered.transpose(0, 2, 1, 3).reshape(seq_tokens, width_in)
    scale_factor = 1.0 / (seq_tokens * groups_count * group_width)
    block_width = width_in // group_width
    blocks = lax.all_to_all(reordered, "fsdp", split_axis=1, concat_axis=0, tiled=True)
    grads_all = lax.all_gather(key_grad, "fsdp", axis=0, tiled=True)
    gradient = jnp.einsum(
        "stc,stk->sck",
        blocks.reshape(group_width, seq_tokens, block_width),
        grads_all.reshape(group_width, seq_tokens, width_out),
        preferred_element_type=jnp.float32,
    )
    seq_terms = (gradient * gradient * scale_factor).astype(jnp.bfloat16)
    seq_terms = lax.optimization_barrier(seq_terms)
    group_fisher = jnp.sum(seq_terms.astype(jnp.float32), axis=0).astype(jnp.bfloat16)
    received = lax.all_to_all(
        group_fisher.reshape(1, block_width, width_out),
        "dp",
        split_axis=1,
        concat_axis=0,
        tiled=True,
    )
    fisher = jnp.sum(received.astype(jnp.float32), axis=0).astype(jnp.bfloat16)
    selector = (head_order[:, None] == jnp.arange(width_out, dtype=jnp.int32)[None, :]).astype(
        jnp.bfloat16
    )
    fisher_served = lax.dot_general(
        fisher, selector, (((1,), (1,)), ((), ())), preferred_element_type=jnp.float32
    )
    fisher_served = fisher_served.astype(jnp.bfloat16)
    back = lax.dot_general(
        key_grad,
        lax.all_gather(key_weight, "fsdp", axis=0, tiled=True),
        (((1,), (1,)), ((), ())),
        preferred_element_type=jnp.float32,
    )
    grad_unit = back * norm_gain
    input_grad = inverse_rms * (
        grad_unit - unit_rows * jnp.mean(grad_unit * unit_rows, axis=-1, keepdims=True)
    )
    return (fisher_served, input_grad.astype(jnp.bfloat16))


def solution(mesh):
    in_specs = (P(("dp", "fsdp"), None), P(("dp", "fsdp"), None), P("fsdp", None), P(), P())
    out_specs = (P(("dp", "fsdp"), None), P(("dp", "fsdp"), None))
    return jax.shard_map(body, mesh=mesh, in_specs=in_specs, out_specs=out_specs, check_vma=False)
```

profile of v0, /device:TPU:1, one launch (start us, length us, event | category | flops | bytes accessed | tf_op | source)
XLA Modules:
  0.0 603.6 jit_solution(6374627534204088062)
XLA Ops:
  7.2 0.0 all-gather.5.cloned.1.call-start
  7.2 0.7 all-gather.5.cloned.1.call-update
  7.9 0.0 all-gather.3.cloned.1.call-start
  7.9 0.7 all-gather.3.cloned.1.call-update
  8.6 2.1 fusion.8
  10.7 0.0 copy-start
  10.8 0.0 copy-start.1
  10.8 223.0 %all-gather.5.cloned.1.call-done = bf16[4096,512]{1,0:T(8,128)(2,1)} async-done(((bf16[128,512]{1,0:T(8,128)(2,1)}), bf16[4096,512]{1,0:T(8,128)(2,1)}) %all-gather.5.cloned.1.call-update) | async-done | bytes 4194320 | tf_op jit(solution)/shard_map/all_gather | solution.py:51
  233.8 4.4 fusion.4
  238.1 0.0 copy-done
  238.1 0.0 copy-done.1
  238.1 3.5 fusion.7
  241.7 3.3 copy.12
  244.9 0.2 copy.19
  245.2 142.6 %all_to_all.28 = bf16[256,32,128]{0,2,1:T(8,128)(2,1)S(1)} all-to-all(bf16[256,32,128]{0,2,1:T(8,128)(2,1)S(1)} %bitcast.23), channel_id=1, replica_groups=mesh['dp'=16,'fsdp'=32] {'fsdp'}, dimensions={1} | all-to-all | bytes 4194304 | tf_op jit(solution)/shard_map/all_to_all | solution.py:23
  387.8 157.3 %all-gather.3.cloned.1.call-done = bf16[8192,512]{1,0:T(8,128)(2,1)} async-done(((bf16[256,512]{1,0:T(8,128)(2,1)}), bf16[8192,512]{1,0:T(8,128)(2,1)}) %all-gather.3.cloned.1.call-update) | async-done | bytes 8388624 | tf_op jit(solution)/shard_map/all_gather | solution.py:24
  545.1 6.6 %multiply_convert_fusion = bf16[32,128,512]{2,1,0:T(8,128)(2,1)} fusion(bf16[32,256,512]{2,1,0:T(8,128)(2,1)} %bitcast.21, bf16[256,32,128]{0,2,1:T(8,128)(2,1)S(1)} %all_to_all.28), kind=kOutput, calls=%fused_computation | convolution fusion | flops 1080033280 | bytes 14680064 | tf_op jit(solution)/shard_map/stc,stk->sck/dot_general | solution.py:25
  551.8 0.0 copy-start.2
  551.8 2.8 reduce_sum.43
  554.6 0.2 copy.20
  554.8 0.5 broadcast.25
  555.3 1.4 reduce.4
  556.7 0.1 reshape.40
  556.8 38.8 %all_to_all.29 = bf16[16,2,2048]{2,1,0:T(2,128)(2,1)S(1)} all-to-all(bf16[16,2,2048]{2,1,0:T(2,128)(2,1)S(1)} %reshape.40), channel_id=1, replica_groups=mesh['dp'=16,'fsdp'=32] {'dp'}, dimensions={0} | all-to-all | bytes 262144 | tf_op jit(solution)/shard_map/all_to_all | solution.py:34
  595.6 0.1 reshape.41
  595.7 0.0 copy-done.2
  595.8 1.0 convolution_convert_fusion
  (3 shorter events, 0.0 us)
Async XLA Ops:
  7.2 226.6 %all-gather.5.cloned.1.call-start = ((), (), s32[]{:S(2)}) async-start(), calls=%async_computation.3 | async-start | bytes 4325376 | tf_op jit(solution)/shard_map/all_gather | solution.py:51
  7.9 537.2 %all-gather.3.cloned.1.call-start = ((), (), s32[]{:S(2)}) async-start(), calls=%async_computation.2 | async-start | bytes 8650752 | tf_op jit(solution)/shard_map/all_gather | solution.py:24
  10.7 227.4 %copy-start = (bf16[256,4096]{1,0:T(8,128)(2,1)S(1)}, bf16[256,4096]{1,0:T(8,128)(2,1)}, u32[]{:S(2)}) copy-start(bf16[256,4096]{1,0:T(8,128)(2,1)} %param.5) | copy-start | bytes 6291460
  10.8 227.4 %copy-start.1 = (f32[4096]{0:T(1024)S(1)}, f32[4096]{0:T(1024)}, u32[]{:S(2)}) copy-start(f32[4096]{0:T(1024)} %param.8) | copy-start | bytes 49156
  551.8 44.0 %copy-start.2 = (s32[512]{0:T(512)S(1)}, s32[512]{0:T(512)}, u32[]{:S(2)}) copy-start(s32[512]{0:T(512)} %param.9) | copy-start | bytes 6148
Sparse Core Ops, SparseCore 0:
  10.1 223.6 all-gather.4
  235.8 309.2 all-gather.2
where the time goes:
time: 604 us
  waiting for transfers between devices  382 us (63%)
  blocking collectives  181 us (30%)
  between operations  14.1 us (2%)
  matrix products  12 us (2%)
  other arithmetic  9.85 us (2%)
    all_gather x1, waiting for transfers between devices, body(): lax.all_gather(key_weight, 'fsdp', axis=0, tiled=True)  223 us
    all_gather x1, waiting for transfers between devices, body(): grads_all = lax.all_gather(key_grad, 'fsdp', axis=0, tiled=True)  157 us
    all_to_all x1, blocking collectives, body(): lax.all_to_all(reordered, 'fsdp', split_axis=1, concat_axis=0, tiled=True)  143 us
    all_to_all x1, blocking collectives, body(): lax.all_to_all(group_fisher.reshape(1, block_width, width_out), 'dp', spl...  38.8 us
  transfers between devices with their start and end apart: 2, of which 2 were waited for; matrix products, arithmetic and copies ran while one was open for 2% of the time, Pallas kernels for 0%

commit v1 on v0

v1 whole, which is shorter than its diff:
```python
import jax
import jax.numpy as jnp
from jax import lax
from jax.experimental import pallas as pl
from jax.experimental.pallas import tpu as pltpu
from jax.sharding import PartitionSpec as P

AXES = ("dp", "fsdp")
NX, NZH, NC, NY, NZL = 4, 2, 2, 4, 8
D, K = 4096, 512
SEQ = 256
TOKENS = SEQ * NX * NZH * NC * NY * NZL
COLS = 256
GRAD_ROWS = 1024
PIECE = 32
BLOCK = NZL * PIECE
ROWS = GRAD_ROWS + BLOCK
BF16, F32 = jnp.bfloat16, jnp.float32


def device(x, zh, c, y, zl):
    return (((x * NZH + zh) * NC + c) * NY + y) * NZL + zl


def ring_groups(first):
    groups = []
    for zh in range(NZH):
        for zl in range(NZL):
            groups += [[device(x, zh, first, y, zl) for x in range(NX)] for y in range(NY)]
            groups += [[device(x, zh, 1 - first, y, zl) for y in range(NY)] for x in range(NX)]
    return groups


Z_LINES = [
    [device(x, zh, c, y, zl) for zl in range(NZL)]
    for x in range(NX)
    for zh in range(NZH)
    for c in range(NC)
    for y in range(NY)
]
Z_RINGS = [
    [device(x, zh, c, y, zl) for zh in range(NZH) for zl in range(NZL)]
    for x in range(NX)
    for c in range(NC)
    for y in range(NY)
]
CORE_SWAP = [
    (device(x, zh, c, y, zl), device(x, zh, 1 - c, y, zl))
    for x in range(NX)
    for zh in range(NZH)
    for c in range(NC)
    for y in range(NY)
    for zl in range(NZL)
]


def exchange(value, groups):
    return lax.all_to_all(
        value, AXES, split_axis=0, concat_axis=0, axis_index_groups=groups, tiled=True
    )


def call(kernel, outs, *args, grid=None, in_specs=None, out_specs=None, scratch=(), mib=24):
    whole = pl.BlockSpec(memory_space=pltpu.VMEM)
    kwargs = {}
    if grid is not None:
        kwargs["grid"] = grid
    return pl.pallas_call(
        kernel,
        out_shape=outs,
        in_specs=in_specs or [pl.BlockSpec(memory_space=pltpu.SMEM)] + [whole] * (len(args) - 1),
        out_specs=out_specs or jax.tree.map(lambda _: whole, outs),
        scratch_shapes=list(scratch),
        compiler_params=pltpu.CompilerParams(vmem_limit_bytes=mib * 2**20),
        **kwargs,
    )(*args)


def shape(dims, dtype=BF16):
    return jax.ShapeDtypeStruct(dims, dtype)


def norm_kernel(core_ref, hidden_ref, key_ref, gain_ref, own_ref, send_ref, inv_ref):
    core = core_ref[0]
    step = 16

    def rows_of(i, carry):
        rows = pl.ds(pl.multiple_of(i * step, step), step)
        values = hidden_ref[rows, :].astype(F32)
        inv = lax.rsqrt(jnp.sum(values * values, axis=-1, keepdims=True) * (1.0 / D) + 1e-06)
        inv_ref[rows, :] = jnp.broadcast_to(inv, (step, 128))
        for ref, part in ((own_ref, core), (send_ref, 1 - core)):
            for k in range(NX * NZH):
                cols = pl.ds(pl.multiple_of((2 * k + part) * COLS, COLS), COLS)
                unit = hidden_ref[rows, cols].astype(F32) * inv
                ref[k, rows, :] = (unit * gain_ref[:, cols]).astype(BF16)
        return carry

    lax.fori_loop(0, hidden_ref.shape[0] // step, rows_of, 0)
    for half in range(2):
        send_ref[NX * NZH + half] = key_ref[:, half * COLS : (half + 1) * COLS]


def square_kernel(core_ref, own_ref, other_ref, key_ref, weight_ref, out_ref):
    core = core_ref[0]
    over_tokens = (((0,), (0,)), ((), ()))

    def block(k, carry):
        x, zh = k // NZH, k % NZH
        outer = jnp.where(core == 0, x, 0)
        for half in range(2):
            cols = slice(half * COLS, (half + 1) * COLS)
            g0 = lax.dot_general(
                own_ref[k], key_ref[:, cols], over_tokens, preferred_element_type=F32
            )
            g1 = lax.dot_general(
                other_ref[k], other_ref[NX * NZH + half], over_tokens, preferred_element_type=F32
            )
            total = ((g0 * g0 + g1 * g1) * (1.0 / TOKENS)).astype(BF16)
            for y in range(NY):
                chunk = jnp.where(core == 0, outer, y)
                inner = jnp.where(core == 0, y, x)
                start = inner * 256 + zh * 128 + half * 64
                out_ref[chunk, pl.ds(pl.multiple_of(start, 64), 64), :] = total[
                    y * 64 : (y + 1) * 64
                ]
        return carry

    lax.fori_loop(0, NX * NZH, block, 0)
    for chunk in range(4):
        out_ref[chunk, GRAD_ROWS:, :] = weight_ref[...]


def middle_kernel(in_ref, out_ref):
    for b in range(4):
        rows = slice(b * 256, (b + 1) * 256)
        total = in_ref[0, rows, :].astype(F32)
        for j in range(1, 4):
            total += in_ref[j, rows, :].astype(F32)
        out_ref[b, 0:256, :] = total.astype(BF16)
        for j in range(4):
            out_ref[b, 256 + j * BLOCK : 256 + (j + 1) * BLOCK, :] = in_ref[j, GRAD_ROWS:, :]


def split_kernel(in_ref, out_ref):
    total = in_ref[0, 0:256, :].astype(F32)
    for j in range(1, 4):
        total += in_ref[j, 0:256, :].astype(F32)
    total = total.reshape(NZH, 2, NZL, 8, COLS)
    for zh in range(NZH):
        for zl in range(NZL):
            rows = jnp.concatenate([total[zh, 0, zl], total[zh, 1, zl]], axis=0)
            out_ref[zh * NZL + zl] = rows.astype(BF16)


def serve_kernel(order_ref, in_ref, out_ref):
    total = in_ref[0].astype(F32)
    for z in range(1, NZH * NZL):
        total += in_ref[z].astype(F32)
    fisher = jnp.concatenate([total[0:8], total[8:16]], axis=1).astype(BF16)
    column = lax.broadcasted_iota(jnp.int32, (K, K), 0)
    pick = jnp.where(column == order_ref[...], 1.0, 0.0).astype(BF16)
    out_ref[...] = jnp.dot(fisher, pick, preferred_element_type=F32).astype(BF16)


def input_kernel(
    core_ref, hidden_ref, key_ref, gain_ref, inv_ref, own_ref, other_ref, out_ref, du_ref
):
    core = core_ref[0]
    key_own = key_ref[:, pl.ds(pl.multiple_of(core * COLS, COLS), COLS)]
    key_other = key_ref[:, pl.ds(pl.multiple_of((1 - core) * COLS, COLS), COLS)]
    inv = inv_ref[:, 0:1]
    over_cols = (((1,), (1,)), ((), ()))

    def rows_of(ref, y, zl, x, along_y):
        a = jnp.where(along_y, y, x)
        b = jnp.where(along_y, x, y)
        start = pl.multiple_of(256 + b * BLOCK + zl * PIECE, PIECE)
        return ref[a, pl.ds(start, PIECE), :]

    def forward(t, acc):
        y, pair = t // 4, t % 4
        places = [(2 * pair + i, x) for i in range(2) for x in range(NX)]
        own = jnp.concatenate([rows_of(own_ref, y, zl, x, core == 0) for zl, x in places], axis=0)
        other = jnp.concatenate(
            [rows_of(other_ref, y, zl, x, core != 0) for zl, x in places], axis=0
        )
        back = lax.dot_general(key_own, own, over_cols, preferred_element_type=F32)
        back += lax.dot_general(key_other, other, over_cols, preferred_element_type=F32)
        cols = pl.ds(pl.multiple_of(t * 256, 256), 256)
        du = back * gain_ref[:, cols]
        du_ref[:, cols] = du
        both = du * (hidden_ref[:, cols].astype(F32) * inv)
        return acc + both[:, :128] + both[:, 128:]

    acc = lax.fori_loop(0, D // 256, forward, jnp.zeros((SEQ, 128), F32))
    mean = jnp.sum(acc, axis=-1, keepdims=True) * (1.0 / D)

    def finish(t, carry):
        cols = pl.ds(pl.multiple_of(t * 256, 256), 256)
        unit = hidden_ref[:, cols].astype(F32) * inv
        out_ref[:, cols] = (inv * (du_ref[:, cols] - unit * mean)).astype(BF16)
        return carry

    lax.fori_loop(0, D // 256, finish, 0)


def body(hidden_in, key_grad, key_weight, norm_gain, head_order):
    dp = lax.axis_index("dp")
    x, core = lax.div(dp, NZH * NC), lax.rem(dp, NC)
    core_id = core.reshape(1).astype(jnp.int32)
    gain = norm_gain.reshape(1, D)

    with jax.named_scope("norm"):
        rows = 64
        blocks = NX * NZH
        own, send, inv = call(
            norm_kernel,
            (shape((blocks, SEQ, COLS)), shape((blocks + 2, SEQ, COLS)), shape((SEQ, 128), F32)),
            core_id,
            hidden_in,
            key_grad,
            gain,
            grid=(SEQ // rows,),
            in_specs=[
                pl.BlockSpec(memory_space=pltpu.SMEM),
                pl.BlockSpec((rows, D), lambda i: (i, 0)),
                pl.BlockSpec((rows, K), lambda i: (i, 0)),
                pl.BlockSpec((1, D), lambda i: (0, 0)),
            ],
            out_specs=(
                pl.BlockSpec((blocks, rows, COLS), lambda i: (0, i, 0)),
                pl.BlockSpec((blocks + 2, rows, COLS), lambda i: (0, i, 0)),
                pl.BlockSpec((rows, 128), lambda i: (i, 0)),
            ),
        )
    with jax.named_scope("weight_z"):
        piece = lax.dynamic_slice(key_weight, (x * PIECE, core * COLS), (PIECE, COLS))
        piece, send = lax.optimization_barrier((piece, send))
        other = lax.ppermute(send, AXES, CORE_SWAP)
        gathered = exchange(jnp.broadcast_to(piece, (NZL, PIECE, COLS)), Z_LINES)
    with jax.named_scope("squares"):
        chunks = call(
            square_kernel,
            shape((4, ROWS, COLS)),
            core_id,
            own,
            other,
            key_grad,
            gathered.reshape(BLOCK, COLS),
        )
    with jax.named_scope("ring_a"):
        first = exchange(chunks, ring_groups(0))
    with jax.named_scope("middle"):
        whole = pl.BlockSpec(memory_space=pltpu.VMEM)
        chunks = call(middle_kernel, shape((4, ROWS, COLS)), first, in_specs=[whole])
    with jax.named_scope("ring_b"):
        second = exchange(chunks, ring_groups(1))
    with jax.named_scope("weight_swap"):
        swapped = lax.ppermute(second, AXES, CORE_SWAP)
    with jax.named_scope("ring_z"):
        parts = call(split_kernel, shape((NZH * NZL, 16, COLS)), second, in_specs=[whole])
        parts = exchange(parts, Z_RINGS)
    with jax.named_scope("serve"):
        served = call(
            serve_kernel,
            shape((8, K)),
            head_order.reshape(1, K),
            parts,
            in_specs=[whole, whole],
        )
    with jax.named_scope("input_grad"):
        input_grad = call(
            input_kernel,
            shape((SEQ, D)),
            core_id,
            hidden_in,
            key_grad,
            gain,
            inv,
            second,
            swapped,
            scratch=[pltpu.VMEM((SEQ, D), F32)],
            mib=32,
        )
    return served, input_grad


def solution(mesh):
    in_specs = (P(AXES, None), P(AXES, None), P("fsdp", None), P(), P())
    out_specs = (P(AXES, None), P(AXES, None))
    return jax.shard_map(body, mesh=mesh, in_specs=in_specs, out_specs=out_specs, check_vma=False)
```

time: 604 us -> 118 us (0.20)
  waiting for transfers between devices: 382 us -> 0.01 us
  blocking collectives: 181 us -> 81.4 us
  starting transfers between devices: 0.08 us -> 15.6 us
  Pallas kernels: 0 us -> 14.9 us
  between operations: 14.1 us -> 0.71 us
  matrix products: 12 us -> 0 us
  other arithmetic: 9.85 us -> 0 us
    all_gather x2 -> x0, waiting for transfers between devices: 380 us -> none  [the longest x1 223 us: body(): lax.all_gather(key_weight, 'fsdp', axis=0, tiled=True)]
    all_to_all x2 -> x4, blocking collectives: 181 us -> 81.4 us  [exchange(): lax.all_to_all(value, AXES, split_axis=0, concat_axis=0, axis_index_group...]
    ppermute x0 -> x2, starting transfers between devices: none -> 15.6 us  [the longest x1 8.79 us: body(): other = lax.ppermute(send, AXES, CORE_SWAP)]
    pallas_call x0 -> x6, Pallas kernels: none -> 14.9 us  [call(): pl.pallas_call(kernel, out_shape=outs, in_specs=in_specs or [pl.BlockSpec...]
    dot_general x3 -> x0, matrix products: 12 us -> none  [the longest x1 6.63 us: body(): jnp.einsum('stc,stk->sck', blocks.reshape(group_width, seq_tokens, block_...]
  transfers between devices with their start and end apart: 2 -> 2, of which waited for: 2 -> 0; matrix products, arithmetic and copies ran while one was open for 2% -> 0% of each run, Pallas kernels for 0% -> 1%
where the time goes in v1:
time: 118 us; the launch traced here: 117 us
  blocking collectives  81.4 us (69%)
  starting transfers between devices  15.6 us (13%)
  Pallas kernels  14.9 us (13%)
  local copies, waits for them, and re-layouts  4.01 us (3%)
    all_to_all x4, blocking collectives, exchange(): lax.all_to_all(value, AXES, split_axis=0, concat_axis=0, axis_index_group...  81.4 us
    pallas_call x6, Pallas kernels, call(): pl.pallas_call(kernel, out_shape=outs, in_specs=in_specs or [pl.BlockSpec...  14.9 us
    ppermute x1, starting transfers between devices, body(): other = lax.ppermute(send, AXES, CORE_SWAP)  8.79 us
    ppermute x1, starting transfers between devices, body(): swapped = lax.ppermute(second, AXES, CORE_SWAP)  6.86 us
    unnamed x14, local copies, waits for them, and re-layouts  3.27 us
  transfers between devices with their start and end apart: 2, of which 0 were waited for; matrix products, arithmetic and copies ran while one was open for 0% of the time, Pallas kernels for 1%

profile of v1, /device:TPU:1, one launch (start us, length us, event | category | flops | bytes accessed | tf_op | source)
XLA Modules:
  0.0 116.7 jit_solution(15790615692470682715)
XLA Ops:
  0.6 0.7 dynamic_slice.3
  1.4 0.0 copy-start
  1.4 1.6 %copy-done = bf16[256,4096]{1,0:T(8,128)(2,1)S(1)} copy-done((bf16[256,4096]{1,0:T(8,128)(2,1)S(1)}, bf16[256,4096]{1,0:T(8,128)(2,1)}, u32[]{:S(2)}) %copy-start) | copy-done | bytes 2097176
  3.0 0.0 copy-start.2
  3.0 0.9 copy-done.2
  3.9 0.0 copy-start.4
  3.9 0.7 copy-done.4
  4.6 0.0 copy-start.3
  4.6 2.6 %norm.1 = (bf16[8,256,256]{2,1,0:T(8,128)(2,1)S(1)}, bf16[10,256,256]{2,1,0:T(8,128)(2,1)S(1)}, f32[256,128]{1,0:T(8,128)S(1)}) custom-call(s32[1]{0:T(128)} %bitcast.1.core_ref, bf16[256,4096]{1,0:T(8,128)(2,1)S(1)} %copy-done, bf16[256,512]{1,0:T(8,128)(2,1)S(1)} %copy-done.2, f32[1,4096]{1,0:T(1,128)S(1)} %bitcast.5), custom_call_target="tpu_custom_call" | custom-call | tf_op jit(solution)/shard_map/norm/pallas_call | solution.py:68
  7.3 8.8 %collective-permute-start = (bf16[10,256,256]{2,1,0:T(8,128)(2,1)S(1)}, bf16[10,256,256]{2,1,0:T(8,128)(2,1)S(1)}, u32[]{:S(2)}, u32[]{:S(2)}) collective-permute-start(bf16[10,256,256]{2,1,0:T(8,128)(2,1)S(1)} %get-tuple-element.9), channel_id=1, source_target_pairs={{0,32},{1,33},{2,34},{3,35},{4,36},{5,37},{6,38},{7,39},{8,40},{9,... | collective-permute-start | bytes 3932168 | tf_op jit(solution)/shard_map/weight_z/ppermute | solution.py:240
  16.1 17.3 %all_to_all.20 = bf16[8,32,256]{2,1,0:T(8,128)(2,1)S(1)} all-to-all(bf16[8,32,256]{2,1,0:T(8,128)(2,1)S(1)} %broadcast_in_dim.3), channel_id=1, replica_groups={{0,1,2,3,4,5,6,7},{8,9,10,11,12,13,14,15},{16,17,18,19,20,21,22,23},{24..., dimensions={0} | all-to-all | bytes 262144 | tf_op jit(solution)/shard_map/weight_z/all_to_all | solution.py:58
  33.4 0.0 collective-permute-done.other_ref
  33.4 0.0 copy-done.3
  33.4 2.9 %squares.1 = bf16[4,1280,256]{2,1,0:T(8,128)(2,1)S(1)} custom-call(s32[1]{0:T(128)} %bitcast.1.core_ref, bf16[8,256,256]{2,1,0:T(8,128)(2,1)S(1)} %get-tuple-element.7.own_ref, bf16[10,256,256]{2,1,0:T(8,128)(2,1)S(1)} %collective-permute-done.other_ref, bf16[256,512]{1,0:T(8,128)(2,1)S(1)} %copy-done.3, bf16[256,256]{1,0:T(8,128)(2,1)S(1)} %bitcast.4), custom_call_target="tpu_custom_call" | custom-call | tf_op jit(solution)/shard_map/squares/pallas_call | solution.py:68
  36.3 22.4 %all_to_all.21.in_ref = bf16[4,1280,256]{2,1,0:T(8,128)(2,1)S(1)} all-to-all(bf16[4,1280,256]{2,1,0:T(8,128)(2,1)S(1)} %squares.1), channel_id=1, replica_groups={{0,128,256,384},{8,136,264,392},{16,144,272,400},{24,152,280,408},{32,4..., dimensions={0} | all-to-all | bytes 5242880 | tf_op jit(solution)/shard_map/ring_a/all_to_all | solution.py:58
  58.7 0.3 middle.1
  59.0 22.0 %all_to_all.22.in_ref.own_ref = bf16[4,1280,256]{2,1,0:T(8,128)(2,1)S(1)} all-to-all(bf16[4,1280,256]{2,1,0:T(8,128)(2,1)S(1)} %middle.1), channel_id=1, replica_groups={{32,160,288,416},{40,168,296,424},{48,176,304,432},{56,184,312,440},{0,..., dimensions={0} | all-to-all | bytes 5242880 | tf_op jit(solution)/shard_map/ring_b/all_to_all | solution.py:58
  81.0 0.0 copy-start.6
  81.0 0.0 copy-start.1
  81.0 0.0 copy-start.5
  81.0 6.9 %collective-permute-start.1 = (bf16[4,1280,256]{2,1,0:T(8,128)(2,1)S(1)}, bf16[4,1280,256]{2,1,0:T(8,128)(2,1)S(1)}, u32[]{:S(2)}, u32[]{:S(2)}) collective-permute-start(bf16[4,1280,256]{2,1,0:T(8,128)(2,1)S(1)} %all_to_all.22.in_ref.own_ref), channel_id=1, source_target_pairs={{0,32},{1,33},{2,34},{3,35},{4,36},{5,37},{6,38},{7,39},{8,40},{9,... | collective-permute-start | bytes 7864328 | tf_op jit(solution)/shard_map/weight_swap/ppermute | solution.py:260
  87.9 0.1 ring_z.1
  88.0 19.7 %all_to_all.23.in_ref = bf16[16,16,256]{2,1,0:T(8,128)(2,1)S(1)} all-to-all(bf16[16,16,256]{2,1,0:T(8,128)(2,1)S(1)} %ring_z.1), channel_id=1, replica_groups={{0,1,2,3,4,5,6,7,64,65,66,67,68,69,70,71},{8,9,10,11,12,13,14,15,72,73,..., dimensions={0} | all-to-all | bytes 262144 | tf_op jit(solution)/shard_map/ring_z/all_to_all | solution.py:58
  107.6 0.0 copy-done.6
  107.6 0.8 serve.1
  108.4 0.0 collective-permute-done.1.other_ref
  108.4 0.0 copy-done.1
  108.5 0.0 copy-done.5
  108.5 8.2 %input_grad.1 = bf16[256,4096]{1,0:T(8,128)(2,1)} custom-call(s32[1]{0:T(128)} %bitcast.1.core_ref, bf16[256,4096]{1,0:T(8,128)(2,1)S(1)} %copy-done.1, bf16[256,512]{1,0:T(8,128)(2,1)S(1)} %copy-done.3, f32[1,4096]{1,0:T(1,128)S(1)} %bitcast.6, f32[256,128]{1,0:T(8,128)S(1)} %get-tuple-element.11.inv_ref, ...), custom_call_target="tpu_custom_call" | custom-call | tf_op jit(solution)/shard_map/input_grad/pallas_call | solution.py:68
  (1 shorter events, 0.0 us)
Async XLA Ops:
  1.4 1.6 %copy-start = (bf16[256,4096]{1,0:T(8,128)(2,1)S(1)}, bf16[256,4096]{1,0:T(8,128)(2,1)}, u32[]{:S(2)}) copy-start(bf16[256,4096]{1,0:T(8,128)(2,1)} %hidden_ref.3) | copy-start | bytes 6291460
  3.0 0.9 copy-start.2
  3.9 0.7 copy-start.4
  4.6 28.8 %copy-start.3 = (bf16[256,512]{1,0:T(8,128)(2,1)S(1)}, bf16[256,512]{1,0:T(8,128)(2,1)}, u32[]{:S(2)}) copy-start(bf16[256,512]{1,0:T(8,128)(2,1)} %key_ref.5) | copy-start | bytes 786436
  7.3 26.1 %collective-permute-start = (bf16[10,256,256]{2,1,0:T(8,128)(2,1)S(1)}, bf16[10,256,256]{2,1,0:T(8,128)(2,1)S(1)}, u32[]{:S(2)}, u32[]{:S(2)}) collective-permute-start(bf16[10,256,256]{2,1,0:T(8,128)(2,1)S(1)} %get-tuple-element.9), channel_id=1, source_target_pairs={{0,32},{1,33},{2,34},{3,35},{4,36},{5,37},{6,38},{7,39},{8,40},{9,... | collective-permute-start | bytes 3932168 | tf_op jit(solution)/shard_map/weight_z/ppermute | solution.py:240
  81.0 26.6 %copy-start.6 = (s32[512]{0:T(512)S(1)}, s32[512]{0:T(512)}, u32[]{:S(2)}) copy-start(s32[512]{0:T(512)} %param.9) | copy-start | bytes 6148
  81.0 27.4 %copy-start.1 = (bf16[256,4096]{1,0:T(8,128)(2,1)S(1)}, bf16[256,4096]{1,0:T(8,128)(2,1)}, u32[]{:S(2)}) copy-start(bf16[256,4096]{1,0:T(8,128)(2,1)} %hidden_ref.3) | copy-start | bytes 6291460
  81.0 27.4 %copy-start.5 = (f32[4096]{0:T(1024)S(1)}, f32[4096]{0:T(1024)}, u32[]{:S(2)}) copy-start(f32[4096]{0:T(1024)} %param.8) | copy-start | bytes 49156
  81.0 27.4 %collective-permute-start.1 = (bf16[4,1280,256]{2,1,0:T(8,128)(2,1)S(1)}, bf16[4,1280,256]{2,1,0:T(8,128)(2,1)S(1)}, u32[]{:S(2)}, u32[]{:S(2)}) collective-permute-start(bf16[4,1280,256]{2,1,0:T(8,128)(2,1)S(1)} %all_to_all.22.in_ref.own_ref), channel_id=1, source_target_pairs={{0,32},{1,33},{2,34},{3,35},{4,36},{5,37},{6,38},{7,39},{8,40},{9,... | collective-permute-start | bytes 7864328 | tf_op jit(solution)/shard_map/weight_swap/ppermute | solution.py:260

commit v2 on v1

v2 whole, which is shorter than its diff:
```python
import jax
import jax.numpy as jnp
from jax import lax
from jax.experimental import pallas as pl
from jax.experimental.pallas import tpu as pltpu
from jax.sharding import PartitionSpec as P

AXES = ("dp", "fsdp")
NX, NZH, NC, NY, NZL = 4, 2, 2, 4, 8
D, K = 4096, 512
SEQ = 256
TOKENS = SEQ * NX * NZH * NC * NY * NZL
COLS = 256
BF16, F32 = jnp.bfloat16, jnp.float32


def device(x, zh, c, y, zl):
    return (((x * NZH + zh) * NC + c) * NY + y) * NZL + zl


def places():
    return [
        (x, zh, c, y, zl)
        for x in range(NX)
        for zh in range(NZH)
        for c in range(NC)
        for y in range(NY)
        for zl in range(NZL)
    ]


def ring_groups(first):
    groups = []
    for zh in range(NZH):
        for zl in range(NZL):
            groups += [[device(x, zh, first, y, zl) for x in range(NX)] for y in range(NY)]
            groups += [[device(x, zh, 1 - first, y, zl) for y in range(NY)] for x in range(NX)]
    return groups


def from_z(distance):
    pairs = []
    for x, zh, c, y, zl in places():
        z = (zh * NZL + zl + (distance if c == 0 else -distance)) % (NZH * NZL)
        pairs.append((device(x, z // NZL, c, y, z % NZL), device(x, zh, c, y, zl)))
    return pairs


Y_RINGS = [
    [device(x, zh, c, y, zl) for y in range(NY)]
    for x in range(NX)
    for zh in range(NZH)
    for c in range(NC)
    for zl in range(NZL)
]
Z_RINGS = [
    [device(x, zh, c, y, zl) for zh in range(NZH) for zl in range(NZL)]
    for x in range(NX)
    for c in range(NC)
    for y in range(NY)
]
CORE_SWAP = [(device(x, zh, c, y, zl), device(x, zh, 1 - c, y, zl)) for x, zh, c, y, zl in places()]


def exchange(value, groups):
    return lax.all_to_all(
        value, AXES, split_axis=0, concat_axis=0, axis_index_groups=groups, tiled=True
    )


def call(kernel, outs, ins, in_spaces, out_spaces, scratch=(), mib=24):
    return pl.pallas_call(
        kernel,
        out_shape=outs,
        in_specs=[pl.BlockSpec(memory_space=space) for space in in_spaces],
        out_specs=jax.tree.map(lambda space: pl.BlockSpec(memory_space=space), out_spaces),
        scratch_shapes=list(scratch),
        compiler_params=pltpu.CompilerParams(vmem_limit_bytes=mib * 2**20),
    )(*ins)


def my_core():
    return lax.rem(lax.axis_index("dp"), NC)


def shape(dims, dtype=BF16):
    return jax.ShapeDtypeStruct(dims, dtype)


def norm_kernel(
    hidden_hbm, key_hbm, gain_hbm, own_ref, send_ref, inv_ref, hidden_ref, gain_ref, sems
):
    core = my_core()
    step, parts = 16, 4
    rows_each = SEQ // parts
    gain_copy = pltpu.make_async_copy(gain_hbm, gain_ref, sems.at[0])
    gain_copy.start()
    copies = []
    for i in range(parts):
        rows = pl.ds(i * rows_each, rows_each)
        copies.append(
            pltpu.make_async_copy(hidden_hbm.at[rows], hidden_ref.at[rows], sems.at[1 + i])
        )
        copies[-1].start()
    key_copies = []
    for half in range(2):
        source = key_hbm.at[:, pl.ds(half * COLS, COLS)]
        target = send_ref.at[NX * NZH + half]
        key_copies.append(pltpu.make_async_copy(source, target, sems.at[1 + parts + half]))
        key_copies[-1].start()

    def rows_of(i, carry):
        rows = pl.ds(pl.multiple_of(i * step, step), step)
        squares = jnp.zeros((step, 512), F32)
        for t in range(0, D, 512):
            values = hidden_ref[rows, t : t + 512].astype(F32)
            squares += values * values
        inv = lax.rsqrt(jnp.sum(squares, axis=-1, keepdims=True) * (1.0 / D) + 1e-06)
        inv_ref[rows, :] = jnp.broadcast_to(inv, (step, 128))
        for ref, part in ((own_ref, core), (send_ref, 1 - core)):
            for k in range(NX * NZH):
                cols = pl.ds(pl.multiple_of((2 * k + part) * COLS, COLS), COLS)
                unit = hidden_ref[rows, cols].astype(F32) * inv
                ref[k, rows, :] = (unit * gain_ref[:, cols]).astype(BF16)
        return carry

    gain_copy.wait()
    for i in range(parts):
        copies[i].wait()
        lax.fori_loop(i * rows_each // step, (i + 1) * rows_each // step, rows_of, 0)
    for copy in key_copies:
        copy.wait()


def piece_kernel(own_ref, far_ref, out_ref):
    cols = pl.ds(pl.multiple_of(my_core() * COLS, COLS), COLS)
    for y in range(NY):
        out_ref[y, 0:128, :] = own_ref[:, cols]
        out_ref[y, 128:256, :] = far_ref[:, cols]


def square_kernel(own_ref, other_ref, key_ref, out_ref):
    core = my_core()
    over_tokens = (((0,), (0,)), ((), ()))
    key_other = jnp.concatenate([other_ref[NX * NZH], other_ref[NX * NZH + 1]], axis=1)

    def block(k, carry):
        x, zh = k // NZH, k % NZH
        g0 = lax.dot_general(own_ref[k], key_ref[...], over_tokens, preferred_element_type=F32)
        g1 = lax.dot_general(other_ref[k], key_other, over_tokens, preferred_element_type=F32)
        total = ((g0 * g0 + g1 * g1) * (1.0 / TOKENS)).astype(BF16)
        for y in range(NY):
            chunk = jnp.where(core == 0, x, y)
            inner = jnp.where(core == 0, y, x)
            for half in range(2):
                start = pl.multiple_of(inner * 256 + zh * 128 + half * 64, 64)
                out_ref[chunk, pl.ds(start, 64), :] = total[
                    y * 64 : (y + 1) * 64, half * COLS : (half + 1) * COLS
                ]
        return carry

    lax.fori_loop(0, NX * NZH, block, 0)


def middle_kernel(in_ref, near_ref, far_ref, out_ref, weight_ref):
    for b in range(4):
        rows = slice(b * 256, (b + 1) * 256)
        total = in_ref[0, rows, :].astype(F32)
        for j in range(1, 4):
            total += in_ref[j, rows, :].astype(F32)
        out_ref[b] = total.astype(BF16)
        weight_ref[b] = near_ref[b]
        weight_ref[4 + b] = far_ref[b]


def split_kernel(in_ref, near_ref, far_ref, out_ref, weight_ref):
    total = in_ref[0].astype(F32)
    for j in range(1, 4):
        total += in_ref[j].astype(F32)
    total = total.reshape(NZH, 2, NZL, 8, COLS)
    for zh in range(NZH):
        for zl in range(NZL):
            rows = jnp.concatenate([total[zh, 0, zl], total[zh, 1, zl]], axis=0)
            out_ref[zh * NZL + zl] = rows.astype(BF16)
    for b in range(8):
        weight_ref[b] = near_ref[b]
        weight_ref[8 + b] = far_ref[b]


def serve_kernel(order_ref, in_ref, out_ref):
    total = in_ref[0].astype(F32)
    for z in range(1, NZH * NZL):
        total += in_ref[z].astype(F32)
    fisher = jnp.concatenate([total[0:8], total[8:16]], axis=1).astype(BF16)
    column = lax.broadcasted_iota(jnp.int32, (K, K), 0)
    pick = jnp.where(column == order_ref[...], 1.0, 0.0).astype(BF16)
    out_ref[...] = jnp.dot(fisher, pick, preferred_element_type=F32).astype(BF16)


def input_kernel(
    hidden_ref, key_ref, gain_ref, inv_ref, own_ref, other_ref, out_hbm, back_ref, out_ref, sems
):
    core = my_core()
    z_here = lax.rem(lax.axis_index("fsdp"), NZL)
    own_cols = pl.ds(pl.multiple_of(core * COLS, COLS), COLS)
    other_cols = pl.ds(pl.multiple_of((1 - core) * COLS, COLS), COLS)
    keys = jnp.concatenate([key_ref[:, own_cols], key_ref[:, other_cols]], axis=1)
    sign = 1 - 2 * core

    def shard(ref, y, zl, sign):
        away = (sign * (zl - z_here)) & (NZL - 1)
        index = (away & 1) * 8 + ((away >> 1) & 1) * 4 + y
        return ref[index, pl.ds(pl.multiple_of((away >> 2) * 128, 128), 128), :]

    def tile(t, carry):
        y, pair = t // 4, t % 4
        weight = jnp.concatenate(
            [
                jnp.concatenate(
                    [shard(own_ref, y, 2 * pair + i, sign), shard(other_ref, y, 2 * pair + i, -sign)],
                    axis=1,
                )
                for i in range(2)
            ],
            axis=0,
        )
        cols = pl.ds(pl.multiple_of(t * 256, 256), 256)
        back_ref[:, cols] = lax.dot_general(
            keys, weight, (((1,), (1,)), ((), ())), preferred_element_type=F32
        )
        return carry

    lax.fori_loop(0, D // 256, tile, 0)

    step, parts, width = 16, 4, 512

    def rows_of(i, carry):
        rows = pl.ds(pl.multiple_of(i * step, step), step)
        inv = inv_ref[rows, 0:1]
        total = jnp.zeros((step, width), F32)
        for t in range(0, D, width):
            cols = slice(t, t + width)
            du = back_ref[rows, cols] * gain_ref[:, cols]
            total += du * hidden_ref[rows, cols].astype(F32)
        mean = inv * jnp.sum(total, axis=-1, keepdims=True) * (1.0 / D)
        factor = inv * inv * mean
        for t in range(0, D, width):
            cols = slice(t, t + width)
            du = back_ref[rows, cols] * gain_ref[:, cols]
            out = du * inv - hidden_ref[rows, cols].astype(F32) * factor
            out_ref[rows, cols] = out.astype(BF16)
        return carry

    rows_each = SEQ // parts
    copies = []
    for i in range(parts):
        lax.fori_loop(i * rows_each // step, (i + 1) * rows_each // step, rows_of, 0)
        rows = pl.ds(i * rows_each, rows_each)
        copies.append(pltpu.make_async_copy(out_ref.at[rows], out_hbm.at[rows], sems.at[i]))
        copies[-1].start()
    for copy in copies:
        copy.wait()


def body(hidden_in, key_grad, key_weight, norm_gain, head_order):
    gain = norm_gain.reshape(1, D)
    vmem, hbm = pltpu.VMEM, pltpu.HBM

    with jax.named_scope("weight_z4"):
        far = lax.ppermute(key_weight, AXES, from_z(4))
    with jax.named_scope("norm"):
        blocks = NX * NZH
        own, send, inv = call(
            norm_kernel,
            (shape((blocks, SEQ, COLS)), shape((blocks + 2, SEQ, COLS)), shape((SEQ, 128), F32)),
            (hidden_in, key_grad, gain),
            (hbm, hbm, hbm),
            (vmem, vmem, vmem),
            [pltpu.VMEM((SEQ, D), BF16), pltpu.VMEM((1, D), F32), pltpu.SemaphoreType.DMA((7,))],
        )
        far, send = lax.optimization_barrier((far, send))
        other = lax.ppermute(send, AXES, CORE_SWAP)
    with jax.named_scope("weight_y"):
        pieces = call(
            piece_kernel, shape((NY, 256, COLS)), (key_weight, far), (vmem, vmem), vmem
        )
        near = exchange(pieces, Y_RINGS)
    with jax.named_scope("weight_z2"):
        far = lax.ppermute(near, AXES, from_z(2))
    with jax.named_scope("squares"):
        chunks = call(
            square_kernel, shape((4, 1024, COLS)), (own, other, key_grad), (vmem,) * 3, vmem
        )
    with jax.named_scope("ring_a"):
        chunks = exchange(chunks, ring_groups(0))
    with jax.named_scope("middle"):
        chunks, near = call(
            middle_kernel,
            (shape((4, 256, COLS)), shape((8, 256, COLS))),
            (chunks, near, far),
            (vmem,) * 3,
            (vmem, vmem),
        )
    with jax.named_scope("weight_z1"):
        far = lax.ppermute(near, AXES, from_z(1))
    with jax.named_scope("ring_b"):
        chunks = exchange(chunks, ring_groups(1))
    with jax.named_scope("split"):
        parts, weight_own = call(
            split_kernel,
            (shape((NZH * NZL, 16, COLS)), shape((16, 256, COLS))),
            (chunks, near, far),
            (vmem,) * 3,
            (vmem, vmem),
        )
    with jax.named_scope("weight_swap"):
        weight_other = lax.ppermute(weight_own, AXES, CORE_SWAP)
    with jax.named_scope("ring_z"):
        parts = exchange(parts, Z_RINGS)
    with jax.named_scope("serve"):
        served = call(
            serve_kernel, shape((8, K)), (head_order.reshape(1, K), parts), (vmem, vmem), vmem
        )
    with jax.named_scope("input_grad"):
        input_grad = call(
            input_kernel,
            shape((SEQ, D)),
            (hidden_in, key_grad, gain, inv, weight_own, weight_other),
            (vmem,) * 6,
            hbm,
            [
                pltpu.VMEM((SEQ, D), F32),
                pltpu.VMEM((SEQ, D), BF16),
                pltpu.SemaphoreType.DMA((4,)),
            ],
            mib=32,
        )
    return served, input_grad


def solution(mesh):
    in_specs = (P(AXES, None), P(AXES, None), P("fsdp", None), P(), P())
    out_specs = (P(AXES, None), P(AXES, None))
    return jax.shard_map(body, mesh=mesh, in_specs=in_specs, out_specs=out_specs, check_vma=False)
```

time: 118 us -> 114 us (0.966)
  blocking collectives: 81.4 us -> 31 us
  starting transfers between devices: 15.6 us -> 37 us
  waiting for transfers between devices: 0.01 us -> 19.8 us
  local copies, waits for them, and re-layouts: 4.01 us -> 6.8 us
  Pallas kernels: 14.9 us -> 16.6 us
    all_to_all x4 -> x2, blocking collectives: 81.4 us -> 31 us  [exchange(): lax.all_to_all(value, AXES, split_axis=0, concat_axis=0, axis_index_group...]
    ppermute x1 -> x4, starting transfers between devices: 6.86 us -> 22.7 us  [the longest x1 9.65 us: body(): far = lax.ppermute(key_weight, AXES, from_z(4))]
    ppermute x1 -> x4, waiting for transfers between devices: 0.01 us -> 15.7 us  [the longest x1 12.5 us: body(): far = lax.ppermute(near, AXES, from_z(2))]
    all_to_all x0 -> x2, starting transfers between devices: none -> 7.79 us  [exchange(): lax.all_to_all(value, AXES, split_axis=0, concat_axis=0, axis_index_group...]
    all_to_all x0 -> x2, waiting for transfers between devices: none -> 4.09 us  [exchange(): lax.all_to_all(value, AXES, split_axis=0, concat_axis=0, axis_index_group...]
    unnamed x14 -> x22, local copies, waits for them, and re-layouts: 3.27 us -> 6.8 us
    ppermute x1, starting transfers between devices: 8.79 us -> 6.48 us  [body(): other = lax.ppermute(send, AXES, CORE_SWAP)]
    pallas_call x6 -> x7, Pallas kernels: 14.9 us -> 16.6 us  [call(): pl.pallas_call(kernel, out_shape=outs, in_specs=[pl.BlockSpec(memory_spac...]
  transfers between devices with their start and end apart: 2 -> 7, of which waited for: 0 -> 3; matrix products, arithmetic and copies ran while one was open for 0% -> 0% of each run, Pallas kernels for 1% -> 7%
where the time goes in v2:
time: 114 us; the launch traced here: 112 us
  starting transfers between devices  37 us (32%)
  blocking collectives  31 us (27%)
  waiting for transfers between devices  19.8 us (17%)
  Pallas kernels  16.6 us (15%)
  local copies, waits for them, and re-layouts  6.8 us (6%)
    all_to_all x2, blocking collectives, exchange(): lax.all_to_all(value, AXES, split_axis=0, concat_axis=0, axis_index_group...  31 us
    pallas_call x7, Pallas kernels, call(): pl.pallas_call(kernel, out_shape=outs, in_specs=[pl.BlockSpec(memory_spac...  16.6 us
    ppermute x1, waiting for transfers between devices, body(): far = lax.ppermute(near, AXES, from_z(2))  12.5 us
    ppermute x1, starting transfers between devices, body(): far = lax.ppermute(key_weight, AXES, from_z(4))  9.65 us
    all_to_all x2, starting transfers between devices, exchange(): lax.all_to_all(value, AXES, split_axis=0, concat_axis=0, axis_index_group...  7.79 us
    unnamed x22, local copies, waits for them, and re-layouts  6.8 us
    ppermute x1, starting transfers between devices, body(): other = lax.ppermute(send, AXES, CORE_SWAP)  6.48 us
    ppermute x1, starting transfers between devices, body(): far = lax.ppermute(near, AXES, from_z(1))  5.06 us
  transfers between devices with their start and end apart: 7, of which 3 were waited for; matrix products, arithmetic and copies ran while one was open for 0% of the time, Pallas kernels for 7%

profile of v2, /device:TPU:1, one launch (start us, length us, event | category | flops | bytes accessed | tf_op | source)
XLA Modules:
  0.0 111.9 jit_solution(4377844330880842537)
XLA Ops:
  0.6 9.6 %collective-permute-start = (bf16[128,512]{1,0:T(8,128)(2,1)}, bf16[128,512]{1,0:T(8,128)(2,1)S(1)}, u32[]{:S(2)}, u32[]{:S(2)}) collective-permute-start(bf16[128,512]{1,0:T(8,128)(2,1)} %own_ref.1), channel_id=1, source_target_pairs={{4,0},{5,1},{6,2},{7,3},{64,4},{65,5},{66,6},{67,7},{12,8},{13,9},... | collective-permute-start | bytes 393224 | tf_op jit(solution)/shard_map/weight_z4/ppermute | solution.py:270
  10.3 0.0 copy-start.1
  10.3 1.6 %copy-done.1 = bf16[256,4096]{1,0:T(8,128)(2,1)S(1)} copy-done((bf16[256,4096]{1,0:T(8,128)(2,1)S(1)}, bf16[256,4096]{1,0:T(8,128)(2,1)}, u32[]{:S(2)}) %copy-start.1) | copy-done | bytes 2097176
  11.9 0.9 copy-done.3
  12.8 0.7 copy-done.8
  13.6 3.3 %norm.1 = (bf16[8,256,256]{2,1,0:T(8,128)(2,1)S(1)}, bf16[10,256,256]{2,1,0:T(8,128)(2,1)}, f32[256,128]{1,0:T(8,128)S(1)}) custom-call(bf16[256,4096]{1,0:T(8,128)(2,1)S(1)} %copy-done.1, bf16[256,512]{1,0:T(8,128)(2,1)S(1)} %copy-done.3, f32[1,4096]{1,0:T(1,128)S(1)} %bitcast.2), custom_call_target="tpu_custom_call" | custom-call | tf_op jit(solution)/shard_map/norm/pallas_call | solution.py:72
  16.9 1.0 copy-done.5
  17.9 0.0 collective-permute-done.far_ref
  17.9 6.5 %collective-permute-start.1 = (bf16[10,256,256]{2,1,0:T(8,128)(2,1)}, bf16[10,256,256]{2,1,0:T(8,128)(2,1)S(1)}, u32[]{:S(2)}, u32[]{:S(2)}) collective-permute-start(bf16[10,256,256]{2,1,0:T(8,128)(2,1)} %get-tuple-element.13), channel_id=1, source_target_pairs={{0,32},{1,33},{2,34},{3,35},{4,36},{5,37},{6,38},{7,39},{8,40},{9,... | collective-permute-start | bytes 3932168 | tf_op jit(solution)/shard_map/norm/ppermute | solution.py:282
  24.4 0.8 weight_y.1
  25.2 4.2 %all-to-all-start.1 = ((bf16[4,256,256]{2,1,0:T(8,128)(2,1)}), bf16[4,256,256]{2,1,0:T(8,128)(2,1)S(1)}, u32[]{:S(2)}, u32[]{:S(2)}) async-start(bf16[4,256,256]{2,1,0:T(8,128)(2,1)} %weight_y.1), calls=%async_computation.1 | async-start | bytes 1048576 | tf_op jit(solution)/shard_map/weight_y/all_to_all | solution.py:66
  29.4 1.2 %copy-done.6 = bf16[8,256,256]{2,1,0:T(8,128)(2,1)S(1)} copy-done((bf16[8,256,256]{2,1,0:T(8,128)(2,1)S(1)}, bf16[8,256,256]{2,1,0:T(8,128)(2,1)}, u32[]{:S(2)}) %copy-start.6) | copy-done | bytes 1048600
  30.7 2.7 %squares.1 = bf16[4,1024,256]{2,1,0:T(8,128)(2,1)S(1)} custom-call(bf16[8,256,256]{2,1,0:T(8,128)(2,1)S(1)} %copy-done.6, bf16[10,256,256]{2,1,0:T(8,128)(2,1)S(1)} %collective-permute-done.1.other_ref, bf16[256,512]{1,0:T(8,128)(2,1)S(1)} %copy-done.4), custom_call_target="tpu_custom_call" | custom-call | tf_op jit(solution)/shard_map/squares/pallas_call | solution.py:72
  33.3 0.0 copy-start
  33.3 1.3 %copy-done = bf16[4,1024,256]{2,1,0:T(8,128)(2,1)} copy-done((bf16[4,1024,256]{2,1,0:T(8,128)(2,1)}, bf16[4,1024,256]{2,1,0:T(8,128)(2,1)S(1)}, u32[]{:S(2)}) %copy-start) | copy-done | bytes 2097176
  34.7 4.1 %all-to-all-done.1.near_ref = bf16[4,256,256]{2,1,0:T(8,128)(2,1)S(1)} async-done(((bf16[4,256,256]{2,1,0:T(8,128)(2,1)}), bf16[4,256,256]{2,1,0:T(8,128)(2,1)S(1)}, u32[]{:S(2)}, u32[]{:S(2)}) %all-to-all-start.1) | async-done | bytes 524320 | tf_op jit(solution)/shard_map/weight_y/all_to_all | solution.py:66
  38.7 3.6 %all-to-all-start = ((bf16[4,1024,256]{2,1,0:T(8,128)(2,1)}), bf16[4,1024,256]{2,1,0:T(8,128)(2,1)S(1)}, u32[]{:S(2)}, u32[]{:S(2)}) async-start(bf16[4,1024,256]{2,1,0:T(8,128)(2,1)} %copy-done), calls=%async_computation | async-start | bytes 4194304 | tf_op jit(solution)/shard_map/ring_a/all_to_all | solution.py:66
  42.4 3.1 %collective-permute-start.2 = (bf16[4,256,256]{2,1,0:T(8,128)(2,1)S(1)}, bf16[4,256,256]{2,1,0:T(8,128)(2,1)S(1)}, u32[]{:S(2)}, u32[]{:S(2)}) collective-permute-start(bf16[4,256,256]{2,1,0:T(8,128)(2,1)S(1)} %all-to-all-done.1.near_ref), channel_id=1, source_target_pairs={{2,0},{3,1},{4,2},{5,3},{6,4},{7,5},{64,6},{65,7},{10,8},{11,9},{1... | collective-permute-start | bytes 1572872 | tf_op jit(solution)/shard_map/weight_z2/ppermute | solution.py:289
  45.5 12.5 %collective-permute-done.2.far_ref = bf16[4,256,256]{2,1,0:T(8,128)(2,1)S(1)} collective-permute-done((bf16[4,256,256]{2,1,0:T(8,128)(2,1)S(1)}, bf16[4,256,256]{2,1,0:T(8,128)(2,1)S(1)}, u32[]{:S(2)}, u32[]{:S(2)}) %collective-permute-start.2) | collective-permute-done | bytes 524320 | tf_op jit(solution)/shard_map/weight_z2/ppermute | solution.py:289
  58.0 0.3 middle.1
  58.3 0.0 copy-start.10
  58.3 0.0 copy-start.2
  58.3 0.0 copy-start.9
  58.3 5.1 %collective-permute-start.3 = (bf16[8,256,256]{2,1,0:T(8,128)(2,1)S(1)}, bf16[8,256,256]{2,1,0:T(8,128)(2,1)S(1)}, u32[]{:S(2)}, u32[]{:S(2)}) collective-permute-start(bf16[8,256,256]{2,1,0:T(8,128)(2,1)S(1)} %get-tuple-element.16.near_ref), channel_id=1, source_target_pairs={{1,0},{2,1},{3,2},{4,3},{5,4},{6,5},{7,6},{64,7},{9,8},{10,9},{11,... | collective-permute-start | bytes 3145736 | tf_op jit(solution)/shard_map/weight_z1/ppermute | solution.py:305
  63.4 9.9 %all_to_all.20.in_ref = bf16[4,256,256]{2,1,0:T(8,128)(2,1)S(1)} all-to-all(bf16[4,256,256]{2,1,0:T(8,128)(2,1)S(1)} %get-tuple-element.15), channel_id=1, replica_groups={{32,160,288,416},{40,168,296,424},{48,176,304,432},{56,184,312,440},{0,..., dimensions={0} | all-to-all | bytes 1048576 | tf_op jit(solution)/shard_map/ring_b/all_to_all | solution.py:66
  73.2 3.2 %collective-permute-done.3.far_ref = bf16[8,256,256]{2,1,0:T(8,128)(2,1)S(1)} collective-permute-done((bf16[8,256,256]{2,1,0:T(8,128)(2,1)S(1)}, bf16[8,256,256]{2,1,0:T(8,128)(2,1)S(1)}, u32[]{:S(2)}, u32[]{:S(2)}) %collective-permute-start.3) | collective-permute-done | bytes 1048608 | tf_op jit(solution)/shard_map/weight_z1/ppermute | solution.py:305
  76.4 0.2 split.1
  76.5 4.9 %collective-permute-start.4 = (bf16[16,256,256]{2,1,0:T(8,128)(2,1)S(1)}, bf16[16,256,256]{2,1,0:T(8,128)(2,1)S(1)}, u32[]{:S(2)}, u32[]{:S(2)}) collective-permute-start(bf16[16,256,256]{2,1,0:T(8,128)(2,1)S(1)} %get-tuple-element.19.own_ref), channel_id=1, source_target_pairs={{0,32},{1,33},{2,34},{3,35},{4,36},{5,37},{6,38},{7,39},{8,40},{9,... | collective-permute-start | bytes 6291464 | tf_op jit(solution)/shard_map/weight_swap/ppermute | solution.py:317
  81.4 21.2 %all_to_all.21.in_ref = bf16[16,16,256]{2,1,0:T(8,128)(2,1)S(1)} all-to-all(bf16[16,16,256]{2,1,0:T(8,128)(2,1)S(1)} %get-tuple-element.17), channel_id=1, replica_groups={{0,1,2,3,4,5,6,7,64,65,66,67,68,69,70,71},{8,9,10,11,12,13,14,15,72,73,..., dimensions={0} | all-to-all | bytes 262144 | tf_op jit(solution)/shard_map/ring_z/all_to_all | solution.py:66
  102.6 0.8 serve.1
  103.4 0.0 collective-permute-done.4.other_ref
  103.4 8.5 %input_grad.1 = bf16[256,4096]{1,0:T(8,128)(2,1)} custom-call(bf16[256,4096]{1,0:T(8,128)(2,1)S(1)} %copy-done.2, bf16[256,512]{1,0:T(8,128)(2,1)S(1)} %copy-done.4, f32[1,4096]{1,0:T(1,128)S(1)} %bitcast.3, f32[256,128]{1,0:T(8,128)S(1)} %get-tuple-element.18.inv_ref, bf16[16,256,256]{2,1,0:T(8,128)(2,1)S(1)} %get-tuple-element.19.own_ref, ...), custom_call_target="tpu_custom_call" | custom-call | tf_op jit(solution)/shard_map/input_grad/pallas_call | solution.py:72
  (13 shorter events, 0.0 us)
Async XLA Ops:
  0.6 17.3 %collective-permute-start = (bf16[128,512]{1,0:T(8,128)(2,1)}, bf16[128,512]{1,0:T(8,128)(2,1)S(1)}, u32[]{:S(2)}, u32[]{:S(2)}) collective-permute-start(bf16[128,512]{1,0:T(8,128)(2,1)} %own_ref.1), channel_id=1, source_target_pairs={{4,0},{5,1},{6,2},{7,3},{64,4},{65,5},{66,6},{67,7},{12,8},{13,9},... | collective-permute-start | bytes 393224 | tf_op jit(solution)/shard_map/weight_z4/ppermute | solution.py:270
  10.3 1.6 %copy-start.1 = (bf16[256,4096]{1,0:T(8,128)(2,1)S(1)}, bf16[256,4096]{1,0:T(8,128)(2,1)}, u32[]{:S(2)}) copy-start(bf16[256,4096]{1,0:T(8,128)(2,1)} %hidden_ref.1) | copy-start | bytes 6291460
  11.9 0.9 copy-start.3
  12.8 0.7 copy-start.8
  13.5 10.8 %copy-start.7 = (bf16[128,512]{1,0:T(8,128)(2,1)S(1)}, bf16[128,512]{1,0:T(8,128)(2,1)}, u32[]{:S(2)}) copy-start(bf16[128,512]{1,0:T(8,128)(2,1)} %own_ref.1) | copy-start | bytes 393220
  13.5 15.9 %copy-start.4 = (bf16[256,512]{1,0:T(8,128)(2,1)S(1)}, bf16[256,512]{1,0:T(8,128)(2,1)}, u32[]{:S(2)}) copy-start(bf16[256,512]{1,0:T(8,128)(2,1)} %key_ref.3) | copy-start | bytes 786436
  16.9 1.0 copy-start.5
  17.9 11.5 %collective-permute-start.1 = (bf16[10,256,256]{2,1,0:T(8,128)(2,1)}, bf16[10,256,256]{2,1,0:T(8,128)(2,1)S(1)}, u32[]{:S(2)}, u32[]{:S(2)}) collective-permute-start(bf16[10,256,256]{2,1,0:T(8,128)(2,1)} %get-tuple-element.13), channel_id=1, source_target_pairs={{0,32},{1,33},{2,34},{3,35},{4,36},{5,37},{6,38},{7,39},{8,40},{9,... | collective-permute-start | bytes 3932168 | tf_op jit(solution)/shard_map/norm/ppermute | solution.py:282
  25.2 13.5 %all-to-all-start.1 = ((bf16[4,256,256]{2,1,0:T(8,128)(2,1)}), bf16[4,256,256]{2,1,0:T(8,128)(2,1)S(1)}, u32[]{:S(2)}, u32[]{:S(2)}) async-start(bf16[4,256,256]{2,1,0:T(8,128)(2,1)} %weight_y.1), calls=%async_computation.1 | async-start | bytes 1048576 | tf_op jit(solution)/shard_map/weight_y/all_to_all | solution.py:66
  29.4 1.2 %copy-start.6 = (bf16[8,256,256]{2,1,0:T(8,128)(2,1)S(1)}, bf16[8,256,256]{2,1,0:T(8,128)(2,1)}, u32[]{:S(2)}) copy-start(bf16[8,256,256]{2,1,0:T(8,128)(2,1)} %copy-done.5) | copy-start | bytes 3145732
  33.3 1.3 %copy-start = (bf16[4,1024,256]{2,1,0:T(8,128)(2,1)}, bf16[4,1024,256]{2,1,0:T(8,128)(2,1)S(1)}, u32[]{:S(2)}) copy-start(bf16[4,1024,256]{2,1,0:T(8,128)(2,1)S(1)} %squares.1) | copy-start | bytes 6291460
  38.7 19.2 %all-to-all-start = ((bf16[4,1024,256]{2,1,0:T(8,128)(2,1)}), bf16[4,1024,256]{2,1,0:T(8,128)(2,1)S(1)}, u32[]{:S(2)}, u32[]{:S(2)}) async-start(bf16[4,1024,256]{2,1,0:T(8,128)(2,1)} %copy-done), calls=%async_computation | async-start | bytes 4194304 | tf_op jit(solution)/shard_map/ring_a/all_to_all | solution.py:66
  42.4 15.6 %collective-permute-start.2 = (bf16[4,256,256]{2,1,0:T(8,128)(2,1)S(1)}, bf16[4,256,256]{2,1,0:T(8,128)(2,1)S(1)}, u32[]{:S(2)}, u32[]{:S(2)}) collective-permute-start(bf16[4,256,256]{2,1,0:T(8,128)(2,1)S(1)} %all-to-all-done.1.near_ref), channel_id=1, source_target_pairs={{2,0},{3,1},{4,2},{5,3},{6,4},{7,5},{64,6},{65,7},{10,8},{11,9},{1... | collective-permute-start | bytes 1572872 | tf_op jit(solution)/shard_map/weight_z2/ppermute | solution.py:289
  58.3 44.3 %copy-start.10 = (s32[512]{0:T(512)S(1)}, s32[512]{0:T(512)}, u32[]{:S(2)}) copy-start(s32[512]{0:T(512)} %param.9) | copy-start | bytes 6148
  58.3 45.2 %copy-start.2 = (bf16[256,4096]{1,0:T(8,128)(2,1)S(1)}, bf16[256,4096]{1,0:T(8,128)(2,1)}, u32[]{:S(2)}) copy-start(bf16[256,4096]{1,0:T(8,128)(2,1)} %hidden_ref.1) | copy-start | bytes 6291460
  58.3 45.1 %copy-start.9 = (f32[4096]{0:T(1024)S(1)}, f32[4096]{0:T(1024)}, u32[]{:S(2)}) copy-start(f32[4096]{0:T(1024)} %param.8) | copy-start | bytes 49156
  58.3 18.1 %collective-permute-start.3 = (bf16[8,256,256]{2,1,0:T(8,128)(2,1)S(1)}, bf16[8,256,256]{2,1,0:T(8,128)(2,1)S(1)}, u32[]{:S(2)}, u32[]{:S(2)}) collective-permute-start(bf16[8,256,256]{2,1,0:T(8,128)(2,1)S(1)} %get-tuple-element.16.near_ref), channel_id=1, source_target_pairs={{1,0},{2,1},{3,2},{4,3},{5,4},{6,5},{7,6},{64,7},{9,8},{10,9},{11,... | collective-permute-start | bytes 3145736 | tf_op jit(solution)/shard_map/weight_z1/ppermute | solution.py:305
  76.5 26.9 %collective-permute-start.4 = (bf16[16,256,256]{2,1,0:T(8,128)(2,1)S(1)}, bf16[16,256,256]{2,1,0:T(8,128)(2,1)S(1)}, u32[]{:S(2)}, u32[]{:S(2)}) collective-permute-start(bf16[16,256,256]{2,1,0:T(8,128)(2,1)S(1)} %get-tuple-element.19.own_ref), channel_id=1, source_target_pairs={{0,32},{1,33},{2,34},{3,35},{4,36},{5,37},{6,38},{7,39},{8,40},{9,... | collective-permute-start | bytes 6291464 | tf_op jit(solution)/shard_map/weight_swap/ppermute | solution.py:317

commit v3 on v2

v3 whole, which is shorter than its diff:
```python
import jax
import jax.numpy as jnp
from jax import lax
from jax.experimental import pallas as pl
from jax.experimental.pallas import tpu as pltpu
from jax.sharding import PartitionSpec as P

AXES = ("dp", "fsdp")
NX, NZH, NC, NY, NZL = 4, 2, 2, 4, 8
D, K = 4096, 512
SEQ = 256
TOKENS = SEQ * NX * NZH * NC * NY * NZL
COLS = 256
BF16, F32 = jnp.bfloat16, jnp.float32


def device(x, zh, c, y, zl):
    return (((x * NZH + zh) * NC + c) * NY + y) * NZL + zl


def places():
    return [
        (x, zh, c, y, zl)
        for x in range(NX)
        for zh in range(NZH)
        for c in range(NC)
        for y in range(NY)
        for zl in range(NZL)
    ]


def ring_groups(first):
    groups = []
    for zh in range(NZH):
        for zl in range(NZL):
            groups += [[device(x, zh, first, y, zl) for x in range(NX)] for y in range(NY)]
            groups += [[device(x, zh, 1 - first, y, zl) for y in range(NY)] for x in range(NX)]
    return groups


def from_z(distance):
    pairs = []
    for x, zh, c, y, zl in places():
        z = (zh * NZL + zl + (distance if c == 0 else -distance)) % (NZH * NZL)
        pairs.append((device(x, z // NZL, c, y, z % NZL), device(x, zh, c, y, zl)))
    return pairs


Y_RINGS = [
    [device(x, zh, c, y, zl) for y in range(NY)]
    for x in range(NX)
    for zh in range(NZH)
    for c in range(NC)
    for zl in range(NZL)
]
Z_RINGS = [
    [device(x, zh, c, y, zl) for zh in range(NZH) for zl in range(NZL)]
    for x in range(NX)
    for c in range(NC)
    for y in range(NY)
]
CORE_SWAP = [(device(x, zh, c, y, zl), device(x, zh, 1 - c, y, zl)) for x, zh, c, y, zl in places()]


def exchange(value, groups):
    return lax.all_to_all(
        value, AXES, split_axis=0, concat_axis=0, axis_index_groups=groups, tiled=True
    )


def call(kernel, outs, ins, in_spaces, out_spaces, scratch=(), mib=24, us=1.0):
    return pl.pallas_call(
        kernel,
        out_shape=outs,
        in_specs=[pl.BlockSpec(memory_space=space) for space in in_spaces],
        out_specs=jax.tree.map(lambda space: pl.BlockSpec(memory_space=space), out_spaces),
        scratch_shapes=list(scratch),
        compiler_params=pltpu.CompilerParams(vmem_limit_bytes=mib and mib * 2**20),
        cost_estimate=pl.CostEstimate(
            flops=0, bytes_accessed=int(us * 3.0e6), transcendentals=0
        ),
    )(*ins)


def my_core():
    return lax.rem(lax.axis_index("dp"), NC)


def shape(dims, dtype=BF16):
    return jax.ShapeDtypeStruct(dims, dtype)


def start(source, target, sem):
    copy = pltpu.make_async_copy(source, target, sem)
    copy.start()
    return copy


def norm_kernel(
    hidden_hbm, key_hbm, gain_hbm, own_hbm, send_hbm, inv_hbm,
    hidden_ref, key_ref, gain_ref, own_ref, send_ref, inv_ref, in_sems, out_sems,
):
    core = my_core()
    step, parts, blocks = 16, 4, NX * NZH
    rows_each = SEQ // parts
    pieces = [pl.ds(i * rows_each, rows_each) for i in range(parts)]
    gain_copy = start(gain_hbm, gain_ref, in_sems.at[parts])
    copies = [
        start(hidden_hbm.at[rows], hidden_ref.at[rows], in_sems.at[i])
        for i, rows in enumerate(pieces)
    ]
    key_copy = start(key_hbm, key_ref, in_sems.at[parts + 1])

    def rows_of(i, carry):
        rows = pl.ds(pl.multiple_of(i * step, step), step)
        squares = jnp.zeros((step, 512), F32)
        for t in range(0, D, 512):
            values = hidden_ref[rows, t : t + 512].astype(F32)
            squares += values * values
        inv = lax.rsqrt(jnp.sum(squares, axis=-1, keepdims=True) * (1.0 / D) + 1e-06)
        inv_ref[rows, :] = jnp.broadcast_to(inv, (step, 128))
        for ref, part in ((own_ref, core), (send_ref, 1 - core)):
            for k in range(blocks):
                cols = pl.ds(pl.multiple_of((2 * k + part) * COLS, COLS), COLS)
                unit = hidden_ref[rows, cols].astype(F32) * inv
                ref[k, rows, :] = (unit * gain_ref[:, cols]).astype(BF16)
        return carry

    gain_copy.wait()
    out_copies = []
    for i, rows in enumerate(pieces):
        copies[i].wait()
        lax.fori_loop(i * rows_each // step, (i + 1) * rows_each // step, rows_of, 0)
        out_copies += [
            start(send_ref.at[:, rows], send_hbm.at[pl.ds(0, blocks), rows], out_sems.at[2 * i]),
            start(own_ref.at[:, rows], own_hbm.at[:, rows], out_sems.at[2 * i + 1]),
        ]
    key_copy.wait()
    for half in range(2):
        source = key_ref.at[:, pl.ds(half * COLS, COLS)]
        out_copies.append(start(source, send_hbm.at[blocks + half], out_sems.at[2 * parts + half]))
    out_copies.append(start(inv_ref, inv_hbm, out_sems.at[2 * parts + 2]))
    for copy in out_copies:
        copy.wait()


def piece_kernel(own_hbm, far_hbm, out_hbm, sems):
    cols = pl.ds(pl.multiple_of(my_core() * COLS, COLS), COLS)
    copies = []
    for y in range(NY):
        for i, source in enumerate((own_hbm, far_hbm)):
            target = out_hbm.at[y, pl.ds(i * 128, 128)]
            copies.append(start(source.at[:, cols], target, sems.at[2 * y + i]))
    for copy in copies:
        copy.wait()


def square_kernel(
    own_hbm, other_hbm, key_hbm, out_hbm, own_ref, other_ref, key_ref, out_ref, in_sems, out_sems
):
    core = my_core()
    blocks = NX * NZH
    over_tokens = (((0,), (0,)), ((), ()))
    keys = [
        start(key_hbm, key_ref, in_sems.at[0]),
        start(other_hbm.at[pl.ds(blocks, 2)], other_ref.at[pl.ds(blocks, 2)], in_sems.at[1]),
    ]
    copies = []
    for part in range(4):
        some = pl.ds(2 * part, 2)
        copies += [
            start(own_hbm.at[some], own_ref.at[some], in_sems.at[2 + 2 * part]),
            start(other_hbm.at[some], other_ref.at[some], in_sems.at[3 + 2 * part]),
        ]
    for copy in keys:
        copy.wait()
    key_other = jnp.concatenate([other_ref[blocks], other_ref[blocks + 1]], axis=1)

    out_copies = []
    for k in range(blocks):
        x, zh = k // NZH, k % NZH
        if zh == 0:
            copies[2 * x].wait()
            copies[2 * x + 1].wait()
        g0 = lax.dot_general(own_ref[k], key_ref[...], over_tokens, preferred_element_type=F32)
        g1 = lax.dot_general(other_ref[k], key_other, over_tokens, preferred_element_type=F32)
        total = ((g0 * g0 + g1 * g1) * (1.0 / TOKENS)).astype(BF16)
        for y in range(NY):
            rows = slice(y * 64, (y + 1) * 64)
            out_ref[k, y, 0:64, :] = total[rows, 0:COLS]
            out_ref[k, y, 64:128, :] = total[rows, COLS:K]
            chunk = jnp.where(core == 0, x, y)
            place = pl.multiple_of(jnp.where(core == 0, y, x) * 256 + zh * 128, 128)
            target = out_hbm.at[chunk, pl.ds(place, 128)]
            out_copies.append(start(out_ref.at[k, y], target, out_sems.at[k, y]))
    for copy in out_copies:
        copy.wait()


def middle_kernel(in_ref, out_ref):
    for b in range(4):
        rows = slice(b * 256, (b + 1) * 256)
        total = in_ref[0, rows, :].astype(F32)
        for j in range(1, 4):
            total += in_ref[j, rows, :].astype(F32)
        out_ref[b] = total.astype(BF16)


def join_kernel(near_hbm, far_hbm, out_hbm, sems):
    copies = [
        start(near_hbm, out_hbm.at[pl.ds(0, 4)], sems.at[0]),
        start(far_hbm, out_hbm.at[pl.ds(4, 4)], sems.at[1]),
    ]
    for copy in copies:
        copy.wait()


def split_kernel(in_ref, out_ref):
    total = in_ref[0].astype(F32)
    for j in range(1, 4):
        total += in_ref[j].astype(F32)
    total = total.reshape(NZH, 2, NZL, 8, COLS)
    for zh in range(NZH):
        for zl in range(NZL):
            rows = jnp.concatenate([total[zh, 0, zl], total[zh, 1, zl]], axis=0)
            out_ref[zh * NZL + zl] = rows.astype(BF16)


def serve_kernel(order_hbm, in_ref, out_ref, order_ref, sem):
    copy = start(order_hbm, order_ref, sem)
    total = in_ref[0].astype(F32)
    for z in range(1, NZH * NZL):
        total += in_ref[z].astype(F32)
    fisher = jnp.concatenate([total[0:8], total[8:16]], axis=1).astype(BF16)
    copy.wait()
    column = lax.broadcasted_iota(jnp.int32, (K, K), 0)
    pick = jnp.where(column == order_ref[...], 1.0, 0.0).astype(BF16)
    out_ref[...] = jnp.dot(fisher, pick, preferred_element_type=F32).astype(BF16)


def input_kernel(
    hidden_hbm, key_hbm, gain_hbm, inv_hbm, own_a, own_b, other_a, other_b, out_hbm,
    hidden_ref, key_ref, gain_ref, inv_ref, own_ref, other_ref, back_ref, out_ref,
    in_sems, out_sems,
):
    first = [
        start(key_hbm, key_ref, in_sems.at[0]),
        start(own_a, own_ref.at[pl.ds(0, 8)], in_sems.at[1]),
        start(other_a, other_ref.at[pl.ds(0, 8)], in_sems.at[2]),
        start(own_b, own_ref.at[pl.ds(8, 8)], in_sems.at[3]),
        start(other_b, other_ref.at[pl.ds(8, 8)], in_sems.at[4]),
    ]
    second = [
        start(gain_hbm, gain_ref, in_sems.at[5]),
        start(inv_hbm, inv_ref, in_sems.at[6]),
        start(hidden_hbm, hidden_ref, in_sems.at[7]),
    ]
    for copy in first:
        copy.wait()
    core = my_core()
    z_here = lax.rem(lax.axis_index("fsdp"), NZL)
    own_cols = pl.ds(pl.multiple_of(core * COLS, COLS), COLS)
    other_cols = pl.ds(pl.multiple_of((1 - core) * COLS, COLS), COLS)
    keys = jnp.concatenate([key_ref[:, own_cols], key_ref[:, other_cols]], axis=1)
    sign = 1 - 2 * core

    def shard(ref, y, zl, sign):
        away = (sign * (zl - z_here)) & (NZL - 1)
        index = (away & 1) * 8 + ((away >> 1) & 1) * 4 + y
        return ref[index, pl.ds(pl.multiple_of((away >> 2) * 128, 128), 128), :]

    def tile(t, carry):
        y, pair = t // 4, t % 4
        weight = jnp.concatenate(
            [
                jnp.concatenate(
                    [shard(own_ref, y, 2 * pair + i, sign), shard(other_ref, y, 2 * pair + i, -sign)],
                    axis=1,
                )
                for i in range(2)
            ],
            axis=0,
        )
        cols = pl.ds(pl.multiple_of(t * 256, 256), 256)
        back_ref[:, cols] = lax.dot_general(
            keys, weight, (((1,), (1,)), ((), ())), preferred_element_type=F32
        )
        return carry

    lax.fori_loop(0, D // 256, tile, 0)
    for copy in second:
        copy.wait()

    step, parts, width = 16, 4, 512

    def rows_of(i, carry):
        rows = pl.ds(pl.multiple_of(i * step, step), step)
        inv = inv_ref[rows, 0:1]
        total = jnp.zeros((step, width), F32)
        for t in range(0, D, width):
            cols = slice(t, t + width)
            du = back_ref[rows, cols] * gain_ref[:, cols]
            total += du * hidden_ref[rows, cols].astype(F32)
        mean = inv * jnp.sum(total, axis=-1, keepdims=True) * (1.0 / D)
        factor = inv * inv * mean
        for t in range(0, D, width):
            cols = slice(t, t + width)
            du = back_ref[rows, cols] * gain_ref[:, cols]
            out = du * inv - hidden_ref[rows, cols].astype(F32) * factor
            out_ref[rows, cols] = out.astype(BF16)
        return carry

    rows_each = SEQ // parts
    copies = []
    for i in range(parts):
        lax.fori_loop(i * rows_each // step, (i + 1) * rows_each // step, rows_of, 0)
        rows = pl.ds(i * rows_each, rows_each)
        copies.append(start(out_ref.at[rows], out_hbm.at[rows], out_sems.at[i]))
    for copy in copies:
        copy.wait()


def body(hidden_in, key_grad, key_weight, norm_gain, head_order):
    gain = norm_gain.reshape(1, D)
    vmem, hbm, any_ = pltpu.VMEM, pltpu.HBM, pl.ANY
    dma = pltpu.SemaphoreType.DMA
    blocks = NX * NZH
    barrier = lax.optimization_barrier

    with jax.named_scope("weight_z4"):
        far = lax.ppermute(key_weight, AXES, from_z(4))
    with jax.named_scope("norm"):
        own, send, inv = call(
            norm_kernel,
            (shape((blocks, SEQ, COLS)), shape((blocks + 2, SEQ, COLS)), shape((SEQ, 128), F32)),
            (hidden_in, key_grad, gain),
            (any_,) * 3,
            (hbm, hbm, hbm),
            [
                pltpu.VMEM((SEQ, D), BF16),
                pltpu.VMEM((SEQ, K), BF16),
                pltpu.VMEM((1, D), F32),
                pltpu.VMEM((blocks, SEQ, COLS), BF16),
                pltpu.VMEM((blocks, SEQ, COLS), BF16),
                pltpu.VMEM((SEQ, 128), F32),
                dma((6,)),
                dma((11,)),
            ],
            mib=None,
            us=3.5,
        )
        far, send = barrier((far, send))
        other = lax.ppermute(send, AXES, CORE_SWAP)
    with jax.named_scope("weight_y"):
        pieces = call(
            piece_kernel, shape((NY, 256, COLS)), (key_weight, far), (any_, any_), hbm, [dma((8,))]
        )
        near = exchange(pieces, Y_RINGS)
    with jax.named_scope("squares"):
        chunks = call(
            square_kernel,
            shape((4, 1024, COLS)),
            (own, other, key_grad),
            (any_,) * 3,
            hbm,
            [
                pltpu.VMEM((blocks, SEQ, COLS), BF16),
                pltpu.VMEM((blocks + 2, SEQ, COLS), BF16),
                pltpu.VMEM((SEQ, K), BF16),
                pltpu.VMEM((blocks, NY, 128, COLS), BF16),
                dma((10,)),
                dma((blocks, NY)),
            ],
            mib=51,
            us=3.0,
        )
    with jax.named_scope("weight_z2"):
        far = lax.ppermute(near, AXES, from_z(2))
    with jax.named_scope("ring_a"):
        chunks = exchange(chunks, ring_groups(0))
    with jax.named_scope("middle"):
        chunks = call(middle_kernel, shape((4, 256, COLS)), (chunks,), (vmem,), vmem, us=0.3)
        chunks, far = barrier((chunks, far))
    with jax.named_scope("ring_b"):
        chunks = exchange(chunks, ring_groups(1))
    with jax.named_scope("weight_z1"):
        own_a = call(
            join_kernel, shape((8, 256, COLS)), (near, far), (any_, any_), hbm, [dma((2,))], mib=52
        )
        own_b = lax.ppermute(own_a, AXES, from_z(1))
        other_a = lax.ppermute(own_a, AXES, CORE_SWAP)
    with jax.named_scope("split"):
        parts = call(
            split_kernel, shape((NZH * NZL, 16, COLS)), (chunks,), (vmem,), vmem, us=0.3
        )
        parts, own_b = barrier((parts, own_b))
    with jax.named_scope("ring_z"):
        parts = exchange(parts, Z_RINGS)
    with jax.named_scope("weight_swap"):
        other_b = lax.ppermute(own_b, AXES, CORE_SWAP)
    with jax.named_scope("input_grad"):
        input_grad = call(
            input_kernel,
            shape((SEQ, D)),
            (hidden_in, key_grad, gain, inv, own_a, own_b, other_a, other_b),
            (any_,) * 8,
            hbm,
            [
                pltpu.VMEM((SEQ, D), BF16),
                pltpu.VMEM((SEQ, K), BF16),
                pltpu.VMEM((1, D), F32),
                pltpu.VMEM((SEQ, 128), F32),
                pltpu.VMEM((16, 256, COLS), BF16),
                pltpu.VMEM((16, 256, COLS), BF16),
                pltpu.VMEM((SEQ, D), F32),
                pltpu.VMEM((SEQ, D), BF16),
                dma((8,)),
                dma((4,)),
            ],
            mib=60,
            us=6.0,
        )
        parts, input_grad = barrier((parts, input_grad))
    with jax.named_scope("serve"):
        served = call(
            serve_kernel,
            shape((8, K)),
            (head_order.reshape(1, K), parts),
            (any_, vmem),
            vmem,
            [pltpu.VMEM((1, K), jnp.int32), dma],
            us=0.8,
        )
    return served, input_grad


def solution(mesh):
    in_specs = (P(AXES, None), P(AXES, None), P("fsdp", None), P(), P())
    out_specs = (P(AXES, None), P(AXES, None))
    return jax.shard_map(body, mesh=mesh, in_specs=in_specs, out_specs=out_specs, check_vma=False)
```

time: 114 us -> 106 us (0.930)
  blocking collectives: 31 us -> 0 us
  starting transfers between devices: 37 us -> 54.4 us
  Pallas kernels: 16.6 us -> 22.5 us
  waiting for transfers between devices: 19.8 us -> 24.9 us
  local copies, waits for them, and re-layouts: 6.8 us -> 2.19 us
    all_to_all x2 -> x0, blocking collectives: 31 us -> none  [exchange(): lax.all_to_all(value, AXES, split_axis=0, concat_axis=0, axis_index_group...]
    all_to_all x2 -> x4, waiting for transfers between devices: 4.09 us -> 19.5 us  [exchange(): lax.all_to_all(value, AXES, split_axis=0, concat_axis=0, axis_index_group...]
    all_to_all x2 -> x4, starting transfers between devices: 7.79 us -> 22.3 us  [exchange(): lax.all_to_all(value, AXES, split_axis=0, concat_axis=0, axis_index_group...]
    ppermute x1, waiting for transfers between devices: 12.5 us -> 0.01 us  [body(): far = lax.ppermute(near, AXES, from_z(2))]
    pallas_call x7 -> x8, Pallas kernels: 16.6 us -> 22.5 us  [call(): pl.pallas_call(kernel, out_shape=outs, in_specs=[pl.BlockSpec(memory_spac...]
    ppermute x2 -> x3, starting transfers between devices: 9.95 us -> 15.2 us  [the longest x1 6.78 us: body(): other_a = lax.ppermute(own_a, AXES, CORE_SWAP)]
    unnamed x22 -> x12, local copies, waits for them, and re-layouts: 6.8 us -> 2.19 us
    ppermute x1, waiting for transfers between devices: 0.01 us -> 2.36 us  [body(): far = lax.ppermute(key_weight, AXES, from_z(4))]
  transfers between devices with their start and end apart: 7 -> 10, of which waited for: 3 -> 6; matrix products, arithmetic and copies ran while one was open for 0% -> 0% of each run, Pallas kernels for 7% -> 20%
where the time goes in v3:
time: 106 us; the launch traced here: 105 us
  starting transfers between devices  54.4 us (51%)
  waiting for transfers between devices  24.9 us (23%)
  Pallas kernels  22.5 us (21%)
  local copies, waits for them, and re-layouts  2.19 us (2%)
    pallas_call x8, Pallas kernels, call(): pl.pallas_call(kernel, out_shape=outs, in_specs=[pl.BlockSpec(memory_spac...  22.5 us
    all_to_all x4, starting transfers between devices, exchange(): lax.all_to_all(value, AXES, split_axis=0, concat_axis=0, axis_index_group...  22.3 us
    all_to_all x4, waiting for transfers between devices, exchange(): lax.all_to_all(value, AXES, split_axis=0, concat_axis=0, axis_index_group...  19.5 us
    ppermute x1, starting transfers between devices, body(): far = lax.ppermute(key_weight, AXES, from_z(4))  9.78 us
    ppermute x1, starting transfers between devices, body(): other_a = lax.ppermute(own_a, AXES, CORE_SWAP)  6.78 us
    ppermute x1, starting transfers between devices, body(): other = lax.ppermute(send, AXES, CORE_SWAP)  5.3 us
    ppermute x1, starting transfers between devices, body(): other_b = lax.ppermute(own_b, AXES, CORE_SWAP)  5.27 us
    ppermute x1, starting transfers between devices, body(): own_b = lax.ppermute(own_a, AXES, from_z(1))  3.12 us
  transfers between devices with their start and end apart: 10, of which 6 were waited for; matrix products, arithmetic and copies ran while one was open for 0% of the time, Pallas kernels for 20%

profile of v3, /device:TPU:1, one launch (start us, length us, event | category | flops | bytes accessed | tf_op | source)
XLA Modules:
  0.0 104.8 jit_solution(9166121918267083744)
XLA Ops:
  0.6 0.0 copy-start.2
  0.6 9.8 %collective-permute-start = (bf16[128,512]{1,0:T(8,128)(2,1)}, bf16[128,512]{1,0:T(8,128)(2,1)S(1)}, u32[]{:S(2)}, u32[]{:S(2)}) collective-permute-start(bf16[128,512]{1,0:T(8,128)(2,1)} %own_hbm.1), channel_id=1, source_target_pairs={{4,0},{5,1},{6,2},{7,3},{64,4},{65,5},{66,6},{67,7},{12,8},{13,9},... | collective-permute-start | bytes 393224 | tf_op jit(solution)/shard_map/weight_z4/ppermute | solution.py:331
  10.4 0.0 copy-start
  10.4 4.2 %norm.1 = (bf16[8,256,256]{2,1,0:T(8,128)(2,1)}, bf16[10,256,256]{2,1,0:T(8,128)(2,1)}, f32[256,128]{1,0:T(8,128)}) custom-call(bf16[256,4096]{1,0:T(8,128)(2,1)} %hidden_hbm.3, bf16[256,512]{1,0:T(8,128)(2,1)} %key_hbm.5, f32[1,4096]{1,0:T(1,128)} %bitcast.3), custom_call_target="tpu_custom_call" | custom-call | bytes 10500000 | tf_op jit(solution)/shard_map/norm/pallas_call | solution.py:72
  14.6 2.4 %collective-permute-done.far_hbm = bf16[128,512]{1,0:T(8,128)(2,1)S(1)} collective-permute-done((bf16[128,512]{1,0:T(8,128)(2,1)}, bf16[128,512]{1,0:T(8,128)(2,1)S(1)}, u32[]{:S(2)}, u32[]{:S(2)}) %collective-permute-start) | collective-permute-done | bytes 131104 | tf_op jit(solution)/shard_map/weight_z4/ppermute | solution.py:331
  17.0 5.3 %collective-permute-start.1 = (bf16[10,256,256]{2,1,0:T(8,128)(2,1)}, bf16[10,256,256]{2,1,0:T(8,128)(2,1)S(1)}, u32[]{:S(2)}, u32[]{:S(2)}) collective-permute-start(bf16[10,256,256]{2,1,0:T(8,128)(2,1)} %get-tuple-element.15), channel_id=1, source_target_pairs={{0,32},{1,33},{2,34},{3,35},{4,36},{5,37},{6,38},{7,39},{8,40},{9,... | collective-permute-start | bytes 3932168 | tf_op jit(solution)/shard_map/norm/ppermute | solution.py:353
  22.3 0.9 weight_y.1
  23.2 5.8 %all-to-all-start.1 = ((bf16[4,256,256]{2,1,0:T(8,128)(2,1)}), bf16[4,256,256]{2,1,0:T(8,128)(2,1)S(1)}, u32[]{:S(2)}, u32[]{:S(2)}) async-start(bf16[4,256,256]{2,1,0:T(8,128)(2,1)} %weight_y.1), calls=%async_computation.1 | async-start | bytes 1048576 | tf_op jit(solution)/shard_map/weight_y/all_to_all | solution.py:66
  29.1 0.0 collective-permute-done.1.other_hbm
  29.1 1.2 %copy-done.1 = bf16[8,256,256]{2,1,0:T(8,128)(2,1)S(1)} copy-done((bf16[8,256,256]{2,1,0:T(8,128)(2,1)S(1)}, bf16[8,256,256]{2,1,0:T(8,128)(2,1)}, u32[]{:S(2)}) %copy-start.1) | copy-done | bytes 1048600
  30.3 3.1 %squares.1 = bf16[4,1024,256]{2,1,0:T(8,128)(2,1)} custom-call(bf16[8,256,256]{2,1,0:T(8,128)(2,1)S(1)} %copy-done.1, bf16[10,256,256]{2,1,0:T(8,128)(2,1)S(1)} %collective-permute-done.1.other_hbm, bf16[256,512]{1,0:T(8,128)(2,1)S(1)} %copy-done), custom_call_target="tpu_custom_call" | custom-call | bytes 9000000 | tf_op jit(solution)/shard_map/squares/pallas_call | solution.py:72
  33.4 4.9 %all-to-all-done.1.near_hbm = bf16[4,256,256]{2,1,0:T(8,128)(2,1)S(1)} async-done(((bf16[4,256,256]{2,1,0:T(8,128)(2,1)}), bf16[4,256,256]{2,1,0:T(8,128)(2,1)S(1)}, u32[]{:S(2)}, u32[]{:S(2)}) %all-to-all-start.1) | async-done | bytes 524320 | tf_op jit(solution)/shard_map/weight_y/all_to_all | solution.py:66
  38.4 3.6 %all-to-all-start = ((bf16[4,1024,256]{2,1,0:T(8,128)(2,1)}), bf16[4,1024,256]{2,1,0:T(8,128)(2,1)S(1)}, u32[]{:S(2)}, u32[]{:S(2)}) async-start(bf16[4,1024,256]{2,1,0:T(8,128)(2,1)} %squares.1), calls=%async_computation | async-start | bytes 4194304 | tf_op jit(solution)/shard_map/ring_a/all_to_all | solution.py:66
  42.0 1.9 %collective-permute-start.2 = (bf16[4,256,256]{2,1,0:T(8,128)(2,1)S(1)}, bf16[4,256,256]{2,1,0:T(8,128)(2,1)S(1)}, u32[]{:S(2)}, u32[]{:S(2)}) collective-permute-start(bf16[4,256,256]{2,1,0:T(8,128)(2,1)S(1)} %all-to-all-done.1.near_hbm), channel_id=1, source_target_pairs={{2,0},{3,1},{4,2},{5,3},{6,4},{7,5},{64,6},{65,7},{10,8},{11,9},{1... | collective-permute-start | bytes 1572872 | tf_op jit(solution)/shard_map/weight_z2/ppermute | solution.py:378
  43.9 13.7 %all-to-all-done.in_ref = bf16[4,1024,256]{2,1,0:T(8,128)(2,1)S(1)} async-done(((bf16[4,1024,256]{2,1,0:T(8,128)(2,1)}), bf16[4,1024,256]{2,1,0:T(8,128)(2,1)S(1)}, u32[]{:S(2)}, u32[]{:S(2)}) %all-to-all-start) | async-done | bytes 2097184 | tf_op jit(solution)/shard_map/ring_a/all_to_all | solution.py:66
  57.6 1.0 %middle.1 = bf16[4,256,256]{2,1,0:T(8,128)(2,1)} custom-call(bf16[4,1024,256]{2,1,0:T(8,128)(2,1)S(1)} %all-to-all-done.in_ref), custom_call_target="tpu_custom_call" | custom-call | bytes 900000 | tf_op jit(solution)/shard_map/middle/pallas_call | solution.py:72
  58.7 0.0 collective-permute-done.2.far_hbm
  58.7 1.0 weight_z1.1.own_a
  59.7 3.1 %collective-permute-start.3 = (bf16[8,256,256]{2,1,0:T(8,128)(2,1)}, bf16[8,256,256]{2,1,0:T(8,128)(2,1)S(1)}, u32[]{:S(2)}, u32[]{:S(2)}) collective-permute-start(bf16[8,256,256]{2,1,0:T(8,128)(2,1)} %weight_z1.1.own_a), channel_id=1, source_target_pairs={{1,0},{2,1},{3,2},{4,3},{5,4},{6,5},{7,6},{64,7},{9,8},{10,9},{11,... | collective-permute-start | bytes 3145736 | tf_op jit(solution)/shard_map/weight_z1/ppermute | solution.py:390
  62.8 3.9 %all-to-all-start.2 = ((bf16[4,256,256]{2,1,0:T(8,128)(2,1)}), bf16[4,256,256]{2,1,0:T(8,128)(2,1)S(1)}, u32[]{:S(2)}, u32[]{:S(2)}) async-start(bf16[4,256,256]{2,1,0:T(8,128)(2,1)} %middle.1), calls=%async_computation.2 | async-start | bytes 1048576 | tf_op jit(solution)/shard_map/ring_b/all_to_all | solution.py:66
  66.7 6.8 %collective-permute-start.4 = (bf16[8,256,256]{2,1,0:T(8,128)(2,1)}, bf16[8,256,256]{2,1,0:T(8,128)(2,1)S(1)}, u32[]{:S(2)}, u32[]{:S(2)}) collective-permute-start(bf16[8,256,256]{2,1,0:T(8,128)(2,1)} %weight_z1.1.own_a), channel_id=1, source_target_pairs={{0,32},{1,33},{2,34},{3,35},{4,36},{5,37},{6,38},{7,39},{8,40},{9,... | collective-permute-start | bytes 3145736 | tf_op jit(solution)/shard_map/weight_z1/ppermute | solution.py:391
  73.5 0.1 all-to-all-done.2.in_ref
  73.6 0.7 split.1
  74.4 3.0 %collective-permute-done.3.own_b = bf16[8,256,256]{2,1,0:T(8,128)(2,1)S(1)} collective-permute-done((bf16[8,256,256]{2,1,0:T(8,128)(2,1)}, bf16[8,256,256]{2,1,0:T(8,128)(2,1)S(1)}, u32[]{:S(2)}, u32[]{:S(2)}) %collective-permute-start.3) | collective-permute-done | bytes 1048608 | tf_op jit(solution)/shard_map/weight_z1/ppermute | solution.py:390
  77.3 5.3 %collective-permute-start.5 = (bf16[8,256,256]{2,1,0:T(8,128)(2,1)S(1)}, bf16[8,256,256]{2,1,0:T(8,128)(2,1)}, u32[]{:S(2)}, u32[]{:S(2)}) collective-permute-start(bf16[8,256,256]{2,1,0:T(8,128)(2,1)S(1)} %collective-permute-done.3.own_b), channel_id=1, source_target_pairs={{0,32},{1,33},{2,34},{3,35},{4,36},{5,37},{6,38},{7,39},{8,40},{9,... | collective-permute-start | bytes 3145736 | tf_op jit(solution)/shard_map/weight_swap/ppermute | solution.py:400
  82.6 8.9 %all-to-all-start.3 = ((bf16[16,16,256]{2,1,0:T(8,128)(2,1)}), bf16[16,16,256]{2,1,0:T(8,128)(2,1)S(1)}, u32[]{:S(2)}, u32[]{:S(2)}) async-start(bf16[16,16,256]{2,1,0:T(8,128)(2,1)} %split.1), calls=%async_computation.3 | async-start | bytes 262144 | tf_op jit(solution)/shard_map/ring_z/all_to_all | solution.py:66
  91.5 0.0 collective-permute-done.4.other_a
  91.6 0.0 collective-permute-done.5.other_b
  91.6 1.0 copy-done.5
  92.5 10.7 %input_grad.1 = bf16[256,4096]{1,0:T(8,128)(2,1)} custom-call(bf16[256,4096]{1,0:T(8,128)(2,1)} %hidden_hbm.3, bf16[256,512]{1,0:T(8,128)(2,1)} %key_hbm.5, f32[1,4096]{1,0:T(1,128)} %bitcast.4, f32[256,128]{1,0:T(8,128)} %get-tuple-element.20.inv_hbm, bf16[8,256,256]{2,1,0:T(8,128)(2,1)} %weight_z1.1.own_a, bf16[8,256,256]{2,1,0:T(8,128)(2,1)} %copy-done.4, ...), custom_call_target="tpu_custom_call" | custom-call | bytes 18000000 | tf_op jit(solution)/shard_map/input_grad/pallas_call | solution.py:72
  103.2 0.7 all-to-all-done.3.in_ref
  104.0 0.8 serve.1
  (8 shorter events, 0.0 us)
Async XLA Ops:
  0.6 21.7 %copy-start.2 = (bf16[128,512]{1,0:T(8,128)(2,1)S(1)}, bf16[128,512]{1,0:T(8,128)(2,1)}, u32[]{:S(2)}) copy-start(bf16[128,512]{1,0:T(8,128)(2,1)} %own_hbm.1) | copy-start | bytes 393220
  0.6 16.4 %collective-permute-start = (bf16[128,512]{1,0:T(8,128)(2,1)}, bf16[128,512]{1,0:T(8,128)(2,1)S(1)}, u32[]{:S(2)}, u32[]{:S(2)}) collective-permute-start(bf16[128,512]{1,0:T(8,128)(2,1)} %own_hbm.1), channel_id=1, source_target_pairs={{4,0},{5,1},{6,2},{7,3},{64,4},{65,5},{66,6},{67,7},{12,8},{13,9},... | collective-permute-start | bytes 393224 | tf_op jit(solution)/shard_map/weight_z4/ppermute | solution.py:331
  10.4 18.6 %copy-start = (bf16[256,512]{1,0:T(8,128)(2,1)S(1)}, bf16[256,512]{1,0:T(8,128)(2,1)}, u32[]{:S(2)}) copy-start(bf16[256,512]{1,0:T(8,128)(2,1)} %key_hbm.5) | copy-start | bytes 786436
  17.0 12.1 %collective-permute-start.1 = (bf16[10,256,256]{2,1,0:T(8,128)(2,1)}, bf16[10,256,256]{2,1,0:T(8,128)(2,1)S(1)}, u32[]{:S(2)}, u32[]{:S(2)}) collective-permute-start(bf16[10,256,256]{2,1,0:T(8,128)(2,1)} %get-tuple-element.15), channel_id=1, source_target_pairs={{0,32},{1,33},{2,34},{3,35},{4,36},{5,37},{6,38},{7,39},{8,40},{9,... | collective-permute-start | bytes 3932168 | tf_op jit(solution)/shard_map/norm/ppermute | solution.py:353
  23.2 15.2 %all-to-all-start.1 = ((bf16[4,256,256]{2,1,0:T(8,128)(2,1)}), bf16[4,256,256]{2,1,0:T(8,128)(2,1)S(1)}, u32[]{:S(2)}, u32[]{:S(2)}) async-start(bf16[4,256,256]{2,1,0:T(8,128)(2,1)} %weight_y.1), calls=%async_computation.1 | async-start | bytes 1048576 | tf_op jit(solution)/shard_map/weight_y/all_to_all | solution.py:66
  29.1 1.2 %copy-start.1 = (bf16[8,256,256]{2,1,0:T(8,128)(2,1)S(1)}, bf16[8,256,256]{2,1,0:T(8,128)(2,1)}, u32[]{:S(2)}) copy-start(bf16[8,256,256]{2,1,0:T(8,128)(2,1)} %get-tuple-element.13.own_hbm) | copy-start | bytes 3145732
  38.4 19.2 %all-to-all-start = ((bf16[4,1024,256]{2,1,0:T(8,128)(2,1)}), bf16[4,1024,256]{2,1,0:T(8,128)(2,1)S(1)}, u32[]{:S(2)}, u32[]{:S(2)}) async-start(bf16[4,1024,256]{2,1,0:T(8,128)(2,1)} %squares.1), calls=%async_computation | async-start | bytes 4194304 | tf_op jit(solution)/shard_map/ring_a/all_to_all | solution.py:66
  42.0 16.7 %collective-permute-start.2 = (bf16[4,256,256]{2,1,0:T(8,128)(2,1)S(1)}, bf16[4,256,256]{2,1,0:T(8,128)(2,1)S(1)}, u32[]{:S(2)}, u32[]{:S(2)}) collective-permute-start(bf16[4,256,256]{2,1,0:T(8,128)(2,1)S(1)} %all-to-all-done.1.near_hbm), channel_id=1, source_target_pairs={{2,0},{3,1},{4,2},{5,3},{6,4},{7,5},{64,6},{65,7},{10,8},{11,9},{1... | collective-permute-start | bytes 1572872 | tf_op jit(solution)/shard_map/weight_z2/ppermute | solution.py:378
  59.7 17.6 %collective-permute-start.3 = (bf16[8,256,256]{2,1,0:T(8,128)(2,1)}, bf16[8,256,256]{2,1,0:T(8,128)(2,1)S(1)}, u32[]{:S(2)}, u32[]{:S(2)}) collective-permute-start(bf16[8,256,256]{2,1,0:T(8,128)(2,1)} %weight_z1.1.own_a), channel_id=1, source_target_pairs={{1,0},{2,1},{3,2},{4,3},{5,4},{6,5},{7,6},{64,7},{9,8},{10,9},{11,... | collective-permute-start | bytes 3145736 | tf_op jit(solution)/shard_map/weight_z1/ppermute | solution.py:390
  62.8 10.8 %all-to-all-start.2 = ((bf16[4,256,256]{2,1,0:T(8,128)(2,1)}), bf16[4,256,256]{2,1,0:T(8,128)(2,1)S(1)}, u32[]{:S(2)}, u32[]{:S(2)}) async-start(bf16[4,256,256]{2,1,0:T(8,128)(2,1)} %middle.1), calls=%async_computation.2 | async-start | bytes 1048576 | tf_op jit(solution)/shard_map/ring_b/all_to_all | solution.py:66
  66.7 24.8 %collective-permute-start.4 = (bf16[8,256,256]{2,1,0:T(8,128)(2,1)}, bf16[8,256,256]{2,1,0:T(8,128)(2,1)S(1)}, u32[]{:S(2)}, u32[]{:S(2)}) collective-permute-start(bf16[8,256,256]{2,1,0:T(8,128)(2,1)} %weight_z1.1.own_a), channel_id=1, source_target_pairs={{0,32},{1,33},{2,34},{3,35},{4,36},{5,37},{6,38},{7,39},{8,40},{9,... | collective-permute-start | bytes 3145736 | tf_op jit(solution)/shard_map/weight_z1/ppermute | solution.py:391
  77.3 14.2 %copy-start.4 = (bf16[8,256,256]{2,1,0:T(8,128)(2,1)}, bf16[8,256,256]{2,1,0:T(8,128)(2,1)S(1)}, u32[]{:S(2)}) copy-start(bf16[8,256,256]{2,1,0:T(8,128)(2,1)S(1)} %collective-permute-done.3.own_b) | copy-start | bytes 3145732
  77.3 14.2 %collective-permute-start.5 = (bf16[8,256,256]{2,1,0:T(8,128)(2,1)S(1)}, bf16[8,256,256]{2,1,0:T(8,128)(2,1)}, u32[]{:S(2)}, u32[]{:S(2)}) collective-permute-start(bf16[8,256,256]{2,1,0:T(8,128)(2,1)S(1)} %collective-permute-done.3.own_b), channel_id=1, source_target_pairs={{0,32},{1,33},{2,34},{3,35},{4,36},{5,37},{6,38},{7,39},{8,40},{9,... | collective-permute-start | bytes 3145736 | tf_op jit(solution)/shard_map/weight_swap/ppermute | solution.py:400
  82.6 21.4 %all-to-all-start.3 = ((bf16[16,16,256]{2,1,0:T(8,128)(2,1)}), bf16[16,16,256]{2,1,0:T(8,128)(2,1)S(1)}, u32[]{:S(2)}, u32[]{:S(2)}) async-start(bf16[16,16,256]{2,1,0:T(8,128)(2,1)} %split.1), calls=%async_computation.3 | async-start | bytes 262144 | tf_op jit(solution)/shard_map/ring_z/all_to_all | solution.py:66
  91.5 1.0 copy-start.5
  92.5 11.4 %copy-start.3 = (s32[512]{0:T(512)S(1)}, s32[512]{0:T(512)}, u32[]{:S(2)}) copy-start(s32[512]{0:T(512)} %param.9) | copy-start | bytes 6148

commit v4 on v3

--- a/solution.py
+++ b/solution.py
@@ -29,19 +29,10 @@
     ]
 
 
-def ring_groups(first):
-    groups = []
-    for zh in range(NZH):
-        for zl in range(NZL):
-            groups += [[device(x, zh, first, y, zl) for x in range(NX)] for y in range(NY)]
-            groups += [[device(x, zh, 1 - first, y, zl) for y in range(NY)] for x in range(NX)]
-    return groups
-
-
-def from_z(distance):
+def from_z(above_0, above_1):
     pairs = []
     for x, zh, c, y, zl in places():
-        z = (zh * NZL + zl + (distance if c == 0 else -distance)) % (NZH * NZL)
+        z = (zh * NZL + zl + (above_0, above_1)[c]) % (NZH * NZL)
         pairs.append((device(x, z // NZL, c, y, z % NZL), device(x, zh, c, y, zl)))
     return pairs
 
@@ -49,6 +40,12 @@
 Y_RINGS = [
     [device(x, zh, c, y, zl) for y in range(NY)]
     for x in range(NX)
+    for zh in range(NZH)
+    for c in range(NC)
+    for zl in range(NZL)
+]
+PLANES = [
+    [device(x, zh, c, y, zl) for x in range(NX) for y in range(NY)]
     for zh in range(NZH)
     for c in range(NC)
     for zl in range(NZL)
@@ -68,7 +65,7 @@
     )
 
 
-def call(kernel, outs, ins, in_spaces, out_spaces, scratch=(), mib=24, us=1.0):
+def call(kernel, outs, ins, in_spaces, out_spaces, scratch=(), mib=24, us=0.05):
     return pl.pallas_call(
         kernel,
         out_shape=outs,
@@ -158,7 +155,6 @@
 def square_kernel(
     own_hbm, other_hbm, key_hbm, out_hbm, own_ref, other_ref, key_ref, out_ref, in_sems, out_sems
 ):
-    core = my_core()
     blocks = NX * NZH
     over_tokens = (((0,), (0,)), ((), ()))
     keys = [
@@ -189,41 +185,22 @@
             rows = slice(y * 64, (y + 1) * 64)
             out_ref[k, y, 0:64, :] = total[rows, 0:COLS]
             out_ref[k, y, 64:128, :] = total[rows, COLS:K]
-            chunk = jnp.where(core == 0, x, y)
-            place = pl.multiple_of(jnp.where(core == 0, y, x) * 256 + zh * 128, 128)
-            target = out_hbm.at[chunk, pl.ds(place, 128)]
+            target = out_hbm.at[x * NY + y, pl.ds(zh * 128, 128)]
             out_copies.append(start(out_ref.at[k, y], target, out_sems.at[k, y]))
     for copy in out_copies:
         copy.wait()
 
 
-def middle_kernel(in_ref, out_ref):
-    for b in range(4):
-        rows = slice(b * 256, (b + 1) * 256)
+def split_kernel(in_ref, out_ref):
+    for zh in range(NZH):
+        rows = slice(zh * 128, (zh + 1) * 128)
         total = in_ref[0, rows, :].astype(F32)
-        for j in range(1, 4):
+        for j in range(1, NX * NY):
             total += in_ref[j, rows, :].astype(F32)
-        out_ref[b] = total.astype(BF16)
-
-
-def join_kernel(near_hbm, far_hbm, out_hbm, sems):
-    copies = [
-        start(near_hbm, out_hbm.at[pl.ds(0, 4)], sems.at[0]),
-        start(far_hbm, out_hbm.at[pl.ds(4, 4)], sems.at[1]),
-    ]
-    for copy in copies:
-        copy.wait()
-
-
-def split_kernel(in_ref, out_ref):
-    total = in_ref[0].astype(F32)
-    for j in range(1, 4):
-        total += in_ref[j].astype(F32)
-    total = total.reshape(NZH, 2, NZL, 8, COLS)
-    for zh in range(NZH):
+        total = total.reshape(2, NZL, 8, COLS)
         for zl in range(NZL):
-            rows = jnp.concatenate([total[zh, 0, zl], total[zh, 1, zl]], axis=0)
-            out_ref[zh * NZL + zl] = rows.astype(BF16)
+            both = jnp.concatenate([total[0, zl], total[1, zl]], axis=0)
+            out_ref[zh * NZL + zl] = both.astype(BF16)
 
 
 def serve_kernel(order_hbm, in_ref, out_ref, order_ref, sem):
@@ -239,21 +216,22 @@
 
 
 def input_kernel(
-    hidden_hbm, key_hbm, gain_hbm, inv_hbm, own_a, own_b, other_a, other_b, out_hbm,
+    hidden_hbm, key_hbm, gain_hbm, inv_hbm, own_0, own_1, own_2a, own_2b, own_3,
+    other_0, other_1, other_2a, other_2b, other_3, out_hbm,
     hidden_ref, key_ref, gain_ref, inv_ref, own_ref, other_ref, back_ref, out_ref,
     in_sems, out_sems,
 ):
-    first = [
-        start(key_hbm, key_ref, in_sems.at[0]),
-        start(own_a, own_ref.at[pl.ds(0, 8)], in_sems.at[1]),
-        start(other_a, other_ref.at[pl.ds(0, 8)], in_sems.at[2]),
-        start(own_b, own_ref.at[pl.ds(8, 8)], in_sems.at[3]),
-        start(other_b, other_ref.at[pl.ds(8, 8)], in_sems.at[4]),
-    ]
+    first = [start(key_hbm, key_ref, in_sems.at[0])]
+    for ref, parts in (
+        (own_ref, (own_0, own_1, own_2a, own_2b, own_3)),
+        (other_ref, (other_0, other_1, other_2a, other_2b, other_3)),
+    ):
+        for part, (place, size) in zip(parts, ((0, 4), (4, 4), (8, 2), (10, 2), (12, 4))):
+            first.append(start(part, ref.at[pl.ds(place, size)], in_sems.at[len(first)]))
     second = [
-        start(gain_hbm, gain_ref, in_sems.at[5]),
-        start(inv_hbm, inv_ref, in_sems.at[6]),
-        start(hidden_hbm, hidden_ref, in_sems.at[7]),
+        start(gain_hbm, gain_ref, in_sems.at[11]),
+        start(inv_hbm, inv_ref, in_sems.at[12]),
+        start(hidden_hbm, hidden_ref, in_sems.at[13]),
     ]
     for copy in first:
         copy.wait()
@@ -262,20 +240,20 @@
     own_cols = pl.ds(pl.multiple_of(core * COLS, COLS), COLS)
     other_cols = pl.ds(pl.multiple_of((1 - core) * COLS, COLS), COLS)
     keys = jnp.concatenate([key_ref[:, own_cols], key_ref[:, other_cols]], axis=1)
-    sign = 1 - 2 * core
-
-    def shard(ref, y, zl, sign):
-        away = (sign * (zl - z_here)) & (NZL - 1)
-        index = (away & 1) * 8 + ((away >> 1) & 1) * 4 + y
-        return ref[index, pl.ds(pl.multiple_of((away >> 2) * 128, 128), 128), :]
+
+    def shard(ref, y, zl):
+        away = (zl - z_here) & (NZL - 1)
+        step = away & 3
+        from_below = (step == 3) | ((step == 2) & (y >= 2))
+        second = jnp.where(from_below, 1 - (away >> 2), away >> 2)
+        return ref[step * 4 + y, pl.ds(pl.multiple_of(second * 128, 128), 128), :]
 
     def tile(t, carry):
         y, pair = t // 4, t % 4
         weight = jnp.concatenate(
             [
                 jnp.concatenate(
-                    [shard(own_ref, y, 2 * pair + i, sign), shard(other_ref, y, 2 * pair + i, -sign)],
-                    axis=1,
+                    [shard(own_ref, y, 2 * pair + i), shard(other_ref, y, 2 * pair + i)], axis=1
                 )
                 for i in range(2)
             ],
@@ -328,7 +306,7 @@
     barrier = lax.optimization_barrier
 
     with jax.named_scope("weight_z4"):
-        far = lax.ppermute(key_weight, AXES, from_z(4))
+        far = lax.ppermute(key_weight, AXES, from_z(4, -4))
     with jax.named_scope("norm"):
         own, send, inv = call(
             norm_kernel,
@@ -347,10 +325,9 @@
                 dma((11,)),
             ],
             mib=None,
-            us=3.5,
-        )
+        )
+        other = lax.ppermute(send, AXES, CORE_SWAP)
         far, send = barrier((far, send))
-        other = lax.ppermute(send, AXES, CORE_SWAP)
     with jax.named_scope("weight_y"):
         pieces = call(
             piece_kernel, shape((NY, 256, COLS)), (key_weight, far), (any_, any_), hbm, [dma((8,))]
@@ -359,7 +336,7 @@
     with jax.named_scope("squares"):
         chunks = call(
             square_kernel,
-            shape((4, 1024, COLS)),
+            shape((NX * NY, 256, COLS)),
             (own, other, key_grad),
             (any_,) * 3,
             hbm,
@@ -372,38 +349,28 @@
                 dma((blocks, NY)),
             ],
             mib=51,
-            us=3.0,
-        )
+        )
+    with jax.named_scope("plane"):
+        chunks = exchange(chunks, PLANES)
+    with jax.named_scope("weight_z1"):
+        up = lax.ppermute(near, AXES, from_z(1, 1))
+        down = lax.ppermute(near, AXES, from_z(-1, -1))
     with jax.named_scope("weight_z2"):
-        far = lax.ppermute(near, AXES, from_z(2))
-    with jax.named_scope("ring_a"):
-        chunks = exchange(chunks, ring_groups(0))
-    with jax.named_scope("middle"):
-        chunks = call(middle_kernel, shape((4, 256, COLS)), (chunks,), (vmem,), vmem, us=0.3)
-        chunks, far = barrier((chunks, far))
-    with jax.named_scope("ring_b"):
-        chunks = exchange(chunks, ring_groups(1))
-    with jax.named_scope("weight_z1"):
-        own_a = call(
-            join_kernel, shape((8, 256, COLS)), (near, far), (any_, any_), hbm, [dma((2,))], mib=52
-        )
-        own_b = lax.ppermute(own_a, AXES, from_z(1))
-        other_a = lax.ppermute(own_a, AXES, CORE_SWAP)
+        far_up = lax.ppermute(up[:2], AXES, from_z(1, 1))
+        far_down = lax.ppermute(down[2:], AXES, from_z(-1, -1))
     with jax.named_scope("split"):
-        parts = call(
-            split_kernel, shape((NZH * NZL, 16, COLS)), (chunks,), (vmem,), vmem, us=0.3
-        )
-        parts, own_b = barrier((parts, own_b))
+        parts = call(split_kernel, shape((NZH * NZL, 16, COLS)), (chunks,), (vmem,), vmem)
     with jax.named_scope("ring_z"):
         parts = exchange(parts, Z_RINGS)
     with jax.named_scope("weight_swap"):
-        other_b = lax.ppermute(own_b, AXES, CORE_SWAP)
+        weights = (near, up, far_up, far_down, down)
+        swapped = tuple(lax.ppermute(part, AXES, CORE_SWAP) for part in weights)
     with jax.named_scope("input_grad"):
         input_grad = call(
             input_kernel,
             shape((SEQ, D)),
-            (hidden_in, key_grad, gain, inv, own_a, own_b, other_a, other_b),
-            (any_,) * 8,
+            (hidden_in, key_grad, gain, inv, *weights, *swapped),
+            (any_,) * 14,
             hbm,
             [
                 pltpu.VMEM((SEQ, D), BF16),
@@ -414,11 +381,10 @@
                 pltpu.VMEM((16, 256, COLS), BF16),
                 pltpu.VMEM((SEQ, D), F32),
                 pltpu.VMEM((SEQ, D), BF16),
-                dma((8,)),
+                dma((14,)),
                 dma((4,)),
             ],
             mib=60,
-            us=6.0,
         )
         parts, input_grad = barrier((parts, input_grad))
     with jax.named_scope("serve"):
@@ -429,7 +395,6 @@
             (any_, vmem),
             vmem,
             [pltpu.VMEM((1, K), jnp.int32), dma],
-            us=0.8,
         )
     return served, input_grad
 

time: 106 us -> 105 us (level)
  starting transfers between devices: 54.4 us -> 60.3 us
  waiting for transfers between devices: 24.9 us -> 19.5 us
  Pallas kernels: 22.5 us -> 20.8 us
    all_to_all x4 -> x3, waiting for transfers between devices: 19.5 us -> 3.77 us  [exchange(): lax.all_to_all(value, AXES, split_axis=0, concat_axis=0, axis_index_group...]
    ppermute x5 -> x10, waiting for transfers between devices: 5.33 us -> 15.7 us  [the longest x1 7.48 us: body(): up = lax.ppermute(near, AXES, from_z(1, 1))]
    ppermute x5 -> x10, starting transfers between devices: 26.9 us -> 35.1 us  [the longest x5 11.8 us: body(): swapped = tuple((lax.ppermute(part, AXES, CORE_SWAP) for part in weights))]
    all_to_all x4 -> x3, starting transfers between devices: 22.3 us -> 16.3 us  [exchange(): lax.all_to_all(value, AXES, split_axis=0, concat_axis=0, axis_index_group...]
    ppermute x1, starting transfers between devices: 5.3 us -> 8.91 us  [body(): other = lax.ppermute(send, AXES, CORE_SWAP)]
    slice x0 -> x2, local copies, waits for them, and re-layouts: none -> 2.42 us  [the longest x1 1.66 us: body(): far_down = lax.ppermute(down[2:], AXES, from_z(-1, -1))]
    pallas_call x8 -> x6, Pallas kernels: 22.5 us -> 20.8 us  [call(): pl.pallas_call(kernel, out_shape=outs, in_specs=[pl.BlockSpec(memory_spac...]
    unnamed x12 -> x18, local copies, waits for them, and re-layouts: 2.19 us -> 0.72 us
  transfers between devices with their start and end apart: 10 -> 14, of which waited for: 6 -> 4; matrix products, arithmetic and copies ran while one was open for 0% -> 2% of each run, Pallas kernels for 20% -> 15%
where the time goes in v4:
time: 105 us
  starting transfers between devices  60.3 us (57%)
  Pallas kernels  20.8 us (20%)
  waiting for transfers between devices  19.5 us (19%)
  local copies, waits for them, and re-layouts  3.14 us (3%)
    pallas_call x6, Pallas kernels, call(): pl.pallas_call(kernel, out_shape=outs, in_specs=[pl.BlockSpec(memory_spac...  20.8 us
    all_to_all x3, starting transfers between devices, exchange(): lax.all_to_all(value, AXES, split_axis=0, concat_axis=0, axis_index_group...  16.3 us
    ppermute x5, starting transfers between devices, body(): swapped = tuple((lax.ppermute(part, AXES, CORE_SWAP) for part in weights))  11.8 us
    ppermute x1, starting transfers between devices, body(): up = lax.ppermute(near, AXES, from_z(1, 1))  10.6 us
    ppermute x1, starting transfers between devices, body(): other = lax.ppermute(send, AXES, CORE_SWAP)  8.91 us
    ppermute x1, waiting for transfers between devices, body(): up = lax.ppermute(near, AXES, from_z(1, 1))  7.48 us
    ppermute x1, waiting for transfers between devices, body(): far = lax.ppermute(key_weight, AXES, from_z(4, -4))  6.55 us
    ppermute x1, starting transfers between devices, body(): far_up = lax.ppermute(up[:2], AXES, from_z(1, 1))  5.32 us
  transfers between devices with their start and end apart: 14, of which 4 were waited for; matrix products, arithmetic and copies ran while one was open for 2% of the time, Pallas kernels for 15%

profile of v4, /device:TPU:1, one launch (start us, length us, event | category | flops | bytes accessed | tf_op | source)
XLA Modules:
  0.0 104.6 jit_solution(1253655805934269254)
XLA Ops:
  0.6 0.0 copy-start
  0.7 4.2 %norm.1 = (bf16[8,256,256]{2,1,0:T(8,128)(2,1)}, bf16[10,256,256]{2,1,0:T(8,128)(2,1)}, f32[256,128]{1,0:T(8,128)}) custom-call(bf16[256,4096]{1,0:T(8,128)(2,1)} %hidden_hbm.3, bf16[256,512]{1,0:T(8,128)(2,1)} %key_hbm.5, f32[1,4096]{1,0:T(1,128)} %bitcast.3), custom_call_target="tpu_custom_call" | custom-call | bytes 150000 | tf_op jit(solution)/shard_map/norm/pallas_call | solution.py:69
  4.9 8.9 %collective-permute-start = (bf16[10,256,256]{2,1,0:T(8,128)(2,1)}, bf16[10,256,256]{2,1,0:T(8,128)(2,1)S(1)}, u32[]{:S(2)}, u32[]{:S(2)}) collective-permute-start(bf16[10,256,256]{2,1,0:T(8,128)(2,1)} %get-tuple-element.9), channel_id=1, source_target_pairs={{0,32},{1,33},{2,34},{3,35},{4,36},{5,37},{6,38},{7,39},{8,40},{9,... | collective-permute-start | bytes 3932168 | tf_op jit(solution)/shard_map/norm/ppermute | solution.py:329
  13.8 3.4 %collective-permute-start.1 = (bf16[128,512]{1,0:T(8,128)(2,1)S(1)}, bf16[128,512]{1,0:T(8,128)(2,1)S(1)}, u32[]{:S(2)}, u32[]{:S(2)}) collective-permute-start(bf16[128,512]{1,0:T(8,128)(2,1)S(1)} %copy-done.2), channel_id=1, source_target_pairs={{4,0},{5,1},{6,2},{7,3},{64,4},{65,5},{66,6},{67,7},{12,8},{13,9},... | collective-permute-start | bytes 393224 | tf_op jit(solution)/shard_map/weight_z4/ppermute | solution.py:309
  17.3 6.6 %collective-permute-done.1.far_hbm = bf16[128,512]{1,0:T(8,128)(2,1)S(1)} collective-permute-done((bf16[128,512]{1,0:T(8,128)(2,1)S(1)}, bf16[128,512]{1,0:T(8,128)(2,1)S(1)}, u32[]{:S(2)}, u32[]{:S(2)}) %collective-permute-start.1) | collective-permute-done | bytes 131104 | tf_op jit(solution)/shard_map/weight_z4/ppermute | solution.py:309
  23.8 0.9 weight_y.1
  24.7 3.9 %all-to-all-start.2 = ((bf16[4,256,256]{2,1,0:T(8,128)(2,1)}), bf16[4,256,256]{2,1,0:T(8,128)(2,1)S(1)}, u32[]{:S(2)}, u32[]{:S(2)}) async-start(bf16[4,256,256]{2,1,0:T(8,128)(2,1)} %weight_y.1), calls=%async_computation.2 | async-start | bytes 1048576 | tf_op jit(solution)/shard_map/weight_y/all_to_all | solution.py:63
  28.6 0.0 collective-permute-done.other_hbm
  28.6 3.1 %squares.1 = bf16[16,256,256]{2,1,0:T(8,128)(2,1)} custom-call(bf16[8,256,256]{2,1,0:T(8,128)(2,1)S(1)} %copy-done.1, bf16[10,256,256]{2,1,0:T(8,128)(2,1)S(1)} %collective-permute-done.other_hbm, bf16[256,512]{1,0:T(8,128)(2,1)S(1)} %copy-done), custom_call_target="tpu_custom_call" | custom-call | bytes 150000 | tf_op jit(solution)/shard_map/squares/pallas_call | solution.py:69
  31.8 3.8 %all-to-all-done.2.own_0 = bf16[4,256,256]{2,1,0:T(8,128)(2,1)S(1)} async-done(((bf16[4,256,256]{2,1,0:T(8,128)(2,1)}), bf16[4,256,256]{2,1,0:T(8,128)(2,1)S(1)}, u32[]{:S(2)}, u32[]{:S(2)}) %all-to-all-start.2) | async-done | bytes 524320 | tf_op jit(solution)/shard_map/weight_y/all_to_all | solution.py:63
  35.6 4.7 %all-to-all-start = ((bf16[16,256,256]{2,1,0:T(8,128)(2,1)}), bf16[16,256,256]{2,1,0:T(8,128)(2,1)S(1)}, u32[]{:S(2)}, u32[]{:S(2)}) async-start(bf16[16,256,256]{2,1,0:T(8,128)(2,1)} %squares.1), calls=%async_computation | async-start | bytes 4194304 | tf_op jit(solution)/shard_map/plane/all_to_all | solution.py:63
  40.3 10.6 %collective-permute-start.2 = (bf16[4,256,256]{2,1,0:T(8,128)(2,1)S(1)}, bf16[4,256,256]{2,1,0:T(8,128)(2,1)S(1)}, u32[]{:S(2)}, u32[]{:S(2)}) collective-permute-start(bf16[4,256,256]{2,1,0:T(8,128)(2,1)S(1)} %all-to-all-done.2.own_0), channel_id=1, source_target_pairs={{1,0},{2,1},{3,2},{4,3},{5,4},{6,5},{7,6},{64,7},{9,8},{10,9},{11,... | collective-permute-start | bytes 1572872 | tf_op jit(solution)/shard_map/weight_z1/ppermute | solution.py:356
  51.0 1.9 %collective-permute-start.4 = (bf16[4,256,256]{2,1,0:T(8,128)(2,1)S(1)}, bf16[4,256,256]{2,1,0:T(8,128)(2,1)}, u32[]{:S(2)}, u32[]{:S(2)}) collective-permute-start(bf16[4,256,256]{2,1,0:T(8,128)(2,1)S(1)} %all-to-all-done.2.own_0), channel_id=1, source_target_pairs={{71,0},{0,1},{1,2},{2,3},{3,4},{4,5},{5,6},{6,7},{79,8},{8,9},{9,1... | collective-permute-start | bytes 1572872 | tf_op jit(solution)/shard_map/weight_z1/ppermute | solution.py:357
  52.9 1.9 %collective-permute-start.6 = (bf16[4,256,256]{2,1,0:T(8,128)(2,1)S(1)}, bf16[4,256,256]{2,1,0:T(8,128)(2,1)}, u32[]{:S(2)}, u32[]{:S(2)}) collective-permute-start(bf16[4,256,256]{2,1,0:T(8,128)(2,1)S(1)} %all-to-all-done.2.own_0), channel_id=1, source_target_pairs={{0,32},{1,33},{2,34},{3,35},{4,36},{5,37},{6,38},{7,39},{8,40},{9,... | collective-permute-start | bytes 1572872 | tf_op jit(solution)/shard_map/weight_swap/ppermute | solution.py:367
  54.8 7.5 %collective-permute-done.2.own_1 = bf16[4,256,256]{2,1,0:T(8,128)(2,1)S(1)} collective-permute-done((bf16[4,256,256]{2,1,0:T(8,128)(2,1)S(1)}, bf16[4,256,256]{2,1,0:T(8,128)(2,1)S(1)}, u32[]{:S(2)}, u32[]{:S(2)}) %collective-permute-start.2) | collective-permute-done | bytes 524320 | tf_op jit(solution)/shard_map/weight_z1/ppermute | solution.py:356
  62.3 0.8 slice.8
  63.1 5.3 %collective-permute-start.3 = (bf16[2,256,256]{2,1,0:T(8,128)(2,1)}, bf16[2,256,256]{2,1,0:T(8,128)(2,1)S(1)}, u32[]{:S(2)}, u32[]{:S(2)}) collective-permute-start(bf16[2,256,256]{2,1,0:T(8,128)(2,1)} %slice.8), channel_id=1, source_target_pairs={{1,0},{2,1},{3,2},{4,3},{5,4},{6,5},{7,6},{64,7},{9,8},{10,9},{11,... | collective-permute-start | bytes 786440 | tf_op jit(solution)/shard_map/weight_z2/ppermute | solution.py:359
  68.4 2.3 %collective-permute-start.7 = (bf16[4,256,256]{2,1,0:T(8,128)(2,1)S(1)}, bf16[4,256,256]{2,1,0:T(8,128)(2,1)}, u32[]{:S(2)}, u32[]{:S(2)}) collective-permute-start(bf16[4,256,256]{2,1,0:T(8,128)(2,1)S(1)} %collective-permute-done.2.own_1), channel_id=1, source_target_pairs={{0,32},{1,33},{2,34},{3,35},{4,36},{5,37},{6,38},{7,39},{8,40},{9,... | collective-permute-start | bytes 1572872 | tf_op jit(solution)/shard_map/weight_swap/ppermute | solution.py:367
  70.7 0.0 collective-permute-done.4.own_3
  70.7 1.7 %slice.9 = bf16[2,256,256]{2,1,0:T(8,128)(2,1)} slice(bf16[4,256,256]{2,1,0:T(8,128)(2,1)} %collective-permute-done.4.own_3), slice={[2:4], [0:256], [0:256]} | slice | bytes 524288 | tf_op jit(solution)/shard_map/weight_z2/slice | solution.py:360
  72.3 2.0 %collective-permute-start.10 = (bf16[4,256,256]{2,1,0:T(8,128)(2,1)}, bf16[4,256,256]{2,1,0:T(8,128)(2,1)}, u32[]{:S(2)}, u32[]{:S(2)}) collective-permute-start(bf16[4,256,256]{2,1,0:T(8,128)(2,1)} %collective-permute-done.4.own_3), channel_id=1, source_target_pairs={{0,32},{1,33},{2,34},{3,35},{4,36},{5,37},{6,38},{7,39},{8,40},{9,... | collective-permute-start | bytes 1572872 | tf_op jit(solution)/shard_map/weight_swap/ppermute | solution.py:367
  74.4 1.9 %collective-permute-start.5 = (bf16[2,256,256]{2,1,0:T(8,128)(2,1)}, bf16[2,256,256]{2,1,0:T(8,128)(2,1)}, u32[]{:S(2)}, u32[]{:S(2)}) collective-permute-start(bf16[2,256,256]{2,1,0:T(8,128)(2,1)} %slice.9), channel_id=1, source_target_pairs={{71,0},{0,1},{1,2},{2,3},{3,4},{4,5},{5,6},{6,7},{79,8},{8,9},{9,1... | collective-permute-start | bytes 786440 | tf_op jit(solution)/shard_map/weight_z2/ppermute | solution.py:360
  76.3 0.0 all-to-all-done.in_ref
  76.3 0.9 split.1
  77.3 7.6 %all-to-all-start.1 = ((bf16[16,16,256]{2,1,0:T(8,128)(2,1)}), bf16[16,16,256]{2,1,0:T(8,128)(2,1)S(1)}, u32[]{:S(2)}, u32[]{:S(2)}) async-start(bf16[16,16,256]{2,1,0:T(8,128)(2,1)} %split.1), calls=%async_computation.1 | async-start | bytes 262144 | tf_op jit(solution)/shard_map/ring_z/all_to_all | solution.py:63
  84.9 0.0 collective-permute-done.3.own_2a
  84.9 3.7 %collective-permute-start.8 = (bf16[2,256,256]{2,1,0:T(8,128)(2,1)S(1)}, bf16[2,256,256]{2,1,0:T(8,128)(2,1)S(1)}, u32[]{:S(2)}, u32[]{:S(2)}) collective-permute-start(bf16[2,256,256]{2,1,0:T(8,128)(2,1)S(1)} %collective-permute-done.3.own_2a), channel_id=1, source_target_pairs={{0,32},{1,33},{2,34},{3,35},{4,36},{5,37},{6,38},{7,39},{8,40},{9,... | collective-permute-start | bytes 786440 | tf_op jit(solution)/shard_map/weight_swap/ppermute | solution.py:367
  88.6 1.9 %collective-permute-start.9 = (bf16[2,256,256]{2,1,0:T(8,128)(2,1)}, bf16[2,256,256]{2,1,0:T(8,128)(2,1)S(1)}, u32[]{:S(2)}, u32[]{:S(2)}) collective-permute-start(bf16[2,256,256]{2,1,0:T(8,128)(2,1)} %collective-permute-done.5.own_2b), channel_id=1, source_target_pairs={{0,32},{1,33},{2,34},{3,35},{4,36},{5,37},{6,38},{7,39},{8,40},{9,... | collective-permute-start | bytes 786440 | tf_op jit(solution)/shard_map/weight_swap/ppermute | solution.py:367
  90.6 1.7 %collective-permute-done.9.other_2b = bf16[2,256,256]{2,1,0:T(8,128)(2,1)S(1)} collective-permute-done((bf16[2,256,256]{2,1,0:T(8,128)(2,1)}, bf16[2,256,256]{2,1,0:T(8,128)(2,1)S(1)}, u32[]{:S(2)}, u32[]{:S(2)}) %collective-permute-start.9) | collective-permute-done | bytes 262176 | tf_op jit(solution)/shard_map/weight_swap/ppermute | solution.py:367
  92.3 0.7 copy-done.8
  93.0 10.8 %input_grad.1 = bf16[256,4096]{1,0:T(8,128)(2,1)} custom-call(bf16[256,4096]{1,0:T(8,128)(2,1)} %hidden_hbm.3, bf16[256,512]{1,0:T(8,128)(2,1)} %key_hbm.5, f32[1,4096]{1,0:T(1,128)} %bitcast.4, f32[256,128]{1,0:T(8,128)} %get-tuple-element.10.inv_hbm, bf16[4,256,256]{2,1,0:T(8,128)(2,1)} %copy-done.4, bf16[4,256,256]{2,1,0:T(8,128)(2,1)} %copy-done.5, ...), custom_call_target="tpu_custom_call" | custom-call | bytes 150000 | tf_op jit(solution)/shard_map/input_grad/pallas_call | solution.py:69
  103.8 0.8 serve.1
  (22 shorter events, 0.0 us)
Async XLA Ops:
  0.6 13.2 %copy-start.2 = (bf16[128,512]{1,0:T(8,128)(2,1)S(1)}, bf16[128,512]{1,0:T(8,128)(2,1)}, u32[]{:S(2)}) copy-start(bf16[128,512]{1,0:T(8,128)(2,1)} %own_hbm.1) | copy-start | bytes 393220
  0.6 28.0 %copy-start = (bf16[256,512]{1,0:T(8,128)(2,1)S(1)}, bf16[256,512]{1,0:T(8,128)(2,1)}, u32[]{:S(2)}) copy-start(bf16[256,512]{1,0:T(8,128)(2,1)} %key_hbm.5) | copy-start | bytes 786436
  4.9 23.8 %copy-start.1 = (bf16[8,256,256]{2,1,0:T(8,128)(2,1)S(1)}, bf16[8,256,256]{2,1,0:T(8,128)(2,1)}, u32[]{:S(2)}) copy-start(bf16[8,256,256]{2,1,0:T(8,128)(2,1)} %get-tuple-element.8.own_hbm) | copy-start | bytes 3145732
  4.9 23.8 %collective-permute-start = (bf16[10,256,256]{2,1,0:T(8,128)(2,1)}, bf16[10,256,256]{2,1,0:T(8,128)(2,1)S(1)}, u32[]{:S(2)}, u32[]{:S(2)}) collective-permute-start(bf16[10,256,256]{2,1,0:T(8,128)(2,1)} %get-tuple-element.9), channel_id=1, source_target_pairs={{0,32},{1,33},{2,34},{3,35},{4,36},{5,37},{6,38},{7,39},{8,40},{9,... | collective-permute-start | bytes 3932168 | tf_op jit(solution)/shard_map/norm/ppermute | solution.py:329
  13.8 10.0 %collective-permute-start.1 = (bf16[128,512]{1,0:T(8,128)(2,1)S(1)}, bf16[128,512]{1,0:T(8,128)(2,1)S(1)}, u32[]{:S(2)}, u32[]{:S(2)}) collective-permute-start(bf16[128,512]{1,0:T(8,128)(2,1)S(1)} %copy-done.2), channel_id=1, source_target_pairs={{4,0},{5,1},{6,2},{7,3},{64,4},{65,5},{66,6},{67,7},{12,8},{13,9},... | collective-permute-start | bytes 393224 | tf_op jit(solution)/shard_map/weight_z4/ppermute | solution.py:309
  24.7 10.9 %all-to-all-start.2 = ((bf16[4,256,256]{2,1,0:T(8,128)(2,1)}), bf16[4,256,256]{2,1,0:T(8,128)(2,1)S(1)}, u32[]{:S(2)}, u32[]{:S(2)}) async-start(bf16[4,256,256]{2,1,0:T(8,128)(2,1)} %weight_y.1), calls=%async_computation.2 | async-start | bytes 1048576 | tf_op jit(solution)/shard_map/weight_y/all_to_all | solution.py:63
  35.6 27.5 %copy-start.4 = (bf16[4,256,256]{2,1,0:T(8,128)(2,1)}, bf16[4,256,256]{2,1,0:T(8,128)(2,1)S(1)}, u32[]{:S(2)}) copy-start(bf16[4,256,256]{2,1,0:T(8,128)(2,1)S(1)} %all-to-all-done.2.own_0) | copy-start | bytes 1572868
  35.6 40.8 %all-to-all-start = ((bf16[16,256,256]{2,1,0:T(8,128)(2,1)}), bf16[16,256,256]{2,1,0:T(8,128)(2,1)S(1)}, u32[]{:S(2)}, u32[]{:S(2)}) async-start(bf16[16,256,256]{2,1,0:T(8,128)(2,1)} %squares.1), calls=%async_computation | async-start | bytes 4194304 | tf_op jit(solution)/shard_map/plane/all_to_all | solution.py:63
  40.3 22.0 %collective-permute-start.2 = (bf16[4,256,256]{2,1,0:T(8,128)(2,1)S(1)}, bf16[4,256,256]{2,1,0:T(8,128)(2,1)S(1)}, u32[]{:S(2)}, u32[]{:S(2)}) collective-permute-start(bf16[4,256,256]{2,1,0:T(8,128)(2,1)S(1)} %all-to-all-done.2.own_0), channel_id=1, source_target_pairs={{1,0},{2,1},{3,2},{4,3},{5,4},{6,5},{7,6},{64,7},{9,8},{10,9},{11,... | collective-permute-start | bytes 1572872 | tf_op jit(solution)/shard_map/weight_z1/ppermute | solution.py:356
  51.0 19.7 %collective-permute-start.4 = (bf16[4,256,256]{2,1,0:T(8,128)(2,1)S(1)}, bf16[4,256,256]{2,1,0:T(8,128)(2,1)}, u32[]{:S(2)}, u32[]{:S(2)}) collective-permute-start(bf16[4,256,256]{2,1,0:T(8,128)(2,1)S(1)} %all-to-all-done.2.own_0), channel_id=1, source_target_pairs={{71,0},{0,1},{1,2},{2,3},{3,4},{4,5},{5,6},{6,7},{79,8},{8,9},{9,1... | collective-permute-start | bytes 1572872 | tf_op jit(solution)/shard_map/weight_z1/ppermute | solution.py:357
  52.9 37.7 %collective-permute-start.6 = (bf16[4,256,256]{2,1,0:T(8,128)(2,1)S(1)}, bf16[4,256,256]{2,1,0:T(8,128)(2,1)}, u32[]{:S(2)}, u32[]{:S(2)}) collective-permute-start(bf16[4,256,256]{2,1,0:T(8,128)(2,1)S(1)} %all-to-all-done.2.own_0), channel_id=1, source_target_pairs={{0,32},{1,33},{2,34},{3,35},{4,36},{5,37},{6,38},{7,39},{8,40},{9,... | collective-permute-start | bytes 1572872 | tf_op jit(solution)/shard_map/weight_swap/ppermute | solution.py:367
  62.3 30.0 %copy-start.5 = (bf16[4,256,256]{2,1,0:T(8,128)(2,1)}, bf16[4,256,256]{2,1,0:T(8,128)(2,1)S(1)}, u32[]{:S(2)}) copy-start(bf16[4,256,256]{2,1,0:T(8,128)(2,1)S(1)} %collective-permute-done.2.own_1) | copy-start | bytes 1572868
  63.1 21.9 %collective-permute-start.3 = (bf16[2,256,256]{2,1,0:T(8,128)(2,1)}, bf16[2,256,256]{2,1,0:T(8,128)(2,1)S(1)}, u32[]{:S(2)}, u32[]{:S(2)}) collective-permute-start(bf16[2,256,256]{2,1,0:T(8,128)(2,1)} %slice.8), channel_id=1, source_target_pairs={{1,0},{2,1},{3,2},{4,3},{5,4},{6,5},{7,6},{64,7},{9,8},{10,9},{11,... | collective-permute-start | bytes 786440 | tf_op jit(solution)/shard_map/weight_z2/ppermute | solution.py:359
  68.4 22.2 %collective-permute-start.7 = (bf16[4,256,256]{2,1,0:T(8,128)(2,1)S(1)}, bf16[4,256,256]{2,1,0:T(8,128)(2,1)}, u32[]{:S(2)}, u32[]{:S(2)}) collective-permute-start(bf16[4,256,256]{2,1,0:T(8,128)(2,1)S(1)} %collective-permute-done.2.own_1), channel_id=1, source_target_pairs={{0,32},{1,33},{2,34},{3,35},{4,36},{5,37},{6,38},{7,39},{8,40},{9,... | collective-permute-start | bytes 1572872 | tf_op jit(solution)/shard_map/weight_swap/ppermute | solution.py:367
  72.3 18.2 %collective-permute-start.10 = (bf16[4,256,256]{2,1,0:T(8,128)(2,1)}, bf16[4,256,256]{2,1,0:T(8,128)(2,1)}, u32[]{:S(2)}, u32[]{:S(2)}) collective-permute-start(bf16[4,256,256]{2,1,0:T(8,128)(2,1)} %collective-permute-done.4.own_3), channel_id=1, source_target_pairs={{0,32},{1,33},{2,34},{3,35},{4,36},{5,37},{6,38},{7,39},{8,40},{9,... | collective-permute-start | bytes 1572872 | tf_op jit(solution)/shard_map/weight_swap/ppermute | solution.py:367
  74.4 14.2 %collective-permute-start.5 = (bf16[2,256,256]{2,1,0:T(8,128)(2,1)}, bf16[2,256,256]{2,1,0:T(8,128)(2,1)}, u32[]{:S(2)}, u32[]{:S(2)}) collective-permute-start(bf16[2,256,256]{2,1,0:T(8,128)(2,1)} %slice.9), channel_id=1, source_target_pairs={{71,0},{0,1},{1,2},{2,3},{3,4},{4,5},{5,6},{6,7},{79,8},{8,9},{9,1... | collective-permute-start | bytes 786440 | tf_op jit(solution)/shard_map/weight_z2/ppermute | solution.py:360
  77.3 26.5 %all-to-all-start.1 = ((bf16[16,16,256]{2,1,0:T(8,128)(2,1)}), bf16[16,16,256]{2,1,0:T(8,128)(2,1)S(1)}, u32[]{:S(2)}, u32[]{:S(2)}) async-start(bf16[16,16,256]{2,1,0:T(8,128)(2,1)} %split.1), calls=%async_computation.1 | async-start | bytes 262144 | tf_op jit(solution)/shard_map/ring_z/all_to_all | solution.py:63
  84.9 7.3 %copy-start.6 = (bf16[2,256,256]{2,1,0:T(8,128)(2,1)}, bf16[2,256,256]{2,1,0:T(8,128)(2,1)S(1)}, u32[]{:S(2)}) copy-start(bf16[2,256,256]{2,1,0:T(8,128)(2,1)S(1)} %collective-permute-done.3.own_2a) | copy-start | bytes 786436
  84.9 5.6 %collective-permute-start.8 = (bf16[2,256,256]{2,1,0:T(8,128)(2,1)S(1)}, bf16[2,256,256]{2,1,0:T(8,128)(2,1)S(1)}, u32[]{:S(2)}, u32[]{:S(2)}) collective-permute-start(bf16[2,256,256]{2,1,0:T(8,128)(2,1)S(1)} %collective-permute-done.3.own_2a), channel_id=1, source_target_pairs={{0,32},{1,33},{2,34},{3,35},{4,36},{5,37},{6,38},{7,39},{8,40},{9,... | collective-permute-start | bytes 786440 | tf_op jit(solution)/shard_map/weight_swap/ppermute | solution.py:367
  88.6 3.6 %collective-permute-start.9 = (bf16[2,256,256]{2,1,0:T(8,128)(2,1)}, bf16[2,256,256]{2,1,0:T(8,128)(2,1)S(1)}, u32[]{:S(2)}, u32[]{:S(2)}) collective-permute-start(bf16[2,256,256]{2,1,0:T(8,128)(2,1)} %collective-permute-done.5.own_2b), channel_id=1, source_target_pairs={{0,32},{1,33},{2,34},{3,35},{4,36},{5,37},{6,38},{7,39},{8,40},{9,... | collective-permute-start | bytes 786440 | tf_op jit(solution)/shard_map/weight_swap/ppermute | solution.py:367
  90.6 1.7 %copy-start.7 = (bf16[2,256,256]{2,1,0:T(8,128)(2,1)}, bf16[2,256,256]{2,1,0:T(8,128)(2,1)S(1)}, u32[]{:S(2)}) copy-start(bf16[2,256,256]{2,1,0:T(8,128)(2,1)S(1)} %collective-permute-done.8.other_2a) | copy-start | bytes 786436
  92.3 0.7 copy-start.8
  93.0 10.8 %copy-start.3 = (s32[512]{0:T(512)S(1)}, s32[512]{0:T(512)}, u32[]{:S(2)}) copy-start(s32[512]{0:T(512)} %param.9) | copy-start | bytes 6148

commit v5 on v4

--- a/solution.py
+++ b/solution.py
@@ -11,6 +11,7 @@
 SEQ = 256
 TOKENS = SEQ * NX * NZH * NC * NY * NZL
 COLS = 256
+NORM_PARTS = 4
 BF16, F32 = jnp.bfloat16, jnp.float32
 
 
@@ -98,7 +99,7 @@
     hidden_ref, key_ref, gain_ref, own_ref, send_ref, inv_ref, in_sems, out_sems,
 ):
     core = my_core()
-    step, parts, blocks = 16, 4, NX * NZH
+    step, parts, blocks = 16, NORM_PARTS, NX * NZH
     rows_each = SEQ // parts
     pieces = [pl.ds(i * rows_each, rows_each) for i in range(parts)]
     gain_copy = start(gain_hbm, gain_ref, in_sems.at[parts])
@@ -127,7 +128,7 @@
     out_copies = []
     for i, rows in enumerate(pieces):
         copies[i].wait()
-        lax.fori_loop(i * rows_each // step, (i + 1) * rows_each // step, rows_of, 0)
+        lax.fori_loop(i * rows_each // step, (i + 1) * rows_each // step, rows_of, 0, unroll=4)
         out_copies += [
             start(send_ref.at[:, rows], send_hbm.at[pl.ds(0, blocks), rows], out_sems.at[2 * i]),
             start(own_ref.at[:, rows], own_hbm.at[:, rows], out_sems.at[2 * i + 1]),
@@ -191,6 +192,15 @@
         copy.wait()
 
 
+def halves_kernel(up_hbm, down_hbm, up_half, down_half, sems):
+    copies = [
+        start(up_hbm.at[pl.ds(0, 2)], up_half, sems.at[0]),
+        start(down_hbm.at[pl.ds(2, 2)], down_half, sems.at[1]),
+    ]
+    for copy in copies:
+        copy.wait()
+
+
 def split_kernel(in_ref, out_ref):
     for zh in range(NZH):
         rows = slice(zh * 128, (zh + 1) * 128)
@@ -221,51 +231,47 @@
     hidden_ref, key_ref, gain_ref, inv_ref, own_ref, other_ref, back_ref, out_ref,
     in_sems, out_sems,
 ):
-    first = [start(key_hbm, key_ref, in_sems.at[0])]
-    for ref, parts in (
-        (own_ref, (own_0, own_1, own_2a, own_2b, own_3)),
-        (other_ref, (other_0, other_1, other_2a, other_2b, other_3)),
-    ):
-        for part, (place, size) in zip(parts, ((0, 4), (4, 4), (8, 2), (10, 2), (12, 4))):
-            first.append(start(part, ref.at[pl.ds(place, size)], in_sems.at[len(first)]))
+    key_copy = start(key_hbm, key_ref, in_sems.at[0])
+    places = {0: (0, 4), 1: (4, 4), 3: (12, 4), 2: (8, 2), 4: (10, 2)}
+    sources = {
+        0: (own_0, other_0),
+        1: (own_1, other_1),
+        3: (own_3, other_3),
+        2: (own_2a, other_2a),
+        4: (own_2b, other_2b),
+    }
+    weights = {}
+    for i, (part, (place, size)) in enumerate(places.items()):
+        weights[part] = [
+            start(source, ref.at[pl.ds(place, size)], in_sems.at[1 + 2 * i + j])
+            for j, (source, ref) in enumerate(zip(sources[part], (own_ref, other_ref)))
+        ]
     second = [
         start(gain_hbm, gain_ref, in_sems.at[11]),
         start(inv_hbm, inv_ref, in_sems.at[12]),
         start(hidden_hbm, hidden_ref, in_sems.at[13]),
     ]
-    for copy in first:
-        copy.wait()
     core = my_core()
     z_here = lax.rem(lax.axis_index("fsdp"), NZL)
     own_cols = pl.ds(pl.multiple_of(core * COLS, COLS), COLS)
     other_cols = pl.ds(pl.multiple_of((1 - core) * COLS, COLS), COLS)
+    key_copy.wait()
     keys = jnp.concatenate([key_ref[:, own_cols], key_ref[:, other_cols]], axis=1)
 
-    def shard(ref, y, zl):
-        away = (zl - z_here) & (NZL - 1)
-        step = away & 3
-        from_below = (step == 3) | ((step == 2) & (y >= 2))
-        second = jnp.where(from_below, 1 - (away >> 2), away >> 2)
-        return ref[step * 4 + y, pl.ds(pl.multiple_of(second * 128, 128), 128), :]
-
-    def tile(t, carry):
-        y, pair = t // 4, t % 4
-        weight = jnp.concatenate(
-            [
-                jnp.concatenate(
-                    [shard(own_ref, y, 2 * pair + i), shard(other_ref, y, 2 * pair + i)], axis=1
-                )
-                for i in range(2)
-            ],
-            axis=0,
-        )
-        cols = pl.ds(pl.multiple_of(t * 256, 256), 256)
-        back_ref[:, cols] = lax.dot_general(
-            keys, weight, (((1,), (1,)), ((), ())), preferred_element_type=F32
-        )
-        return carry
-
-    lax.fori_loop(0, D // 256, tile, 0)
+    for part, (place, size) in places.items():
+        for copy in weights[part]:
+            copy.wait()
+        for i in range(size):
+            y = (place + i) % NY
+            away = (0, 1, 2, 7, 6)[part]
+            weight = jnp.concatenate([own_ref[place + i], other_ref[place + i]], axis=1)
+            back = lax.dot_general(
+                keys, weight, (((1,), (1,)), ((), ())), preferred_element_type=F32
+            )
+            for half in range(2):
+                shard = (z_here + away + 4 * half) & (NZL - 1)
+                cols = pl.ds(pl.multiple_of((y * NZL + shard) * 128, 128), 128)
+                back_ref[:, cols] = back[:, half * 128 : (half + 1) * 128]
     for copy in second:
         copy.wait()
 
@@ -291,7 +297,7 @@
     rows_each = SEQ // parts
     copies = []
     for i in range(parts):
-        lax.fori_loop(i * rows_each // step, (i + 1) * rows_each // step, rows_of, 0)
+        lax.fori_loop(i * rows_each // step, (i + 1) * rows_each // step, rows_of, 0, unroll=4)
         rows = pl.ds(i * rows_each, rows_each)
         copies.append(start(out_ref.at[rows], out_hbm.at[rows], out_sems.at[i]))
     for copy in copies:
@@ -321,13 +327,13 @@
                 pltpu.VMEM((blocks, SEQ, COLS), BF16),
                 pltpu.VMEM((blocks, SEQ, COLS), BF16),
                 pltpu.VMEM((SEQ, 128), F32),
-                dma((6,)),
-                dma((11,)),
+                dma((NORM_PARTS + 2,)),
+                dma((2 * NORM_PARTS + 3,)),
             ],
             mib=None,
         )
+        far, send = barrier((far, send))
         other = lax.ppermute(send, AXES, CORE_SWAP)
-        far, send = barrier((far, send))
     with jax.named_scope("weight_y"):
         pieces = call(
             piece_kernel, shape((NY, 256, COLS)), (key_weight, far), (any_, any_), hbm, [dma((8,))]
@@ -356,8 +362,12 @@
         up = lax.ppermute(near, AXES, from_z(1, 1))
         down = lax.ppermute(near, AXES, from_z(-1, -1))
     with jax.named_scope("weight_z2"):
-        far_up = lax.ppermute(up[:2], AXES, from_z(1, 1))
-        far_down = lax.ppermute(down[2:], AXES, from_z(-1, -1))
+        half = shape((2, 256, COLS))
+        up_half, down_half = call(
+            halves_kernel, (half, half), (up, down), (any_, any_), (hbm, hbm), [dma((2,))], mib=52
+        )
+        far_up = lax.ppermute(up_half, AXES, from_z(1, 1))
+        far_down = lax.ppermute(down_half, AXES, from_z(-1, -1))
     with jax.named_scope("split"):
         parts = call(split_kernel, shape((NZH * NZL, 16, COLS)), (chunks,), (vmem,), vmem)
     with jax.named_scope("ring_z"):

time: 105 us -> 100 us (0.952); the launches traced: 105 us -> 98.4 us
  Pallas kernels: 20.8 us -> 15.1 us
  local copies, waits for them, and re-layouts: 3.14 us -> 0.72 us
  starting transfers between devices: 60.3 us -> 61.8 us
    ppermute x1, starting transfers between devices: 10.6 us -> 3.91 us  [body(): up = lax.ppermute(near, AXES, from_z(1, 1))]
    ppermute x1, starting transfers between devices: 3.44 us -> 9.78 us  [body(): far = lax.ppermute(key_weight, AXES, from_z(4, -4))]
    pallas_call x6 -> x7, Pallas kernels: 20.8 us -> 15.1 us  [call(): pl.pallas_call(kernel, out_shape=outs, in_specs=[pl.BlockSpec(memory_spac...]
    ppermute x1, waiting for transfers between devices: 0.01 us -> 4.29 us  [body(): down = lax.ppermute(near, AXES, from_z(-1, -1))]
    ppermute x5, starting transfers between devices: 11.8 us -> 15.5 us  [body(): swapped = tuple((lax.ppermute(part, AXES, CORE_SWAP) for part in weights))]
    ppermute x1, starting transfers between devices: 8.91 us -> 5.3 us  [body(): other = lax.ppermute(send, AXES, CORE_SWAP)]
    ppermute x1, waiting for transfers between devices: 7.48 us -> 4.14 us  [body(): up = lax.ppermute(near, AXES, from_z(1, 1))]
    ppermute x1, waiting for transfers between devices: 6.55 us -> 3.58 us  [body(): far = lax.ppermute(key_weight, AXES, from_z(4, -4))]
  transfers between devices with their start and end apart: 14 -> 14, of which waited for: 4 -> 5; matrix products, arithmetic and copies ran while one was open for 2% -> 0% of each run, Pallas kernels for 15% -> 15%
where the time goes in v5:
time: 100 us; the launch traced here: 98.4 us
  starting transfers between devices  61.8 us (62%)
  waiting for transfers between devices  19.9 us (20%)
  Pallas kernels  15.1 us (15%)
    all_to_all x3, starting transfers between devices, exchange(): lax.all_to_all(value, AXES, split_axis=0, concat_axis=0, axis_index_group...  18.9 us
    ppermute x5, starting transfers between devices, body(): swapped = tuple((lax.ppermute(part, AXES, CORE_SWAP) for part in weights))  15.5 us
    pallas_call x7, Pallas kernels, call(): pl.pallas_call(kernel, out_shape=outs, in_specs=[pl.BlockSpec(memory_spac...  15.1 us
    ppermute x1, starting transfers between devices, body(): far = lax.ppermute(key_weight, AXES, from_z(4, -4))  9.78 us
    all_to_all x3, waiting for transfers between devices, exchange(): lax.all_to_all(value, AXES, split_axis=0, concat_axis=0, axis_index_group...  6.26 us
    ppermute x1, starting transfers between devices, body(): other = lax.ppermute(send, AXES, CORE_SWAP)  5.3 us
    ppermute x1, waiting for transfers between devices, body(): down = lax.ppermute(near, AXES, from_z(-1, -1))  4.29 us
    ppermute x1, waiting for transfers between devices, body(): up = lax.ppermute(near, AXES, from_z(1, 1))  4.14 us
  transfers between devices with their start and end apart: 14, of which 5 were waited for; matrix products, arithmetic and copies ran while one was open for 0% of the time, Pallas kernels for 15%

profile of v5, /device:TPU:1, one launch (start us, length us, event | category | flops | bytes accessed | tf_op | source)
XLA Modules:
  0.0 98.4 jit_solution(3904928761360871958)
XLA Ops:
  0.6 9.8 %collective-permute-start = (bf16[128,512]{1,0:T(8,128)(2,1)}, bf16[128,512]{1,0:T(8,128)(2,1)S(1)}, u32[]{:S(2)}, u32[]{:S(2)}) collective-permute-start(bf16[128,512]{1,0:T(8,128)(2,1)} %own_hbm.1), channel_id=1, source_target_pairs={{4,0},{5,1},{6,2},{7,3},{64,4},{65,5},{66,6},{67,7},{12,8},{13,9},... | collective-permute-start | bytes 393224 | tf_op jit(solution)/shard_map/weight_z4/ppermute | solution.py:315
  10.4 0.0 copy-start
  10.4 3.0 %norm.1 = (bf16[8,256,256]{2,1,0:T(8,128)(2,1)}, bf16[10,256,256]{2,1,0:T(8,128)(2,1)}, f32[256,128]{1,0:T(8,128)}) custom-call(bf16[256,4096]{1,0:T(8,128)(2,1)} %hidden_hbm.3, bf16[256,512]{1,0:T(8,128)(2,1)} %key_hbm.5, f32[1,4096]{1,0:T(1,128)} %bitcast.3), custom_call_target="tpu_custom_call" | custom-call | bytes 150000 | tf_op jit(solution)/shard_map/norm/pallas_call | solution.py:70
  13.4 3.6 %collective-permute-done.far_hbm = bf16[128,512]{1,0:T(8,128)(2,1)S(1)} collective-permute-done((bf16[128,512]{1,0:T(8,128)(2,1)}, bf16[128,512]{1,0:T(8,128)(2,1)S(1)}, u32[]{:S(2)}, u32[]{:S(2)}) %collective-permute-start) | collective-permute-done | bytes 131104 | tf_op jit(solution)/shard_map/weight_z4/ppermute | solution.py:315
  17.0 5.3 %collective-permute-start.1 = (bf16[10,256,256]{2,1,0:T(8,128)(2,1)}, bf16[10,256,256]{2,1,0:T(8,128)(2,1)S(1)}, u32[]{:S(2)}, u32[]{:S(2)}) collective-permute-start(bf16[10,256,256]{2,1,0:T(8,128)(2,1)} %get-tuple-element.13), channel_id=1, source_target_pairs={{0,32},{1,33},{2,34},{3,35},{4,36},{5,37},{6,38},{7,39},{8,40},{9,... | collective-permute-start | bytes 3932168 | tf_op jit(solution)/shard_map/norm/ppermute | solution.py:336
  22.3 0.9 weight_y.1
  23.2 5.8 %all-to-all-start.2 = ((bf16[4,256,256]{2,1,0:T(8,128)(2,1)}), bf16[4,256,256]{2,1,0:T(8,128)(2,1)}, u32[]{:S(2)}, u32[]{:S(2)}) async-start(bf16[4,256,256]{2,1,0:T(8,128)(2,1)} %weight_y.1), calls=%async_computation.2 | async-start | bytes 1048576 | tf_op jit(solution)/shard_map/weight_y/all_to_all | solution.py:64
  29.1 3.1 %squares.1 = bf16[16,256,256]{2,1,0:T(8,128)(2,1)} custom-call(bf16[8,256,256]{2,1,0:T(8,128)(2,1)S(1)} %copy-done.3, bf16[10,256,256]{2,1,0:T(8,128)(2,1)S(1)} %collective-permute-done.1.other_hbm, bf16[256,512]{1,0:T(8,128)(2,1)S(1)} %copy-done), custom_call_target="tpu_custom_call" | custom-call | bytes 150000 | tf_op jit(solution)/shard_map/squares/pallas_call | solution.py:70
  32.2 6.3 %all-to-all-done.2.own_0 = bf16[4,256,256]{2,1,0:T(8,128)(2,1)} async-done(((bf16[4,256,256]{2,1,0:T(8,128)(2,1)}), bf16[4,256,256]{2,1,0:T(8,128)(2,1)}, u32[]{:S(2)}, u32[]{:S(2)}) %all-to-all-start.2) | async-done | bytes 524320 | tf_op jit(solution)/shard_map/weight_y/all_to_all | solution.py:64
  38.5 4.7 %all-to-all-start = ((bf16[16,256,256]{2,1,0:T(8,128)(2,1)}), bf16[16,256,256]{2,1,0:T(8,128)(2,1)S(1)}, u32[]{:S(2)}, u32[]{:S(2)}) async-start(bf16[16,256,256]{2,1,0:T(8,128)(2,1)} %squares.1), calls=%async_computation | async-start | bytes 4194304 | tf_op jit(solution)/shard_map/plane/all_to_all | solution.py:64
  43.2 3.9 %collective-permute-start.2 = (bf16[4,256,256]{2,1,0:T(8,128)(2,1)}, bf16[4,256,256]{2,1,0:T(8,128)(2,1)S(1)}, u32[]{:S(2)}, u32[]{:S(2)}) collective-permute-start(bf16[4,256,256]{2,1,0:T(8,128)(2,1)} %all-to-all-done.2.own_0), channel_id=1, source_target_pairs={{1,0},{2,1},{3,2},{4,3},{5,4},{6,5},{7,6},{64,7},{9,8},{10,9},{11,... | collective-permute-start | bytes 1572872 | tf_op jit(solution)/shard_map/weight_z1/ppermute | solution.py:362
  47.1 1.9 %collective-permute-start.3 = (bf16[4,256,256]{2,1,0:T(8,128)(2,1)}, bf16[4,256,256]{2,1,0:T(8,128)(2,1)S(1)}, u32[]{:S(2)}, u32[]{:S(2)}) collective-permute-start(bf16[4,256,256]{2,1,0:T(8,128)(2,1)} %all-to-all-done.2.own_0), channel_id=1, source_target_pairs={{71,0},{0,1},{1,2},{2,3},{3,4},{4,5},{5,6},{6,7},{79,8},{8,9},{9,1... | collective-permute-start | bytes 1572872 | tf_op jit(solution)/shard_map/weight_z1/ppermute | solution.py:363
  49.1 4.1 %collective-permute-start.6 = (bf16[4,256,256]{2,1,0:T(8,128)(2,1)}, bf16[4,256,256]{2,1,0:T(8,128)(2,1)}, u32[]{:S(2)}, u32[]{:S(2)}) collective-permute-start(bf16[4,256,256]{2,1,0:T(8,128)(2,1)} %all-to-all-done.2.own_0), channel_id=1, source_target_pairs={{0,32},{1,33},{2,34},{3,35},{4,36},{5,37},{6,38},{7,39},{8,40},{9,... | collective-permute-start | bytes 1572872 | tf_op jit(solution)/shard_map/weight_swap/ppermute | solution.py:377
  53.2 4.1 %collective-permute-done.2.up_hbm.own_1 = bf16[4,256,256]{2,1,0:T(8,128)(2,1)S(1)} collective-permute-done((bf16[4,256,256]{2,1,0:T(8,128)(2,1)}, bf16[4,256,256]{2,1,0:T(8,128)(2,1)S(1)}, u32[]{:S(2)}, u32[]{:S(2)}) %collective-permute-start.2) | collective-permute-done | bytes 524320 | tf_op jit(solution)/shard_map/weight_z1/ppermute | solution.py:362
  57.3 4.3 %collective-permute-done.3.down_hbm.own_3 = bf16[4,256,256]{2,1,0:T(8,128)(2,1)S(1)} collective-permute-done((bf16[4,256,256]{2,1,0:T(8,128)(2,1)}, bf16[4,256,256]{2,1,0:T(8,128)(2,1)S(1)}, u32[]{:S(2)}, u32[]{:S(2)}) %collective-permute-start.3) | collective-permute-done | bytes 524320 | tf_op jit(solution)/shard_map/weight_z1/ppermute | solution.py:363
  61.6 0.7 weight_z2.1
  62.4 3.7 %collective-permute-start.4 = (bf16[2,256,256]{2,1,0:T(8,128)(2,1)}, bf16[2,256,256]{2,1,0:T(8,128)(2,1)}, u32[]{:S(2)}, u32[]{:S(2)}) collective-permute-start(bf16[2,256,256]{2,1,0:T(8,128)(2,1)} %get-tuple-element.16), channel_id=1, source_target_pairs={{1,0},{2,1},{3,2},{4,3},{5,4},{6,5},{7,6},{64,7},{9,8},{10,9},{11,... | collective-permute-start | bytes 786440 | tf_op jit(solution)/shard_map/weight_z2/ppermute | solution.py:369
  66.0 4.2 %collective-permute-start.7 = (bf16[4,256,256]{2,1,0:T(8,128)(2,1)S(1)}, bf16[4,256,256]{2,1,0:T(8,128)(2,1)}, u32[]{:S(2)}, u32[]{:S(2)}) collective-permute-start(bf16[4,256,256]{2,1,0:T(8,128)(2,1)S(1)} %collective-permute-done.2.up_hbm.own_1), channel_id=1, source_target_pairs={{0,32},{1,33},{2,34},{3,35},{4,36},{5,37},{6,38},{7,39},{8,40},{9,... | collective-permute-start | bytes 1572872 | tf_op jit(solution)/shard_map/weight_swap/ppermute | solution.py:377
  70.2 1.9 %collective-permute-start.10 = (bf16[4,256,256]{2,1,0:T(8,128)(2,1)S(1)}, bf16[4,256,256]{2,1,0:T(8,128)(2,1)}, u32[]{:S(2)}, u32[]{:S(2)}) collective-permute-start(bf16[4,256,256]{2,1,0:T(8,128)(2,1)S(1)} %collective-permute-done.3.down_hbm.own_3), channel_id=1, source_target_pairs={{0,32},{1,33},{2,34},{3,35},{4,36},{5,37},{6,38},{7,39},{8,40},{9,... | collective-permute-start | bytes 1572872 | tf_op jit(solution)/shard_map/weight_swap/ppermute | solution.py:377
  72.1 2.8 %collective-permute-start.5 = (bf16[2,256,256]{2,1,0:T(8,128)(2,1)S(1)}, bf16[2,256,256]{2,1,0:T(8,128)(2,1)}, u32[]{:S(2)}, u32[]{:S(2)}) collective-permute-start(bf16[2,256,256]{2,1,0:T(8,128)(2,1)S(1)} %get-tuple-element.17), channel_id=1, source_target_pairs={{71,0},{0,1},{1,2},{2,3},{3,4},{4,5},{5,6},{6,7},{79,8},{8,9},{9,1... | collective-permute-start | bytes 786440 | tf_op jit(solution)/shard_map/weight_z2/ppermute | solution.py:370
  74.9 0.0 all-to-all-done.in_ref
  74.9 0.9 split.1
  75.9 8.3 %all-to-all-start.1 = ((bf16[16,16,256]{2,1,0:T(8,128)(2,1)}), bf16[16,16,256]{2,1,0:T(8,128)(2,1)S(1)}, u32[]{:S(2)}, u32[]{:S(2)}) async-start(bf16[16,16,256]{2,1,0:T(8,128)(2,1)} %split.1), calls=%async_computation.1 | async-start | bytes 262144 | tf_op jit(solution)/shard_map/ring_z/all_to_all | solution.py:64
  84.2 0.0 collective-permute-done.4.own_2a
  84.2 3.3 %collective-permute-start.8 = (bf16[2,256,256]{2,1,0:T(8,128)(2,1)}, bf16[2,256,256]{2,1,0:T(8,128)(2,1)S(1)}, u32[]{:S(2)}, u32[]{:S(2)}) collective-permute-start(bf16[2,256,256]{2,1,0:T(8,128)(2,1)} %collective-permute-done.4.own_2a), channel_id=1, source_target_pairs={{0,32},{1,33},{2,34},{3,35},{4,36},{5,37},{6,38},{7,39},{8,40},{9,... | collective-permute-start | bytes 786440 | tf_op jit(solution)/shard_map/weight_swap/ppermute | solution.py:377
  87.6 0.0 collective-permute-done.5.own_2b
  87.6 1.9 %collective-permute-start.9 = (bf16[2,256,256]{2,1,0:T(8,128)(2,1)}, bf16[2,256,256]{2,1,0:T(8,128)(2,1)S(1)}, u32[]{:S(2)}, u32[]{:S(2)}) collective-permute-start(bf16[2,256,256]{2,1,0:T(8,128)(2,1)} %collective-permute-done.5.own_2b), channel_id=1, source_target_pairs={{0,32},{1,33},{2,34},{3,35},{4,36},{5,37},{6,38},{7,39},{8,40},{9,... | collective-permute-start | bytes 786440 | tf_op jit(solution)/shard_map/weight_swap/ppermute | solution.py:377
  89.5 0.0 collective-permute-done.6.other_0
  89.6 1.7 %collective-permute-done.9.other_2b = bf16[2,256,256]{2,1,0:T(8,128)(2,1)S(1)} collective-permute-done((bf16[2,256,256]{2,1,0:T(8,128)(2,1)}, bf16[2,256,256]{2,1,0:T(8,128)(2,1)S(1)}, u32[]{:S(2)}, u32[]{:S(2)}) %collective-permute-start.9) | collective-permute-done | bytes 262176 | tf_op jit(solution)/shard_map/weight_swap/ppermute | solution.py:377
  91.2 0.7 copy-done.7
  91.9 5.7 %input_grad.1 = bf16[256,4096]{1,0:T(8,128)(2,1)} custom-call(bf16[256,4096]{1,0:T(8,128)(2,1)} %hidden_hbm.3, bf16[256,512]{1,0:T(8,128)(2,1)} %key_hbm.5, f32[1,4096]{1,0:T(1,128)} %bitcast.4, f32[256,128]{1,0:T(8,128)} %get-tuple-element.14.inv_hbm, bf16[4,256,256]{2,1,0:T(8,128)(2,1)} %all-to-all-done.2.own_0, bf16[4,256,256]{2,1,0:T(8,128)(2,1)} %copy-done.1, ...), custom_call_target="tpu_custom_call" | custom-call | bytes 150000 | tf_op jit(solution)/shard_map/input_grad/pallas_call | solution.py:70
  97.6 0.8 serve.1
  (19 shorter events, 0.0 us)
Async XLA Ops:
  0.6 21.7 %copy-start.4 = (bf16[128,512]{1,0:T(8,128)(2,1)S(1)}, bf16[128,512]{1,0:T(8,128)(2,1)}, u32[]{:S(2)}) copy-start(bf16[128,512]{1,0:T(8,128)(2,1)} %own_hbm.1) | copy-start | bytes 393220
  0.6 16.4 %collective-permute-start = (bf16[128,512]{1,0:T(8,128)(2,1)}, bf16[128,512]{1,0:T(8,128)(2,1)S(1)}, u32[]{:S(2)}, u32[]{:S(2)}) collective-permute-start(bf16[128,512]{1,0:T(8,128)(2,1)} %own_hbm.1), channel_id=1, source_target_pairs={{4,0},{5,1},{6,2},{7,3},{64,4},{65,5},{66,6},{67,7},{12,8},{13,9},... | collective-permute-start | bytes 393224 | tf_op jit(solution)/shard_map/weight_z4/ppermute | solution.py:315
  10.4 18.6 %copy-start = (bf16[256,512]{1,0:T(8,128)(2,1)S(1)}, bf16[256,512]{1,0:T(8,128)(2,1)}, u32[]{:S(2)}) copy-start(bf16[256,512]{1,0:T(8,128)(2,1)} %key_hbm.5) | copy-start | bytes 786436
  13.4 15.6 %copy-start.3 = (bf16[8,256,256]{2,1,0:T(8,128)(2,1)S(1)}, bf16[8,256,256]{2,1,0:T(8,128)(2,1)}, u32[]{:S(2)}) copy-start(bf16[8,256,256]{2,1,0:T(8,128)(2,1)} %get-tuple-element.11.own_hbm) | copy-start | bytes 3145732
  17.0 12.0 %collective-permute-start.1 = (bf16[10,256,256]{2,1,0:T(8,128)(2,1)}, bf16[10,256,256]{2,1,0:T(8,128)(2,1)S(1)}, u32[]{:S(2)}, u32[]{:S(2)}) collective-permute-start(bf16[10,256,256]{2,1,0:T(8,128)(2,1)} %get-tuple-element.13), channel_id=1, source_target_pairs={{0,32},{1,33},{2,34},{3,35},{4,36},{5,37},{6,38},{7,39},{8,40},{9,... | collective-permute-start | bytes 3932168 | tf_op jit(solution)/shard_map/norm/ppermute | solution.py:336
  23.2 15.3 %all-to-all-start.2 = ((bf16[4,256,256]{2,1,0:T(8,128)(2,1)}), bf16[4,256,256]{2,1,0:T(8,128)(2,1)}, u32[]{:S(2)}, u32[]{:S(2)}) async-start(bf16[4,256,256]{2,1,0:T(8,128)(2,1)} %weight_y.1), calls=%async_computation.2 | async-start | bytes 1048576 | tf_op jit(solution)/shard_map/weight_y/all_to_all | solution.py:64
  38.5 36.5 %all-to-all-start = ((bf16[16,256,256]{2,1,0:T(8,128)(2,1)}), bf16[16,256,256]{2,1,0:T(8,128)(2,1)S(1)}, u32[]{:S(2)}, u32[]{:S(2)}) async-start(bf16[16,256,256]{2,1,0:T(8,128)(2,1)} %squares.1), calls=%async_computation | async-start | bytes 4194304 | tf_op jit(solution)/shard_map/plane/all_to_all | solution.py:64
  43.2 14.1 %collective-permute-start.2 = (bf16[4,256,256]{2,1,0:T(8,128)(2,1)}, bf16[4,256,256]{2,1,0:T(8,128)(2,1)S(1)}, u32[]{:S(2)}, u32[]{:S(2)}) collective-permute-start(bf16[4,256,256]{2,1,0:T(8,128)(2,1)} %all-to-all-done.2.own_0), channel_id=1, source_target_pairs={{1,0},{2,1},{3,2},{4,3},{5,4},{6,5},{7,6},{64,7},{9,8},{10,9},{11,... | collective-permute-start | bytes 1572872 | tf_op jit(solution)/shard_map/weight_z1/ppermute | solution.py:362
  47.1 14.5 %collective-permute-start.3 = (bf16[4,256,256]{2,1,0:T(8,128)(2,1)}, bf16[4,256,256]{2,1,0:T(8,128)(2,1)S(1)}, u32[]{:S(2)}, u32[]{:S(2)}) collective-permute-start(bf16[4,256,256]{2,1,0:T(8,128)(2,1)} %all-to-all-done.2.own_0), channel_id=1, source_target_pairs={{71,0},{0,1},{1,2},{2,3},{3,4},{4,5},{5,6},{6,7},{79,8},{8,9},{9,1... | collective-permute-start | bytes 1572872 | tf_op jit(solution)/shard_map/weight_z1/ppermute | solution.py:363
  49.1 40.5 %collective-permute-start.6 = (bf16[4,256,256]{2,1,0:T(8,128)(2,1)}, bf16[4,256,256]{2,1,0:T(8,128)(2,1)}, u32[]{:S(2)}, u32[]{:S(2)}) collective-permute-start(bf16[4,256,256]{2,1,0:T(8,128)(2,1)} %all-to-all-done.2.own_0), channel_id=1, source_target_pairs={{0,32},{1,33},{2,34},{3,35},{4,36},{5,37},{6,38},{7,39},{8,40},{9,... | collective-permute-start | bytes 1572872 | tf_op jit(solution)/shard_map/weight_swap/ppermute | solution.py:377
  57.3 33.9 %copy-start.1 = (bf16[4,256,256]{2,1,0:T(8,128)(2,1)}, bf16[4,256,256]{2,1,0:T(8,128)(2,1)S(1)}, u32[]{:S(2)}) copy-start(bf16[4,256,256]{2,1,0:T(8,128)(2,1)S(1)} %collective-permute-done.2.up_hbm.own_1) | copy-start | bytes 1572868
  61.6 29.6 %copy-start.2 = (bf16[4,256,256]{2,1,0:T(8,128)(2,1)}, bf16[4,256,256]{2,1,0:T(8,128)(2,1)S(1)}, u32[]{:S(2)}) copy-start(bf16[4,256,256]{2,1,0:T(8,128)(2,1)S(1)} %collective-permute-done.3.down_hbm.own_3) | copy-start | bytes 1572868
  62.4 21.9 %collective-permute-start.4 = (bf16[2,256,256]{2,1,0:T(8,128)(2,1)}, bf16[2,256,256]{2,1,0:T(8,128)(2,1)}, u32[]{:S(2)}, u32[]{:S(2)}) collective-permute-start(bf16[2,256,256]{2,1,0:T(8,128)(2,1)} %get-tuple-element.16), channel_id=1, source_target_pairs={{1,0},{2,1},{3,2},{4,3},{5,4},{6,5},{7,6},{64,7},{9,8},{10,9},{11,... | collective-permute-start | bytes 786440 | tf_op jit(solution)/shard_map/weight_z2/ppermute | solution.py:369
  66.0 23.5 %collective-permute-start.7 = (bf16[4,256,256]{2,1,0:T(8,128)(2,1)S(1)}, bf16[4,256,256]{2,1,0:T(8,128)(2,1)}, u32[]{:S(2)}, u32[]{:S(2)}) collective-permute-start(bf16[4,256,256]{2,1,0:T(8,128)(2,1)S(1)} %collective-permute-done.2.up_hbm.own_1), channel_id=1, source_target_pairs={{0,32},{1,33},{2,34},{3,35},{4,36},{5,37},{6,38},{7,39},{8,40},{9,... | collective-permute-start | bytes 1572872 | tf_op jit(solution)/shard_map/weight_swap/ppermute | solution.py:377
  70.2 19.3 %collective-permute-start.10 = (bf16[4,256,256]{2,1,0:T(8,128)(2,1)S(1)}, bf16[4,256,256]{2,1,0:T(8,128)(2,1)}, u32[]{:S(2)}, u32[]{:S(2)}) collective-permute-start(bf16[4,256,256]{2,1,0:T(8,128)(2,1)S(1)} %collective-permute-done.3.down_hbm.own_3), channel_id=1, source_target_pairs={{0,32},{1,33},{2,34},{3,35},{4,36},{5,37},{6,38},{7,39},{8,40},{9,... | collective-permute-start | bytes 1572872 | tf_op jit(solution)/shard_map/weight_swap/ppermute | solution.py:377
  72.1 15.4 %collective-permute-start.5 = (bf16[2,256,256]{2,1,0:T(8,128)(2,1)S(1)}, bf16[2,256,256]{2,1,0:T(8,128)(2,1)}, u32[]{:S(2)}, u32[]{:S(2)}) collective-permute-start(bf16[2,256,256]{2,1,0:T(8,128)(2,1)S(1)} %get-tuple-element.17), channel_id=1, source_target_pairs={{71,0},{0,1},{1,2},{2,3},{3,4},{4,5},{5,6},{6,7},{79,8},{8,9},{9,1... | collective-permute-start | bytes 786440 | tf_op jit(solution)/shard_map/weight_z2/ppermute | solution.py:370
  75.9 21.7 %all-to-all-start.1 = ((bf16[16,16,256]{2,1,0:T(8,128)(2,1)}), bf16[16,16,256]{2,1,0:T(8,128)(2,1)S(1)}, u32[]{:S(2)}, u32[]{:S(2)}) async-start(bf16[16,16,256]{2,1,0:T(8,128)(2,1)} %split.1), calls=%async_computation.1 | async-start | bytes 262144 | tf_op jit(solution)/shard_map/ring_z/all_to_all | solution.py:64
  84.2 5.3 %collective-permute-start.8 = (bf16[2,256,256]{2,1,0:T(8,128)(2,1)}, bf16[2,256,256]{2,1,0:T(8,128)(2,1)S(1)}, u32[]{:S(2)}, u32[]{:S(2)}) collective-permute-start(bf16[2,256,256]{2,1,0:T(8,128)(2,1)} %collective-permute-done.4.own_2a), channel_id=1, source_target_pairs={{0,32},{1,33},{2,34},{3,35},{4,36},{5,37},{6,38},{7,39},{8,40},{9,... | collective-permute-start | bytes 786440 | tf_op jit(solution)/shard_map/weight_swap/ppermute | solution.py:377
  87.6 3.6 %collective-permute-start.9 = (bf16[2,256,256]{2,1,0:T(8,128)(2,1)}, bf16[2,256,256]{2,1,0:T(8,128)(2,1)S(1)}, u32[]{:S(2)}, u32[]{:S(2)}) collective-permute-start(bf16[2,256,256]{2,1,0:T(8,128)(2,1)} %collective-permute-done.5.own_2b), channel_id=1, source_target_pairs={{0,32},{1,33},{2,34},{3,35},{4,36},{5,37},{6,38},{7,39},{8,40},{9,... | collective-permute-start | bytes 786440 | tf_op jit(solution)/shard_map/weight_swap/ppermute | solution.py:377
  89.6 1.7 %copy-start.6 = (bf16[2,256,256]{2,1,0:T(8,128)(2,1)}, bf16[2,256,256]{2,1,0:T(8,128)(2,1)S(1)}, u32[]{:S(2)}) copy-start(bf16[2,256,256]{2,1,0:T(8,128)(2,1)S(1)} %collective-permute-done.8.other_2a) | copy-start | bytes 786436
  91.2 0.7 copy-start.7
  91.9 5.7 %copy-start.5 = (s32[512]{0:T(512)S(1)}, s32[512]{0:T(512)}, u32[]{:S(2)}) copy-start(s32[512]{0:T(512)} %param.9) | copy-start | bytes 6148

commit v6 on v5

--- a/solution.py
+++ b/solution.py
@@ -30,21 +30,29 @@
     ]
 
 
-def from_z(above_0, above_1):
+def from_z(distance):
     pairs = []
     for x, zh, c, y, zl in places():
-        z = (zh * NZL + zl + (above_0, above_1)[c]) % (NZH * NZL)
+        z = (zh * NZL + zl + distance) % (NZH * NZL)
         pairs.append((device(x, z // NZL, c, y, z % NZL), device(x, zh, c, y, zl)))
     return pairs
 
 
-Y_RINGS = [
-    [device(x, zh, c, y, zl) for y in range(NY)]
-    for x in range(NX)
-    for zh in range(NZH)
-    for c in range(NC)
-    for zl in range(NZL)
-]
+def from_y(ahead):
+    return [
+        (device(x, zh, c, (y + ahead) % NY, zl), device(x, zh, c, y, zl))
+        for x, zh, c, y, zl in places()
+    ]
+
+
+def origins():
+    pairs = []
+    for x, zh, c, y, zl in places():
+        z = (zh * NZL + zl + c * (4 if zl % 2 == 0 else -4)) % (NZH * NZL)
+        pairs.append((device(x, z // NZL, c, y, z % NZL), device(x, zh, c, y, zl)))
+    return pairs
+
+
 PLANES = [
     [device(x, zh, c, y, zl) for x in range(NX) for y in range(NY)]
     for zh in range(NZH)
@@ -142,15 +150,57 @@
         copy.wait()
 
 
-def piece_kernel(own_hbm, far_hbm, out_hbm, sems):
-    cols = pl.ds(pl.multiple_of(my_core() * COLS, COLS), COLS)
-    copies = []
-    for y in range(NY):
-        for i, source in enumerate((own_hbm, far_hbm)):
-            target = out_hbm.at[y, pl.ds(i * 128, 128)]
-            copies.append(start(source.at[:, cols], target, sems.at[2 * y + i]))
+def column_kernel(*refs):
+    *blocks, out_hbm, sems = refs
+    copies = [start(block, out_hbm.at[j], sems.at[j]) for j, block in enumerate(blocks)]
     for copy in copies:
         copy.wait()
+
+
+def partner_kernel(key_hbm, after_hbm, *refs):
+    del after_hbm
+    *sources, out_hbm, key_ref, weight_ref, out_ref, in_sems, out_sems = refs
+    key_copy = start(key_hbm.at[pl.ds(NX * NZH, 2)], key_ref, in_sems.at[0])
+    copies, place = [], 0
+    for i, source in enumerate(sources):
+        size = source.shape[0]
+        target = weight_ref.at[pl.ds(place, size)]
+        copies.append((start(source, target, in_sems.at[1 + i]), place // 2, size // 2))
+        place += size
+    key_copy.wait()
+    keys = jnp.concatenate([key_ref[0], key_ref[1]], axis=1)
+    out_copies = []
+    for copy, first, size in copies:
+        copy.wait()
+        for block in range(first, first + size):
+            weight = weight_ref[2 * block : 2 * block + 2].reshape(256, K)
+            back = lax.dot_general(
+                keys, weight, (((1,), (1,)), ((), ())), preferred_element_type=F32
+            )
+            out_ref[block] = back.astype(BF16)
+            out_copies.append(start(out_ref.at[block], out_hbm.at[block], out_sems.at[block]))
+    for copy in out_copies:
+        copy.wait()
+
+
+def partner(other, after, *sources):
+    size = sum(source.shape[0] for source in sources)
+    dma = pltpu.SemaphoreType.DMA
+    return call(
+        partner_kernel,
+        shape((size // 2, SEQ, COLS)),
+        (other, after, *sources),
+        (pl.ANY,) * (2 + len(sources)),
+        pltpu.HBM,
+        [
+            pltpu.VMEM((2, SEQ, COLS), BF16),
+            pltpu.VMEM((size, 128, K), BF16),
+            pltpu.VMEM((size // 2, SEQ, COLS), BF16),
+            dma((1 + len(sources),)),
+            dma((size // 2,)),
+        ],
+        mib=52,
+    )
 
 
 def square_kernel(
@@ -226,53 +276,60 @@
 
 
 def input_kernel(
-    hidden_hbm, key_hbm, gain_hbm, inv_hbm, own_0, own_1, own_2a, own_2b, own_3,
-    other_0, other_1, other_2a, other_2b, other_3, out_hbm,
-    hidden_ref, key_ref, gain_ref, inv_ref, own_ref, other_ref, back_ref, out_ref,
+    hidden_hbm, key_hbm, gain_hbm, inv_hbm, weight_0, weight_1, weight_3, weight_2a, weight_2b,
+    early_hbm, late_hbm, out_hbm,
+    hidden_ref, key_ref, gain_ref, inv_ref, weight_ref, early_ref, late_ref, back_ref, out_ref,
     in_sems, out_sems,
 ):
     key_copy = start(key_hbm, key_ref, in_sems.at[0])
-    places = {0: (0, 4), 1: (4, 4), 3: (12, 4), 2: (8, 2), 4: (10, 2)}
-    sources = {
-        0: (own_0, other_0),
-        1: (own_1, other_1),
-        3: (own_3, other_3),
-        2: (own_2a, other_2a),
-        4: (own_2b, other_2b),
-    }
-    weights = {}
-    for i, (part, (place, size)) in enumerate(places.items()):
-        weights[part] = [
-            start(source, ref.at[pl.ds(place, size)], in_sems.at[1 + 2 * i + j])
-            for j, (source, ref) in enumerate(zip(sources[part], (own_ref, other_ref)))
-        ]
+    groups = (
+        (weight_0, 0, 0),
+        (weight_1, 1, 0),
+        (weight_3, 7, 0),
+        (weight_2a, 2, 0),
+        (weight_2b, 6, 2),
+    )
+    copies, blocks = [], []
+    for i, (source, away, row) in enumerate(groups):
+        size = source.shape[0]
+        target = weight_ref.at[pl.ds(2 * len(blocks), size)]
+        copies.append(start(source, target, in_sems.at[1 + i]))
+        blocks += [(i, away, row + j) for j in range(0, size, 2)]
     second = [
-        start(gain_hbm, gain_ref, in_sems.at[11]),
-        start(inv_hbm, inv_ref, in_sems.at[12]),
-        start(hidden_hbm, hidden_ref, in_sems.at[13]),
+        start(early_hbm, early_ref, in_sems.at[6]),
+        start(late_hbm, late_ref, in_sems.at[7]),
+        start(gain_hbm, gain_ref, in_sems.at[8]),
+        start(inv_hbm, inv_ref, in_sems.at[9]),
+        start(hidden_hbm, hidden_ref, in_sems.at[10]),
     ]
     core = my_core()
     z_here = lax.rem(lax.axis_index("fsdp"), NZL)
-    own_cols = pl.ds(pl.multiple_of(core * COLS, COLS), COLS)
-    other_cols = pl.ds(pl.multiple_of((1 - core) * COLS, COLS), COLS)
+    y_here = lax.div(lax.axis_index("fsdp"), NZL)
+
+    def put(back, origin, away, row):
+        zl = (z_here + origin + away) & (NZL - 1)
+        for half in range(2):
+            y = (y_here + row + half) & (NY - 1)
+            cols = pl.ds(pl.multiple_of((y * NZL + zl) * 128, 128), 128)
+            back_ref[:, cols] = back[:, half * 128 : (half + 1) * 128]
+
     key_copy.wait()
-    keys = jnp.concatenate([key_ref[:, own_cols], key_ref[:, other_cols]], axis=1)
-
-    for part, (place, size) in places.items():
-        for copy in weights[part]:
-            copy.wait()
-        for i in range(size):
-            y = (place + i) % NY
-            away = (0, 1, 2, 7, 6)[part]
-            weight = jnp.concatenate([own_ref[place + i], other_ref[place + i]], axis=1)
-            back = lax.dot_general(
-                keys, weight, (((1,), (1,)), ((), ())), preferred_element_type=F32
-            )
-            for half in range(2):
-                shard = (z_here + away + 4 * half) & (NZL - 1)
-                cols = pl.ds(pl.multiple_of((y * NZL + shard) * 128, 128), 128)
-                back_ref[:, cols] = back[:, half * 128 : (half + 1) * 128]
-    for copy in second:
+    keys = key_ref[...]
+    waited = 0
+    for block, (group, away, row) in enumerate(blocks):
+        if waited == group:
+            copies[group].wait()
+            waited += 1
+        weight = weight_ref[2 * block : 2 * block + 2].reshape(256, K)
+        back = lax.dot_general(keys, weight, (((1,), (1,)), ((), ())), preferred_element_type=F32)
+        put(back, 4 * core, away, row)
+    second[0].wait()
+    second[1].wait()
+    early = early_ref.shape[0]
+    for block, (_, away, row) in enumerate(blocks):
+        back = early_ref[block] if block < early else late_ref[block - early]
+        put(back.astype(F32), 4 * (1 - core), away, row)
+    for copy in second[2:]:
         copy.wait()
 
     step, parts, width = 16, 4, 512
@@ -312,7 +369,7 @@
     barrier = lax.optimization_barrier
 
     with jax.named_scope("weight_z4"):
-        far = lax.ppermute(key_weight, AXES, from_z(4, -4))
+        origin = lax.ppermute(key_weight, AXES, origins())
     with jax.named_scope("norm"):
         own, send, inv = call(
             norm_kernel,
@@ -332,13 +389,7 @@
             ],
             mib=None,
         )
-        far, send = barrier((far, send))
         other = lax.ppermute(send, AXES, CORE_SWAP)
-    with jax.named_scope("weight_y"):
-        pieces = call(
-            piece_kernel, shape((NY, 256, COLS)), (key_weight, far), (any_, any_), hbm, [dma((8,))]
-        )
-        near = exchange(pieces, Y_RINGS)
     with jax.named_scope("squares"):
         chunks = call(
             square_kernel,
@@ -356,42 +407,51 @@
             ],
             mib=51,
         )
+        chunks, origin = barrier((chunks, origin))
     with jax.named_scope("plane"):
         chunks = exchange(chunks, PLANES)
+    with jax.named_scope("weight_y"):
+        column = [origin] + [lax.ppermute(origin, AXES, from_y(ahead)) for ahead in (1, 2, 3)]
+        near = call(
+            column_kernel, shape((NY, 128, K)), column, (any_,) * NY, hbm, [dma((NY,))], mib=52
+        )
     with jax.named_scope("weight_z1"):
-        up = lax.ppermute(near, AXES, from_z(1, 1))
-        down = lax.ppermute(near, AXES, from_z(-1, -1))
+        up = lax.ppermute(near, AXES, from_z(1))
+        down = lax.ppermute(near, AXES, from_z(-1))
     with jax.named_scope("weight_z2"):
-        half = shape((2, 256, COLS))
+        half = shape((2, 128, K))
         up_half, down_half = call(
             halves_kernel, (half, half), (up, down), (any_, any_), (hbm, hbm), [dma((2,))], mib=52
         )
-        far_up = lax.ppermute(up_half, AXES, from_z(1, 1))
-        far_down = lax.ppermute(down_half, AXES, from_z(-1, -1))
+        far_up = lax.ppermute(up_half, AXES, from_z(1))
+        far_down = lax.ppermute(down_half, AXES, from_z(-1))
+    with jax.named_scope("back_early"):
+        early = lax.ppermute(partner(other, up_half, near, up, down), AXES, CORE_SWAP)
     with jax.named_scope("split"):
         parts = call(split_kernel, shape((NZH * NZL, 16, COLS)), (chunks,), (vmem,), vmem)
     with jax.named_scope("ring_z"):
         parts = exchange(parts, Z_RINGS)
-    with jax.named_scope("weight_swap"):
-        weights = (near, up, far_up, far_down, down)
-        swapped = tuple(lax.ppermute(part, AXES, CORE_SWAP) for part in weights)
+    with jax.named_scope("back_late"):
+        late = lax.ppermute(partner(other, far_up, far_up, far_down), AXES, CORE_SWAP)
     with jax.named_scope("input_grad"):
+        weights = (near, up, down, far_up, far_down)
         input_grad = call(
             input_kernel,
             shape((SEQ, D)),
-            (hidden_in, key_grad, gain, inv, *weights, *swapped),
-            (any_,) * 14,
+            (hidden_in, key_grad, gain, inv, *weights, early, late),
+            (any_,) * 11,
             hbm,
             [
                 pltpu.VMEM((SEQ, D), BF16),
                 pltpu.VMEM((SEQ, K), BF16),
                 pltpu.VMEM((1, D), F32),
                 pltpu.VMEM((SEQ, 128), F32),
-                pltpu.VMEM((16, 256, COLS), BF16),
-                pltpu.VMEM((16, 256, COLS), BF16),
+                pltpu.VMEM((16, 128, K), BF16),
+                pltpu.VMEM((6, SEQ, COLS), BF16),
+                pltpu.VMEM((2, SEQ, COLS), BF16),
                 pltpu.VMEM((SEQ, D), F32),
                 pltpu.VMEM((SEQ, D), BF16),
-                dma((14,)),
+                dma((11,)),
                 dma((4,)),
             ],
             mib=60,

time: 100 us -> 118 us (1.18)
  the two profiles are of different devices: /device:TPU:1 before, /device:TPU:6 now
where the time goes in v6:
time: 118 us
  starting transfers between devices  56.9 us (48%)
  waiting for transfers between devices  37.7 us (32%)
  Pallas kernels  19.8 us (17%)
  local copies, waits for them, and re-layouts  2.41 us (2%)
    pallas_call x9, Pallas kernels, call(): pl.pallas_call(kernel, out_shape=outs, in_specs=[pl.BlockSpec(memory_spac...  19.8 us
    ppermute x3, waiting for transfers between devices, body(): lax.ppermute(origin, AXES, from_y(ahead))  19.4 us
    all_to_all x2, starting transfers between devices, exchange(): lax.all_to_all(value, AXES, split_axis=0, concat_axis=0, axis_index_group...  17.9 us
    ppermute x1, starting transfers between devices, body(): up = lax.ppermute(near, AXES, from_z(1))  11.5 us
    ppermute x3, starting transfers between devices, body(): lax.ppermute(origin, AXES, from_y(ahead))  11.3 us
    ppermute x1, waiting for transfers between devices, body(): down = lax.ppermute(near, AXES, from_z(-1))  10.3 us
    ppermute x1, starting transfers between devices, body(): far_up = lax.ppermute(up_half, AXES, from_z(1))  5.6 us
    all_to_all x2, waiting for transfers between devices, exchange(): lax.all_to_all(value, AXES, split_axis=0, concat_axis=0, axis_index_group...  2.83 us
  transfers between devices with their start and end apart: 13, of which 7 were waited for; matrix products, arithmetic and copies ran while one was open for 0% of the time, Pallas kernels for 14%

profile of v6, /device:TPU:6, one launch (start us, length us, event | category | flops | bytes accessed | tf_op | source)
XLA Modules:
  0.0 117.7 jit_solution(10429764900794121329)
XLA Ops:
  0.6 0.0 copy-start.4
  0.7 3.0 %norm.1 = (bf16[8,256,256]{2,1,0:T(8,128)(2,1)}, bf16[10,256,256]{2,1,0:T(8,128)(2,1)}, f32[256,128]{1,0:T(8,128)}) custom-call(bf16[256,4096]{1,0:T(8,128)(2,1)} %hidden_hbm.3, bf16[256,512]{1,0:T(8,128)(2,1)} %key_hbm.5, f32[1,4096]{1,0:T(1,128)} %bitcast.3), custom_call_target="tpu_custom_call" | custom-call | bytes 150000 | tf_op jit(solution)/shard_map/norm/pallas_call | solution.py:78
  3.6 1.9 %collective-permute-start = (bf16[10,256,256]{2,1,0:T(8,128)(2,1)}, bf16[10,256,256]{2,1,0:T(8,128)(2,1)S(1)}, u32[]{:S(2)}, u32[]{:S(2)}) collective-permute-start(bf16[10,256,256]{2,1,0:T(8,128)(2,1)} %get-tuple-element.12), channel_id=1, source_target_pairs={{0,32},{1,33},{2,34},{3,35},{4,36},{5,37},{6,38},{7,39},{8,40},{9,... | collective-permute-start | bytes 3932168 | tf_op jit(solution)/shard_map/norm/ppermute | solution.py:392
  5.6 0.7 collective-permute-start.1
  6.3 2.5 %collective-permute-done.other_hbm.key_hbm = bf16[10,256,256]{2,1,0:T(8,128)(2,1)S(1)} collective-permute-done((bf16[10,256,256]{2,1,0:T(8,128)(2,1)}, bf16[10,256,256]{2,1,0:T(8,128)(2,1)S(1)}, u32[]{:S(2)}, u32[]{:S(2)}) %collective-permute-start) | collective-permute-done | bytes 1310752 | tf_op jit(solution)/shard_map/norm/ppermute | solution.py:392
  8.8 1.7 %copy-done.6 = bf16[8,256,256]{2,1,0:T(8,128)(2,1)S(1)} copy-done((bf16[8,256,256]{2,1,0:T(8,128)(2,1)S(1)}, bf16[8,256,256]{2,1,0:T(8,128)(2,1)}, u32[]{:S(2)}) %copy-start.6) | copy-done | bytes 1048600
  10.5 3.1 %squares.1 = bf16[16,256,256]{2,1,0:T(8,128)(2,1)} custom-call(bf16[8,256,256]{2,1,0:T(8,128)(2,1)S(1)} %copy-done.6, bf16[10,256,256]{2,1,0:T(8,128)(2,1)S(1)} %collective-permute-done.other_hbm.key_hbm, bf16[256,512]{1,0:T(8,128)(2,1)S(1)} %copy-done.4), custom_call_target="tpu_custom_call" | custom-call | bytes 150000 | tf_op jit(solution)/shard_map/squares/pallas_call | solution.py:78
  13.6 9.4 %all-to-all-start = ((bf16[16,256,256]{2,1,0:T(8,128)(2,1)}), bf16[16,256,256]{2,1,0:T(8,128)(2,1)S(1)}, u32[]{:S(2)}, u32[]{:S(2)}) async-start(bf16[16,256,256]{2,1,0:T(8,128)(2,1)} %squares.1), calls=%async_computation | async-start | bytes 4194304 | tf_op jit(solution)/shard_map/plane/all_to_all | solution.py:72
  23.1 3.4 %collective-permute-start.4 = (bf16[128,512]{1,0:T(8,128)(2,1)S(1)}, bf16[128,512]{1,0:T(8,128)(2,1)S(1)}, u32[]{:S(2)}, u32[]{:S(2)}) collective-permute-start(bf16[128,512]{1,0:T(8,128)(2,1)S(1)} %collective-permute-done.1.refs_0_), channel_id=1, source_target_pairs={{24,0},{25,1},{26,2},{27,3},{28,4},{29,5},{30,6},{31,7},{0,8},{1,9... | collective-permute-start | bytes 393224 | tf_op jit(solution)/shard_map/weight_y/ppermute | solution.py:414
  26.5 4.6 %collective-permute-start.3 = (bf16[128,512]{1,0:T(8,128)(2,1)S(1)}, bf16[128,512]{1,0:T(8,128)(2,1)S(1)}, u32[]{:S(2)}, u32[]{:S(2)}) collective-permute-start(bf16[128,512]{1,0:T(8,128)(2,1)S(1)} %collective-permute-done.1.refs_0_), channel_id=1, source_target_pairs={{16,0},{17,1},{18,2},{19,3},{20,4},{21,5},{22,6},{23,7},{24,8},{25... | collective-permute-start | bytes 393224 | tf_op jit(solution)/shard_map/weight_y/ppermute | solution.py:414
  31.1 3.4 %collective-permute-start.2 = (bf16[128,512]{1,0:T(8,128)(2,1)S(1)}, bf16[128,512]{1,0:T(8,128)(2,1)S(1)}, u32[]{:S(2)}, u32[]{:S(2)}) collective-permute-start(bf16[128,512]{1,0:T(8,128)(2,1)S(1)} %collective-permute-done.1.refs_0_), channel_id=1, source_target_pairs={{8,0},{9,1},{10,2},{11,3},{12,4},{13,5},{14,6},{15,7},{16,8},{17,9... | collective-permute-start | bytes 393224 | tf_op jit(solution)/shard_map/weight_y/ppermute | solution.py:414
  34.4 19.4 %collective-permute-done.4.refs_3_ = bf16[128,512]{1,0:T(8,128)(2,1)S(1)} collective-permute-done((bf16[128,512]{1,0:T(8,128)(2,1)S(1)}, bf16[128,512]{1,0:T(8,128)(2,1)S(1)}, u32[]{:S(2)}, u32[]{:S(2)}) %collective-permute-start.4) | collective-permute-done | bytes 131104 | tf_op jit(solution)/shard_map/weight_y/ppermute | solution.py:414
  53.8 0.1 collective-permute-done.2.refs_1_
  53.9 0.7 weight_y.1.refs_0_.weight_0
  54.6 2.1 %collective-permute-start.6 = (bf16[4,128,512]{2,1,0:T(8,128)(2,1)S(1)}, bf16[4,128,512]{2,1,0:T(8,128)(2,1)S(1)}, u32[]{:S(2)}, u32[]{:S(2)}) collective-permute-start(bf16[4,128,512]{2,1,0:T(8,128)(2,1)S(1)} %weight_y.1.refs_0_.weight_0), channel_id=1, source_target_pairs={{71,0},{0,1},{1,2},{2,3},{3,4},{4,5},{5,6},{6,7},{79,8},{8,9},{9,1... | collective-permute-start | bytes 1572872 | tf_op jit(solution)/shard_map/weight_z1/ppermute | solution.py:420
  56.7 11.5 %collective-permute-start.5 = (bf16[4,128,512]{2,1,0:T(8,128)(2,1)S(1)}, bf16[4,128,512]{2,1,0:T(8,128)(2,1)S(1)}, u32[]{:S(2)}, u32[]{:S(2)}) collective-permute-start(bf16[4,128,512]{2,1,0:T(8,128)(2,1)S(1)} %weight_y.1.refs_0_.weight_0), channel_id=1, source_target_pairs={{1,0},{2,1},{3,2},{4,3},{5,4},{6,5},{7,6},{64,7},{9,8},{10,9},{11,... | collective-permute-start | bytes 1572872 | tf_op jit(solution)/shard_map/weight_z1/ppermute | solution.py:419
  68.3 10.3 %collective-permute-done.6.down_hbm.refs_2_.weight_3 = bf16[4,128,512]{2,1,0:T(8,128)(2,1)S(1)} collective-permute-done((bf16[4,128,512]{2,1,0:T(8,128)(2,1)S(1)}, bf16[4,128,512]{2,1,0:T(8,128)(2,1)S(1)}, u32[]{:S(2)}, u32[]{:S(2)}) %collective-permute-start.6) | collective-permute-done | bytes 524320 | tf_op jit(solution)/shard_map/weight_z1/ppermute | solution.py:420
  78.5 1.2 %collective-permute-done.5.up_hbm.refs_1_.weight_1 = bf16[4,128,512]{2,1,0:T(8,128)(2,1)S(1)} collective-permute-done((bf16[4,128,512]{2,1,0:T(8,128)(2,1)S(1)}, bf16[4,128,512]{2,1,0:T(8,128)(2,1)S(1)}, u32[]{:S(2)}, u32[]{:S(2)}) %collective-permute-start.5) | collective-permute-done | bytes 524320 | tf_op jit(solution)/shard_map/weight_z1/ppermute | solution.py:419
  79.7 0.8 weight_z2.1
  80.5 2.8 %back_early.1 = bf16[6,256,256]{2,1,0:T(8,128)(2,1)} custom-call(bf16[10,256,256]{2,1,0:T(8,128)(2,1)} %copy-done, bf16[2,128,512]{2,1,0:T(8,128)(2,1)S(1)} %get-tuple-element.16.after_hbm, bf16[4,128,512]{2,1,0:T(8,128)(2,1)S(1)} %weight_y.1.refs_0_.weight_0, bf16[4,128,512]{2,1,0:T(8,128)(2,1)S(1)} %collective-permute-done.5.up_hbm.refs_1_.weight_1, ...), custom_call_target="tpu_custom_call" | custom-call | bytes 150000 | tf_op jit(solution)/shard_map/back_early/pallas_call | solution.py:78
  83.3 1.9 %collective-permute-start.9 = (bf16[6,256,256]{2,1,0:T(8,128)(2,1)}, bf16[6,256,256]{2,1,0:T(8,128)(2,1)}, u32[]{:S(2)}, u32[]{:S(2)}) collective-permute-start(bf16[6,256,256]{2,1,0:T(8,128)(2,1)} %back_early.1), channel_id=1, source_target_pairs={{0,32},{1,33},{2,34},{3,35},{4,36},{5,37},{6,38},{7,39},{8,40},{9,... | collective-permute-start | bytes 2359304 | tf_op jit(solution)/shard_map/back_early/ppermute | solution.py:429
  85.3 1.9 %collective-permute-start.8 = (bf16[2,128,512]{2,1,0:T(8,128)(2,1)}, bf16[2,128,512]{2,1,0:T(8,128)(2,1)S(1)}, u32[]{:S(2)}, u32[]{:S(2)}) collective-permute-start(bf16[2,128,512]{2,1,0:T(8,128)(2,1)} %get-tuple-element.17), channel_id=1, source_target_pairs={{71,0},{0,1},{1,2},{2,3},{3,4},{4,5},{5,6},{6,7},{79,8},{8,9},{9,1... | collective-permute-start | bytes 786440 | tf_op jit(solution)/shard_map/weight_z2/ppermute | solution.py:427
  87.2 5.6 %collective-permute-start.7 = (bf16[2,128,512]{2,1,0:T(8,128)(2,1)S(1)}, bf16[2,128,512]{2,1,0:T(8,128)(2,1)S(1)}, u32[]{:S(2)}, u32[]{:S(2)}) collective-permute-start(bf16[2,128,512]{2,1,0:T(8,128)(2,1)S(1)} %get-tuple-element.16.after_hbm), channel_id=1, source_target_pairs={{1,0},{2,1},{3,2},{4,3},{5,4},{6,5},{7,6},{64,7},{9,8},{10,9},{11,... | collective-permute-start | bytes 786440 | tf_op jit(solution)/shard_map/weight_z2/ppermute | solution.py:426
  92.8 0.9 split.1
  93.7 8.5 %all-to-all-start.1 = ((bf16[16,16,256]{2,1,0:T(8,128)(2,1)}), bf16[16,16,256]{2,1,0:T(8,128)(2,1)S(1)}, u32[]{:S(2)}, u32[]{:S(2)}) async-start(bf16[16,16,256]{2,1,0:T(8,128)(2,1)} %split.1), calls=%async_computation.1 | async-start | bytes 262144 | tf_op jit(solution)/shard_map/ring_z/all_to_all | solution.py:72
  102.2 2.1 %back_late.1 = bf16[2,256,256]{2,1,0:T(8,128)(2,1)S(1)} custom-call(bf16[10,256,256]{2,1,0:T(8,128)(2,1)} %copy-done, bf16[2,128,512]{2,1,0:T(8,128)(2,1)S(1)} %collective-permute-done.7.after_hbm.refs_0_.weight_2a, bf16[2,128,512]{2,1,0:T(8,128)(2,1)S(1)} %collective-permute-done.7.after_hbm.refs_0_.weight_2a, ...), custom_call_target="tpu_custom_call" | custom-call | bytes 150000 | tf_op jit(solution)/shard_map/back_late/pallas_call | solution.py:78
  104.4 1.9 %collective-permute-start.10 = (bf16[2,256,256]{2,1,0:T(8,128)(2,1)S(1)}, bf16[2,256,256]{2,1,0:T(8,128)(2,1)S(1)}, u32[]{:S(2)}, u32[]{:S(2)}) collective-permute-start(bf16[2,256,256]{2,1,0:T(8,128)(2,1)S(1)} %back_late.1), channel_id=1, source_target_pairs={{0,32},{1,33},{2,34},{3,35},{4,36},{5,37},{6,38},{7,39},{8,40},{9,... | collective-permute-start | bytes 786440 | tf_op jit(solution)/shard_map/back_late/ppermute | solution.py:435
  106.3 1.5 %collective-permute-done.10.late_hbm = bf16[2,256,256]{2,1,0:T(8,128)(2,1)S(1)} collective-permute-done((bf16[2,256,256]{2,1,0:T(8,128)(2,1)S(1)}, bf16[2,256,256]{2,1,0:T(8,128)(2,1)S(1)}, u32[]{:S(2)}, u32[]{:S(2)}) %collective-permute-start.10) | collective-permute-done | bytes 262176 | tf_op jit(solution)/shard_map/back_late/ppermute | solution.py:435
  107.9 0.7 copy-done.9
  108.5 5.5 %input_grad.1 = bf16[256,4096]{1,0:T(8,128)(2,1)} custom-call(bf16[256,4096]{1,0:T(8,128)(2,1)} %hidden_hbm.3, bf16[256,512]{1,0:T(8,128)(2,1)} %key_hbm.5, f32[1,4096]{1,0:T(1,128)} %bitcast.4, f32[256,128]{1,0:T(8,128)} %get-tuple-element.14.inv_hbm, bf16[4,128,512]{2,1,0:T(8,128)(2,1)} %copy-done.1, bf16[4,128,512]{2,1,0:T(8,128)(2,1)} %copy-done.3, ...), custom_call_target="tpu_custom_call" | custom-call | bytes 150000 | tf_op jit(solution)/shard_map/input_grad/pallas_call | solution.py:78
  114.0 2.8 %all-to-all-done.1.in_ref = bf16[16,16,256]{2,1,0:T(8,128)(2,1)S(1)} async-done(((bf16[16,16,256]{2,1,0:T(8,128)(2,1)}), bf16[16,16,256]{2,1,0:T(8,128)(2,1)S(1)}, u32[]{:S(2)}, u32[]{:S(2)}) %all-to-all-start.1) | async-done | bytes 131104 | tf_op jit(solution)/shard_map/ring_z/all_to_all | solution.py:72
  116.9 0.8 serve.1
  (25 shorter events, 0.1 us)
Async XLA Ops:
  0.6 8.2 %copy-start.4 = (bf16[256,512]{1,0:T(8,128)(2,1)S(1)}, bf16[256,512]{1,0:T(8,128)(2,1)}, u32[]{:S(2)}) copy-start(bf16[256,512]{1,0:T(8,128)(2,1)} %key_hbm.5) | copy-start | bytes 786436
  0.6 4.9 %copy-start.10 = (bf16[128,512]{1,0:T(8,128)(2,1)S(1)}, bf16[128,512]{1,0:T(8,128)(2,1)}, u32[]{:S(2)}) copy-start(bf16[128,512]{1,0:T(8,128)(2,1)} %param.7) | copy-start | bytes 393220
  3.6 5.1 %collective-permute-start = (bf16[10,256,256]{2,1,0:T(8,128)(2,1)}, bf16[10,256,256]{2,1,0:T(8,128)(2,1)S(1)}, u32[]{:S(2)}, u32[]{:S(2)}) collective-permute-start(bf16[10,256,256]{2,1,0:T(8,128)(2,1)} %get-tuple-element.12), channel_id=1, source_target_pairs={{0,32},{1,33},{2,34},{3,35},{4,36},{5,37},{6,38},{7,39},{8,40},{9,... | collective-permute-start | bytes 3932168 | tf_op jit(solution)/shard_map/norm/ppermute | solution.py:392
  5.6 8.1 %collective-permute-start.1 = (bf16[128,512]{1,0:T(8,128)(2,1)S(1)}, bf16[128,512]{1,0:T(8,128)(2,1)S(1)}, u32[]{:S(2)}, u32[]{:S(2)}) collective-permute-start(bf16[128,512]{1,0:T(8,128)(2,1)S(1)} %copy-done.10), channel_id=1, source_target_pairs={{0,0},{1,1},{2,2},{3,3},{4,4},{5,5},{6,6},{7,7},{8,8},{9,9},{10,10... | collective-permute-start | bytes 393224 | tf_op jit(solution)/shard_map/weight_z4/ppermute | solution.py:372
  8.8 4.8 %copy-start = (bf16[10,256,256]{2,1,0:T(8,128)(2,1)}, bf16[10,256,256]{2,1,0:T(8,128)(2,1)S(1)}, u32[]{:S(2)}) copy-start(bf16[10,256,256]{2,1,0:T(8,128)(2,1)S(1)} %collective-permute-done.other_hbm.key_hbm) | copy-start | bytes 3932164
  8.8 1.7 %copy-start.6 = (bf16[8,256,256]{2,1,0:T(8,128)(2,1)S(1)}, bf16[8,256,256]{2,1,0:T(8,128)(2,1)}, u32[]{:S(2)}) copy-start(bf16[8,256,256]{2,1,0:T(8,128)(2,1)} %get-tuple-element.11.own_hbm) | copy-start | bytes 3145732
  13.6 79.2 %all-to-all-start = ((bf16[16,256,256]{2,1,0:T(8,128)(2,1)}), bf16[16,256,256]{2,1,0:T(8,128)(2,1)S(1)}, u32[]{:S(2)}, u32[]{:S(2)}) async-start(bf16[16,256,256]{2,1,0:T(8,128)(2,1)} %squares.1), calls=%async_computation | async-start | bytes 4194304 | tf_op jit(solution)/shard_map/plane/all_to_all | solution.py:72
  23.1 30.7 %collective-permute-start.4 = (bf16[128,512]{1,0:T(8,128)(2,1)S(1)}, bf16[128,512]{1,0:T(8,128)(2,1)S(1)}, u32[]{:S(2)}, u32[]{:S(2)}) collective-permute-start(bf16[128,512]{1,0:T(8,128)(2,1)S(1)} %collective-permute-done.1.refs_0_), channel_id=1, source_target_pairs={{24,0},{25,1},{26,2},{27,3},{28,4},{29,5},{30,6},{31,7},{0,8},{1,9... | collective-permute-start | bytes 393224 | tf_op jit(solution)/shard_map/weight_y/ppermute | solution.py:414
  26.5 27.3 %collective-permute-start.3 = (bf16[128,512]{1,0:T(8,128)(2,1)S(1)}, bf16[128,512]{1,0:T(8,128)(2,1)S(1)}, u32[]{:S(2)}, u32[]{:S(2)}) collective-permute-start(bf16[128,512]{1,0:T(8,128)(2,1)S(1)} %collective-permute-done.1.refs_0_), channel_id=1, source_target_pairs={{16,0},{17,1},{18,2},{19,3},{20,4},{21,5},{22,6},{23,7},{24,8},{25... | collective-permute-start | bytes 393224 | tf_op jit(solution)/shard_map/weight_y/ppermute | solution.py:414
  31.1 22.8 %collective-permute-start.2 = (bf16[128,512]{1,0:T(8,128)(2,1)S(1)}, bf16[128,512]{1,0:T(8,128)(2,1)S(1)}, u32[]{:S(2)}, u32[]{:S(2)}) collective-permute-start(bf16[128,512]{1,0:T(8,128)(2,1)S(1)} %collective-permute-done.1.refs_0_), channel_id=1, source_target_pairs={{8,0},{9,1},{10,2},{11,3},{12,4},{13,5},{14,6},{15,7},{16,8},{17,9... | collective-permute-start | bytes 393224 | tf_op jit(solution)/shard_map/weight_y/ppermute | solution.py:414
  54.6 28.7 %copy-start.1 = (bf16[4,128,512]{2,1,0:T(8,128)(2,1)}, bf16[4,128,512]{2,1,0:T(8,128)(2,1)S(1)}, u32[]{:S(2)}) copy-start(bf16[4,128,512]{2,1,0:T(8,128)(2,1)S(1)} %weight_y.1.refs_0_.weight_0) | copy-start | bytes 1572868
  54.6 23.9 %collective-permute-start.6 = (bf16[4,128,512]{2,1,0:T(8,128)(2,1)S(1)}, bf16[4,128,512]{2,1,0:T(8,128)(2,1)S(1)}, u32[]{:S(2)}, u32[]{:S(2)}) collective-permute-start(bf16[4,128,512]{2,1,0:T(8,128)(2,1)S(1)} %weight_y.1.refs_0_.weight_0), channel_id=1, source_target_pairs={{71,0},{0,1},{1,2},{2,3},{3,4},{4,5},{5,6},{6,7},{79,8},{8,9},{9,1... | collective-permute-start | bytes 1572872 | tf_op jit(solution)/shard_map/weight_z1/ppermute | solution.py:420
  56.7 23.0 %collective-permute-start.5 = (bf16[4,128,512]{2,1,0:T(8,128)(2,1)S(1)}, bf16[4,128,512]{2,1,0:T(8,128)(2,1)S(1)}, u32[]{:S(2)}, u32[]{:S(2)}) collective-permute-start(bf16[4,128,512]{2,1,0:T(8,128)(2,1)S(1)} %weight_y.1.refs_0_.weight_0), channel_id=1, source_target_pairs={{1,0},{2,1},{3,2},{4,3},{5,4},{6,5},{7,6},{64,7},{9,8},{10,9},{11,... | collective-permute-start | bytes 1572872 | tf_op jit(solution)/shard_map/weight_z1/ppermute | solution.py:419
  78.5 4.8 %copy-start.2 = (bf16[4,128,512]{2,1,0:T(8,128)(2,1)}, bf16[4,128,512]{2,1,0:T(8,128)(2,1)S(1)}, u32[]{:S(2)}) copy-start(bf16[4,128,512]{2,1,0:T(8,128)(2,1)S(1)} %collective-permute-done.6.down_hbm.refs_2_.weight_3) | copy-start | bytes 1572868
  79.7 3.6 %copy-start.3 = (bf16[4,128,512]{2,1,0:T(8,128)(2,1)}, bf16[4,128,512]{2,1,0:T(8,128)(2,1)S(1)}, u32[]{:S(2)}) copy-start(bf16[4,128,512]{2,1,0:T(8,128)(2,1)S(1)} %collective-permute-done.5.up_hbm.refs_1_.weight_1) | copy-start | bytes 1572868
  83.3 24.5 %collective-permute-start.9 = (bf16[6,256,256]{2,1,0:T(8,128)(2,1)}, bf16[6,256,256]{2,1,0:T(8,128)(2,1)}, u32[]{:S(2)}, u32[]{:S(2)}) collective-permute-start(bf16[6,256,256]{2,1,0:T(8,128)(2,1)} %back_early.1), channel_id=1, source_target_pairs={{0,32},{1,33},{2,34},{3,35},{4,36},{5,37},{6,38},{7,39},{8,40},{9,... | collective-permute-start | bytes 2359304 | tf_op jit(solution)/shard_map/back_early/ppermute | solution.py:429
  85.3 16.9 %collective-permute-start.8 = (bf16[2,128,512]{2,1,0:T(8,128)(2,1)}, bf16[2,128,512]{2,1,0:T(8,128)(2,1)S(1)}, u32[]{:S(2)}, u32[]{:S(2)}) collective-permute-start(bf16[2,128,512]{2,1,0:T(8,128)(2,1)} %get-tuple-element.17), channel_id=1, source_target_pairs={{71,0},{0,1},{1,2},{2,3},{3,4},{4,5},{5,6},{6,7},{79,8},{8,9},{9,1... | collective-permute-start | bytes 786440 | tf_op jit(solution)/shard_map/weight_z2/ppermute | solution.py:427
  87.2 15.0 %collective-permute-start.7 = (bf16[2,128,512]{2,1,0:T(8,128)(2,1)S(1)}, bf16[2,128,512]{2,1,0:T(8,128)(2,1)S(1)}, u32[]{:S(2)}, u32[]{:S(2)}) collective-permute-start(bf16[2,128,512]{2,1,0:T(8,128)(2,1)S(1)} %get-tuple-element.16.after_hbm), channel_id=1, source_target_pairs={{1,0},{2,1},{3,2},{4,3},{5,4},{6,5},{7,6},{64,7},{9,8},{10,9},{11,... | collective-permute-start | bytes 786440 | tf_op jit(solution)/shard_map/weight_z2/ppermute | solution.py:426
  93.7 23.1 %all-to-all-start.1 = ((bf16[16,16,256]{2,1,0:T(8,128)(2,1)}), bf16[16,16,256]{2,1,0:T(8,128)(2,1)S(1)}, u32[]{:S(2)}, u32[]{:S(2)}) async-start(bf16[16,16,256]{2,1,0:T(8,128)(2,1)} %split.1), calls=%async_computation.1 | async-start | bytes 262144 | tf_op jit(solution)/shard_map/ring_z/all_to_all | solution.py:72
  102.2 5.6 %copy-start.7 = (bf16[2,128,512]{2,1,0:T(8,128)(2,1)}, bf16[2,128,512]{2,1,0:T(8,128)(2,1)S(1)}, u32[]{:S(2)}) copy-start(bf16[2,128,512]{2,1,0:T(8,128)(2,1)S(1)} %collective-permute-done.8.refs_1_.weight_2b) | copy-start | bytes 786436
  102.2 5.6 %copy-start.5 = (bf16[2,128,512]{2,1,0:T(8,128)(2,1)}, bf16[2,128,512]{2,1,0:T(8,128)(2,1)S(1)}, u32[]{:S(2)}) copy-start(bf16[2,128,512]{2,1,0:T(8,128)(2,1)S(1)} %collective-permute-done.7.after_hbm.refs_0_.weight_2a) | copy-start | bytes 786436
  104.4 3.4 %collective-permute-start.10 = (bf16[2,256,256]{2,1,0:T(8,128)(2,1)S(1)}, bf16[2,256,256]{2,1,0:T(8,128)(2,1)S(1)}, u32[]{:S(2)}, u32[]{:S(2)}) collective-permute-start(bf16[2,256,256]{2,1,0:T(8,128)(2,1)S(1)} %back_late.1), channel_id=1, source_target_pairs={{0,32},{1,33},{2,34},{3,35},{4,36},{5,37},{6,38},{7,39},{8,40},{9,... | collective-permute-start | bytes 786440 | tf_op jit(solution)/shard_map/back_late/ppermute | solution.py:435
  107.8 0.7 copy-start.9
  108.5 8.3 %copy-start.8 = (s32[512]{0:T(512)S(1)}, s32[512]{0:T(512)}, u32[]{:S(2)}) copy-start(s32[512]{0:T(512)} %param.9) | copy-start | bytes 6148

commit v7 on v6

--- a/solution.py
+++ b/solution.py
@@ -389,6 +389,7 @@
             ],
             mib=None,
         )
+        origin, send = barrier((origin, send))
         other = lax.ppermute(send, AXES, CORE_SWAP)
     with jax.named_scope("squares"):
         chunks = call(
@@ -405,13 +406,14 @@
                 dma((10,)),
                 dma((blocks, NY)),
             ],
-            mib=51,
-        )
-        chunks, origin = barrier((chunks, origin))
+            mib=60,
+        )
+    with jax.named_scope("weight_y"):
+        column = [origin] + [lax.ppermute(origin, AXES, from_y(ahead)) for ahead in (1, 2, 3)]
+        chunks, *column = barrier((chunks, *column))
     with jax.named_scope("plane"):
         chunks = exchange(chunks, PLANES)
     with jax.named_scope("weight_y"):
-        column = [origin] + [lax.ppermute(origin, AXES, from_y(ahead)) for ahead in (1, 2, 3)]
         near = call(
             column_kernel, shape((NY, 128, K)), column, (any_,) * NY, hbm, [dma((NY,))], mib=52
         )

time: 118 us -> 98 us (0.83)
  the two profiles are of different devices: /device:TPU:6 before, /device:TPU:2 now
where the time goes in v7:
time: 98 us; the launch traced here: 97.4 us
  starting transfers between devices  59.9 us (61%)
  Pallas kernels  20.8 us (21%)
  waiting for transfers between devices  14 us (14%)
  local copies, waits for them, and re-layouts  1.77 us (2%)
    pallas_call x9, Pallas kernels, call(): pl.pallas_call(kernel, out_shape=outs, in_specs=[pl.BlockSpec(memory_spac...  20.8 us
    all_to_all x2, starting transfers between devices, exchange(): lax.all_to_all(value, AXES, split_axis=0, concat_axis=0, axis_index_group...  13.6 us
    ppermute x1, starting transfers between devices, body(): other = lax.ppermute(send, AXES, CORE_SWAP)  13.3 us
    ppermute x3, starting transfers between devices, body(): lax.ppermute(origin, AXES, from_y(ahead))  11.6 us
    ppermute x1, waiting for transfers between devices, body(): down = lax.ppermute(near, AXES, from_z(-1))  8.52 us
    ppermute x1, starting transfers between devices, body(): up = lax.ppermute(near, AXES, from_z(1))  6.52 us
    ppermute x1, starting transfers between devices, body(): far_up = lax.ppermute(up_half, AXES, from_z(1))  5.61 us
    all_to_all x2, waiting for transfers between devices, exchange(): lax.all_to_all(value, AXES, split_axis=0, concat_axis=0, axis_index_group...  2.82 us
  transfers between devices with their start and end apart: 13, of which 4 were waited for; matrix products, arithmetic and copies ran while one was open for 0% of the time, Pallas kernels for 20%

profile of v7, /device:TPU:2, one launch (start us, length us, event | category | flops | bytes accessed | tf_op | source)
XLA Modules:
  0.0 97.4 jit_solution(419436733505609460)
XLA Ops:
  0.6 1.6 %collective-permute-start = (bf16[128,512]{1,0:T(8,128)(2,1)}, bf16[128,512]{1,0:T(8,128)(2,1)S(1)}, u32[]{:S(2)}, u32[]{:S(2)}) collective-permute-start(bf16[128,512]{1,0:T(8,128)(2,1)} %param.7), channel_id=1, source_target_pairs={{0,0},{1,1},{2,2},{3,3},{4,4},{5,5},{6,6},{7,7},{8,8},{9,9},{10,10... | collective-permute-start | bytes 393224 | tf_op jit(solution)/shard_map/weight_z4/ppermute | solution.py:372
  2.2 2.9 %norm.1 = (bf16[8,256,256]{2,1,0:T(8,128)(2,1)}, bf16[10,256,256]{2,1,0:T(8,128)(2,1)}, f32[256,128]{1,0:T(8,128)}) custom-call(bf16[256,4096]{1,0:T(8,128)(2,1)} %hidden_hbm.3, bf16[256,512]{1,0:T(8,128)(2,1)} %key_hbm.5, f32[1,4096]{1,0:T(1,128)} %bitcast.3), custom_call_target="tpu_custom_call" | custom-call | bytes 150000 | tf_op jit(solution)/shard_map/norm/pallas_call | solution.py:78
  5.1 0.0 collective-permute-done.refs_0_
  5.1 13.3 %collective-permute-start.1 = (bf16[10,256,256]{2,1,0:T(8,128)(2,1)}, bf16[10,256,256]{2,1,0:T(8,128)(2,1)S(1)}, u32[]{:S(2)}, u32[]{:S(2)}) collective-permute-start(bf16[10,256,256]{2,1,0:T(8,128)(2,1)} %get-tuple-element.18), channel_id=1, source_target_pairs={{0,32},{1,33},{2,34},{3,35},{4,36},{5,37},{6,38},{7,39},{8,40},{9,... | collective-permute-start | bytes 3932168 | tf_op jit(solution)/shard_map/norm/ppermute | solution.py:393
  18.5 3.5 %collective-permute-start.4 = (bf16[128,512]{1,0:T(8,128)(2,1)S(1)}, bf16[128,512]{1,0:T(8,128)(2,1)S(1)}, u32[]{:S(2)}, u32[]{:S(2)}) collective-permute-start(bf16[128,512]{1,0:T(8,128)(2,1)S(1)} %collective-permute-done.refs_0_), channel_id=1, source_target_pairs={{24,0},{25,1},{26,2},{27,3},{28,4},{29,5},{30,6},{31,7},{0,8},{1,9... | collective-permute-start | bytes 393224 | tf_op jit(solution)/shard_map/weight_y/ppermute | solution.py:412
  22.0 4.8 %collective-permute-start.3 = (bf16[128,512]{1,0:T(8,128)(2,1)S(1)}, bf16[128,512]{1,0:T(8,128)(2,1)S(1)}, u32[]{:S(2)}, u32[]{:S(2)}) collective-permute-start(bf16[128,512]{1,0:T(8,128)(2,1)S(1)} %collective-permute-done.refs_0_), channel_id=1, source_target_pairs={{16,0},{17,1},{18,2},{19,3},{20,4},{21,5},{22,6},{23,7},{24,8},{25... | collective-permute-start | bytes 393224 | tf_op jit(solution)/shard_map/weight_y/ppermute | solution.py:412
  26.8 3.3 %collective-permute-start.2 = (bf16[128,512]{1,0:T(8,128)(2,1)S(1)}, bf16[128,512]{1,0:T(8,128)(2,1)S(1)}, u32[]{:S(2)}, u32[]{:S(2)}) collective-permute-start(bf16[128,512]{1,0:T(8,128)(2,1)S(1)} %collective-permute-done.refs_0_), channel_id=1, source_target_pairs={{8,0},{9,1},{10,2},{11,3},{12,4},{13,5},{14,6},{15,7},{16,8},{17,9... | collective-permute-start | bytes 393224 | tf_op jit(solution)/shard_map/weight_y/ppermute | solution.py:412
  30.0 0.0 collective-permute-done.1.other_hbm.key_hbm
  30.1 1.1 %copy-done.6 = bf16[10,256,256]{2,1,0:T(8,128)(2,1)} copy-done((bf16[10,256,256]{2,1,0:T(8,128)(2,1)}, bf16[10,256,256]{2,1,0:T(8,128)(2,1)S(1)}, u32[]{:S(2)}) %copy-start.6) | copy-done | bytes 1310744
  31.1 4.1 %squares.1 = bf16[16,256,256]{2,1,0:T(8,128)(2,1)} custom-call(bf16[8,256,256]{2,1,0:T(8,128)(2,1)} %get-tuple-element.16.own_hbm, bf16[10,256,256]{2,1,0:T(8,128)(2,1)} %copy-done.6, bf16[256,512]{1,0:T(8,128)(2,1)} %key_hbm.5), custom_call_target="tpu_custom_call" | custom-call | bytes 150000 | tf_op jit(solution)/shard_map/squares/pallas_call | solution.py:78
  35.2 0.0 collective-permute-done.4.refs_3_
  35.3 0.0 collective-permute-done.3.refs_2_
  35.3 5.2 %all-to-all-start = ((bf16[16,256,256]{2,1,0:T(8,128)(2,1)}), bf16[16,256,256]{2,1,0:T(8,128)(2,1)S(1)}, u32[]{:S(2)}, u32[]{:S(2)}) async-start(bf16[16,256,256]{2,1,0:T(8,128)(2,1)} %squares.1), calls=%async_computation | async-start | bytes 4194304 | tf_op jit(solution)/shard_map/plane/all_to_all | solution.py:72
  40.5 0.7 weight_y.1.refs_0_.weight_0
  41.2 1.9 %collective-permute-start.6 = (bf16[4,128,512]{2,1,0:T(8,128)(2,1)S(1)}, bf16[4,128,512]{2,1,0:T(8,128)(2,1)S(1)}, u32[]{:S(2)}, u32[]{:S(2)}) collective-permute-start(bf16[4,128,512]{2,1,0:T(8,128)(2,1)S(1)} %weight_y.1.refs_0_.weight_0), channel_id=1, source_target_pairs={{71,0},{0,1},{1,2},{2,3},{3,4},{4,5},{5,6},{6,7},{79,8},{8,9},{9,1... | collective-permute-start | bytes 1572872 | tf_op jit(solution)/shard_map/weight_z1/ppermute | solution.py:422
  43.2 6.5 %collective-permute-start.5 = (bf16[4,128,512]{2,1,0:T(8,128)(2,1)S(1)}, bf16[4,128,512]{2,1,0:T(8,128)(2,1)S(1)}, u32[]{:S(2)}, u32[]{:S(2)}) collective-permute-start(bf16[4,128,512]{2,1,0:T(8,128)(2,1)S(1)} %weight_y.1.refs_0_.weight_0), channel_id=1, source_target_pairs={{1,0},{2,1},{3,2},{4,3},{5,4},{6,5},{7,6},{64,7},{9,8},{10,9},{11,... | collective-permute-start | bytes 1572872 | tf_op jit(solution)/shard_map/weight_z1/ppermute | solution.py:421
  49.7 8.5 %collective-permute-done.6.down_hbm.refs_2_.weight_3 = bf16[4,128,512]{2,1,0:T(8,128)(2,1)S(1)} collective-permute-done((bf16[4,128,512]{2,1,0:T(8,128)(2,1)S(1)}, bf16[4,128,512]{2,1,0:T(8,128)(2,1)S(1)}, u32[]{:S(2)}, u32[]{:S(2)}) %collective-permute-start.6) | collective-permute-done | bytes 524320 | tf_op jit(solution)/shard_map/weight_z1/ppermute | solution.py:422
  58.2 1.2 %collective-permute-done.5.up_hbm.refs_1_.weight_1 = bf16[4,128,512]{2,1,0:T(8,128)(2,1)S(1)} collective-permute-done((bf16[4,128,512]{2,1,0:T(8,128)(2,1)S(1)}, bf16[4,128,512]{2,1,0:T(8,128)(2,1)S(1)}, u32[]{:S(2)}, u32[]{:S(2)}) %collective-permute-start.5) | collective-permute-done | bytes 524320 | tf_op jit(solution)/shard_map/weight_z1/ppermute | solution.py:421
  59.4 0.8 weight_z2.1
  60.2 2.8 %back_early.1 = bf16[6,256,256]{2,1,0:T(8,128)(2,1)} custom-call(bf16[10,256,256]{2,1,0:T(8,128)(2,1)} %copy-done.6, bf16[2,128,512]{2,1,0:T(8,128)(2,1)S(1)} %get-tuple-element.26.after_hbm, bf16[4,128,512]{2,1,0:T(8,128)(2,1)S(1)} %weight_y.1.refs_0_.weight_0, bf16[4,128,512]{2,1,0:T(8,128)(2,1)S(1)} %collective-permute-done.5.up_hbm.refs_1_.weight_1, ...), custom_call_target="tpu_custom_call" | custom-call | bytes 150000 | tf_op jit(solution)/shard_map/back_early/pallas_call | solution.py:78
  63.0 1.9 %collective-permute-start.9 = (bf16[6,256,256]{2,1,0:T(8,128)(2,1)}, bf16[6,256,256]{2,1,0:T(8,128)(2,1)}, u32[]{:S(2)}, u32[]{:S(2)}) collective-permute-start(bf16[6,256,256]{2,1,0:T(8,128)(2,1)} %back_early.1), channel_id=1, source_target_pairs={{0,32},{1,33},{2,34},{3,35},{4,36},{5,37},{6,38},{7,39},{8,40},{9,... | collective-permute-start | bytes 2359304 | tf_op jit(solution)/shard_map/back_early/ppermute | solution.py:431
  64.9 1.9 %collective-permute-start.8 = (bf16[2,128,512]{2,1,0:T(8,128)(2,1)}, bf16[2,128,512]{2,1,0:T(8,128)(2,1)S(1)}, u32[]{:S(2)}, u32[]{:S(2)}) collective-permute-start(bf16[2,128,512]{2,1,0:T(8,128)(2,1)} %get-tuple-element.27), channel_id=1, source_target_pairs={{71,0},{0,1},{1,2},{2,3},{3,4},{4,5},{5,6},{6,7},{79,8},{8,9},{9,1... | collective-permute-start | bytes 786440 | tf_op jit(solution)/shard_map/weight_z2/ppermute | solution.py:429
  66.9 5.6 %collective-permute-start.7 = (bf16[2,128,512]{2,1,0:T(8,128)(2,1)S(1)}, bf16[2,128,512]{2,1,0:T(8,128)(2,1)S(1)}, u32[]{:S(2)}, u32[]{:S(2)}) collective-permute-start(bf16[2,128,512]{2,1,0:T(8,128)(2,1)S(1)} %get-tuple-element.26.after_hbm), channel_id=1, source_target_pairs={{1,0},{2,1},{3,2},{4,3},{5,4},{6,5},{7,6},{64,7},{9,8},{10,9},{11,... | collective-permute-start | bytes 786440 | tf_op jit(solution)/shard_map/weight_z2/ppermute | solution.py:428
  72.5 1.0 split.1
  73.5 8.4 %all-to-all-start.1 = ((bf16[16,16,256]{2,1,0:T(8,128)(2,1)}), bf16[16,16,256]{2,1,0:T(8,128)(2,1)S(1)}, u32[]{:S(2)}, u32[]{:S(2)}) async-start(bf16[16,16,256]{2,1,0:T(8,128)(2,1)} %split.1), calls=%async_computation.1 | async-start | bytes 262144 | tf_op jit(solution)/shard_map/ring_z/all_to_all | solution.py:72
  81.9 2.1 %back_late.1 = bf16[2,256,256]{2,1,0:T(8,128)(2,1)S(1)} custom-call(bf16[10,256,256]{2,1,0:T(8,128)(2,1)} %copy-done.6, bf16[2,128,512]{2,1,0:T(8,128)(2,1)S(1)} %collective-permute-done.7.after_hbm.refs_0_.weight_2a, bf16[2,128,512]{2,1,0:T(8,128)(2,1)S(1)} %collective-permute-done.7.after_hbm.refs_0_.weight_2a, ...), custom_call_target="tpu_custom_call" | custom-call | bytes 150000 | tf_op jit(solution)/shard_map/back_late/pallas_call | solution.py:78
  84.1 1.9 %collective-permute-start.10 = (bf16[2,256,256]{2,1,0:T(8,128)(2,1)S(1)}, bf16[2,256,256]{2,1,0:T(8,128)(2,1)S(1)}, u32[]{:S(2)}, u32[]{:S(2)}) collective-permute-start(bf16[2,256,256]{2,1,0:T(8,128)(2,1)S(1)} %back_late.1), channel_id=1, source_target_pairs={{0,32},{1,33},{2,34},{3,35},{4,36},{5,37},{6,38},{7,39},{8,40},{9,... | collective-permute-start | bytes 786440 | tf_op jit(solution)/shard_map/back_late/ppermute | solution.py:437
  86.0 1.5 %collective-permute-done.10.late_hbm = bf16[2,256,256]{2,1,0:T(8,128)(2,1)S(1)} collective-permute-done((bf16[2,256,256]{2,1,0:T(8,128)(2,1)S(1)}, bf16[2,256,256]{2,1,0:T(8,128)(2,1)S(1)}, u32[]{:S(2)}, u32[]{:S(2)}) %collective-permute-start.10) | collective-permute-done | bytes 262176 | tf_op jit(solution)/shard_map/back_late/ppermute | solution.py:437
  87.5 0.7 copy-done.7
  88.2 5.5 %input_grad.1 = bf16[256,4096]{1,0:T(8,128)(2,1)} custom-call(bf16[256,4096]{1,0:T(8,128)(2,1)} %hidden_hbm.3, bf16[256,512]{1,0:T(8,128)(2,1)} %key_hbm.5, f32[1,4096]{1,0:T(1,128)} %bitcast.4, f32[256,128]{1,0:T(8,128)} %get-tuple-element.21.inv_hbm, bf16[4,128,512]{2,1,0:T(8,128)(2,1)} %copy-done, bf16[4,128,512]{2,1,0:T(8,128)(2,1)} %copy-done.2, ...), custom_call_target="tpu_custom_call" | custom-call | bytes 150000 | tf_op jit(solution)/shard_map/input_grad/pallas_call | solution.py:78
  93.8 2.8 %all-to-all-done.1.in_ref = bf16[16,16,256]{2,1,0:T(8,128)(2,1)S(1)} async-done(((bf16[16,16,256]{2,1,0:T(8,128)(2,1)}), bf16[16,16,256]{2,1,0:T(8,128)(2,1)S(1)}, u32[]{:S(2)}, u32[]{:S(2)}) %all-to-all-start.1) | async-done | bytes 131104 | tf_op jit(solution)/shard_map/ring_z/all_to_all | solution.py:72
  96.6 0.8 serve.1
  (19 shorter events, 0.0 us)
Async XLA Ops:
  0.6 4.5 %collective-permute-start = (bf16[128,512]{1,0:T(8,128)(2,1)}, bf16[128,512]{1,0:T(8,128)(2,1)S(1)}, u32[]{:S(2)}, u32[]{:S(2)}) collective-permute-start(bf16[128,512]{1,0:T(8,128)(2,1)} %param.7), channel_id=1, source_target_pairs={{0,0},{1,1},{2,2},{3,3},{4,4},{5,5},{6,6},{7,7},{8,8},{9,9},{10,10... | collective-permute-start | bytes 393224 | tf_op jit(solution)/shard_map/weight_z4/ppermute | solution.py:372
  5.1 24.9 %collective-permute-start.1 = (bf16[10,256,256]{2,1,0:T(8,128)(2,1)}, bf16[10,256,256]{2,1,0:T(8,128)(2,1)S(1)}, u32[]{:S(2)}, u32[]{:S(2)}) collective-permute-start(bf16[10,256,256]{2,1,0:T(8,128)(2,1)} %get-tuple-element.18), channel_id=1, source_target_pairs={{0,32},{1,33},{2,34},{3,35},{4,36},{5,37},{6,38},{7,39},{8,40},{9,... | collective-permute-start | bytes 3932168 | tf_op jit(solution)/shard_map/norm/ppermute | solution.py:393
  18.5 16.8 %collective-permute-start.4 = (bf16[128,512]{1,0:T(8,128)(2,1)S(1)}, bf16[128,512]{1,0:T(8,128)(2,1)S(1)}, u32[]{:S(2)}, u32[]{:S(2)}) collective-permute-start(bf16[128,512]{1,0:T(8,128)(2,1)S(1)} %collective-permute-done.refs_0_), channel_id=1, source_target_pairs={{24,0},{25,1},{26,2},{27,3},{28,4},{29,5},{30,6},{31,7},{0,8},{1,9... | collective-permute-start | bytes 393224 | tf_op jit(solution)/shard_map/weight_y/ppermute | solution.py:412
  22.0 13.3 %collective-permute-start.3 = (bf16[128,512]{1,0:T(8,128)(2,1)S(1)}, bf16[128,512]{1,0:T(8,128)(2,1)S(1)}, u32[]{:S(2)}, u32[]{:S(2)}) collective-permute-start(bf16[128,512]{1,0:T(8,128)(2,1)S(1)} %collective-permute-done.refs_0_), channel_id=1, source_target_pairs={{16,0},{17,1},{18,2},{19,3},{20,4},{21,5},{22,6},{23,7},{24,8},{25... | collective-permute-start | bytes 393224 | tf_op jit(solution)/shard_map/weight_y/ppermute | solution.py:412
  26.8 8.5 %collective-permute-start.2 = (bf16[128,512]{1,0:T(8,128)(2,1)S(1)}, bf16[128,512]{1,0:T(8,128)(2,1)S(1)}, u32[]{:S(2)}, u32[]{:S(2)}) collective-permute-start(bf16[128,512]{1,0:T(8,128)(2,1)S(1)} %collective-permute-done.refs_0_), channel_id=1, source_target_pairs={{8,0},{9,1},{10,2},{11,3},{12,4},{13,5},{14,6},{15,7},{16,8},{17,9... | collective-permute-start | bytes 393224 | tf_op jit(solution)/shard_map/weight_y/ppermute | solution.py:412
  30.1 1.1 %copy-start.6 = (bf16[10,256,256]{2,1,0:T(8,128)(2,1)}, bf16[10,256,256]{2,1,0:T(8,128)(2,1)S(1)}, u32[]{:S(2)}) copy-start(bf16[10,256,256]{2,1,0:T(8,128)(2,1)S(1)} %collective-permute-done.1.other_hbm.key_hbm) | copy-start | bytes 3932164
  35.3 37.2 %all-to-all-start = ((bf16[16,256,256]{2,1,0:T(8,128)(2,1)}), bf16[16,256,256]{2,1,0:T(8,128)(2,1)S(1)}, u32[]{:S(2)}, u32[]{:S(2)}) async-start(bf16[16,256,256]{2,1,0:T(8,128)(2,1)} %squares.1), calls=%async_computation | async-start | bytes 4194304 | tf_op jit(solution)/shard_map/plane/all_to_all | solution.py:72
  41.2 21.8 %copy-start = (bf16[4,128,512]{2,1,0:T(8,128)(2,1)}, bf16[4,128,512]{2,1,0:T(8,128)(2,1)S(1)}, u32[]{:S(2)}) copy-start(bf16[4,128,512]{2,1,0:T(8,128)(2,1)S(1)} %weight_y.1.refs_0_.weight_0) | copy-start | bytes 1572868
  41.2 17.0 %collective-permute-start.6 = (bf16[4,128,512]{2,1,0:T(8,128)(2,1)S(1)}, bf16[4,128,512]{2,1,0:T(8,128)(2,1)S(1)}, u32[]{:S(2)}, u32[]{:S(2)}) collective-permute-start(bf16[4,128,512]{2,1,0:T(8,128)(2,1)S(1)} %weight_y.1.refs_0_.weight_0), channel_id=1, source_target_pairs={{71,0},{0,1},{1,2},{2,3},{3,4},{4,5},{5,6},{6,7},{79,8},{8,9},{9,1... | collective-permute-start | bytes 1572872 | tf_op jit(solution)/shard_map/weight_z1/ppermute | solution.py:422
  43.2 16.2 %collective-permute-start.5 = (bf16[4,128,512]{2,1,0:T(8,128)(2,1)S(1)}, bf16[4,128,512]{2,1,0:T(8,128)(2,1)S(1)}, u32[]{:S(2)}, u32[]{:S(2)}) collective-permute-start(bf16[4,128,512]{2,1,0:T(8,128)(2,1)S(1)} %weight_y.1.refs_0_.weight_0), channel_id=1, source_target_pairs={{1,0},{2,1},{3,2},{4,3},{5,4},{6,5},{7,6},{64,7},{9,8},{10,9},{11,... | collective-permute-start | bytes 1572872 | tf_op jit(solution)/shard_map/weight_z1/ppermute | solution.py:421
  58.2 4.8 %copy-start.1 = (bf16[4,128,512]{2,1,0:T(8,128)(2,1)}, bf16[4,128,512]{2,1,0:T(8,128)(2,1)S(1)}, u32[]{:S(2)}) copy-start(bf16[4,128,512]{2,1,0:T(8,128)(2,1)S(1)} %collective-permute-done.6.down_hbm.refs_2_.weight_3) | copy-start | bytes 1572868
  59.4 3.6 %copy-start.2 = (bf16[4,128,512]{2,1,0:T(8,128)(2,1)}, bf16[4,128,512]{2,1,0:T(8,128)(2,1)S(1)}, u32[]{:S(2)}) copy-start(bf16[4,128,512]{2,1,0:T(8,128)(2,1)S(1)} %collective-permute-done.5.up_hbm.refs_1_.weight_1) | copy-start | bytes 1572868
  63.0 24.5 %collective-permute-start.9 = (bf16[6,256,256]{2,1,0:T(8,128)(2,1)}, bf16[6,256,256]{2,1,0:T(8,128)(2,1)}, u32[]{:S(2)}, u32[]{:S(2)}) collective-permute-start(bf16[6,256,256]{2,1,0:T(8,128)(2,1)} %back_early.1), channel_id=1, source_target_pairs={{0,32},{1,33},{2,34},{3,35},{4,36},{5,37},{6,38},{7,39},{8,40},{9,... | collective-permute-start | bytes 2359304 | tf_op jit(solution)/shard_map/back_early/ppermute | solution.py:431
  64.9 17.0 %collective-permute-start.8 = (bf16[2,128,512]{2,1,0:T(8,128)(2,1)}, bf16[2,128,512]{2,1,0:T(8,128)(2,1)S(1)}, u32[]{:S(2)}, u32[]{:S(2)}) collective-permute-start(bf16[2,128,512]{2,1,0:T(8,128)(2,1)} %get-tuple-element.27), channel_id=1, source_target_pairs={{71,0},{0,1},{1,2},{2,3},{3,4},{4,5},{5,6},{6,7},{79,8},{8,9},{9,1... | collective-permute-start | bytes 786440 | tf_op jit(solution)/shard_map/weight_z2/ppermute | solution.py:429
  66.9 15.0 %collective-permute-start.7 = (bf16[2,128,512]{2,1,0:T(8,128)(2,1)S(1)}, bf16[2,128,512]{2,1,0:T(8,128)(2,1)S(1)}, u32[]{:S(2)}, u32[]{:S(2)}) collective-permute-start(bf16[2,128,512]{2,1,0:T(8,128)(2,1)S(1)} %get-tuple-element.26.after_hbm), channel_id=1, source_target_pairs={{1,0},{2,1},{3,2},{4,3},{5,4},{6,5},{7,6},{64,7},{9,8},{10,9},{11,... | collective-permute-start | bytes 786440 | tf_op jit(solution)/shard_map/weight_z2/ppermute | solution.py:428
  73.5 23.1 %all-to-all-start.1 = ((bf16[16,16,256]{2,1,0:T(8,128)(2,1)}), bf16[16,16,256]{2,1,0:T(8,128)(2,1)S(1)}, u32[]{:S(2)}, u32[]{:S(2)}) async-start(bf16[16,16,256]{2,1,0:T(8,128)(2,1)} %split.1), calls=%async_computation.1 | async-start | bytes 262144 | tf_op jit(solution)/shard_map/ring_z/all_to_all | solution.py:72
  81.9 5.6 %copy-start.4 = (bf16[2,128,512]{2,1,0:T(8,128)(2,1)}, bf16[2,128,512]{2,1,0:T(8,128)(2,1)S(1)}, u32[]{:S(2)}) copy-start(bf16[2,128,512]{2,1,0:T(8,128)(2,1)S(1)} %collective-permute-done.8.refs_1_.weight_2b) | copy-start | bytes 786436
  81.9 5.6 %copy-start.3 = (bf16[2,128,512]{2,1,0:T(8,128)(2,1)}, bf16[2,128,512]{2,1,0:T(8,128)(2,1)S(1)}, u32[]{:S(2)}) copy-start(bf16[2,128,512]{2,1,0:T(8,128)(2,1)S(1)} %collective-permute-done.7.after_hbm.refs_0_.weight_2a) | copy-start | bytes 786436
  84.1 3.4 %collective-permute-start.10 = (bf16[2,256,256]{2,1,0:T(8,128)(2,1)S(1)}, bf16[2,256,256]{2,1,0:T(8,128)(2,1)S(1)}, u32[]{:S(2)}, u32[]{:S(2)}) collective-permute-start(bf16[2,256,256]{2,1,0:T(8,128)(2,1)S(1)} %back_late.1), channel_id=1, source_target_pairs={{0,32},{1,33},{2,34},{3,35},{4,36},{5,37},{6,38},{7,39},{8,40},{9,... | collective-permute-start | bytes 786440 | tf_op jit(solution)/shard_map/back_late/ppermute | solution.py:437
  87.5 0.7 copy-start.7
  88.2 8.3 %copy-start.5 = (s32[512]{0:T(512)S(1)}, s32[512]{0:T(512)}, u32[]{:S(2)}) copy-start(s32[512]{0:T(512)} %param.9) | copy-start | bytes 6148

commit v8 on v7

--- a/solution.py
+++ b/solution.py
@@ -34,6 +34,14 @@
     pairs = []
     for x, zh, c, y, zl in places():
         z = (zh * NZL + zl + distance) % (NZH * NZL)
+        pairs.append((device(x, z // NZL, c, y, z % NZL), device(x, zh, c, y, zl)))
+    return pairs
+
+
+def two_away():
+    pairs = []
+    for x, zh, c, y, zl in places():
+        z = (zh * NZL + zl + (2 if zl % 2 == 0 else -2)) % (NZH * NZL)
         pairs.append((device(x, z // NZL, c, y, z % NZL), device(x, zh, c, y, zl)))
     return pairs
 
@@ -157,8 +165,7 @@
         copy.wait()
 
 
-def partner_kernel(key_hbm, after_hbm, *refs):
-    del after_hbm
+def partner_kernel(key_hbm, *refs):
     *sources, out_hbm, key_ref, weight_ref, out_ref, in_sems, out_sems = refs
     key_copy = start(key_hbm.at[pl.ds(NX * NZH, 2)], key_ref, in_sems.at[0])
     copies, place = [], 0
@@ -183,14 +190,14 @@
         copy.wait()
 
 
-def partner(other, after, *sources):
+def partner(other, *sources):
     size = sum(source.shape[0] for source in sources)
     dma = pltpu.SemaphoreType.DMA
     return call(
         partner_kernel,
         shape((size // 2, SEQ, COLS)),
-        (other, after, *sources),
-        (pl.ANY,) * (2 + len(sources)),
+        (other, *sources),
+        (pl.ANY,) * (1 + len(sources)),
         pltpu.HBM,
         [
             pltpu.VMEM((2, SEQ, COLS), BF16),
@@ -242,15 +249,6 @@
         copy.wait()
 
 
-def halves_kernel(up_hbm, down_hbm, up_half, down_half, sems):
-    copies = [
-        start(up_hbm.at[pl.ds(0, 2)], up_half, sems.at[0]),
-        start(down_hbm.at[pl.ds(2, 2)], down_half, sems.at[1]),
-    ]
-    for copy in copies:
-        copy.wait()
-
-
 def split_kernel(in_ref, out_ref):
     for zh in range(NZH):
         rows = slice(zh * 128, (zh + 1) * 128)
@@ -276,35 +274,34 @@
 
 
 def input_kernel(
-    hidden_hbm, key_hbm, gain_hbm, inv_hbm, weight_0, weight_1, weight_3, weight_2a, weight_2b,
+    hidden_hbm, key_hbm, gain_hbm, inv_hbm, weight_0, weight_1, weight_3, weight_2,
     early_hbm, late_hbm, out_hbm,
     hidden_ref, key_ref, gain_ref, inv_ref, weight_ref, early_ref, late_ref, back_ref, out_ref,
     in_sems, out_sems,
 ):
     key_copy = start(key_hbm, key_ref, in_sems.at[0])
+    core = my_core()
+    z_here = lax.rem(lax.axis_index("fsdp"), NZL)
+    y_here = lax.div(lax.axis_index("fsdp"), NZL)
     groups = (
-        (weight_0, 0, 0),
-        (weight_1, 1, 0),
-        (weight_3, 7, 0),
-        (weight_2a, 2, 0),
-        (weight_2b, 6, 2),
+        (weight_0, 0),
+        (weight_1, 1),
+        (weight_3, 7),
+        (weight_2, jnp.where((z_here & 1) == 0, 2, 6)),
     )
     copies, blocks = [], []
-    for i, (source, away, row) in enumerate(groups):
+    for i, (source, away) in enumerate(groups):
         size = source.shape[0]
         target = weight_ref.at[pl.ds(2 * len(blocks), size)]
         copies.append(start(source, target, in_sems.at[1 + i]))
-        blocks += [(i, away, row + j) for j in range(0, size, 2)]
+        blocks += [(i, away, row) for row in range(0, size, 2)]
     second = [
-        start(early_hbm, early_ref, in_sems.at[6]),
-        start(late_hbm, late_ref, in_sems.at[7]),
-        start(gain_hbm, gain_ref, in_sems.at[8]),
-        start(inv_hbm, inv_ref, in_sems.at[9]),
-        start(hidden_hbm, hidden_ref, in_sems.at[10]),
+        start(early_hbm, early_ref, in_sems.at[5]),
+        start(late_hbm, late_ref, in_sems.at[6]),
+        start(gain_hbm, gain_ref, in_sems.at[7]),
+        start(inv_hbm, inv_ref, in_sems.at[8]),
+        start(hidden_hbm, hidden_ref, in_sems.at[9]),
     ]
-    core = my_core()
-    z_here = lax.rem(lax.axis_index("fsdp"), NZL)
-    y_here = lax.div(lax.axis_index("fsdp"), NZL)
 
     def put(back, origin, away, row):
         zl = (z_here + origin + away) & (NZL - 1)
@@ -420,28 +417,22 @@
     with jax.named_scope("weight_z1"):
         up = lax.ppermute(near, AXES, from_z(1))
         down = lax.ppermute(near, AXES, from_z(-1))
-    with jax.named_scope("weight_z2"):
-        half = shape((2, 128, K))
-        up_half, down_half = call(
-            halves_kernel, (half, half), (up, down), (any_, any_), (hbm, hbm), [dma((2,))], mib=52
-        )
-        far_up = lax.ppermute(up_half, AXES, from_z(1))
-        far_down = lax.ppermute(down_half, AXES, from_z(-1))
+        far = lax.ppermute(near, AXES, two_away())
     with jax.named_scope("back_early"):
-        early = lax.ppermute(partner(other, up_half, near, up, down), AXES, CORE_SWAP)
+        early = lax.ppermute(partner(other, near, up, down), AXES, CORE_SWAP)
     with jax.named_scope("split"):
         parts = call(split_kernel, shape((NZH * NZL, 16, COLS)), (chunks,), (vmem,), vmem)
     with jax.named_scope("ring_z"):
         parts = exchange(parts, Z_RINGS)
     with jax.named_scope("back_late"):
-        late = lax.ppermute(partner(other, far_up, far_up, far_down), AXES, CORE_SWAP)
+        late = lax.ppermute(partner(other, far), AXES, CORE_SWAP)
     with jax.named_scope("input_grad"):
-        weights = (near, up, down, far_up, far_down)
+        weights = (near, up, down, far)
         input_grad = call(
             input_kernel,
             shape((SEQ, D)),
             (hidden_in, key_grad, gain, inv, *weights, early, late),
-            (any_,) * 11,
+            (any_,) * 10,
             hbm,
             [
                 pltpu.VMEM((SEQ, D), BF16),
@@ -453,7 +444,7 @@
                 pltpu.VMEM((2, SEQ, COLS), BF16),
                 pltpu.VMEM((SEQ, D), F32),
                 pltpu.VMEM((SEQ, D), BF16),
-                dma((11,)),
+                dma((10,)),
                 dma((4,)),
             ],
             mib=60,

time: 98 us -> 95.7 us (0.977)
  the two profiles are of different devices: /device:TPU:2 before, /device:TPU:32 now
where the time goes in v8:
time: 95.7 us; the launch traced here: 95.1 us
  starting transfers between devices  55.7 us (58%)
  Pallas kernels  19.8 us (21%)
  waiting for transfers between devices  17 us (18%)
  local copies, waits for them, and re-layouts  1.79 us (2%)
    pallas_call x8, Pallas kernels, call(): pl.pallas_call(kernel, out_shape=outs, in_specs=[pl.BlockSpec(memory_spac...  19.8 us
    all_to_all x2, starting transfers between devices, exchange(): lax.all_to_all(value, AXES, split_axis=0, concat_axis=0, axis_index_group...  16.6 us
    ppermute x3, starting transfers between devices, body(): lax.ppermute(origin, AXES, from_y(ahead))  11.6 us
    ppermute x1, starting transfers between devices, body(): other = lax.ppermute(send, AXES, CORE_SWAP)  11.5 us
    all_to_all x2, waiting for transfers between devices, exchange(): lax.all_to_all(value, AXES, split_axis=0, concat_axis=0, axis_index_group...  6.21 us
    ppermute x1, starting transfers between devices, body(): far = lax.ppermute(near, AXES, two_away())  4.86 us
    ppermute x1, waiting for transfers between devices, body(): down = lax.ppermute(near, AXES, from_z(-1))  4.85 us
    ppermute x1, waiting for transfers between devices, body(): up = lax.ppermute(near, AXES, from_z(1))  4.42 us
  transfers between devices with their start and end apart: 12, of which 5 were waited for; matrix products, arithmetic and copies ran while one was open for 0% of the time, Pallas kernels for 20%

profile of v8, /device:TPU:32, one launch (start us, length us, event | category | flops | bytes accessed | tf_op | source)
XLA Modules:
  0.0 95.1 jit_solution(3948054817750184334)
XLA Ops:
  0.6 1.6 %collective-permute-start = (bf16[128,512]{1,0:T(8,128)(2,1)}, bf16[128,512]{1,0:T(8,128)(2,1)S(1)}, u32[]{:S(2)}, u32[]{:S(2)}) collective-permute-start(bf16[128,512]{1,0:T(8,128)(2,1)} %param.7), channel_id=1, source_target_pairs={{0,0},{1,1},{2,2},{3,3},{4,4},{5,5},{6,6},{7,7},{8,8},{9,9},{10,10... | collective-permute-start | bytes 393224 | tf_op jit(solution)/shard_map/weight_z4/ppermute | solution.py:369
  2.2 2.9 %norm.1 = (bf16[8,256,256]{2,1,0:T(8,128)(2,1)}, bf16[10,256,256]{2,1,0:T(8,128)(2,1)}, f32[256,128]{1,0:T(8,128)}) custom-call(bf16[256,4096]{1,0:T(8,128)(2,1)} %hidden_hbm.3, bf16[256,512]{1,0:T(8,128)(2,1)} %key_hbm.5, f32[1,4096]{1,0:T(1,128)} %bitcast.3), custom_call_target="tpu_custom_call" | custom-call | bytes 150000 | tf_op jit(solution)/shard_map/norm/pallas_call | solution.py:86
  5.1 0.0 collective-permute-done.refs_0_
  5.1 11.5 %collective-permute-start.1 = (bf16[10,256,256]{2,1,0:T(8,128)(2,1)}, bf16[10,256,256]{2,1,0:T(8,128)(2,1)S(1)}, u32[]{:S(2)}, u32[]{:S(2)}) collective-permute-start(bf16[10,256,256]{2,1,0:T(8,128)(2,1)} %get-tuple-element.16), channel_id=1, source_target_pairs={{0,32},{1,33},{2,34},{3,35},{4,36},{5,37},{6,38},{7,39},{8,40},{9,... | collective-permute-start | bytes 3932168 | tf_op jit(solution)/shard_map/norm/ppermute | solution.py:390
  16.6 3.5 %collective-permute-start.4 = (bf16[128,512]{1,0:T(8,128)(2,1)S(1)}, bf16[128,512]{1,0:T(8,128)(2,1)S(1)}, u32[]{:S(2)}, u32[]{:S(2)}) collective-permute-start(bf16[128,512]{1,0:T(8,128)(2,1)S(1)} %collective-permute-done.refs_0_), channel_id=1, source_target_pairs={{24,0},{25,1},{26,2},{27,3},{28,4},{29,5},{30,6},{31,7},{0,8},{1,9... | collective-permute-start | bytes 393224 | tf_op jit(solution)/shard_map/weight_y/ppermute | solution.py:409
  20.1 4.8 %collective-permute-start.3 = (bf16[128,512]{1,0:T(8,128)(2,1)S(1)}, bf16[128,512]{1,0:T(8,128)(2,1)S(1)}, u32[]{:S(2)}, u32[]{:S(2)}) collective-permute-start(bf16[128,512]{1,0:T(8,128)(2,1)S(1)} %collective-permute-done.refs_0_), channel_id=1, source_target_pairs={{16,0},{17,1},{18,2},{19,3},{20,4},{21,5},{22,6},{23,7},{24,8},{25... | collective-permute-start | bytes 393224 | tf_op jit(solution)/shard_map/weight_y/ppermute | solution.py:409
  24.9 3.3 %collective-permute-start.2 = (bf16[128,512]{1,0:T(8,128)(2,1)S(1)}, bf16[128,512]{1,0:T(8,128)(2,1)S(1)}, u32[]{:S(2)}, u32[]{:S(2)}) collective-permute-start(bf16[128,512]{1,0:T(8,128)(2,1)S(1)} %collective-permute-done.refs_0_), channel_id=1, source_target_pairs={{8,0},{9,1},{10,2},{11,3},{12,4},{13,5},{14,6},{15,7},{16,8},{17,9... | collective-permute-start | bytes 393224 | tf_op jit(solution)/shard_map/weight_y/ppermute | solution.py:409
  28.2 0.0 collective-permute-done.1.other_hbm.key_hbm
  28.2 1.1 %copy-done.4 = bf16[10,256,256]{2,1,0:T(8,128)(2,1)} copy-done((bf16[10,256,256]{2,1,0:T(8,128)(2,1)}, bf16[10,256,256]{2,1,0:T(8,128)(2,1)S(1)}, u32[]{:S(2)}) %copy-start.4) | copy-done | bytes 1310744
  29.3 4.1 %squares.1 = bf16[16,256,256]{2,1,0:T(8,128)(2,1)} custom-call(bf16[8,256,256]{2,1,0:T(8,128)(2,1)} %get-tuple-element.14.own_hbm, bf16[10,256,256]{2,1,0:T(8,128)(2,1)} %copy-done.4, bf16[256,512]{1,0:T(8,128)(2,1)} %key_hbm.5), custom_call_target="tpu_custom_call" | custom-call | bytes 150000 | tf_op jit(solution)/shard_map/squares/pallas_call | solution.py:86
  33.4 0.0 collective-permute-done.3.refs_2_
  33.4 0.0 collective-permute-done.2.refs_1_
  33.4 4.7 %all-to-all-start = ((bf16[16,256,256]{2,1,0:T(8,128)(2,1)}), bf16[16,256,256]{2,1,0:T(8,128)(2,1)S(1)}, u32[]{:S(2)}, u32[]{:S(2)}) async-start(bf16[16,256,256]{2,1,0:T(8,128)(2,1)} %squares.1), calls=%async_computation | async-start | bytes 4194304 | tf_op jit(solution)/shard_map/plane/all_to_all | solution.py:80
  38.2 0.7 weight_y.1.refs_0_.weight_0
  38.9 3.2 %collective-permute-start.6 = (bf16[4,128,512]{2,1,0:T(8,128)(2,1)S(1)}, bf16[4,128,512]{2,1,0:T(8,128)(2,1)S(1)}, u32[]{:S(2)}, u32[]{:S(2)}) collective-permute-start(bf16[4,128,512]{2,1,0:T(8,128)(2,1)S(1)} %weight_y.1.refs_0_.weight_0), channel_id=1, source_target_pairs={{71,0},{0,1},{1,2},{2,3},{3,4},{4,5},{5,6},{6,7},{79,8},{8,9},{9,1... | collective-permute-start | bytes 1572872 | tf_op jit(solution)/shard_map/weight_z1/ppermute | solution.py:419
  42.1 2.6 %collective-permute-start.5 = (bf16[4,128,512]{2,1,0:T(8,128)(2,1)S(1)}, bf16[4,128,512]{2,1,0:T(8,128)(2,1)S(1)}, u32[]{:S(2)}, u32[]{:S(2)}) collective-permute-start(bf16[4,128,512]{2,1,0:T(8,128)(2,1)S(1)} %weight_y.1.refs_0_.weight_0), channel_id=1, source_target_pairs={{1,0},{2,1},{3,2},{4,3},{5,4},{6,5},{7,6},{64,7},{9,8},{10,9},{11,... | collective-permute-start | bytes 1572872 | tf_op jit(solution)/shard_map/weight_z1/ppermute | solution.py:418
  44.8 4.9 %collective-permute-start.7 = (bf16[4,128,512]{2,1,0:T(8,128)(2,1)S(1)}, bf16[4,128,512]{2,1,0:T(8,128)(2,1)}, u32[]{:S(2)}, u32[]{:S(2)}) collective-permute-start(bf16[4,128,512]{2,1,0:T(8,128)(2,1)S(1)} %weight_y.1.refs_0_.weight_0), channel_id=1, source_target_pairs={{2,0},{71,1},{4,2},{1,3},{6,4},{3,5},{64,6},{5,7},{10,8},{79,9},{1... | collective-permute-start | bytes 1572872 | tf_op jit(solution)/shard_map/weight_z1/ppermute | solution.py:420
  49.6 4.9 %collective-permute-done.6.refs_2_.weight_3 = bf16[4,128,512]{2,1,0:T(8,128)(2,1)S(1)} collective-permute-done((bf16[4,128,512]{2,1,0:T(8,128)(2,1)S(1)}, bf16[4,128,512]{2,1,0:T(8,128)(2,1)S(1)}, u32[]{:S(2)}, u32[]{:S(2)}) %collective-permute-start.6) | collective-permute-done | bytes 524320 | tf_op jit(solution)/shard_map/weight_z1/ppermute | solution.py:419
  54.5 4.4 %collective-permute-done.5.refs_1_.weight_1 = bf16[4,128,512]{2,1,0:T(8,128)(2,1)S(1)} collective-permute-done((bf16[4,128,512]{2,1,0:T(8,128)(2,1)S(1)}, bf16[4,128,512]{2,1,0:T(8,128)(2,1)S(1)}, u32[]{:S(2)}, u32[]{:S(2)}) %collective-permute-start.5) | collective-permute-done | bytes 524320 | tf_op jit(solution)/shard_map/weight_z1/ppermute | solution.py:418
  58.9 3.0 %back_early.1 = bf16[6,256,256]{2,1,0:T(8,128)(2,1)} custom-call(bf16[10,256,256]{2,1,0:T(8,128)(2,1)} %copy-done.4, bf16[4,128,512]{2,1,0:T(8,128)(2,1)S(1)} %weight_y.1.refs_0_.weight_0, bf16[4,128,512]{2,1,0:T(8,128)(2,1)S(1)} %collective-permute-done.5.refs_1_.weight_1, bf16[4,128,512]{2,1,0:T(8,128)(2,1)S(1)} %collective-permute-done.6.refs_2_.weight_3), custom_call_target="tpu_custom_call" | custom-call | bytes 150000 | tf_op jit(solution)/shard_map/back_early/pallas_call | solution.py:86
  61.9 1.9 %collective-permute-start.8 = (bf16[6,256,256]{2,1,0:T(8,128)(2,1)}, bf16[6,256,256]{2,1,0:T(8,128)(2,1)}, u32[]{:S(2)}, u32[]{:S(2)}) collective-permute-start(bf16[6,256,256]{2,1,0:T(8,128)(2,1)} %back_early.1), channel_id=1, source_target_pairs={{0,32},{1,33},{2,34},{3,35},{4,36},{5,37},{6,38},{7,39},{8,40},{9,... | collective-permute-start | bytes 2359304 | tf_op jit(solution)/shard_map/back_early/ppermute | solution.py:422
  63.8 3.2 %all-to-all-done.in_ref = bf16[16,256,256]{2,1,0:T(8,128)(2,1)S(1)} async-done(((bf16[16,256,256]{2,1,0:T(8,128)(2,1)}), bf16[16,256,256]{2,1,0:T(8,128)(2,1)S(1)}, u32[]{:S(2)}, u32[]{:S(2)}) %all-to-all-start) | async-done | bytes 2097184 | tf_op jit(solution)/shard_map/plane/all_to_all | solution.py:80
  67.0 0.9 split.1
  68.0 11.8 %all-to-all-start.1 = ((bf16[16,16,256]{2,1,0:T(8,128)(2,1)}), bf16[16,16,256]{2,1,0:T(8,128)(2,1)S(1)}, u32[]{:S(2)}, u32[]{:S(2)}) async-start(bf16[16,16,256]{2,1,0:T(8,128)(2,1)} %split.1), calls=%async_computation.1 | async-start | bytes 262144 | tf_op jit(solution)/shard_map/ring_z/all_to_all | solution.py:80
  79.8 0.0 collective-permute-done.7.refs_0_.weight_2
  79.8 2.1 %back_late.1 = bf16[2,256,256]{2,1,0:T(8,128)(2,1)S(1)} custom-call(bf16[10,256,256]{2,1,0:T(8,128)(2,1)} %copy-done.4, bf16[4,128,512]{2,1,0:T(8,128)(2,1)} %collective-permute-done.7.refs_0_.weight_2), custom_call_target="tpu_custom_call" | custom-call | bytes 150000 | tf_op jit(solution)/shard_map/back_late/pallas_call | solution.py:86
  81.9 1.9 %collective-permute-start.9 = (bf16[2,256,256]{2,1,0:T(8,128)(2,1)S(1)}, bf16[2,256,256]{2,1,0:T(8,128)(2,1)S(1)}, u32[]{:S(2)}, u32[]{:S(2)}) collective-permute-start(bf16[2,256,256]{2,1,0:T(8,128)(2,1)S(1)} %back_late.1), channel_id=1, source_target_pairs={{0,32},{1,33},{2,34},{3,35},{4,36},{5,37},{6,38},{7,39},{8,40},{9,... | collective-permute-start | bytes 786440 | tf_op jit(solution)/shard_map/back_late/ppermute | solution.py:428
  83.9 1.5 %collective-permute-done.9.late_hbm = bf16[2,256,256]{2,1,0:T(8,128)(2,1)S(1)} collective-permute-done((bf16[2,256,256]{2,1,0:T(8,128)(2,1)S(1)}, bf16[2,256,256]{2,1,0:T(8,128)(2,1)S(1)}, u32[]{:S(2)}, u32[]{:S(2)}) %collective-permute-start.9) | collective-permute-done | bytes 262176 | tf_op jit(solution)/shard_map/back_late/ppermute | solution.py:428
  85.4 0.7 copy-done.5
  86.1 5.2 %input_grad.1 = bf16[256,4096]{1,0:T(8,128)(2,1)} custom-call(bf16[256,4096]{1,0:T(8,128)(2,1)} %hidden_hbm.3, bf16[256,512]{1,0:T(8,128)(2,1)} %key_hbm.5, f32[1,4096]{1,0:T(1,128)} %bitcast.4, f32[256,128]{1,0:T(8,128)} %get-tuple-element.19.inv_hbm, bf16[4,128,512]{2,1,0:T(8,128)(2,1)} %copy-done, bf16[4,128,512]{2,1,0:T(8,128)(2,1)} %copy-done.2, ...), custom_call_target="tpu_custom_call" | custom-call | bytes 150000 | tf_op jit(solution)/shard_map/input_grad/pallas_call | solution.py:86
  91.3 3.0 %all-to-all-done.1.in_ref = bf16[16,16,256]{2,1,0:T(8,128)(2,1)S(1)} async-done(((bf16[16,16,256]{2,1,0:T(8,128)(2,1)}), bf16[16,16,256]{2,1,0:T(8,128)(2,1)S(1)}, u32[]{:S(2)}, u32[]{:S(2)}) %all-to-all-start.1) | async-done | bytes 131104 | tf_op jit(solution)/shard_map/ring_z/all_to_all | solution.py:80
  94.3 0.8 serve.1
  (12 shorter events, 0.0 us)
Async XLA Ops:
  0.6 4.5 %collective-permute-start = (bf16[128,512]{1,0:T(8,128)(2,1)}, bf16[128,512]{1,0:T(8,128)(2,1)S(1)}, u32[]{:S(2)}, u32[]{:S(2)}) collective-permute-start(bf16[128,512]{1,0:T(8,128)(2,1)} %param.7), channel_id=1, source_target_pairs={{0,0},{1,1},{2,2},{3,3},{4,4},{5,5},{6,6},{7,7},{8,8},{9,9},{10,10... | collective-permute-start | bytes 393224 | tf_op jit(solution)/shard_map/weight_z4/ppermute | solution.py:369
  5.1 23.0 %collective-permute-start.1 = (bf16[10,256,256]{2,1,0:T(8,128)(2,1)}, bf16[10,256,256]{2,1,0:T(8,128)(2,1)S(1)}, u32[]{:S(2)}, u32[]{:S(2)}) collective-permute-start(bf16[10,256,256]{2,1,0:T(8,128)(2,1)} %get-tuple-element.16), channel_id=1, source_target_pairs={{0,32},{1,33},{2,34},{3,35},{4,36},{5,37},{6,38},{7,39},{8,40},{9,... | collective-permute-start | bytes 3932168 | tf_op jit(solution)/shard_map/norm/ppermute | solution.py:390
  16.6 16.8 %collective-permute-start.4 = (bf16[128,512]{1,0:T(8,128)(2,1)S(1)}, bf16[128,512]{1,0:T(8,128)(2,1)S(1)}, u32[]{:S(2)}, u32[]{:S(2)}) collective-permute-start(bf16[128,512]{1,0:T(8,128)(2,1)S(1)} %collective-permute-done.refs_0_), channel_id=1, source_target_pairs={{24,0},{25,1},{26,2},{27,3},{28,4},{29,5},{30,6},{31,7},{0,8},{1,9... | collective-permute-start | bytes 393224 | tf_op jit(solution)/shard_map/weight_y/ppermute | solution.py:409
  20.1 13.3 %collective-permute-start.3 = (bf16[128,512]{1,0:T(8,128)(2,1)S(1)}, bf16[128,512]{1,0:T(8,128)(2,1)S(1)}, u32[]{:S(2)}, u32[]{:S(2)}) collective-permute-start(bf16[128,512]{1,0:T(8,128)(2,1)S(1)} %collective-permute-done.refs_0_), channel_id=1, source_target_pairs={{16,0},{17,1},{18,2},{19,3},{20,4},{21,5},{22,6},{23,7},{24,8},{25... | collective-permute-start | bytes 393224 | tf_op jit(solution)/shard_map/weight_y/ppermute | solution.py:409
  24.9 8.5 %collective-permute-start.2 = (bf16[128,512]{1,0:T(8,128)(2,1)S(1)}, bf16[128,512]{1,0:T(8,128)(2,1)S(1)}, u32[]{:S(2)}, u32[]{:S(2)}) collective-permute-start(bf16[128,512]{1,0:T(8,128)(2,1)S(1)} %collective-permute-done.refs_0_), channel_id=1, source_target_pairs={{8,0},{9,1},{10,2},{11,3},{12,4},{13,5},{14,6},{15,7},{16,8},{17,9... | collective-permute-start | bytes 393224 | tf_op jit(solution)/shard_map/weight_y/ppermute | solution.py:409
  28.2 1.1 %copy-start.4 = (bf16[10,256,256]{2,1,0:T(8,128)(2,1)}, bf16[10,256,256]{2,1,0:T(8,128)(2,1)S(1)}, u32[]{:S(2)}) copy-start(bf16[10,256,256]{2,1,0:T(8,128)(2,1)S(1)} %collective-permute-done.1.other_hbm.key_hbm) | copy-start | bytes 3932164
  33.4 33.6 %all-to-all-start = ((bf16[16,256,256]{2,1,0:T(8,128)(2,1)}), bf16[16,256,256]{2,1,0:T(8,128)(2,1)S(1)}, u32[]{:S(2)}, u32[]{:S(2)}) async-start(bf16[16,256,256]{2,1,0:T(8,128)(2,1)} %squares.1), calls=%async_computation | async-start | bytes 4194304 | tf_op jit(solution)/shard_map/plane/all_to_all | solution.py:80
  38.9 29.1 %copy-start = (bf16[4,128,512]{2,1,0:T(8,128)(2,1)}, bf16[4,128,512]{2,1,0:T(8,128)(2,1)S(1)}, u32[]{:S(2)}) copy-start(bf16[4,128,512]{2,1,0:T(8,128)(2,1)S(1)} %weight_y.1.refs_0_.weight_0) | copy-start | bytes 1572868
  38.9 15.6 %collective-permute-start.6 = (bf16[4,128,512]{2,1,0:T(8,128)(2,1)S(1)}, bf16[4,128,512]{2,1,0:T(8,128)(2,1)S(1)}, u32[]{:S(2)}, u32[]{:S(2)}) collective-permute-start(bf16[4,128,512]{2,1,0:T(8,128)(2,1)S(1)} %weight_y.1.refs_0_.weight_0), channel_id=1, source_target_pairs={{71,0},{0,1},{1,2},{2,3},{3,4},{4,5},{5,6},{6,7},{79,8},{8,9},{9,1... | collective-permute-start | bytes 1572872 | tf_op jit(solution)/shard_map/weight_z1/ppermute | solution.py:419
  42.1 16.8 %collective-permute-start.5 = (bf16[4,128,512]{2,1,0:T(8,128)(2,1)S(1)}, bf16[4,128,512]{2,1,0:T(8,128)(2,1)S(1)}, u32[]{:S(2)}, u32[]{:S(2)}) collective-permute-start(bf16[4,128,512]{2,1,0:T(8,128)(2,1)S(1)} %weight_y.1.refs_0_.weight_0), channel_id=1, source_target_pairs={{1,0},{2,1},{3,2},{4,3},{5,4},{6,5},{7,6},{64,7},{9,8},{10,9},{11,... | collective-permute-start | bytes 1572872 | tf_op jit(solution)/shard_map/weight_z1/ppermute | solution.py:418
  44.8 35.0 %collective-permute-start.7 = (bf16[4,128,512]{2,1,0:T(8,128)(2,1)S(1)}, bf16[4,128,512]{2,1,0:T(8,128)(2,1)}, u32[]{:S(2)}, u32[]{:S(2)}) collective-permute-start(bf16[4,128,512]{2,1,0:T(8,128)(2,1)S(1)} %weight_y.1.refs_0_.weight_0), channel_id=1, source_target_pairs={{2,0},{71,1},{4,2},{1,3},{6,4},{3,5},{64,6},{5,7},{10,8},{79,9},{1... | collective-permute-start | bytes 1572872 | tf_op jit(solution)/shard_map/weight_z1/ppermute | solution.py:420
  54.5 13.5 %copy-start.1 = (bf16[4,128,512]{2,1,0:T(8,128)(2,1)}, bf16[4,128,512]{2,1,0:T(8,128)(2,1)S(1)}, u32[]{:S(2)}) copy-start(bf16[4,128,512]{2,1,0:T(8,128)(2,1)S(1)} %collective-permute-done.6.refs_2_.weight_3) | copy-start | bytes 1572868
  58.9 3.0 %copy-start.2 = (bf16[4,128,512]{2,1,0:T(8,128)(2,1)}, bf16[4,128,512]{2,1,0:T(8,128)(2,1)S(1)}, u32[]{:S(2)}) copy-start(bf16[4,128,512]{2,1,0:T(8,128)(2,1)S(1)} %collective-permute-done.5.refs_1_.weight_1) | copy-start | bytes 1572868
  61.9 23.5 %collective-permute-start.8 = (bf16[6,256,256]{2,1,0:T(8,128)(2,1)}, bf16[6,256,256]{2,1,0:T(8,128)(2,1)}, u32[]{:S(2)}, u32[]{:S(2)}) collective-permute-start(bf16[6,256,256]{2,1,0:T(8,128)(2,1)} %back_early.1), channel_id=1, source_target_pairs={{0,32},{1,33},{2,34},{3,35},{4,36},{5,37},{6,38},{7,39},{8,40},{9,... | collective-permute-start | bytes 2359304 | tf_op jit(solution)/shard_map/back_early/ppermute | solution.py:422
  68.0 26.3 %all-to-all-start.1 = ((bf16[16,16,256]{2,1,0:T(8,128)(2,1)}), bf16[16,16,256]{2,1,0:T(8,128)(2,1)S(1)}, u32[]{:S(2)}, u32[]{:S(2)}) async-start(bf16[16,16,256]{2,1,0:T(8,128)(2,1)} %split.1), calls=%async_computation.1 | async-start | bytes 262144 | tf_op jit(solution)/shard_map/ring_z/all_to_all | solution.py:80
  81.9 3.4 %collective-permute-start.9 = (bf16[2,256,256]{2,1,0:T(8,128)(2,1)S(1)}, bf16[2,256,256]{2,1,0:T(8,128)(2,1)S(1)}, u32[]{:S(2)}, u32[]{:S(2)}) collective-permute-start(bf16[2,256,256]{2,1,0:T(8,128)(2,1)S(1)} %back_late.1), channel_id=1, source_target_pairs={{0,32},{1,33},{2,34},{3,35},{4,36},{5,37},{6,38},{7,39},{8,40},{9,... | collective-permute-start | bytes 786440 | tf_op jit(solution)/shard_map/back_late/ppermute | solution.py:428
  85.4 0.7 copy-start.5
  86.1 8.2 %copy-start.3 = (s32[512]{0:T(512)S(1)}, s32[512]{0:T(512)}, u32[]{:S(2)}) copy-start(s32[512]{0:T(512)} %param.9) | copy-start | bytes 6148

commit v9 on v8

--- a/solution.py
+++ b/solution.py
@@ -46,13 +46,6 @@
     return pairs
 
 
-def from_y(ahead):
-    return [
-        (device(x, zh, c, (y + ahead) % NY, zl), device(x, zh, c, y, zl))
-        for x, zh, c, y, zl in places()
-    ]
-
-
 def origins():
     pairs = []
     for x, zh, c, y, zl in places():
@@ -61,6 +54,13 @@
     return pairs
 
 
+Y_RINGS = [
+    [device(x, zh, c, y, zl) for y in range(NY)]
+    for x in range(NX)
+    for zh in range(NZH)
+    for c in range(NC)
+    for zl in range(NZL)
+]
 PLANES = [
     [device(x, zh, c, y, zl) for x in range(NX) for y in range(NY)]
     for zh in range(NZH)
@@ -155,13 +155,6 @@
         out_copies.append(start(source, send_hbm.at[blocks + half], out_sems.at[2 * parts + half]))
     out_copies.append(start(inv_ref, inv_hbm, out_sems.at[2 * parts + 2]))
     for copy in out_copies:
-        copy.wait()
-
-
-def column_kernel(*refs):
-    *blocks, out_hbm, sems = refs
-    copies = [start(block, out_hbm.at[j], sems.at[j]) for j, block in enumerate(blocks)]
-    for copy in copies:
         copy.wait()
 
 
@@ -282,7 +275,6 @@
     key_copy = start(key_hbm, key_ref, in_sems.at[0])
     core = my_core()
     z_here = lax.rem(lax.axis_index("fsdp"), NZL)
-    y_here = lax.div(lax.axis_index("fsdp"), NZL)
     groups = (
         (weight_0, 0),
         (weight_1, 1),
@@ -306,8 +298,7 @@
     def put(back, origin, away, row):
         zl = (z_here + origin + away) & (NZL - 1)
         for half in range(2):
-            y = (y_here + row + half) & (NY - 1)
-            cols = pl.ds(pl.multiple_of((y * NZL + zl) * 128, 128), 128)
+            cols = pl.ds(pl.multiple_of(((row + half) * NZL + zl) * 128, 128), 128)
             back_ref[:, cols] = back[:, half * 128 : (half + 1) * 128]
 
     key_copy.wait()
@@ -388,6 +379,9 @@
         )
         origin, send = barrier((origin, send))
         other = lax.ppermute(send, AXES, CORE_SWAP)
+    with jax.named_scope("weight_y"):
+        near = lax.all_gather(origin, AXES, axis=0, tiled=True, axis_index_groups=Y_RINGS)
+        near, other = barrier((near.reshape(NY, 128, K), other))
     with jax.named_scope("squares"):
         chunks = call(
             square_kernel,
@@ -405,19 +399,13 @@
             ],
             mib=60,
         )
-    with jax.named_scope("weight_y"):
-        column = [origin] + [lax.ppermute(origin, AXES, from_y(ahead)) for ahead in (1, 2, 3)]
-        chunks, *column = barrier((chunks, *column))
     with jax.named_scope("plane"):
         chunks = exchange(chunks, PLANES)
-    with jax.named_scope("weight_y"):
-        near = call(
-            column_kernel, shape((NY, 128, K)), column, (any_,) * NY, hbm, [dma((NY,))], mib=52
-        )
     with jax.named_scope("weight_z1"):
         up = lax.ppermute(near, AXES, from_z(1))
         down = lax.ppermute(near, AXES, from_z(-1))
-        far = lax.ppermute(near, AXES, two_away())
+        *now, up, down = barrier((near, up, down))
+        far = lax.ppermute(now[0], AXES, two_away())
     with jax.named_scope("back_early"):
         early = lax.ppermute(partner(other, near, up, down), AXES, CORE_SWAP)
     with jax.named_scope("split"):

time: 95.7 us -> 95.8 us (level)
  the two profiles are of different devices: /device:TPU:32 before, /device:TPU:1 now
where the time goes in v9:
time: 95.8 us; the launch traced here: 95.1 us
  starting transfers between devices  50.2 us (52%)
  Pallas kernels  18.7 us (20%)
  waiting for transfers between devices  12 us (13%)
  blocking collectives  11.6 us (12%)
  local copies, waits for them, and re-layouts  1.83 us (2%)
    pallas_call x7, Pallas kernels, call(): pl.pallas_call(kernel, out_shape=outs, in_specs=[pl.BlockSpec(memory_spac...  18.7 us
    ppermute x1, starting transfers between devices, body(): origin = lax.ppermute(key_weight, AXES, origins())  13.3 us
    all_gather x1, blocking collectives, body(): lax.all_gather(origin, AXES, axis=0, tiled=True, axis_index_groups=Y_RINGS)  11.6 us
    all_to_all x2, starting transfers between devices, exchange(): lax.all_to_all(value, AXES, split_axis=0, concat_axis=0, axis_index_group...  10.6 us
    ppermute x1, starting transfers between devices, body(): early = lax.ppermute(partner(other, near, up, down), AXES, CORE_SWAP)  7.59 us
    ppermute x1, starting transfers between devices, body(): late = lax.ppermute(partner(other, far), AXES, CORE_SWAP)  6.74 us
    ppermute x1, starting transfers between devices, body(): up = lax.ppermute(near, AXES, from_z(1))  6.25 us
    ppermute x1, waiting for transfers between devices, body(): up = lax.ppermute(near, AXES, from_z(1))  5.1 us
  transfers between devices with their start and end apart: 9, of which 4 were waited for; matrix products, arithmetic and copies ran while one was open for 0% of the time, Pallas kernels for 14%

profile of v9, /device:TPU:1, one launch (start us, length us, event | category | flops | bytes accessed | tf_op | source)
XLA Modules:
  0.0 95.1 jit_solution(2460288546726731191)
XLA Ops:
  0.6 13.3 %collective-permute-start = (bf16[128,512]{1,0:T(8,128)(2,1)}, bf16[128,512]{1,0:T(8,128)(2,1)S(1)}, u32[]{:S(2)}, u32[]{:S(2)}) collective-permute-start(bf16[128,512]{1,0:T(8,128)(2,1)} %param.7), channel_id=1, source_target_pairs={{0,0},{1,1},{2,2},{3,3},{4,4},{5,5},{6,6},{7,7},{8,8},{9,9},{10,10... | collective-permute-start | bytes 393224 | tf_op jit(solution)/shard_map/weight_z4/ppermute | solution.py:360
  13.9 2.9 %norm.1 = (bf16[8,256,256]{2,1,0:T(8,128)(2,1)}, bf16[10,256,256]{2,1,0:T(8,128)(2,1)}, f32[256,128]{1,0:T(8,128)}) custom-call(bf16[256,4096]{1,0:T(8,128)(2,1)} %hidden_hbm.3, bf16[256,512]{1,0:T(8,128)(2,1)} %key_hbm.5, f32[1,4096]{1,0:T(1,128)} %bitcast.9), custom_call_target="tpu_custom_call" | custom-call | bytes 150000 | tf_op jit(solution)/shard_map/norm/pallas_call | solution.py:86
  16.8 0.7 collective-permute-done
  17.6 1.9 %collective-permute-start.1 = (bf16[10,256,256]{2,1,0:T(8,128)(2,1)}, bf16[10,256,256]{2,1,0:T(8,128)(2,1)S(1)}, u32[]{:S(2)}, u32[]{:S(2)}) collective-permute-start(bf16[10,256,256]{2,1,0:T(8,128)(2,1)} %get-tuple-element.17), channel_id=1, source_target_pairs={{0,32},{1,33},{2,34},{3,35},{4,36},{5,37},{6,38},{7,39},{8,40},{9,... | collective-permute-start | bytes 3932168 | tf_op jit(solution)/shard_map/norm/ppermute | solution.py:381
  19.5 11.6 %all_gather.3 = bf16[512,512]{1,0:T(8,128)(2,1)S(1)} all-gather(bf16[128,512]{1,0:T(8,128)(2,1)S(1)} %collective-permute-done), channel_id=1, replica_groups={{0,8,16,24},{1,9,17,25},{2,10,18,26},{3,11,19,27},{4,12,20,28},{5,13,21..., dimensions={0}, use_global_device_ids=true | all-gather | bytes 655360 | tf_op jit(solution)/shard_map/weight_y/all_gather | solution.py:383
  31.1 0.0 collective-permute-done.1.other_hbm.key_hbm
  31.1 1.1 %copy-done.4 = bf16[10,256,256]{2,1,0:T(8,128)(2,1)} copy-done((bf16[10,256,256]{2,1,0:T(8,128)(2,1)}, bf16[10,256,256]{2,1,0:T(8,128)(2,1)S(1)}, u32[]{:S(2)}) %copy-start.4) | copy-done | bytes 1310744
  32.2 4.1 %squares.1 = bf16[16,256,256]{2,1,0:T(8,128)(2,1)} custom-call(bf16[8,256,256]{2,1,0:T(8,128)(2,1)} %get-tuple-element.14.own_hbm, bf16[10,256,256]{2,1,0:T(8,128)(2,1)} %copy-done.4, bf16[256,512]{1,0:T(8,128)(2,1)} %key_hbm.5), custom_call_target="tpu_custom_call" | custom-call | bytes 150000 | tf_op jit(solution)/shard_map/squares/pallas_call | solution.py:86
  36.3 5.0 %all-to-all-start = ((bf16[16,256,256]{2,1,0:T(8,128)(2,1)}), bf16[16,256,256]{2,1,0:T(8,128)(2,1)S(1)}, u32[]{:S(2)}, u32[]{:S(2)}) async-start(bf16[16,256,256]{2,1,0:T(8,128)(2,1)} %squares.1), calls=%async_computation | async-start | bytes 4194304 | tf_op jit(solution)/shard_map/plane/all_to_all | solution.py:80
  41.3 6.3 %collective-permute-start.2 = (bf16[4,128,512]{2,1,0:T(8,128)(2,1)S(1)}, bf16[4,128,512]{2,1,0:T(8,128)(2,1)S(1)}, u32[]{:S(2)}, u32[]{:S(2)}) collective-permute-start(bf16[4,128,512]{2,1,0:T(8,128)(2,1)S(1)} %bitcast.3), channel_id=1, source_target_pairs={{1,0},{2,1},{3,2},{4,3},{5,4},{6,5},{7,6},{64,7},{9,8},{10,9},{11,... | collective-permute-start | bytes 1572872 | tf_op jit(solution)/shard_map/weight_z1/ppermute | solution.py:405
  47.6 1.9 %collective-permute-start.3 = (bf16[4,128,512]{2,1,0:T(8,128)(2,1)S(1)}, bf16[4,128,512]{2,1,0:T(8,128)(2,1)S(1)}, u32[]{:S(2)}, u32[]{:S(2)}) collective-permute-start(bf16[4,128,512]{2,1,0:T(8,128)(2,1)S(1)} %bitcast.4), channel_id=1, source_target_pairs={{71,0},{0,1},{1,2},{2,3},{3,4},{4,5},{5,6},{6,7},{79,8},{8,9},{9,1... | collective-permute-start | bytes 1572872 | tf_op jit(solution)/shard_map/weight_z1/ppermute | solution.py:406
  49.5 5.1 %collective-permute-done.2.refs_1_.weight_1 = bf16[4,128,512]{2,1,0:T(8,128)(2,1)S(1)} collective-permute-done((bf16[4,128,512]{2,1,0:T(8,128)(2,1)S(1)}, bf16[4,128,512]{2,1,0:T(8,128)(2,1)S(1)}, u32[]{:S(2)}, u32[]{:S(2)}) %collective-permute-start.2) | collective-permute-done | bytes 524320 | tf_op jit(solution)/shard_map/weight_z1/ppermute | solution.py:405
  54.6 5.0 %collective-permute-done.3.refs_2_.weight_3 = bf16[4,128,512]{2,1,0:T(8,128)(2,1)S(1)} collective-permute-done((bf16[4,128,512]{2,1,0:T(8,128)(2,1)S(1)}, bf16[4,128,512]{2,1,0:T(8,128)(2,1)S(1)}, u32[]{:S(2)}, u32[]{:S(2)}) %collective-permute-start.3) | collective-permute-done | bytes 524320 | tf_op jit(solution)/shard_map/weight_z1/ppermute | solution.py:406
  59.7 1.9 %collective-permute-start.4 = (bf16[4,128,512]{2,1,0:T(8,128)(2,1)S(1)}, bf16[4,128,512]{2,1,0:T(8,128)(2,1)}, u32[]{:S(2)}, u32[]{:S(2)}) collective-permute-start(bf16[4,128,512]{2,1,0:T(8,128)(2,1)S(1)} %bitcast.5), channel_id=1, source_target_pairs={{2,0},{71,1},{4,2},{1,3},{6,4},{3,5},{64,6},{5,7},{10,8},{79,9},{1... | collective-permute-start | bytes 1572872 | tf_op jit(solution)/shard_map/weight_z1/ppermute | solution.py:408
  61.6 0.0 copy-done
  61.6 2.8 %back_early.1 = bf16[6,256,256]{2,1,0:T(8,128)(2,1)} custom-call(bf16[10,256,256]{2,1,0:T(8,128)(2,1)} %copy-done.4, bf16[4,128,512]{2,1,0:T(8,128)(2,1)S(1)} %bitcast.6, bf16[4,128,512]{2,1,0:T(8,128)(2,1)S(1)} %collective-permute-done.2.refs_1_.weight_1, bf16[4,128,512]{2,1,0:T(8,128)(2,1)S(1)} %collective-permute-done.3.refs_2_.weight_3), custom_call_target="tpu_custom_call" | custom-call | bytes 150000 | tf_op jit(solution)/shard_map/back_early/pallas_call | solution.py:86
  64.4 0.0 copy-done.2
  64.4 7.6 %collective-permute-start.5 = (bf16[6,256,256]{2,1,0:T(8,128)(2,1)}, bf16[6,256,256]{2,1,0:T(8,128)(2,1)}, u32[]{:S(2)}, u32[]{:S(2)}) collective-permute-start(bf16[6,256,256]{2,1,0:T(8,128)(2,1)} %back_early.1), channel_id=1, source_target_pairs={{0,32},{1,33},{2,34},{3,35},{4,36},{5,37},{6,38},{7,39},{8,40},{9,... | collective-permute-start | bytes 2359304 | tf_op jit(solution)/shard_map/back_early/ppermute | solution.py:410
  72.0 0.0 all-to-all-done.in_ref
  72.0 0.9 split.1
  73.0 0.0 copy-done.1
  73.0 5.6 %all-to-all-start.1 = ((bf16[16,16,256]{2,1,0:T(8,128)(2,1)}), bf16[16,16,256]{2,1,0:T(8,128)(2,1)S(1)}, u32[]{:S(2)}, u32[]{:S(2)}) async-start(bf16[16,16,256]{2,1,0:T(8,128)(2,1)} %split.1), calls=%async_computation.1 | async-start | bytes 262144 | tf_op jit(solution)/shard_map/ring_z/all_to_all | solution.py:80
  78.5 0.0 collective-permute-done.4.refs_0_.weight_2
  78.5 2.1 %back_late.1 = bf16[2,256,256]{2,1,0:T(8,128)(2,1)S(1)} custom-call(bf16[10,256,256]{2,1,0:T(8,128)(2,1)} %copy-done.4, bf16[4,128,512]{2,1,0:T(8,128)(2,1)} %collective-permute-done.4.refs_0_.weight_2), custom_call_target="tpu_custom_call" | custom-call | bytes 150000 | tf_op jit(solution)/shard_map/back_late/pallas_call | solution.py:86
  80.7 6.7 %collective-permute-start.6 = (bf16[2,256,256]{2,1,0:T(8,128)(2,1)S(1)}, bf16[2,256,256]{2,1,0:T(8,128)(2,1)S(1)}, u32[]{:S(2)}, u32[]{:S(2)}) collective-permute-start(bf16[2,256,256]{2,1,0:T(8,128)(2,1)S(1)} %back_late.1), channel_id=1, source_target_pairs={{0,32},{1,33},{2,34},{3,35},{4,36},{5,37},{6,38},{7,39},{8,40},{9,... | collective-permute-start | bytes 786440 | tf_op jit(solution)/shard_map/back_late/ppermute | solution.py:416
  87.4 0.0 collective-permute-done.5.early_hbm
  87.4 1.1 %collective-permute-done.6.late_hbm = bf16[2,256,256]{2,1,0:T(8,128)(2,1)S(1)} collective-permute-done((bf16[2,256,256]{2,1,0:T(8,128)(2,1)S(1)}, bf16[2,256,256]{2,1,0:T(8,128)(2,1)S(1)}, u32[]{:S(2)}, u32[]{:S(2)}) %collective-permute-start.6) | collective-permute-done | bytes 262176 | tf_op jit(solution)/shard_map/back_late/ppermute | solution.py:416
  88.5 0.7 copy-done.5
  89.3 5.0 %input_grad.1 = bf16[256,4096]{1,0:T(8,128)(2,1)} custom-call(bf16[256,4096]{1,0:T(8,128)(2,1)} %hidden_hbm.3, bf16[256,512]{1,0:T(8,128)(2,1)} %key_hbm.5, f32[1,4096]{1,0:T(1,128)} %bitcast.10, f32[256,128]{1,0:T(8,128)} %get-tuple-element.19.inv_hbm, bf16[4,128,512]{2,1,0:T(8,128)(2,1)} %bitcast.7, bf16[4,128,512]{2,1,0:T(8,128)(2,1)} %copy-done.1, ...), custom_call_target="tpu_custom_call" | custom-call | bytes 150000 | tf_op jit(solution)/shard_map/input_grad/pallas_call | solution.py:86
  94.3 0.0 all-to-all-done.1.in_ref
  94.3 0.0 copy-done.3
  94.3 0.8 serve.1
  (6 shorter events, 0.0 us)
Async XLA Ops:
  0.6 16.9 %collective-permute-start = (bf16[128,512]{1,0:T(8,128)(2,1)}, bf16[128,512]{1,0:T(8,128)(2,1)S(1)}, u32[]{:S(2)}, u32[]{:S(2)}) collective-permute-start(bf16[128,512]{1,0:T(8,128)(2,1)} %param.7), channel_id=1, source_target_pairs={{0,0},{1,1},{2,2},{3,3},{4,4},{5,5},{6,6},{7,7},{8,8},{9,9},{10,10... | collective-permute-start | bytes 393224 | tf_op jit(solution)/shard_map/weight_z4/ppermute | solution.py:360
  17.6 13.5 %collective-permute-start.1 = (bf16[10,256,256]{2,1,0:T(8,128)(2,1)}, bf16[10,256,256]{2,1,0:T(8,128)(2,1)S(1)}, u32[]{:S(2)}, u32[]{:S(2)}) collective-permute-start(bf16[10,256,256]{2,1,0:T(8,128)(2,1)} %get-tuple-element.17), channel_id=1, source_target_pairs={{0,32},{1,33},{2,34},{3,35},{4,36},{5,37},{6,38},{7,39},{8,40},{9,... | collective-permute-start | bytes 3932168 | tf_op jit(solution)/shard_map/norm/ppermute | solution.py:381
  31.1 30.5 %copy-start = (bf16[512,512]{1,0:T(8,128)(2,1)}, bf16[512,512]{1,0:T(8,128)(2,1)S(1)}, u32[]{:S(2)}) copy-start(bf16[512,512]{1,0:T(8,128)(2,1)S(1)} %all_gather.3) | copy-start | bytes 1572868
  31.1 1.1 %copy-start.4 = (bf16[10,256,256]{2,1,0:T(8,128)(2,1)}, bf16[10,256,256]{2,1,0:T(8,128)(2,1)S(1)}, u32[]{:S(2)}) copy-start(bf16[10,256,256]{2,1,0:T(8,128)(2,1)S(1)} %collective-permute-done.1.other_hbm.key_hbm) | copy-start | bytes 3932164
  36.3 35.7 %all-to-all-start = ((bf16[16,256,256]{2,1,0:T(8,128)(2,1)}), bf16[16,256,256]{2,1,0:T(8,128)(2,1)S(1)}, u32[]{:S(2)}, u32[]{:S(2)}) async-start(bf16[16,256,256]{2,1,0:T(8,128)(2,1)} %squares.1), calls=%async_computation | async-start | bytes 4194304 | tf_op jit(solution)/shard_map/plane/all_to_all | solution.py:80
  41.3 13.3 %collective-permute-start.2 = (bf16[4,128,512]{2,1,0:T(8,128)(2,1)S(1)}, bf16[4,128,512]{2,1,0:T(8,128)(2,1)S(1)}, u32[]{:S(2)}, u32[]{:S(2)}) collective-permute-start(bf16[4,128,512]{2,1,0:T(8,128)(2,1)S(1)} %bitcast.3), channel_id=1, source_target_pairs={{1,0},{2,1},{3,2},{4,3},{5,4},{6,5},{7,6},{64,7},{9,8},{10,9},{11,... | collective-permute-start | bytes 1572872 | tf_op jit(solution)/shard_map/weight_z1/ppermute | solution.py:405
  47.6 12.1 %collective-permute-start.3 = (bf16[4,128,512]{2,1,0:T(8,128)(2,1)S(1)}, bf16[4,128,512]{2,1,0:T(8,128)(2,1)S(1)}, u32[]{:S(2)}, u32[]{:S(2)}) collective-permute-start(bf16[4,128,512]{2,1,0:T(8,128)(2,1)S(1)} %bitcast.4), channel_id=1, source_target_pairs={{71,0},{0,1},{1,2},{2,3},{3,4},{4,5},{5,6},{6,7},{79,8},{8,9},{9,1... | collective-permute-start | bytes 1572872 | tf_op jit(solution)/shard_map/weight_z1/ppermute | solution.py:406
  54.6 18.3 %copy-start.1 = (bf16[4,128,512]{2,1,0:T(8,128)(2,1)}, bf16[4,128,512]{2,1,0:T(8,128)(2,1)S(1)}, u32[]{:S(2)}) copy-start(bf16[4,128,512]{2,1,0:T(8,128)(2,1)S(1)} %collective-permute-done.2.refs_1_.weight_1) | copy-start | bytes 1572868
  59.7 4.7 %copy-start.2 = (bf16[4,128,512]{2,1,0:T(8,128)(2,1)}, bf16[4,128,512]{2,1,0:T(8,128)(2,1)S(1)}, u32[]{:S(2)}) copy-start(bf16[4,128,512]{2,1,0:T(8,128)(2,1)S(1)} %collective-permute-done.3.refs_2_.weight_3) | copy-start | bytes 1572868
  59.7 18.9 %collective-permute-start.4 = (bf16[4,128,512]{2,1,0:T(8,128)(2,1)S(1)}, bf16[4,128,512]{2,1,0:T(8,128)(2,1)}, u32[]{:S(2)}, u32[]{:S(2)}) collective-permute-start(bf16[4,128,512]{2,1,0:T(8,128)(2,1)S(1)} %bitcast.5), channel_id=1, source_target_pairs={{2,0},{71,1},{4,2},{1,3},{6,4},{3,5},{64,6},{5,7},{10,8},{79,9},{1... | collective-permute-start | bytes 1572872 | tf_op jit(solution)/shard_map/weight_z1/ppermute | solution.py:408
  64.4 23.0 %collective-permute-start.5 = (bf16[6,256,256]{2,1,0:T(8,128)(2,1)}, bf16[6,256,256]{2,1,0:T(8,128)(2,1)}, u32[]{:S(2)}, u32[]{:S(2)}) collective-permute-start(bf16[6,256,256]{2,1,0:T(8,128)(2,1)} %back_early.1), channel_id=1, source_target_pairs={{0,32},{1,33},{2,34},{3,35},{4,36},{5,37},{6,38},{7,39},{8,40},{9,... | collective-permute-start | bytes 2359304 | tf_op jit(solution)/shard_map/back_early/ppermute | solution.py:410
  73.0 21.3 %all-to-all-start.1 = ((bf16[16,16,256]{2,1,0:T(8,128)(2,1)}), bf16[16,16,256]{2,1,0:T(8,128)(2,1)S(1)}, u32[]{:S(2)}, u32[]{:S(2)}) async-start(bf16[16,16,256]{2,1,0:T(8,128)(2,1)} %split.1), calls=%async_computation.1 | async-start | bytes 262144 | tf_op jit(solution)/shard_map/ring_z/all_to_all | solution.py:80
  80.7 7.9 %collective-permute-start.6 = (bf16[2,256,256]{2,1,0:T(8,128)(2,1)S(1)}, bf16[2,256,256]{2,1,0:T(8,128)(2,1)S(1)}, u32[]{:S(2)}, u32[]{:S(2)}) collective-permute-start(bf16[2,256,256]{2,1,0:T(8,128)(2,1)S(1)} %back_late.1), channel_id=1, source_target_pairs={{0,32},{1,33},{2,34},{3,35},{4,36},{5,37},{6,38},{7,39},{8,40},{9,... | collective-permute-start | bytes 786440 | tf_op jit(solution)/shard_map/back_late/ppermute | solution.py:416
  88.5 0.7 copy-start.5
  89.3 5.0 %copy-start.3 = (s32[512]{0:T(512)S(1)}, s32[512]{0:T(512)}, u32[]{:S(2)}) copy-start(s32[512]{0:T(512)} %param.9) | copy-start | bytes 6148

commit v10 on v8

--- a/solution.py
+++ b/solution.py
@@ -403,7 +403,7 @@
                 dma((10,)),
                 dma((blocks, NY)),
             ],
-            mib=60,
+            mib=51,
         )
     with jax.named_scope("weight_y"):
         column = [origin] + [lax.ppermute(origin, AXES, from_y(ahead)) for ahead in (1, 2, 3)]
@@ -417,7 +417,8 @@
     with jax.named_scope("weight_z1"):
         up = lax.ppermute(near, AXES, from_z(1))
         down = lax.ppermute(near, AXES, from_z(-1))
-        far = lax.ppermute(near, AXES, two_away())
+        *now, up, down = barrier((near, up, down))
+        far = lax.ppermute(now[0], AXES, two_away())
     with jax.named_scope("back_early"):
         early = lax.ppermute(partner(other, near, up, down), AXES, CORE_SWAP)
     with jax.named_scope("split"):

time: 95.7 us -> 94.8 us (level)
  the two profiles are of different devices: /device:TPU:32 before, /device:TPU:1 now
where the time goes in v10:
time: 94.8 us; the launch traced here: 93.1 us
  starting transfers between devices  60.2 us (64%)
  Pallas kernels  18.7 us (20%)
  waiting for transfers between devices  10.9 us (11%)
  local copies, waits for them, and re-layouts  2.41 us (3%)
    pallas_call x8, Pallas kernels, call(): pl.pallas_call(kernel, out_shape=outs, in_specs=[pl.BlockSpec(memory_spac...  18.7 us
    ppermute x1, starting transfers between devices, body(): origin = lax.ppermute(key_weight, AXES, origins())  13.4 us
    all_to_all x2, starting transfers between devices, exchange(): lax.all_to_all(value, AXES, split_axis=0, concat_axis=0, axis_index_group...  11.5 us
    ppermute x3, starting transfers between devices, body(): lax.ppermute(origin, AXES, from_y(ahead))  10.7 us
    ppermute x1, waiting for transfers between devices, body(): down = lax.ppermute(near, AXES, from_z(-1))  8.13 us
    ppermute x1, starting transfers between devices, body(): up = lax.ppermute(near, AXES, from_z(1))  6.26 us
    ppermute x1, starting transfers between devices, body(): early = lax.ppermute(partner(other, near, up, down), AXES, CORE_SWAP)  5.56 us
    ppermute x1, starting transfers between devices, body(): far = lax.ppermute(now[0], AXES, two_away())  4.99 us
  transfers between devices with their start and end apart: 12, of which 4 were waited for; matrix products, arithmetic and copies ran while one was open for 0% of the time, Pallas kernels for 19%

profile of v10, /device:TPU:1, one launch (start us, length us, event | category | flops | bytes accessed | tf_op | source)
XLA Modules:
  0.0 93.1 jit_solution(1864128643371849757)
XLA Ops:
  0.6 0.0 copy-start.2
  0.6 13.4 %collective-permute-start = (bf16[128,512]{1,0:T(8,128)(2,1)}, bf16[128,512]{1,0:T(8,128)(2,1)S(1)}, u32[]{:S(2)}, u32[]{:S(2)}) collective-permute-start(bf16[128,512]{1,0:T(8,128)(2,1)} %param.7), channel_id=1, source_target_pairs={{0,0},{1,1},{2,2},{3,3},{4,4},{5,5},{6,6},{7,7},{8,8},{9,9},{10,10... | collective-permute-start | bytes 393224 | tf_op jit(solution)/shard_map/weight_z4/ppermute | solution.py:369
  14.1 2.9 %norm.1 = (bf16[8,256,256]{2,1,0:T(8,128)(2,1)}, bf16[10,256,256]{2,1,0:T(8,128)(2,1)}, f32[256,128]{1,0:T(8,128)}) custom-call(bf16[256,4096]{1,0:T(8,128)(2,1)} %hidden_hbm.3, bf16[256,512]{1,0:T(8,128)(2,1)} %key_hbm.5, f32[1,4096]{1,0:T(1,128)} %bitcast.3), custom_call_target="tpu_custom_call" | custom-call | bytes 150000 | tf_op jit(solution)/shard_map/norm/pallas_call | solution.py:86
  17.0 0.7 collective-permute-done.refs_0_
  17.7 1.9 %collective-permute-start.1 = (bf16[10,256,256]{2,1,0:T(8,128)(2,1)}, bf16[10,256,256]{2,1,0:T(8,128)(2,1)S(1)}, u32[]{:S(2)}, u32[]{:S(2)}) collective-permute-start(bf16[10,256,256]{2,1,0:T(8,128)(2,1)} %get-tuple-element.19), channel_id=1, source_target_pairs={{0,32},{1,33},{2,34},{3,35},{4,36},{5,37},{6,38},{7,39},{8,40},{9,... | collective-permute-start | bytes 3932168 | tf_op jit(solution)/shard_map/norm/ppermute | solution.py:390
  19.6 3.2 %collective-permute-start.4 = (bf16[128,512]{1,0:T(8,128)(2,1)S(1)}, bf16[128,512]{1,0:T(8,128)(2,1)S(1)}, u32[]{:S(2)}, u32[]{:S(2)}) collective-permute-start(bf16[128,512]{1,0:T(8,128)(2,1)S(1)} %collective-permute-done.refs_0_), channel_id=1, source_target_pairs={{24,0},{25,1},{26,2},{27,3},{28,4},{29,5},{30,6},{31,7},{0,8},{1,9... | collective-permute-start | bytes 393224 | tf_op jit(solution)/shard_map/weight_y/ppermute | solution.py:409
  22.8 4.5 %collective-permute-start.3 = (bf16[128,512]{1,0:T(8,128)(2,1)S(1)}, bf16[128,512]{1,0:T(8,128)(2,1)S(1)}, u32[]{:S(2)}, u32[]{:S(2)}) collective-permute-start(bf16[128,512]{1,0:T(8,128)(2,1)S(1)} %collective-permute-done.refs_0_), channel_id=1, source_target_pairs={{16,0},{17,1},{18,2},{19,3},{20,4},{21,5},{22,6},{23,7},{24,8},{25... | collective-permute-start | bytes 393224 | tf_op jit(solution)/shard_map/weight_y/ppermute | solution.py:409
  27.4 3.0 %collective-permute-start.2 = (bf16[128,512]{1,0:T(8,128)(2,1)S(1)}, bf16[128,512]{1,0:T(8,128)(2,1)S(1)}, u32[]{:S(2)}, u32[]{:S(2)}) collective-permute-start(bf16[128,512]{1,0:T(8,128)(2,1)S(1)} %collective-permute-done.refs_0_), channel_id=1, source_target_pairs={{8,0},{9,1},{10,2},{11,3},{12,4},{13,5},{14,6},{15,7},{16,8},{17,9... | collective-permute-start | bytes 393224 | tf_op jit(solution)/shard_map/weight_y/ppermute | solution.py:409
  30.4 0.0 collective-permute-done.1.other_hbm.key_hbm
  30.4 1.7 %copy-done.5 = bf16[8,256,256]{2,1,0:T(8,128)(2,1)S(1)} copy-done((bf16[8,256,256]{2,1,0:T(8,128)(2,1)S(1)}, bf16[8,256,256]{2,1,0:T(8,128)(2,1)}, u32[]{:S(2)}) %copy-start.5) | copy-done | bytes 1048600
  32.1 3.1 %squares.1 = bf16[16,256,256]{2,1,0:T(8,128)(2,1)} custom-call(bf16[8,256,256]{2,1,0:T(8,128)(2,1)S(1)} %copy-done.5, bf16[10,256,256]{2,1,0:T(8,128)(2,1)S(1)} %collective-permute-done.1.other_hbm.key_hbm, bf16[256,512]{1,0:T(8,128)(2,1)S(1)} %copy-done.2), custom_call_target="tpu_custom_call" | custom-call | bytes 150000 | tf_op jit(solution)/shard_map/squares/pallas_call | solution.py:86
  35.2 0.0 collective-permute-done.4.refs_3_
  35.3 0.0 collective-permute-done.3.refs_2_
  35.3 4.3 %all-to-all-start = ((bf16[16,256,256]{2,1,0:T(8,128)(2,1)}), bf16[16,256,256]{2,1,0:T(8,128)(2,1)S(1)}, u32[]{:S(2)}, u32[]{:S(2)}) async-start(bf16[16,256,256]{2,1,0:T(8,128)(2,1)} %squares.1), calls=%async_computation | async-start | bytes 4194304 | tf_op jit(solution)/shard_map/plane/all_to_all | solution.py:80
  39.5 0.7 weight_y.1.refs_0_.weight_0
  40.3 1.9 %collective-permute-start.6 = (bf16[4,128,512]{2,1,0:T(8,128)(2,1)S(1)}, bf16[4,128,512]{2,1,0:T(8,128)(2,1)S(1)}, u32[]{:S(2)}, u32[]{:S(2)}) collective-permute-start(bf16[4,128,512]{2,1,0:T(8,128)(2,1)S(1)} %weight_y.1.refs_0_.weight_0), channel_id=1, source_target_pairs={{71,0},{0,1},{1,2},{2,3},{3,4},{4,5},{5,6},{6,7},{79,8},{8,9},{9,1... | collective-permute-start | bytes 1572872 | tf_op jit(solution)/shard_map/weight_z1/ppermute | solution.py:419
  42.2 6.3 %collective-permute-start.5 = (bf16[4,128,512]{2,1,0:T(8,128)(2,1)S(1)}, bf16[4,128,512]{2,1,0:T(8,128)(2,1)S(1)}, u32[]{:S(2)}, u32[]{:S(2)}) collective-permute-start(bf16[4,128,512]{2,1,0:T(8,128)(2,1)S(1)} %weight_y.1.refs_0_.weight_0), channel_id=1, source_target_pairs={{1,0},{2,1},{3,2},{4,3},{5,4},{6,5},{7,6},{64,7},{9,8},{10,9},{11,... | collective-permute-start | bytes 1572872 | tf_op jit(solution)/shard_map/weight_z1/ppermute | solution.py:418
  48.5 8.1 %collective-permute-done.6.refs_2_.weight_3 = bf16[4,128,512]{2,1,0:T(8,128)(2,1)S(1)} collective-permute-done((bf16[4,128,512]{2,1,0:T(8,128)(2,1)S(1)}, bf16[4,128,512]{2,1,0:T(8,128)(2,1)S(1)}, u32[]{:S(2)}, u32[]{:S(2)}) %collective-permute-start.6) | collective-permute-done | bytes 524320 | tf_op jit(solution)/shard_map/weight_z1/ppermute | solution.py:419
  56.6 0.9 collective-permute-done.5.refs_1_.weight_1
  57.5 5.0 %collective-permute-start.7 = (bf16[4,128,512]{2,1,0:T(8,128)(2,1)S(1)}, bf16[4,128,512]{2,1,0:T(8,128)(2,1)}, u32[]{:S(2)}, u32[]{:S(2)}) collective-permute-start(bf16[4,128,512]{2,1,0:T(8,128)(2,1)S(1)} %weight_y.1.refs_0_.weight_0), channel_id=1, source_target_pairs={{2,0},{71,1},{4,2},{1,3},{6,4},{3,5},{64,6},{5,7},{10,8},{79,9},{1... | collective-permute-start | bytes 1572872 | tf_op jit(solution)/shard_map/weight_z1/ppermute | solution.py:421
  62.5 2.8 %back_early.1 = bf16[6,256,256]{2,1,0:T(8,128)(2,1)} custom-call(bf16[10,256,256]{2,1,0:T(8,128)(2,1)} %copy-done, bf16[4,128,512]{2,1,0:T(8,128)(2,1)S(1)} %weight_y.1.refs_0_.weight_0, bf16[4,128,512]{2,1,0:T(8,128)(2,1)S(1)} %collective-permute-done.5.refs_1_.weight_1, bf16[4,128,512]{2,1,0:T(8,128)(2,1)S(1)} %collective-permute-done.6.refs_2_.weight_3), custom_call_target="tpu_custom_call" | custom-call | bytes 150000 | tf_op jit(solution)/shard_map/back_early/pallas_call | solution.py:86
  65.3 5.6 %collective-permute-start.8 = (bf16[6,256,256]{2,1,0:T(8,128)(2,1)}, bf16[6,256,256]{2,1,0:T(8,128)(2,1)}, u32[]{:S(2)}, u32[]{:S(2)}) collective-permute-start(bf16[6,256,256]{2,1,0:T(8,128)(2,1)} %back_early.1), channel_id=1, source_target_pairs={{0,32},{1,33},{2,34},{3,35},{4,36},{5,37},{6,38},{7,39},{8,40},{9,... | collective-permute-start | bytes 2359304 | tf_op jit(solution)/shard_map/back_early/ppermute | solution.py:423
  70.9 0.9 %split.1 = bf16[16,16,256]{2,1,0:T(8,128)(2,1)} custom-call(bf16[16,256,256]{2,1,0:T(8,128)(2,1)S(1)} %all-to-all-done.in_ref), custom_call_target="tpu_custom_call" | custom-call | bytes 150000 | tf_op jit(solution)/shard_map/split/pallas_call | solution.py:86
  71.8 7.2 %all-to-all-start.1 = ((bf16[16,16,256]{2,1,0:T(8,128)(2,1)}), bf16[16,16,256]{2,1,0:T(8,128)(2,1)S(1)}, u32[]{:S(2)}, u32[]{:S(2)}) async-start(bf16[16,16,256]{2,1,0:T(8,128)(2,1)} %split.1), calls=%async_computation.1 | async-start | bytes 262144 | tf_op jit(solution)/shard_map/ring_z/all_to_all | solution.py:80
  79.1 0.0 collective-permute-done.7.refs_0_.weight_2
  79.1 2.1 %back_late.1 = bf16[2,256,256]{2,1,0:T(8,128)(2,1)S(1)} custom-call(bf16[10,256,256]{2,1,0:T(8,128)(2,1)} %copy-done, bf16[4,128,512]{2,1,0:T(8,128)(2,1)} %collective-permute-done.7.refs_0_.weight_2), custom_call_target="tpu_custom_call" | custom-call | bytes 150000 | tf_op jit(solution)/shard_map/back_late/pallas_call | solution.py:86
  81.2 3.9 %collective-permute-start.9 = (bf16[2,256,256]{2,1,0:T(8,128)(2,1)S(1)}, bf16[2,256,256]{2,1,0:T(8,128)(2,1)S(1)}, u32[]{:S(2)}, u32[]{:S(2)}) collective-permute-start(bf16[2,256,256]{2,1,0:T(8,128)(2,1)S(1)} %back_late.1), channel_id=1, source_target_pairs={{0,32},{1,33},{2,34},{3,35},{4,36},{5,37},{6,38},{7,39},{8,40},{9,... | collective-permute-start | bytes 786440 | tf_op jit(solution)/shard_map/back_late/ppermute | solution.py:429
  85.2 1.1 %collective-permute-done.9.late_hbm = bf16[2,256,256]{2,1,0:T(8,128)(2,1)S(1)} collective-permute-done((bf16[2,256,256]{2,1,0:T(8,128)(2,1)S(1)}, bf16[2,256,256]{2,1,0:T(8,128)(2,1)S(1)}, u32[]{:S(2)}, u32[]{:S(2)}) %collective-permute-start.9) | collective-permute-done | bytes 262176 | tf_op jit(solution)/shard_map/back_late/ppermute | solution.py:429
  86.3 0.7 copy-done.7
  87.0 5.2 %input_grad.1 = bf16[256,4096]{1,0:T(8,128)(2,1)} custom-call(bf16[256,4096]{1,0:T(8,128)(2,1)} %hidden_hbm.3, bf16[256,512]{1,0:T(8,128)(2,1)} %key_hbm.5, f32[1,4096]{1,0:T(1,128)} %bitcast.4, f32[256,128]{1,0:T(8,128)} %get-tuple-element.22.inv_hbm, bf16[4,128,512]{2,1,0:T(8,128)(2,1)} %copy-done.1, bf16[4,128,512]{2,1,0:T(8,128)(2,1)} %copy-done.4, ...), custom_call_target="tpu_custom_call" | custom-call | bytes 150000 | tf_op jit(solution)/shard_map/input_grad/pallas_call | solution.py:86
  92.2 0.0 all-to-all-done.1.in_ref
  92.3 0.8 serve.1
  (16 shorter events, 0.0 us)
Async XLA Ops:
  0.6 29.8 %copy-start.2 = (bf16[256,512]{1,0:T(8,128)(2,1)S(1)}, bf16[256,512]{1,0:T(8,128)(2,1)}, u32[]{:S(2)}) copy-start(bf16[256,512]{1,0:T(8,128)(2,1)} %key_hbm.5) | copy-start | bytes 786436
  0.6 17.1 %collective-permute-start = (bf16[128,512]{1,0:T(8,128)(2,1)}, bf16[128,512]{1,0:T(8,128)(2,1)S(1)}, u32[]{:S(2)}, u32[]{:S(2)}) collective-permute-start(bf16[128,512]{1,0:T(8,128)(2,1)} %param.7), channel_id=1, source_target_pairs={{0,0},{1,1},{2,2},{3,3},{4,4},{5,5},{6,6},{7,7},{8,8},{9,9},{10,10... | collective-permute-start | bytes 393224 | tf_op jit(solution)/shard_map/weight_z4/ppermute | solution.py:369
  17.7 12.7 %collective-permute-start.1 = (bf16[10,256,256]{2,1,0:T(8,128)(2,1)}, bf16[10,256,256]{2,1,0:T(8,128)(2,1)S(1)}, u32[]{:S(2)}, u32[]{:S(2)}) collective-permute-start(bf16[10,256,256]{2,1,0:T(8,128)(2,1)} %get-tuple-element.19), channel_id=1, source_target_pairs={{0,32},{1,33},{2,34},{3,35},{4,36},{5,37},{6,38},{7,39},{8,40},{9,... | collective-permute-start | bytes 3932168 | tf_op jit(solution)/shard_map/norm/ppermute | solution.py:390
  19.6 15.6 %collective-permute-start.4 = (bf16[128,512]{1,0:T(8,128)(2,1)S(1)}, bf16[128,512]{1,0:T(8,128)(2,1)S(1)}, u32[]{:S(2)}, u32[]{:S(2)}) collective-permute-start(bf16[128,512]{1,0:T(8,128)(2,1)S(1)} %collective-permute-done.refs_0_), channel_id=1, source_target_pairs={{24,0},{25,1},{26,2},{27,3},{28,4},{29,5},{30,6},{31,7},{0,8},{1,9... | collective-permute-start | bytes 393224 | tf_op jit(solution)/shard_map/weight_y/ppermute | solution.py:409
  22.8 12.4 %collective-permute-start.3 = (bf16[128,512]{1,0:T(8,128)(2,1)S(1)}, bf16[128,512]{1,0:T(8,128)(2,1)S(1)}, u32[]{:S(2)}, u32[]{:S(2)}) collective-permute-start(bf16[128,512]{1,0:T(8,128)(2,1)S(1)} %collective-permute-done.refs_0_), channel_id=1, source_target_pairs={{16,0},{17,1},{18,2},{19,3},{20,4},{21,5},{22,6},{23,7},{24,8},{25... | collective-permute-start | bytes 393224 | tf_op jit(solution)/shard_map/weight_y/ppermute | solution.py:409
  27.4 7.9 %collective-permute-start.2 = (bf16[128,512]{1,0:T(8,128)(2,1)S(1)}, bf16[128,512]{1,0:T(8,128)(2,1)S(1)}, u32[]{:S(2)}, u32[]{:S(2)}) collective-permute-start(bf16[128,512]{1,0:T(8,128)(2,1)S(1)} %collective-permute-done.refs_0_), channel_id=1, source_target_pairs={{8,0},{9,1},{10,2},{11,3},{12,4},{13,5},{14,6},{15,7},{16,8},{17,9... | collective-permute-start | bytes 393224 | tf_op jit(solution)/shard_map/weight_y/ppermute | solution.py:409
  30.4 4.9 %copy-start = (bf16[10,256,256]{2,1,0:T(8,128)(2,1)}, bf16[10,256,256]{2,1,0:T(8,128)(2,1)S(1)}, u32[]{:S(2)}) copy-start(bf16[10,256,256]{2,1,0:T(8,128)(2,1)S(1)} %collective-permute-done.1.other_hbm.key_hbm) | copy-start | bytes 3932164
  30.4 1.7 %copy-start.5 = (bf16[8,256,256]{2,1,0:T(8,128)(2,1)S(1)}, bf16[8,256,256]{2,1,0:T(8,128)(2,1)}, u32[]{:S(2)}) copy-start(bf16[8,256,256]{2,1,0:T(8,128)(2,1)} %get-tuple-element.17.own_hbm) | copy-start | bytes 3145732
  35.3 35.6 %all-to-all-start = ((bf16[16,256,256]{2,1,0:T(8,128)(2,1)}), bf16[16,256,256]{2,1,0:T(8,128)(2,1)S(1)}, u32[]{:S(2)}, u32[]{:S(2)}) async-start(bf16[16,256,256]{2,1,0:T(8,128)(2,1)} %squares.1), calls=%async_computation | async-start | bytes 4194304 | tf_op jit(solution)/shard_map/plane/all_to_all | solution.py:80
  40.3 31.6 %copy-start.1 = (bf16[4,128,512]{2,1,0:T(8,128)(2,1)}, bf16[4,128,512]{2,1,0:T(8,128)(2,1)S(1)}, u32[]{:S(2)}) copy-start(bf16[4,128,512]{2,1,0:T(8,128)(2,1)S(1)} %weight_y.1.refs_0_.weight_0) | copy-start | bytes 1572868
  40.3 16.3 %collective-permute-start.6 = (bf16[4,128,512]{2,1,0:T(8,128)(2,1)S(1)}, bf16[4,128,512]{2,1,0:T(8,128)(2,1)S(1)}, u32[]{:S(2)}, u32[]{:S(2)}) collective-permute-start(bf16[4,128,512]{2,1,0:T(8,128)(2,1)S(1)} %weight_y.1.refs_0_.weight_0), channel_id=1, source_target_pairs={{71,0},{0,1},{1,2},{2,3},{3,4},{4,5},{5,6},{6,7},{79,8},{8,9},{9,1... | collective-permute-start | bytes 1572872 | tf_op jit(solution)/shard_map/weight_z1/ppermute | solution.py:419
  42.2 15.3 %collective-permute-start.5 = (bf16[4,128,512]{2,1,0:T(8,128)(2,1)S(1)}, bf16[4,128,512]{2,1,0:T(8,128)(2,1)S(1)}, u32[]{:S(2)}, u32[]{:S(2)}) collective-permute-start(bf16[4,128,512]{2,1,0:T(8,128)(2,1)S(1)} %weight_y.1.refs_0_.weight_0), channel_id=1, source_target_pairs={{1,0},{2,1},{3,2},{4,3},{5,4},{6,5},{7,6},{64,7},{9,8},{10,9},{11,... | collective-permute-start | bytes 1572872 | tf_op jit(solution)/shard_map/weight_z1/ppermute | solution.py:418
  56.6 15.2 %copy-start.3 = (bf16[4,128,512]{2,1,0:T(8,128)(2,1)}, bf16[4,128,512]{2,1,0:T(8,128)(2,1)S(1)}, u32[]{:S(2)}) copy-start(bf16[4,128,512]{2,1,0:T(8,128)(2,1)S(1)} %collective-permute-done.6.refs_2_.weight_3) | copy-start | bytes 1572868
  57.5 7.8 %copy-start.4 = (bf16[4,128,512]{2,1,0:T(8,128)(2,1)}, bf16[4,128,512]{2,1,0:T(8,128)(2,1)S(1)}, u32[]{:S(2)}) copy-start(bf16[4,128,512]{2,1,0:T(8,128)(2,1)S(1)} %collective-permute-done.5.refs_1_.weight_1) | copy-start | bytes 1572868
  57.5 21.6 %collective-permute-start.7 = (bf16[4,128,512]{2,1,0:T(8,128)(2,1)S(1)}, bf16[4,128,512]{2,1,0:T(8,128)(2,1)}, u32[]{:S(2)}, u32[]{:S(2)}) collective-permute-start(bf16[4,128,512]{2,1,0:T(8,128)(2,1)S(1)} %weight_y.1.refs_0_.weight_0), channel_id=1, source_target_pairs={{2,0},{71,1},{4,2},{1,3},{6,4},{3,5},{64,6},{5,7},{10,8},{79,9},{1... | collective-permute-start | bytes 1572872 | tf_op jit(solution)/shard_map/weight_z1/ppermute | solution.py:421
  65.3 21.0 %collective-permute-start.8 = (bf16[6,256,256]{2,1,0:T(8,128)(2,1)}, bf16[6,256,256]{2,1,0:T(8,128)(2,1)}, u32[]{:S(2)}, u32[]{:S(2)}) collective-permute-start(bf16[6,256,256]{2,1,0:T(8,128)(2,1)} %back_early.1), channel_id=1, source_target_pairs={{0,32},{1,33},{2,34},{3,35},{4,36},{5,37},{6,38},{7,39},{8,40},{9,... | collective-permute-start | bytes 2359304 | tf_op jit(solution)/shard_map/back_early/ppermute | solution.py:423
  71.8 20.4 %all-to-all-start.1 = ((bf16[16,16,256]{2,1,0:T(8,128)(2,1)}), bf16[16,16,256]{2,1,0:T(8,128)(2,1)S(1)}, u32[]{:S(2)}, u32[]{:S(2)}) async-start(bf16[16,16,256]{2,1,0:T(8,128)(2,1)} %split.1), calls=%async_computation.1 | async-start | bytes 262144 | tf_op jit(solution)/shard_map/ring_z/all_to_all | solution.py:80
  81.2 5.1 %collective-permute-start.9 = (bf16[2,256,256]{2,1,0:T(8,128)(2,1)S(1)}, bf16[2,256,256]{2,1,0:T(8,128)(2,1)S(1)}, u32[]{:S(2)}, u32[]{:S(2)}) collective-permute-start(bf16[2,256,256]{2,1,0:T(8,128)(2,1)S(1)} %back_late.1), channel_id=1, source_target_pairs={{0,32},{1,33},{2,34},{3,35},{4,36},{5,37},{6,38},{7,39},{8,40},{9,... | collective-permute-start | bytes 786440 | tf_op jit(solution)/shard_map/back_late/ppermute | solution.py:429
  86.3 0.7 copy-start.7
  87.0 5.2 %copy-start.6 = (s32[512]{0:T(512)S(1)}, s32[512]{0:T(512)}, u32[]{:S(2)}) copy-start(s32[512]{0:T(512)} %param.9) | copy-start | bytes 6148

commit v11 on v10

--- a/solution.py
+++ b/solution.py
@@ -110,9 +110,25 @@
     return copy
 
 
+OVER_TOKENS = (((0,), (0,)), ((), ()))
+
+
+def put_terms(k, term, ref, hbm, sems):
+    x, zh = k // NZH, k % NZH
+    copies = []
+    for y in range(NY):
+        rows = slice(y * 64, (y + 1) * 64)
+        ref[k, y, 0:64, :] = term[rows, 0:COLS]
+        ref[k, y, 64:128, :] = term[rows, COLS:K]
+        target = hbm.at[x * NY + y, pl.ds(zh * 128, 128)]
+        copies.append(start(ref.at[k, y], target, sems.at[k, y]))
+    return copies
+
+
 def norm_kernel(
-    hidden_hbm, key_hbm, gain_hbm, own_hbm, send_hbm, inv_hbm,
-    hidden_ref, key_ref, gain_ref, own_ref, send_ref, inv_ref, in_sems, out_sems,
+    hidden_hbm, key_hbm, gain_hbm, term_hbm, send_hbm, inv_hbm,
+    hidden_ref, key_ref, gain_ref, own_ref, send_ref, inv_ref, term_ref, in_sems, out_sems,
+    term_sems,
 ):
     core = my_core()
     step, parts, blocks = 16, NORM_PARTS, NX * NZH
@@ -145,15 +161,17 @@
     for i, rows in enumerate(pieces):
         copies[i].wait()
         lax.fori_loop(i * rows_each // step, (i + 1) * rows_each // step, rows_of, 0, unroll=4)
-        out_copies += [
-            start(send_ref.at[:, rows], send_hbm.at[pl.ds(0, blocks), rows], out_sems.at[2 * i]),
-            start(own_ref.at[:, rows], own_hbm.at[:, rows], out_sems.at[2 * i + 1]),
-        ]
+        target = send_hbm.at[pl.ds(0, blocks), rows]
+        out_copies.append(start(send_ref.at[:, rows], target, out_sems.at[i]))
     key_copy.wait()
     for half in range(2):
         source = key_ref.at[:, pl.ds(half * COLS, COLS)]
-        out_copies.append(start(source, send_hbm.at[blocks + half], out_sems.at[2 * parts + half]))
-    out_copies.append(start(inv_ref, inv_hbm, out_sems.at[2 * parts + 2]))
+        out_copies.append(start(source, send_hbm.at[blocks + half], out_sems.at[parts + half]))
+    out_copies.append(start(inv_ref, inv_hbm, out_sems.at[parts + 2]))
+    for k in range(blocks):
+        grad = lax.dot_general(own_ref[k], key_ref[...], OVER_TOKENS, preferred_element_type=F32)
+        term = (grad * grad * (1.0 / TOKENS)).astype(BF16)
+        out_copies += put_terms(k, term, term_ref, term_hbm, term_sems)
     for copy in out_copies:
         copy.wait()
 
@@ -211,40 +229,33 @@
 
 
 def square_kernel(
-    own_hbm, other_hbm, key_hbm, out_hbm, own_ref, other_ref, key_ref, out_ref, in_sems, out_sems
+    own_hbm, other_hbm, out_hbm, own_ref, other_ref, out_ref, in_sems, out_sems
 ):
     blocks = NX * NZH
-    over_tokens = (((0,), (0,)), ((), ()))
-    keys = [
-        start(key_hbm, key_ref, in_sems.at[0]),
-        start(other_hbm.at[pl.ds(blocks, 2)], other_ref.at[pl.ds(blocks, 2)], in_sems.at[1]),
-    ]
+    keys = start(other_hbm.at[pl.ds(blocks, 2)], other_ref.at[pl.ds(blocks, 2)], in_sems.at[0])
     copies = []
-    for part in range(4):
-        some = pl.ds(2 * part, 2)
+    for x in range(NX):
+        some, chunks = pl.ds(NZH * x, NZH), pl.ds(NY * x, NY)
         copies += [
-            start(own_hbm.at[some], own_ref.at[some], in_sems.at[2 + 2 * part]),
-            start(other_hbm.at[some], other_ref.at[some], in_sems.at[3 + 2 * part]),
+            start(other_hbm.at[some], other_ref.at[some], in_sems.at[1 + 2 * x]),
+            start(own_hbm.at[chunks], own_ref.at[chunks], in_sems.at[2 + 2 * x]),
         ]
-    for copy in keys:
-        copy.wait()
+    keys.wait()
     key_other = jnp.concatenate([other_ref[blocks], other_ref[blocks + 1]], axis=1)
-
     out_copies = []
     for k in range(blocks):
         x, zh = k // NZH, k % NZH
         if zh == 0:
             copies[2 * x].wait()
+        grad = lax.dot_general(other_ref[k], key_other, OVER_TOKENS, preferred_element_type=F32)
+        if zh == 0:
             copies[2 * x + 1].wait()
-        g0 = lax.dot_general(own_ref[k], key_ref[...], over_tokens, preferred_element_type=F32)
-        g1 = lax.dot_general(other_ref[k], key_other, over_tokens, preferred_element_type=F32)
-        total = ((g0 * g0 + g1 * g1) * (1.0 / TOKENS)).astype(BF16)
-        for y in range(NY):
-            rows = slice(y * 64, (y + 1) * 64)
-            out_ref[k, y, 0:64, :] = total[rows, 0:COLS]
-            out_ref[k, y, 64:128, :] = total[rows, COLS:K]
-            target = out_hbm.at[x * NY + y, pl.ds(zh * 128, 128)]
-            out_copies.append(start(out_ref.at[k, y], target, out_sems.at[k, y]))
+        own = [own_ref[x * NY + y, zh * 128 : (zh + 1) * 128, :] for y in range(NY)]
+        own = jnp.concatenate(
+            [jnp.concatenate([part[0:64], part[64:128]], axis=1) for part in own], axis=0
+        )
+        term = (grad * grad * (1.0 / TOKENS) + own.astype(F32)).astype(BF16)
+        out_copies += put_terms(k, term, out_ref, out_hbm, out_sems)
     for copy in out_copies:
         copy.wait()
 
@@ -370,7 +381,11 @@
     with jax.named_scope("norm"):
         own, send, inv = call(
             norm_kernel,
-            (shape((blocks, SEQ, COLS)), shape((blocks + 2, SEQ, COLS)), shape((SEQ, 128), F32)),
+            (
+                shape((NX * NY, 256, COLS)),
+                shape((blocks + 2, SEQ, COLS)),
+                shape((SEQ, 128), F32),
+            ),
             (hidden_in, key_grad, gain),
             (any_,) * 3,
             (hbm, hbm, hbm),
@@ -381,8 +396,10 @@
                 pltpu.VMEM((blocks, SEQ, COLS), BF16),
                 pltpu.VMEM((blocks, SEQ, COLS), BF16),
                 pltpu.VMEM((SEQ, 128), F32),
+                pltpu.VMEM((blocks, NY, 128, COLS), BF16),
                 dma((NORM_PARTS + 2,)),
-                dma((2 * NORM_PARTS + 3,)),
+                dma((NORM_PARTS + 3,)),
+                dma((blocks, NY)),
             ],
             mib=None,
         )
@@ -392,15 +409,14 @@
         chunks = call(
             square_kernel,
             shape((NX * NY, 256, COLS)),
-            (own, other, key_grad),
-            (any_,) * 3,
+            (own, other),
+            (any_,) * 2,
             hbm,
             [
-                pltpu.VMEM((blocks, SEQ, COLS), BF16),
+                pltpu.VMEM((NX * NY, 256, COLS), BF16),
                 pltpu.VMEM((blocks + 2, SEQ, COLS), BF16),
-                pltpu.VMEM((SEQ, K), BF16),
                 pltpu.VMEM((blocks, NY, 128, COLS), BF16),
-                dma((10,)),
+                dma((9,)),
                 dma((blocks, NY)),
             ],
             mib=51,

time: 94.8 us -> 94.4 us (level)
  Pallas kernels: 18.7 us -> 20.9 us
  local copies, waits for them, and re-layouts: 2.41 us -> 0.72 us
    pallas_call x8, Pallas kernels: 18.7 us -> 20.9 us  [call(): pl.pallas_call(kernel, out_shape=outs, in_specs=[pl.BlockSpec(memory_spac...]
    unnamed x16 -> x12, local copies, waits for them, and re-layouts: 2.41 us -> 0.72 us
  transfers between devices with their start and end apart: 12 -> 12, of which waited for: 4 -> 3; matrix products, arithmetic and copies ran while one was open for 0% -> 0% of each run, Pallas kernels for 19% -> 22%
where the time goes in v11:
time: 94.4 us; the launch traced here: 92.8 us
  starting transfers between devices  60.3 us (64%)
  Pallas kernels  20.9 us (22%)
  waiting for transfers between devices  10 us (11%)
    pallas_call x8, Pallas kernels, call(): pl.pallas_call(kernel, out_shape=outs, in_specs=[pl.BlockSpec(memory_spac...  20.9 us
    ppermute x1, starting transfers between devices, body(): origin = lax.ppermute(key_weight, AXES, origins())  13.3 us
    all_to_all x2, starting transfers between devices, exchange(): lax.all_to_all(value, AXES, split_axis=0, concat_axis=0, axis_index_group...  11.8 us
    ppermute x3, starting transfers between devices, body(): lax.ppermute(origin, AXES, from_y(ahead))  10.7 us
    ppermute x1, waiting for transfers between devices, body(): down = lax.ppermute(near, AXES, from_z(-1))  7.97 us
    ppermute x1, starting transfers between devices, body(): up = lax.ppermute(near, AXES, from_z(1))  5.93 us
    ppermute x1, starting transfers between devices, body(): early = lax.ppermute(partner(other, near, up, down), AXES, CORE_SWAP)  5.71 us
    ppermute x1, starting transfers between devices, body(): far = lax.ppermute(now[0], AXES, two_away())  4.99 us
  transfers between devices with their start and end apart: 12, of which 3 were waited for; matrix products, arithmetic and copies ran while one was open for 0% of the time, Pallas kernels for 22%

profile of v11, /device:TPU:1, one launch (start us, length us, event | category | flops | bytes accessed | tf_op | source)
XLA Modules:
  0.0 92.8 jit_solution(15035128076017096434)
XLA Ops:
  0.6 13.3 %collective-permute-start = (bf16[128,512]{1,0:T(8,128)(2,1)}, bf16[128,512]{1,0:T(8,128)(2,1)S(1)}, u32[]{:S(2)}, u32[]{:S(2)}) collective-permute-start(bf16[128,512]{1,0:T(8,128)(2,1)} %param.7), channel_id=1, source_target_pairs={{0,0},{1,1},{2,2},{3,3},{4,4},{5,5},{6,6},{7,7},{8,8},{9,9},{10,10... | collective-permute-start | bytes 393224 | tf_op jit(solution)/shard_map/weight_z4/ppermute | solution.py:380
  13.9 3.9 %norm.1 = (bf16[16,256,256]{2,1,0:T(8,128)(2,1)}, bf16[10,256,256]{2,1,0:T(8,128)(2,1)}, f32[256,128]{1,0:T(8,128)}) custom-call(bf16[256,4096]{1,0:T(8,128)(2,1)} %hidden_hbm.3, bf16[256,512]{1,0:T(8,128)(2,1)} %key_hbm.3, f32[1,4096]{1,0:T(1,128)} %bitcast.3), custom_call_target="tpu_custom_call" | custom-call | bytes 150000 | tf_op jit(solution)/shard_map/norm/pallas_call | solution.py:86
  17.9 0.0 collective-permute-done.refs_0_
  17.9 1.9 %collective-permute-start.1 = (bf16[10,256,256]{2,1,0:T(8,128)(2,1)}, bf16[10,256,256]{2,1,0:T(8,128)(2,1)S(1)}, u32[]{:S(2)}, u32[]{:S(2)}) collective-permute-start(bf16[10,256,256]{2,1,0:T(8,128)(2,1)} %get-tuple-element.19), channel_id=1, source_target_pairs={{0,32},{1,33},{2,34},{3,35},{4,36},{5,37},{6,38},{7,39},{8,40},{9,... | collective-permute-start | bytes 3932168 | tf_op jit(solution)/shard_map/norm/ppermute | solution.py:407
  19.8 3.2 %collective-permute-start.4 = (bf16[128,512]{1,0:T(8,128)(2,1)S(1)}, bf16[128,512]{1,0:T(8,128)(2,1)S(1)}, u32[]{:S(2)}, u32[]{:S(2)}) collective-permute-start(bf16[128,512]{1,0:T(8,128)(2,1)S(1)} %collective-permute-done.refs_0_), channel_id=1, source_target_pairs={{24,0},{25,1},{26,2},{27,3},{28,4},{29,5},{30,6},{31,7},{0,8},{1,9... | collective-permute-start | bytes 393224 | tf_op jit(solution)/shard_map/weight_y/ppermute | solution.py:425
  23.0 4.5 %collective-permute-start.3 = (bf16[128,512]{1,0:T(8,128)(2,1)S(1)}, bf16[128,512]{1,0:T(8,128)(2,1)S(1)}, u32[]{:S(2)}, u32[]{:S(2)}) collective-permute-start(bf16[128,512]{1,0:T(8,128)(2,1)S(1)} %collective-permute-done.refs_0_), channel_id=1, source_target_pairs={{16,0},{17,1},{18,2},{19,3},{20,4},{21,5},{22,6},{23,7},{24,8},{25... | collective-permute-start | bytes 393224 | tf_op jit(solution)/shard_map/weight_y/ppermute | solution.py:425
  27.5 3.0 %collective-permute-start.2 = (bf16[128,512]{1,0:T(8,128)(2,1)S(1)}, bf16[128,512]{1,0:T(8,128)(2,1)S(1)}, u32[]{:S(2)}, u32[]{:S(2)}) collective-permute-start(bf16[128,512]{1,0:T(8,128)(2,1)S(1)} %collective-permute-done.refs_0_), channel_id=1, source_target_pairs={{8,0},{9,1},{10,2},{11,3},{12,4},{13,5},{14,6},{15,7},{16,8},{17,9... | collective-permute-start | bytes 393224 | tf_op jit(solution)/shard_map/weight_y/ppermute | solution.py:425
  30.5 0.0 collective-permute-done.1.other_hbm.key_hbm
  30.5 4.4 %squares.1 = bf16[16,256,256]{2,1,0:T(8,128)(2,1)} custom-call(bf16[16,256,256]{2,1,0:T(8,128)(2,1)} %get-tuple-element.17.own_hbm, bf16[10,256,256]{2,1,0:T(8,128)(2,1)S(1)} %collective-permute-done.1.other_hbm.key_hbm), custom_call_target="tpu_custom_call" | custom-call | bytes 150000 | tf_op jit(solution)/shard_map/squares/pallas_call | solution.py:86
  34.9 0.0 collective-permute-done.4.refs_3_
  35.0 0.0 collective-permute-done.3.refs_2_
  35.0 0.0 collective-permute-done.2.refs_1_
  35.0 4.6 %all-to-all-start = ((bf16[16,256,256]{2,1,0:T(8,128)(2,1)}), bf16[16,256,256]{2,1,0:T(8,128)(2,1)S(1)}, u32[]{:S(2)}, u32[]{:S(2)}) async-start(bf16[16,256,256]{2,1,0:T(8,128)(2,1)} %squares.1), calls=%async_computation | async-start | bytes 4194304 | tf_op jit(solution)/shard_map/plane/all_to_all | solution.py:80
  39.6 0.7 weight_y.1.refs_0_.weight_0
  40.3 1.9 %collective-permute-start.6 = (bf16[4,128,512]{2,1,0:T(8,128)(2,1)S(1)}, bf16[4,128,512]{2,1,0:T(8,128)(2,1)S(1)}, u32[]{:S(2)}, u32[]{:S(2)}) collective-permute-start(bf16[4,128,512]{2,1,0:T(8,128)(2,1)S(1)} %weight_y.1.refs_0_.weight_0), channel_id=1, source_target_pairs={{71,0},{0,1},{1,2},{2,3},{3,4},{4,5},{5,6},{6,7},{79,8},{8,9},{9,1... | collective-permute-start | bytes 1572872 | tf_op jit(solution)/shard_map/weight_z1/ppermute | solution.py:435
  42.2 5.9 %collective-permute-start.5 = (bf16[4,128,512]{2,1,0:T(8,128)(2,1)S(1)}, bf16[4,128,512]{2,1,0:T(8,128)(2,1)S(1)}, u32[]{:S(2)}, u32[]{:S(2)}) collective-permute-start(bf16[4,128,512]{2,1,0:T(8,128)(2,1)S(1)} %weight_y.1.refs_0_.weight_0), channel_id=1, source_target_pairs={{1,0},{2,1},{3,2},{4,3},{5,4},{6,5},{7,6},{64,7},{9,8},{10,9},{11,... | collective-permute-start | bytes 1572872 | tf_op jit(solution)/shard_map/weight_z1/ppermute | solution.py:434
  48.2 8.0 %collective-permute-done.6.refs_2_.weight_3 = bf16[4,128,512]{2,1,0:T(8,128)(2,1)S(1)} collective-permute-done((bf16[4,128,512]{2,1,0:T(8,128)(2,1)S(1)}, bf16[4,128,512]{2,1,0:T(8,128)(2,1)S(1)}, u32[]{:S(2)}, u32[]{:S(2)}) %collective-permute-start.6) | collective-permute-done | bytes 524320 | tf_op jit(solution)/shard_map/weight_z1/ppermute | solution.py:435
  56.1 0.9 collective-permute-done.5.refs_1_.weight_1
  57.0 5.0 %collective-permute-start.7 = (bf16[4,128,512]{2,1,0:T(8,128)(2,1)S(1)}, bf16[4,128,512]{2,1,0:T(8,128)(2,1)}, u32[]{:S(2)}, u32[]{:S(2)}) collective-permute-start(bf16[4,128,512]{2,1,0:T(8,128)(2,1)S(1)} %weight_y.1.refs_0_.weight_0), channel_id=1, source_target_pairs={{2,0},{71,1},{4,2},{1,3},{6,4},{3,5},{64,6},{5,7},{10,8},{79,9},{1... | collective-permute-start | bytes 1572872 | tf_op jit(solution)/shard_map/weight_z1/ppermute | solution.py:437
  62.0 2.8 %back_early.1 = bf16[6,256,256]{2,1,0:T(8,128)(2,1)} custom-call(bf16[10,256,256]{2,1,0:T(8,128)(2,1)} %copy-done, bf16[4,128,512]{2,1,0:T(8,128)(2,1)S(1)} %weight_y.1.refs_0_.weight_0, bf16[4,128,512]{2,1,0:T(8,128)(2,1)S(1)} %collective-permute-done.5.refs_1_.weight_1, bf16[4,128,512]{2,1,0:T(8,128)(2,1)S(1)} %collective-permute-done.6.refs_2_.weight_3), custom_call_target="tpu_custom_call" | custom-call | bytes 150000 | tf_op jit(solution)/shard_map/back_early/pallas_call | solution.py:86
  64.8 5.7 %collective-permute-start.8 = (bf16[6,256,256]{2,1,0:T(8,128)(2,1)}, bf16[6,256,256]{2,1,0:T(8,128)(2,1)}, u32[]{:S(2)}, u32[]{:S(2)}) collective-permute-start(bf16[6,256,256]{2,1,0:T(8,128)(2,1)} %back_early.1), channel_id=1, source_target_pairs={{0,32},{1,33},{2,34},{3,35},{4,36},{5,37},{6,38},{7,39},{8,40},{9,... | collective-permute-start | bytes 2359304 | tf_op jit(solution)/shard_map/back_early/ppermute | solution.py:439
  70.6 0.0 all-to-all-done.in_ref
  70.6 0.9 split.1
  71.5 7.3 %all-to-all-start.1 = ((bf16[16,16,256]{2,1,0:T(8,128)(2,1)}), bf16[16,16,256]{2,1,0:T(8,128)(2,1)S(1)}, u32[]{:S(2)}, u32[]{:S(2)}) async-start(bf16[16,16,256]{2,1,0:T(8,128)(2,1)} %split.1), calls=%async_computation.1 | async-start | bytes 262144 | tf_op jit(solution)/shard_map/ring_z/all_to_all | solution.py:80
  78.8 2.1 %back_late.1 = bf16[2,256,256]{2,1,0:T(8,128)(2,1)S(1)} custom-call(bf16[10,256,256]{2,1,0:T(8,128)(2,1)} %copy-done, bf16[4,128,512]{2,1,0:T(8,128)(2,1)} %collective-permute-done.7.refs_0_.weight_2), custom_call_target="tpu_custom_call" | custom-call | bytes 150000 | tf_op jit(solution)/shard_map/back_late/pallas_call | solution.py:86
  80.9 4.0 %collective-permute-start.9 = (bf16[2,256,256]{2,1,0:T(8,128)(2,1)S(1)}, bf16[2,256,256]{2,1,0:T(8,128)(2,1)S(1)}, u32[]{:S(2)}, u32[]{:S(2)}) collective-permute-start(bf16[2,256,256]{2,1,0:T(8,128)(2,1)S(1)} %back_late.1), channel_id=1, source_target_pairs={{0,32},{1,33},{2,34},{3,35},{4,36},{5,37},{6,38},{7,39},{8,40},{9,... | collective-permute-start | bytes 786440 | tf_op jit(solution)/shard_map/back_late/ppermute | solution.py:445
  84.9 1.1 %collective-permute-done.9.late_hbm = bf16[2,256,256]{2,1,0:T(8,128)(2,1)S(1)} collective-permute-done((bf16[2,256,256]{2,1,0:T(8,128)(2,1)S(1)}, bf16[2,256,256]{2,1,0:T(8,128)(2,1)S(1)}, u32[]{:S(2)}, u32[]{:S(2)}) %collective-permute-start.9) | collective-permute-done | bytes 262176 | tf_op jit(solution)/shard_map/back_late/ppermute | solution.py:445
  86.0 0.0 collective-permute-done.8.early_hbm
  86.0 0.7 copy-done.5
  86.7 5.2 %input_grad.1 = bf16[256,4096]{1,0:T(8,128)(2,1)} custom-call(bf16[256,4096]{1,0:T(8,128)(2,1)} %hidden_hbm.3, bf16[256,512]{1,0:T(8,128)(2,1)} %key_hbm.3, f32[1,4096]{1,0:T(1,128)} %bitcast.4, f32[256,128]{1,0:T(8,128)} %get-tuple-element.22.inv_hbm, bf16[4,128,512]{2,1,0:T(8,128)(2,1)} %copy-done.1, bf16[4,128,512]{2,1,0:T(8,128)(2,1)} %copy-done.3, ...), custom_call_target="tpu_custom_call" | custom-call | bytes 150000 | tf_op jit(solution)/shard_map/input_grad/pallas_call | solution.py:86
  91.9 0.0 all-to-all-done.1.in_ref
  92.0 0.8 serve.1
  (12 shorter events, 0.0 us)
Async XLA Ops:
  0.6 17.2 %collective-permute-start = (bf16[128,512]{1,0:T(8,128)(2,1)}, bf16[128,512]{1,0:T(8,128)(2,1)S(1)}, u32[]{:S(2)}, u32[]{:S(2)}) collective-permute-start(bf16[128,512]{1,0:T(8,128)(2,1)} %param.7), channel_id=1, source_target_pairs={{0,0},{1,1},{2,2},{3,3},{4,4},{5,5},{6,6},{7,7},{8,8},{9,9},{10,10... | collective-permute-start | bytes 393224 | tf_op jit(solution)/shard_map/weight_z4/ppermute | solution.py:380
  17.9 12.7 %collective-permute-start.1 = (bf16[10,256,256]{2,1,0:T(8,128)(2,1)}, bf16[10,256,256]{2,1,0:T(8,128)(2,1)S(1)}, u32[]{:S(2)}, u32[]{:S(2)}) collective-permute-start(bf16[10,256,256]{2,1,0:T(8,128)(2,1)} %get-tuple-element.19), channel_id=1, source_target_pairs={{0,32},{1,33},{2,34},{3,35},{4,36},{5,37},{6,38},{7,39},{8,40},{9,... | collective-permute-start | bytes 3932168 | tf_op jit(solution)/shard_map/norm/ppermute | solution.py:407
  19.8 15.2 %collective-permute-start.4 = (bf16[128,512]{1,0:T(8,128)(2,1)S(1)}, bf16[128,512]{1,0:T(8,128)(2,1)S(1)}, u32[]{:S(2)}, u32[]{:S(2)}) collective-permute-start(bf16[128,512]{1,0:T(8,128)(2,1)S(1)} %collective-permute-done.refs_0_), channel_id=1, source_target_pairs={{24,0},{25,1},{26,2},{27,3},{28,4},{29,5},{30,6},{31,7},{0,8},{1,9... | collective-permute-start | bytes 393224 | tf_op jit(solution)/shard_map/weight_y/ppermute | solution.py:425
  23.0 12.0 %collective-permute-start.3 = (bf16[128,512]{1,0:T(8,128)(2,1)S(1)}, bf16[128,512]{1,0:T(8,128)(2,1)S(1)}, u32[]{:S(2)}, u32[]{:S(2)}) collective-permute-start(bf16[128,512]{1,0:T(8,128)(2,1)S(1)} %collective-permute-done.refs_0_), channel_id=1, source_target_pairs={{16,0},{17,1},{18,2},{19,3},{20,4},{21,5},{22,6},{23,7},{24,8},{25... | collective-permute-start | bytes 393224 | tf_op jit(solution)/shard_map/weight_y/ppermute | solution.py:425
  27.5 7.4 %collective-permute-start.2 = (bf16[128,512]{1,0:T(8,128)(2,1)S(1)}, bf16[128,512]{1,0:T(8,128)(2,1)S(1)}, u32[]{:S(2)}, u32[]{:S(2)}) collective-permute-start(bf16[128,512]{1,0:T(8,128)(2,1)S(1)} %collective-permute-done.refs_0_), channel_id=1, source_target_pairs={{8,0},{9,1},{10,2},{11,3},{12,4},{13,5},{14,6},{15,7},{16,8},{17,9... | collective-permute-start | bytes 393224 | tf_op jit(solution)/shard_map/weight_y/ppermute | solution.py:425
  30.5 4.4 %copy-start = (bf16[10,256,256]{2,1,0:T(8,128)(2,1)}, bf16[10,256,256]{2,1,0:T(8,128)(2,1)S(1)}, u32[]{:S(2)}) copy-start(bf16[10,256,256]{2,1,0:T(8,128)(2,1)S(1)} %collective-permute-done.1.other_hbm.key_hbm) | copy-start | bytes 3932164
  35.0 35.6 %all-to-all-start = ((bf16[16,256,256]{2,1,0:T(8,128)(2,1)}), bf16[16,256,256]{2,1,0:T(8,128)(2,1)S(1)}, u32[]{:S(2)}, u32[]{:S(2)}) async-start(bf16[16,256,256]{2,1,0:T(8,128)(2,1)} %squares.1), calls=%async_computation | async-start | bytes 4194304 | tf_op jit(solution)/shard_map/plane/all_to_all | solution.py:80
  40.3 31.2 %copy-start.1 = (bf16[4,128,512]{2,1,0:T(8,128)(2,1)}, bf16[4,128,512]{2,1,0:T(8,128)(2,1)S(1)}, u32[]{:S(2)}) copy-start(bf16[4,128,512]{2,1,0:T(8,128)(2,1)S(1)} %weight_y.1.refs_0_.weight_0) | copy-start | bytes 1572868
  40.3 15.8 %collective-permute-start.6 = (bf16[4,128,512]{2,1,0:T(8,128)(2,1)S(1)}, bf16[4,128,512]{2,1,0:T(8,128)(2,1)S(1)}, u32[]{:S(2)}, u32[]{:S(2)}) collective-permute-start(bf16[4,128,512]{2,1,0:T(8,128)(2,1)S(1)} %weight_y.1.refs_0_.weight_0), channel_id=1, source_target_pairs={{71,0},{0,1},{1,2},{2,3},{3,4},{4,5},{5,6},{6,7},{79,8},{8,9},{9,1... | collective-permute-start | bytes 1572872 | tf_op jit(solution)/shard_map/weight_z1/ppermute | solution.py:435
  42.2 14.8 %collective-permute-start.5 = (bf16[4,128,512]{2,1,0:T(8,128)(2,1)S(1)}, bf16[4,128,512]{2,1,0:T(8,128)(2,1)S(1)}, u32[]{:S(2)}, u32[]{:S(2)}) collective-permute-start(bf16[4,128,512]{2,1,0:T(8,128)(2,1)S(1)} %weight_y.1.refs_0_.weight_0), channel_id=1, source_target_pairs={{1,0},{2,1},{3,2},{4,3},{5,4},{6,5},{7,6},{64,7},{9,8},{10,9},{11,... | collective-permute-start | bytes 1572872 | tf_op jit(solution)/shard_map/weight_z1/ppermute | solution.py:434
  56.1 15.4 %copy-start.2 = (bf16[4,128,512]{2,1,0:T(8,128)(2,1)}, bf16[4,128,512]{2,1,0:T(8,128)(2,1)S(1)}, u32[]{:S(2)}) copy-start(bf16[4,128,512]{2,1,0:T(8,128)(2,1)S(1)} %collective-permute-done.6.refs_2_.weight_3) | copy-start | bytes 1572868
  57.0 7.8 %copy-start.3 = (bf16[4,128,512]{2,1,0:T(8,128)(2,1)}, bf16[4,128,512]{2,1,0:T(8,128)(2,1)S(1)}, u32[]{:S(2)}) copy-start(bf16[4,128,512]{2,1,0:T(8,128)(2,1)S(1)} %collective-permute-done.5.refs_1_.weight_1) | copy-start | bytes 1572868
  57.0 21.7 %collective-permute-start.7 = (bf16[4,128,512]{2,1,0:T(8,128)(2,1)S(1)}, bf16[4,128,512]{2,1,0:T(8,128)(2,1)}, u32[]{:S(2)}, u32[]{:S(2)}) collective-permute-start(bf16[4,128,512]{2,1,0:T(8,128)(2,1)S(1)} %weight_y.1.refs_0_.weight_0), channel_id=1, source_target_pairs={{2,0},{71,1},{4,2},{1,3},{6,4},{3,5},{64,6},{5,7},{10,8},{79,9},{1... | collective-permute-start | bytes 1572872 | tf_op jit(solution)/shard_map/weight_z1/ppermute | solution.py:437
  64.8 21.2 %collective-permute-start.8 = (bf16[6,256,256]{2,1,0:T(8,128)(2,1)}, bf16[6,256,256]{2,1,0:T(8,128)(2,1)}, u32[]{:S(2)}, u32[]{:S(2)}) collective-permute-start(bf16[6,256,256]{2,1,0:T(8,128)(2,1)} %back_early.1), channel_id=1, source_target_pairs={{0,32},{1,33},{2,34},{3,35},{4,36},{5,37},{6,38},{7,39},{8,40},{9,... | collective-permute-start | bytes 2359304 | tf_op jit(solution)/shard_map/back_early/ppermute | solution.py:439
  71.5 20.4 %all-to-all-start.1 = ((bf16[16,16,256]{2,1,0:T(8,128)(2,1)}), bf16[16,16,256]{2,1,0:T(8,128)(2,1)S(1)}, u32[]{:S(2)}, u32[]{:S(2)}) async-start(bf16[16,16,256]{2,1,0:T(8,128)(2,1)} %split.1), calls=%async_computation.1 | async-start | bytes 262144 | tf_op jit(solution)/shard_map/ring_z/all_to_all | solution.py:80
  80.9 5.1 %collective-permute-start.9 = (bf16[2,256,256]{2,1,0:T(8,128)(2,1)S(1)}, bf16[2,256,256]{2,1,0:T(8,128)(2,1)S(1)}, u32[]{:S(2)}, u32[]{:S(2)}) collective-permute-start(bf16[2,256,256]{2,1,0:T(8,128)(2,1)S(1)} %back_late.1), channel_id=1, source_target_pairs={{0,32},{1,33},{2,34},{3,35},{4,36},{5,37},{6,38},{7,39},{8,40},{9,... | collective-permute-start | bytes 786440 | tf_op jit(solution)/shard_map/back_late/ppermute | solution.py:445
  86.0 0.7 copy-start.5
  86.7 5.2 %copy-start.4 = (s32[512]{0:T(512)S(1)}, s32[512]{0:T(512)}, u32[]{:S(2)}) copy-start(s32[512]{0:T(512)} %param.9) | copy-start | bytes 6148

commit v12 on v11

--- a/solution.py
+++ b/solution.py
@@ -229,27 +229,20 @@
 
 
 def square_kernel(
-    own_hbm, other_hbm, out_hbm, own_ref, other_ref, out_ref, in_sems, out_sems
+    own_hbm, other_ref, out_hbm, own_ref, out_ref, in_sems, out_sems
 ):
     blocks = NX * NZH
-    keys = start(other_hbm.at[pl.ds(blocks, 2)], other_ref.at[pl.ds(blocks, 2)], in_sems.at[0])
     copies = []
     for x in range(NX):
-        some, chunks = pl.ds(NZH * x, NZH), pl.ds(NY * x, NY)
-        copies += [
-            start(other_hbm.at[some], other_ref.at[some], in_sems.at[1 + 2 * x]),
-            start(own_hbm.at[chunks], own_ref.at[chunks], in_sems.at[2 + 2 * x]),
-        ]
-    keys.wait()
+        chunks = pl.ds(NY * x, NY)
+        copies.append(start(own_hbm.at[chunks], own_ref.at[chunks], in_sems.at[x]))
     key_other = jnp.concatenate([other_ref[blocks], other_ref[blocks + 1]], axis=1)
     out_copies = []
     for k in range(blocks):
         x, zh = k // NZH, k % NZH
-        if zh == 0:
-            copies[2 * x].wait()
         grad = lax.dot_general(other_ref[k], key_other, OVER_TOKENS, preferred_element_type=F32)
         if zh == 0:
-            copies[2 * x + 1].wait()
+            copies[x].wait()
         own = [own_ref[x * NY + y, zh * 128 : (zh + 1) * 128, :] for y in range(NY)]
         own = jnp.concatenate(
             [jnp.concatenate([part[0:64], part[64:128]], axis=1) for part in own], axis=0
@@ -410,13 +403,12 @@
             square_kernel,
             shape((NX * NY, 256, COLS)),
             (own, other),
-            (any_,) * 2,
+            (any_, vmem),
             hbm,
             [
                 pltpu.VMEM((NX * NY, 256, COLS), BF16),
-                pltpu.VMEM((blocks + 2, SEQ, COLS), BF16),
                 pltpu.VMEM((blocks, NY, 128, COLS), BF16),
-                dma((9,)),
+                dma((NX,)),
                 dma((blocks, NY)),
             ],
             mib=51,

time: 94.4 us -> 94.4 us (level)
  transfers between devices with their start and end apart: 12 -> 12, of which waited for: 3 -> 3; matrix products, arithmetic and copies ran while one was open for 0% -> 0% of each run, Pallas kernels for 22% -> 21%
where the time goes in v12:
time: 94.4 us; the launch traced here: 92.8 us
  starting transfers between devices  60.9 us (65%)
  Pallas kernels  20.3 us (22%)
  waiting for transfers between devices  10 us (11%)
    pallas_call x8, Pallas kernels, call(): pl.pallas_call(kernel, out_shape=outs, in_specs=[pl.BlockSpec(memory_spac...  20.3 us
    ppermute x1, starting transfers between devices, body(): origin = lax.ppermute(key_weight, AXES, origins())  13.3 us
    all_to_all x2, starting transfers between devices, exchange(): lax.all_to_all(value, AXES, split_axis=0, concat_axis=0, axis_index_group...  12.5 us
    ppermute x3, starting transfers between devices, body(): lax.ppermute(origin, AXES, from_y(ahead))  10.7 us
    ppermute x1, waiting for transfers between devices, body(): down = lax.ppermute(near, AXES, from_z(-1))  7.97 us
    ppermute x1, starting transfers between devices, body(): up = lax.ppermute(near, AXES, from_z(1))  5.93 us
    ppermute x1, starting transfers between devices, body(): early = lax.ppermute(partner(other, near, up, down), AXES, CORE_SWAP)  5.71 us
    ppermute x1, starting transfers between devices, body(): far = lax.ppermute(now[0], AXES, two_away())  4.99 us
  transfers between devices with their start and end apart: 12, of which 3 were waited for; matrix products, arithmetic and copies ran while one was open for 0% of the time, Pallas kernels for 21%

profile of v12, /device:TPU:1, one launch (start us, length us, event | category | flops | bytes accessed | tf_op | source)
XLA Modules:
  0.0 92.8 jit_solution(849444903225501092)
XLA Ops:
  0.6 13.3 %collective-permute-start = (bf16[128,512]{1,0:T(8,128)(2,1)}, bf16[128,512]{1,0:T(8,128)(2,1)S(1)}, u32[]{:S(2)}, u32[]{:S(2)}) collective-permute-start(bf16[128,512]{1,0:T(8,128)(2,1)} %param.7), channel_id=1, source_target_pairs={{0,0},{1,1},{2,2},{3,3},{4,4},{5,5},{6,6},{7,7},{8,8},{9,9},{10,10... | collective-permute-start | bytes 393224 | tf_op jit(solution)/shard_map/weight_z4/ppermute | solution.py:373
  13.9 3.9 %norm.1 = (bf16[16,256,256]{2,1,0:T(8,128)(2,1)}, bf16[10,256,256]{2,1,0:T(8,128)(2,1)}, f32[256,128]{1,0:T(8,128)}) custom-call(bf16[256,4096]{1,0:T(8,128)(2,1)} %hidden_hbm.3, bf16[256,512]{1,0:T(8,128)(2,1)} %key_hbm.3, f32[1,4096]{1,0:T(1,128)} %bitcast.3), custom_call_target="tpu_custom_call" | custom-call | bytes 150000 | tf_op jit(solution)/shard_map/norm/pallas_call | solution.py:86
  17.9 0.0 collective-permute-done.refs_0_
  17.9 1.9 %collective-permute-start.1 = (bf16[10,256,256]{2,1,0:T(8,128)(2,1)}, bf16[10,256,256]{2,1,0:T(8,128)(2,1)S(1)}, u32[]{:S(2)}, u32[]{:S(2)}) collective-permute-start(bf16[10,256,256]{2,1,0:T(8,128)(2,1)} %get-tuple-element.19), channel_id=1, source_target_pairs={{0,32},{1,33},{2,34},{3,35},{4,36},{5,37},{6,38},{7,39},{8,40},{9,... | collective-permute-start | bytes 3932168 | tf_op jit(solution)/shard_map/norm/ppermute | solution.py:400
  19.8 3.2 %collective-permute-start.4 = (bf16[128,512]{1,0:T(8,128)(2,1)S(1)}, bf16[128,512]{1,0:T(8,128)(2,1)S(1)}, u32[]{:S(2)}, u32[]{:S(2)}) collective-permute-start(bf16[128,512]{1,0:T(8,128)(2,1)S(1)} %collective-permute-done.refs_0_), channel_id=1, source_target_pairs={{24,0},{25,1},{26,2},{27,3},{28,4},{29,5},{30,6},{31,7},{0,8},{1,9... | collective-permute-start | bytes 393224 | tf_op jit(solution)/shard_map/weight_y/ppermute | solution.py:417
  23.0 4.5 %collective-permute-start.3 = (bf16[128,512]{1,0:T(8,128)(2,1)S(1)}, bf16[128,512]{1,0:T(8,128)(2,1)S(1)}, u32[]{:S(2)}, u32[]{:S(2)}) collective-permute-start(bf16[128,512]{1,0:T(8,128)(2,1)S(1)} %collective-permute-done.refs_0_), channel_id=1, source_target_pairs={{16,0},{17,1},{18,2},{19,3},{20,4},{21,5},{22,6},{23,7},{24,8},{25... | collective-permute-start | bytes 393224 | tf_op jit(solution)/shard_map/weight_y/ppermute | solution.py:417
  27.5 3.0 %collective-permute-start.2 = (bf16[128,512]{1,0:T(8,128)(2,1)S(1)}, bf16[128,512]{1,0:T(8,128)(2,1)S(1)}, u32[]{:S(2)}, u32[]{:S(2)}) collective-permute-start(bf16[128,512]{1,0:T(8,128)(2,1)S(1)} %collective-permute-done.refs_0_), channel_id=1, source_target_pairs={{8,0},{9,1},{10,2},{11,3},{12,4},{13,5},{14,6},{15,7},{16,8},{17,9... | collective-permute-start | bytes 393224 | tf_op jit(solution)/shard_map/weight_y/ppermute | solution.py:417
  30.5 0.0 collective-permute-done.1.other_ref.key_hbm
  30.5 3.8 %squares.1 = bf16[16,256,256]{2,1,0:T(8,128)(2,1)} custom-call(bf16[16,256,256]{2,1,0:T(8,128)(2,1)} %get-tuple-element.17.own_hbm, bf16[10,256,256]{2,1,0:T(8,128)(2,1)S(1)} %collective-permute-done.1.other_ref.key_hbm), custom_call_target="tpu_custom_call" | custom-call | bytes 150000 | tf_op jit(solution)/shard_map/squares/pallas_call | solution.py:86
  34.3 0.0 collective-permute-done.4.refs_3_
  34.3 0.0 collective-permute-done.3.refs_2_
  34.3 0.0 collective-permute-done.2.refs_1_
  34.3 5.2 %all-to-all-start = ((bf16[16,256,256]{2,1,0:T(8,128)(2,1)}), bf16[16,256,256]{2,1,0:T(8,128)(2,1)S(1)}, u32[]{:S(2)}, u32[]{:S(2)}) async-start(bf16[16,256,256]{2,1,0:T(8,128)(2,1)} %squares.1), calls=%async_computation | async-start | bytes 4194304 | tf_op jit(solution)/shard_map/plane/all_to_all | solution.py:80
  39.6 0.7 weight_y.1.refs_0_.weight_0
  40.3 1.9 %collective-permute-start.6 = (bf16[4,128,512]{2,1,0:T(8,128)(2,1)S(1)}, bf16[4,128,512]{2,1,0:T(8,128)(2,1)S(1)}, u32[]{:S(2)}, u32[]{:S(2)}) collective-permute-start(bf16[4,128,512]{2,1,0:T(8,128)(2,1)S(1)} %weight_y.1.refs_0_.weight_0), channel_id=1, source_target_pairs={{71,0},{0,1},{1,2},{2,3},{3,4},{4,5},{5,6},{6,7},{79,8},{8,9},{9,1... | collective-permute-start | bytes 1572872 | tf_op jit(solution)/shard_map/weight_z1/ppermute | solution.py:427
  42.2 5.9 %collective-permute-start.5 = (bf16[4,128,512]{2,1,0:T(8,128)(2,1)S(1)}, bf16[4,128,512]{2,1,0:T(8,128)(2,1)S(1)}, u32[]{:S(2)}, u32[]{:S(2)}) collective-permute-start(bf16[4,128,512]{2,1,0:T(8,128)(2,1)S(1)} %weight_y.1.refs_0_.weight_0), channel_id=1, source_target_pairs={{1,0},{2,1},{3,2},{4,3},{5,4},{6,5},{7,6},{64,7},{9,8},{10,9},{11,... | collective-permute-start | bytes 1572872 | tf_op jit(solution)/shard_map/weight_z1/ppermute | solution.py:426
  48.2 8.0 %collective-permute-done.6.refs_2_.weight_3 = bf16[4,128,512]{2,1,0:T(8,128)(2,1)S(1)} collective-permute-done((bf16[4,128,512]{2,1,0:T(8,128)(2,1)S(1)}, bf16[4,128,512]{2,1,0:T(8,128)(2,1)S(1)}, u32[]{:S(2)}, u32[]{:S(2)}) %collective-permute-start.6) | collective-permute-done | bytes 524320 | tf_op jit(solution)/shard_map/weight_z1/ppermute | solution.py:427
  56.1 0.9 collective-permute-done.5.refs_1_.weight_1
  57.0 5.0 %collective-permute-start.7 = (bf16[4,128,512]{2,1,0:T(8,128)(2,1)S(1)}, bf16[4,128,512]{2,1,0:T(8,128)(2,1)}, u32[]{:S(2)}, u32[]{:S(2)}) collective-permute-start(bf16[4,128,512]{2,1,0:T(8,128)(2,1)S(1)} %weight_y.1.refs_0_.weight_0), channel_id=1, source_target_pairs={{2,0},{71,1},{4,2},{1,3},{6,4},{3,5},{64,6},{5,7},{10,8},{79,9},{1... | collective-permute-start | bytes 1572872 | tf_op jit(solution)/shard_map/weight_z1/ppermute | solution.py:429
  62.0 2.8 %back_early.1 = bf16[6,256,256]{2,1,0:T(8,128)(2,1)} custom-call(bf16[10,256,256]{2,1,0:T(8,128)(2,1)} %copy-done, bf16[4,128,512]{2,1,0:T(8,128)(2,1)S(1)} %weight_y.1.refs_0_.weight_0, bf16[4,128,512]{2,1,0:T(8,128)(2,1)S(1)} %collective-permute-done.5.refs_1_.weight_1, bf16[4,128,512]{2,1,0:T(8,128)(2,1)S(1)} %collective-permute-done.6.refs_2_.weight_3), custom_call_target="tpu_custom_call" | custom-call | bytes 150000 | tf_op jit(solution)/shard_map/back_early/pallas_call | solution.py:86
  64.8 5.7 %collective-permute-start.8 = (bf16[6,256,256]{2,1,0:T(8,128)(2,1)}, bf16[6,256,256]{2,1,0:T(8,128)(2,1)}, u32[]{:S(2)}, u32[]{:S(2)}) collective-permute-start(bf16[6,256,256]{2,1,0:T(8,128)(2,1)} %back_early.1), channel_id=1, source_target_pairs={{0,32},{1,33},{2,34},{3,35},{4,36},{5,37},{6,38},{7,39},{8,40},{9,... | collective-permute-start | bytes 2359304 | tf_op jit(solution)/shard_map/back_early/ppermute | solution.py:431
  70.6 0.0 all-to-all-done.in_ref
  70.6 0.9 split.1
  71.5 7.3 %all-to-all-start.1 = ((bf16[16,16,256]{2,1,0:T(8,128)(2,1)}), bf16[16,16,256]{2,1,0:T(8,128)(2,1)S(1)}, u32[]{:S(2)}, u32[]{:S(2)}) async-start(bf16[16,16,256]{2,1,0:T(8,128)(2,1)} %split.1), calls=%async_computation.1 | async-start | bytes 262144 | tf_op jit(solution)/shard_map/ring_z/all_to_all | solution.py:80
  78.8 0.0 collective-permute-done.7.refs_0_.weight_2
  78.8 2.1 %back_late.1 = bf16[2,256,256]{2,1,0:T(8,128)(2,1)S(1)} custom-call(bf16[10,256,256]{2,1,0:T(8,128)(2,1)} %copy-done, bf16[4,128,512]{2,1,0:T(8,128)(2,1)} %collective-permute-done.7.refs_0_.weight_2), custom_call_target="tpu_custom_call" | custom-call | bytes 150000 | tf_op jit(solution)/shard_map/back_late/pallas_call | solution.py:86
  80.9 4.0 %collective-permute-start.9 = (bf16[2,256,256]{2,1,0:T(8,128)(2,1)S(1)}, bf16[2,256,256]{2,1,0:T(8,128)(2,1)S(1)}, u32[]{:S(2)}, u32[]{:S(2)}) collective-permute-start(bf16[2,256,256]{2,1,0:T(8,128)(2,1)S(1)} %back_late.1), channel_id=1, source_target_pairs={{0,32},{1,33},{2,34},{3,35},{4,36},{5,37},{6,38},{7,39},{8,40},{9,... | collective-permute-start | bytes 786440 | tf_op jit(solution)/shard_map/back_late/ppermute | solution.py:437
  84.9 1.1 %collective-permute-done.9.late_hbm = bf16[2,256,256]{2,1,0:T(8,128)(2,1)S(1)} collective-permute-done((bf16[2,256,256]{2,1,0:T(8,128)(2,1)S(1)}, bf16[2,256,256]{2,1,0:T(8,128)(2,1)S(1)}, u32[]{:S(2)}, u32[]{:S(2)}) %collective-permute-start.9) | collective-permute-done | bytes 262176 | tf_op jit(solution)/shard_map/back_late/ppermute | solution.py:437
  86.0 0.0 collective-permute-done.8.early_hbm
  86.0 0.7 copy-done.5
  86.7 5.2 %input_grad.1 = bf16[256,4096]{1,0:T(8,128)(2,1)} custom-call(bf16[256,4096]{1,0:T(8,128)(2,1)} %hidden_hbm.3, bf16[256,512]{1,0:T(8,128)(2,1)} %key_hbm.3, f32[1,4096]{1,0:T(1,128)} %bitcast.4, f32[256,128]{1,0:T(8,128)} %get-tuple-element.22.inv_hbm, bf16[4,128,512]{2,1,0:T(8,128)(2,1)} %copy-done.1, bf16[4,128,512]{2,1,0:T(8,128)(2,1)} %copy-done.3, ...), custom_call_target="tpu_custom_call" | custom-call | bytes 150000 | tf_op jit(solution)/shard_map/input_grad/pallas_call | solution.py:86
  92.0 0.8 serve.1
  (12 shorter events, 0.0 us)
Async XLA Ops:
  0.6 17.2 %collective-permute-start = (bf16[128,512]{1,0:T(8,128)(2,1)}, bf16[128,512]{1,0:T(8,128)(2,1)S(1)}, u32[]{:S(2)}, u32[]{:S(2)}) collective-permute-start(bf16[128,512]{1,0:T(8,128)(2,1)} %param.7), channel_id=1, source_target_pairs={{0,0},{1,1},{2,2},{3,3},{4,4},{5,5},{6,6},{7,7},{8,8},{9,9},{10,10... | collective-permute-start | bytes 393224 | tf_op jit(solution)/shard_map/weight_z4/ppermute | solution.py:373
  17.9 12.7 %collective-permute-start.1 = (bf16[10,256,256]{2,1,0:T(8,128)(2,1)}, bf16[10,256,256]{2,1,0:T(8,128)(2,1)S(1)}, u32[]{:S(2)}, u32[]{:S(2)}) collective-permute-start(bf16[10,256,256]{2,1,0:T(8,128)(2,1)} %get-tuple-element.19), channel_id=1, source_target_pairs={{0,32},{1,33},{2,34},{3,35},{4,36},{5,37},{6,38},{7,39},{8,40},{9,... | collective-permute-start | bytes 3932168 | tf_op jit(solution)/shard_map/norm/ppermute | solution.py:400
  19.8 14.5 %collective-permute-start.4 = (bf16[128,512]{1,0:T(8,128)(2,1)S(1)}, bf16[128,512]{1,0:T(8,128)(2,1)S(1)}, u32[]{:S(2)}, u32[]{:S(2)}) collective-permute-start(bf16[128,512]{1,0:T(8,128)(2,1)S(1)} %collective-permute-done.refs_0_), channel_id=1, source_target_pairs={{24,0},{25,1},{26,2},{27,3},{28,4},{29,5},{30,6},{31,7},{0,8},{1,9... | collective-permute-start | bytes 393224 | tf_op jit(solution)/shard_map/weight_y/ppermute | solution.py:417
  23.0 11.3 %collective-permute-start.3 = (bf16[128,512]{1,0:T(8,128)(2,1)S(1)}, bf16[128,512]{1,0:T(8,128)(2,1)S(1)}, u32[]{:S(2)}, u32[]{:S(2)}) collective-permute-start(bf16[128,512]{1,0:T(8,128)(2,1)S(1)} %collective-permute-done.refs_0_), channel_id=1, source_target_pairs={{16,0},{17,1},{18,2},{19,3},{20,4},{21,5},{22,6},{23,7},{24,8},{25... | collective-permute-start | bytes 393224 | tf_op jit(solution)/shard_map/weight_y/ppermute | solution.py:417
  27.5 6.8 %collective-permute-start.2 = (bf16[128,512]{1,0:T(8,128)(2,1)S(1)}, bf16[128,512]{1,0:T(8,128)(2,1)S(1)}, u32[]{:S(2)}, u32[]{:S(2)}) collective-permute-start(bf16[128,512]{1,0:T(8,128)(2,1)S(1)} %collective-permute-done.refs_0_), channel_id=1, source_target_pairs={{8,0},{9,1},{10,2},{11,3},{12,4},{13,5},{14,6},{15,7},{16,8},{17,9... | collective-permute-start | bytes 393224 | tf_op jit(solution)/shard_map/weight_y/ppermute | solution.py:417
  30.5 3.8 %copy-start = (bf16[10,256,256]{2,1,0:T(8,128)(2,1)}, bf16[10,256,256]{2,1,0:T(8,128)(2,1)S(1)}, u32[]{:S(2)}) copy-start(bf16[10,256,256]{2,1,0:T(8,128)(2,1)S(1)} %collective-permute-done.1.other_ref.key_hbm) | copy-start | bytes 3932164
  34.3 36.2 %all-to-all-start = ((bf16[16,256,256]{2,1,0:T(8,128)(2,1)}), bf16[16,256,256]{2,1,0:T(8,128)(2,1)S(1)}, u32[]{:S(2)}, u32[]{:S(2)}) async-start(bf16[16,256,256]{2,1,0:T(8,128)(2,1)} %squares.1), calls=%async_computation | async-start | bytes 4194304 | tf_op jit(solution)/shard_map/plane/all_to_all | solution.py:80
  40.3 31.2 %copy-start.1 = (bf16[4,128,512]{2,1,0:T(8,128)(2,1)}, bf16[4,128,512]{2,1,0:T(8,128)(2,1)S(1)}, u32[]{:S(2)}) copy-start(bf16[4,128,512]{2,1,0:T(8,128)(2,1)S(1)} %weight_y.1.refs_0_.weight_0) | copy-start | bytes 1572868
  40.3 15.8 %collective-permute-start.6 = (bf16[4,128,512]{2,1,0:T(8,128)(2,1)S(1)}, bf16[4,128,512]{2,1,0:T(8,128)(2,1)S(1)}, u32[]{:S(2)}, u32[]{:S(2)}) collective-permute-start(bf16[4,128,512]{2,1,0:T(8,128)(2,1)S(1)} %weight_y.1.refs_0_.weight_0), channel_id=1, source_target_pairs={{71,0},{0,1},{1,2},{2,3},{3,4},{4,5},{5,6},{6,7},{79,8},{8,9},{9,1... | collective-permute-start | bytes 1572872 | tf_op jit(solution)/shard_map/weight_z1/ppermute | solution.py:427
  42.2 14.8 %collective-permute-start.5 = (bf16[4,128,512]{2,1,0:T(8,128)(2,1)S(1)}, bf16[4,128,512]{2,1,0:T(8,128)(2,1)S(1)}, u32[]{:S(2)}, u32[]{:S(2)}) collective-permute-start(bf16[4,128,512]{2,1,0:T(8,128)(2,1)S(1)} %weight_y.1.refs_0_.weight_0), channel_id=1, source_target_pairs={{1,0},{2,1},{3,2},{4,3},{5,4},{6,5},{7,6},{64,7},{9,8},{10,9},{11,... | collective-permute-start | bytes 1572872 | tf_op jit(solution)/shard_map/weight_z1/ppermute | solution.py:426
  56.1 15.4 %copy-start.2 = (bf16[4,128,512]{2,1,0:T(8,128)(2,1)}, bf16[4,128,512]{2,1,0:T(8,128)(2,1)S(1)}, u32[]{:S(2)}) copy-start(bf16[4,128,512]{2,1,0:T(8,128)(2,1)S(1)} %collective-permute-done.6.refs_2_.weight_3) | copy-start | bytes 1572868
  57.0 7.8 %copy-start.3 = (bf16[4,128,512]{2,1,0:T(8,128)(2,1)}, bf16[4,128,512]{2,1,0:T(8,128)(2,1)S(1)}, u32[]{:S(2)}) copy-start(bf16[4,128,512]{2,1,0:T(8,128)(2,1)S(1)} %collective-permute-done.5.refs_1_.weight_1) | copy-start | bytes 1572868
  57.0 21.7 %collective-permute-start.7 = (bf16[4,128,512]{2,1,0:T(8,128)(2,1)S(1)}, bf16[4,128,512]{2,1,0:T(8,128)(2,1)}, u32[]{:S(2)}, u32[]{:S(2)}) collective-permute-start(bf16[4,128,512]{2,1,0:T(8,128)(2,1)S(1)} %weight_y.1.refs_0_.weight_0), channel_id=1, source_target_pairs={{2,0},{71,1},{4,2},{1,3},{6,4},{3,5},{64,6},{5,7},{10,8},{79,9},{1... | collective-permute-start | bytes 1572872 | tf_op jit(solution)/shard_map/weight_z1/ppermute | solution.py:429
  64.8 21.2 %collective-permute-start.8 = (bf16[6,256,256]{2,1,0:T(8,128)(2,1)}, bf16[6,256,256]{2,1,0:T(8,128)(2,1)}, u32[]{:S(2)}, u32[]{:S(2)}) collective-permute-start(bf16[6,256,256]{2,1,0:T(8,128)(2,1)} %back_early.1), channel_id=1, source_target_pairs={{0,32},{1,33},{2,34},{3,35},{4,36},{5,37},{6,38},{7,39},{8,40},{9,... | collective-permute-start | bytes 2359304 | tf_op jit(solution)/shard_map/back_early/ppermute | solution.py:431
  71.5 20.4 %all-to-all-start.1 = ((bf16[16,16,256]{2,1,0:T(8,128)(2,1)}), bf16[16,16,256]{2,1,0:T(8,128)(2,1)S(1)}, u32[]{:S(2)}, u32[]{:S(2)}) async-start(bf16[16,16,256]{2,1,0:T(8,128)(2,1)} %split.1), calls=%async_computation.1 | async-start | bytes 262144 | tf_op jit(solution)/shard_map/ring_z/all_to_all | solution.py:80
  80.9 5.1 %collective-permute-start.9 = (bf16[2,256,256]{2,1,0:T(8,128)(2,1)S(1)}, bf16[2,256,256]{2,1,0:T(8,128)(2,1)S(1)}, u32[]{:S(2)}, u32[]{:S(2)}) collective-permute-start(bf16[2,256,256]{2,1,0:T(8,128)(2,1)S(1)} %back_late.1), channel_id=1, source_target_pairs={{0,32},{1,33},{2,34},{3,35},{4,36},{5,37},{6,38},{7,39},{8,40},{9,... | collective-permute-start | bytes 786440 | tf_op jit(solution)/shard_map/back_late/ppermute | solution.py:437
  86.0 0.7 copy-start.5
  86.7 5.2 %copy-start.4 = (s32[512]{0:T(512)S(1)}, s32[512]{0:T(512)}, u32[]{:S(2)}) copy-start(s32[512]{0:T(512)} %param.9) | copy-start | bytes 6148

commit v13 on v12

--- a/solution.py
+++ b/solution.py
@@ -425,10 +425,11 @@
     with jax.named_scope("weight_z1"):
         up = lax.ppermute(near, AXES, from_z(1))
         down = lax.ppermute(near, AXES, from_z(-1))
-        *now, up, down = barrier((near, up, down))
-        far = lax.ppermute(now[0], AXES, two_away())
+        products = partner(other, near, up, down)
+        now, products = barrier((near, products))
+        far = lax.ppermute(now, AXES, two_away())
     with jax.named_scope("back_early"):
-        early = lax.ppermute(partner(other, near, up, down), AXES, CORE_SWAP)
+        early = lax.ppermute(products, AXES, CORE_SWAP)
     with jax.named_scope("split"):
         parts = call(split_kernel, shape((NZH * NZL, 16, COLS)), (chunks,), (vmem,), vmem)
     with jax.named_scope("ring_z"):

time: 94.4 us -> 94.5 us (level)
  no operation moved by 1% of the time
where the time goes in v13:
time: 94.5 us; the launch traced here: 92.8 us
  starting transfers between devices  60.7 us (64%)
  Pallas kernels  20.4 us (22%)
  waiting for transfers between devices  10 us (11%)
    pallas_call x8, Pallas kernels, call(): pl.pallas_call(kernel, out_shape=outs, in_specs=[pl.BlockSpec(memory_spac...  20.4 us
    ppermute x1, starting transfers between devices, body(): origin = lax.ppermute(key_weight, AXES, origins())  13.3 us
    all_to_all x2, starting transfers between devices, exchange(): lax.all_to_all(value, AXES, split_axis=0, concat_axis=0, axis_index_group...  12.4 us
    ppermute x3, starting transfers between devices, body(): lax.ppermute(origin, AXES, from_y(ahead))  10.7 us
    ppermute x1, waiting for transfers between devices, body(): down = lax.ppermute(near, AXES, from_z(-1))  7.97 us
    ppermute x1, starting transfers between devices, body(): up = lax.ppermute(near, AXES, from_z(1))  5.93 us
    ppermute x1, starting transfers between devices, body(): early = lax.ppermute(products, AXES, CORE_SWAP)  5.72 us
    ppermute x1, starting transfers between devices, body(): far = lax.ppermute(now, AXES, two_away())  4.99 us
  transfers between devices with their start and end apart: 12, of which 3 were waited for; matrix products, arithmetic and copies ran while one was open for 0% of the time, Pallas kernels for 21%

profile of v13, /device:TPU:1, one launch (start us, length us, event | category | flops | bytes accessed | tf_op | source)
XLA Modules:
  0.0 92.8 jit_solution(12523462612762014942)
XLA Ops:
  0.6 13.3 %collective-permute-start = (bf16[128,512]{1,0:T(8,128)(2,1)}, bf16[128,512]{1,0:T(8,128)(2,1)S(1)}, u32[]{:S(2)}, u32[]{:S(2)}) collective-permute-start(bf16[128,512]{1,0:T(8,128)(2,1)} %param.7), channel_id=1, source_target_pairs={{0,0},{1,1},{2,2},{3,3},{4,4},{5,5},{6,6},{7,7},{8,8},{9,9},{10,10... | collective-permute-start | bytes 393224 | tf_op jit(solution)/shard_map/weight_z4/ppermute | solution.py:373
  13.9 3.9 %norm.1 = (bf16[16,256,256]{2,1,0:T(8,128)(2,1)}, bf16[10,256,256]{2,1,0:T(8,128)(2,1)}, f32[256,128]{1,0:T(8,128)}) custom-call(bf16[256,4096]{1,0:T(8,128)(2,1)} %hidden_hbm.3, bf16[256,512]{1,0:T(8,128)(2,1)} %key_hbm.3, f32[1,4096]{1,0:T(1,128)} %bitcast.3), custom_call_target="tpu_custom_call" | custom-call | bytes 150000 | tf_op jit(solution)/shard_map/norm/pallas_call | solution.py:86
  17.9 0.0 collective-permute-done.refs_0_
  17.9 1.9 %collective-permute-start.1 = (bf16[10,256,256]{2,1,0:T(8,128)(2,1)}, bf16[10,256,256]{2,1,0:T(8,128)(2,1)S(1)}, u32[]{:S(2)}, u32[]{:S(2)}) collective-permute-start(bf16[10,256,256]{2,1,0:T(8,128)(2,1)} %get-tuple-element.18), channel_id=1, source_target_pairs={{0,32},{1,33},{2,34},{3,35},{4,36},{5,37},{6,38},{7,39},{8,40},{9,... | collective-permute-start | bytes 3932168 | tf_op jit(solution)/shard_map/norm/ppermute | solution.py:400
  19.8 3.2 %collective-permute-start.4 = (bf16[128,512]{1,0:T(8,128)(2,1)S(1)}, bf16[128,512]{1,0:T(8,128)(2,1)S(1)}, u32[]{:S(2)}, u32[]{:S(2)}) collective-permute-start(bf16[128,512]{1,0:T(8,128)(2,1)S(1)} %collective-permute-done.refs_0_), channel_id=1, source_target_pairs={{24,0},{25,1},{26,2},{27,3},{28,4},{29,5},{30,6},{31,7},{0,8},{1,9... | collective-permute-start | bytes 393224 | tf_op jit(solution)/shard_map/weight_y/ppermute | solution.py:417
  23.0 4.5 %collective-permute-start.3 = (bf16[128,512]{1,0:T(8,128)(2,1)S(1)}, bf16[128,512]{1,0:T(8,128)(2,1)S(1)}, u32[]{:S(2)}, u32[]{:S(2)}) collective-permute-start(bf16[128,512]{1,0:T(8,128)(2,1)S(1)} %collective-permute-done.refs_0_), channel_id=1, source_target_pairs={{16,0},{17,1},{18,2},{19,3},{20,4},{21,5},{22,6},{23,7},{24,8},{25... | collective-permute-start | bytes 393224 | tf_op jit(solution)/shard_map/weight_y/ppermute | solution.py:417
  27.5 3.0 %collective-permute-start.2 = (bf16[128,512]{1,0:T(8,128)(2,1)S(1)}, bf16[128,512]{1,0:T(8,128)(2,1)S(1)}, u32[]{:S(2)}, u32[]{:S(2)}) collective-permute-start(bf16[128,512]{1,0:T(8,128)(2,1)S(1)} %collective-permute-done.refs_0_), channel_id=1, source_target_pairs={{8,0},{9,1},{10,2},{11,3},{12,4},{13,5},{14,6},{15,7},{16,8},{17,9... | collective-permute-start | bytes 393224 | tf_op jit(solution)/shard_map/weight_y/ppermute | solution.py:417
  30.5 0.0 collective-permute-done.1.other_ref.key_hbm
  30.5 3.8 %squares.1 = bf16[16,256,256]{2,1,0:T(8,128)(2,1)} custom-call(bf16[16,256,256]{2,1,0:T(8,128)(2,1)} %get-tuple-element.16.own_hbm, bf16[10,256,256]{2,1,0:T(8,128)(2,1)S(1)} %collective-permute-done.1.other_ref.key_hbm), custom_call_target="tpu_custom_call" | custom-call | bytes 150000 | tf_op jit(solution)/shard_map/squares/pallas_call | solution.py:86
  34.3 0.0 collective-permute-done.4.refs_3_
  34.3 0.0 collective-permute-done.3.refs_2_
  34.3 5.2 %all-to-all-start = ((bf16[16,256,256]{2,1,0:T(8,128)(2,1)}), bf16[16,256,256]{2,1,0:T(8,128)(2,1)S(1)}, u32[]{:S(2)}, u32[]{:S(2)}) async-start(bf16[16,256,256]{2,1,0:T(8,128)(2,1)} %squares.1), calls=%async_computation | async-start | bytes 4194304 | tf_op jit(solution)/shard_map/plane/all_to_all | solution.py:80
  39.6 0.7 weight_y.1.refs_0_.weight_0
  40.3 1.9 %collective-permute-start.6 = (bf16[4,128,512]{2,1,0:T(8,128)(2,1)S(1)}, bf16[4,128,512]{2,1,0:T(8,128)(2,1)S(1)}, u32[]{:S(2)}, u32[]{:S(2)}) collective-permute-start(bf16[4,128,512]{2,1,0:T(8,128)(2,1)S(1)} %weight_y.1.refs_0_.weight_0), channel_id=1, source_target_pairs={{71,0},{0,1},{1,2},{2,3},{3,4},{4,5},{5,6},{6,7},{79,8},{8,9},{9,1... | collective-permute-start | bytes 1572872 | tf_op jit(solution)/shard_map/weight_z1/ppermute | solution.py:427
  42.2 5.9 %collective-permute-start.5 = (bf16[4,128,512]{2,1,0:T(8,128)(2,1)S(1)}, bf16[4,128,512]{2,1,0:T(8,128)(2,1)S(1)}, u32[]{:S(2)}, u32[]{:S(2)}) collective-permute-start(bf16[4,128,512]{2,1,0:T(8,128)(2,1)S(1)} %weight_y.1.refs_0_.weight_0), channel_id=1, source_target_pairs={{1,0},{2,1},{3,2},{4,3},{5,4},{6,5},{7,6},{64,7},{9,8},{10,9},{11,... | collective-permute-start | bytes 1572872 | tf_op jit(solution)/shard_map/weight_z1/ppermute | solution.py:426
  48.2 8.0 %collective-permute-done.6.refs_2_.weight_3 = bf16[4,128,512]{2,1,0:T(8,128)(2,1)S(1)} collective-permute-done((bf16[4,128,512]{2,1,0:T(8,128)(2,1)S(1)}, bf16[4,128,512]{2,1,0:T(8,128)(2,1)S(1)}, u32[]{:S(2)}, u32[]{:S(2)}) %collective-permute-start.6) | collective-permute-done | bytes 524320 | tf_op jit(solution)/shard_map/weight_z1/ppermute | solution.py:427
  56.1 0.9 collective-permute-done.5.refs_1_.weight_1
  57.0 2.9 %weight_z1.1 = bf16[6,256,256]{2,1,0:T(8,128)(2,1)} custom-call(bf16[10,256,256]{2,1,0:T(8,128)(2,1)} %copy-done, bf16[4,128,512]{2,1,0:T(8,128)(2,1)S(1)} %weight_y.1.refs_0_.weight_0, bf16[4,128,512]{2,1,0:T(8,128)(2,1)S(1)} %collective-permute-done.5.refs_1_.weight_1, bf16[4,128,512]{2,1,0:T(8,128)(2,1)S(1)} %collective-permute-done.6.refs_2_.weight_3), custom_call_target="tpu_custom_call" | custom-call | bytes 150000 | tf_op jit(solution)/shard_map/weight_z1/pallas_call | solution.py:86
  60.0 5.0 %collective-permute-start.7 = (bf16[4,128,512]{2,1,0:T(8,128)(2,1)S(1)}, bf16[4,128,512]{2,1,0:T(8,128)(2,1)}, u32[]{:S(2)}, u32[]{:S(2)}) collective-permute-start(bf16[4,128,512]{2,1,0:T(8,128)(2,1)S(1)} %weight_y.1.refs_0_.weight_0), channel_id=1, source_target_pairs={{2,0},{71,1},{4,2},{1,3},{6,4},{3,5},{64,6},{5,7},{10,8},{79,9},{1... | collective-permute-start | bytes 1572872 | tf_op jit(solution)/shard_map/weight_z1/ppermute | solution.py:430
  65.0 5.7 %collective-permute-start.8 = (bf16[6,256,256]{2,1,0:T(8,128)(2,1)}, bf16[6,256,256]{2,1,0:T(8,128)(2,1)}, u32[]{:S(2)}, u32[]{:S(2)}) collective-permute-start(bf16[6,256,256]{2,1,0:T(8,128)(2,1)} %weight_z1.1), channel_id=1, source_target_pairs={{0,32},{1,33},{2,34},{3,35},{4,36},{5,37},{6,38},{7,39},{8,40},{9,... | collective-permute-start | bytes 2359304 | tf_op jit(solution)/shard_map/back_early/ppermute | solution.py:432
  70.7 0.0 all-to-all-done.in_ref
  70.7 0.9 split.1
  71.7 7.2 %all-to-all-start.1 = ((bf16[16,16,256]{2,1,0:T(8,128)(2,1)}), bf16[16,16,256]{2,1,0:T(8,128)(2,1)S(1)}, u32[]{:S(2)}, u32[]{:S(2)}) async-start(bf16[16,16,256]{2,1,0:T(8,128)(2,1)} %split.1), calls=%async_computation.1 | async-start | bytes 262144 | tf_op jit(solution)/shard_map/ring_z/all_to_all | solution.py:80
  78.9 0.0 collective-permute-done.7.refs_0_.weight_2
  78.9 2.1 %back_late.1 = bf16[2,256,256]{2,1,0:T(8,128)(2,1)S(1)} custom-call(bf16[10,256,256]{2,1,0:T(8,128)(2,1)} %copy-done, bf16[4,128,512]{2,1,0:T(8,128)(2,1)} %collective-permute-done.7.refs_0_.weight_2), custom_call_target="tpu_custom_call" | custom-call | bytes 150000 | tf_op jit(solution)/shard_map/back_late/pallas_call | solution.py:86
  81.1 3.8 %collective-permute-start.9 = (bf16[2,256,256]{2,1,0:T(8,128)(2,1)S(1)}, bf16[2,256,256]{2,1,0:T(8,128)(2,1)S(1)}, u32[]{:S(2)}, u32[]{:S(2)}) collective-permute-start(bf16[2,256,256]{2,1,0:T(8,128)(2,1)S(1)} %back_late.1), channel_id=1, source_target_pairs={{0,32},{1,33},{2,34},{3,35},{4,36},{5,37},{6,38},{7,39},{8,40},{9,... | collective-permute-start | bytes 786440 | tf_op jit(solution)/shard_map/back_late/ppermute | solution.py:438
  84.9 1.1 %collective-permute-done.9.late_hbm = bf16[2,256,256]{2,1,0:T(8,128)(2,1)S(1)} collective-permute-done((bf16[2,256,256]{2,1,0:T(8,128)(2,1)S(1)}, bf16[2,256,256]{2,1,0:T(8,128)(2,1)S(1)}, u32[]{:S(2)}, u32[]{:S(2)}) %collective-permute-start.9) | collective-permute-done | bytes 262176 | tf_op jit(solution)/shard_map/back_late/ppermute | solution.py:438
  86.0 0.0 collective-permute-done.8.early_hbm
  86.0 0.7 copy-done.5
  86.7 5.2 %input_grad.1 = bf16[256,4096]{1,0:T(8,128)(2,1)} custom-call(bf16[256,4096]{1,0:T(8,128)(2,1)} %hidden_hbm.3, bf16[256,512]{1,0:T(8,128)(2,1)} %key_hbm.3, f32[1,4096]{1,0:T(1,128)} %bitcast.4, f32[256,128]{1,0:T(8,128)} %get-tuple-element.21.inv_hbm, bf16[4,128,512]{2,1,0:T(8,128)(2,1)} %copy-done.1, bf16[4,128,512]{2,1,0:T(8,128)(2,1)} %copy-done.3, ...), custom_call_target="tpu_custom_call" | custom-call | bytes 150000 | tf_op jit(solution)/shard_map/input_grad/pallas_call | solution.py:86
  91.9 0.0 all-to-all-done.1.in_ref
  92.0 0.8 serve.1
  (12 shorter events, 0.0 us)
Async XLA Ops:
  0.6 17.2 %collective-permute-start = (bf16[128,512]{1,0:T(8,128)(2,1)}, bf16[128,512]{1,0:T(8,128)(2,1)S(1)}, u32[]{:S(2)}, u32[]{:S(2)}) collective-permute-start(bf16[128,512]{1,0:T(8,128)(2,1)} %param.7), channel_id=1, source_target_pairs={{0,0},{1,1},{2,2},{3,3},{4,4},{5,5},{6,6},{7,7},{8,8},{9,9},{10,10... | collective-permute-start | bytes 393224 | tf_op jit(solution)/shard_map/weight_z4/ppermute | solution.py:373
  17.9 12.7 %collective-permute-start.1 = (bf16[10,256,256]{2,1,0:T(8,128)(2,1)}, bf16[10,256,256]{2,1,0:T(8,128)(2,1)S(1)}, u32[]{:S(2)}, u32[]{:S(2)}) collective-permute-start(bf16[10,256,256]{2,1,0:T(8,128)(2,1)} %get-tuple-element.18), channel_id=1, source_target_pairs={{0,32},{1,33},{2,34},{3,35},{4,36},{5,37},{6,38},{7,39},{8,40},{9,... | collective-permute-start | bytes 3932168 | tf_op jit(solution)/shard_map/norm/ppermute | solution.py:400
  19.8 14.5 %collective-permute-start.4 = (bf16[128,512]{1,0:T(8,128)(2,1)S(1)}, bf16[128,512]{1,0:T(8,128)(2,1)S(1)}, u32[]{:S(2)}, u32[]{:S(2)}) collective-permute-start(bf16[128,512]{1,0:T(8,128)(2,1)S(1)} %collective-permute-done.refs_0_), channel_id=1, source_target_pairs={{24,0},{25,1},{26,2},{27,3},{28,4},{29,5},{30,6},{31,7},{0,8},{1,9... | collective-permute-start | bytes 393224 | tf_op jit(solution)/shard_map/weight_y/ppermute | solution.py:417
  23.0 11.3 %collective-permute-start.3 = (bf16[128,512]{1,0:T(8,128)(2,1)S(1)}, bf16[128,512]{1,0:T(8,128)(2,1)S(1)}, u32[]{:S(2)}, u32[]{:S(2)}) collective-permute-start(bf16[128,512]{1,0:T(8,128)(2,1)S(1)} %collective-permute-done.refs_0_), channel_id=1, source_target_pairs={{16,0},{17,1},{18,2},{19,3},{20,4},{21,5},{22,6},{23,7},{24,8},{25... | collective-permute-start | bytes 393224 | tf_op jit(solution)/shard_map/weight_y/ppermute | solution.py:417
  27.5 6.8 %collective-permute-start.2 = (bf16[128,512]{1,0:T(8,128)(2,1)S(1)}, bf16[128,512]{1,0:T(8,128)(2,1)S(1)}, u32[]{:S(2)}, u32[]{:S(2)}) collective-permute-start(bf16[128,512]{1,0:T(8,128)(2,1)S(1)} %collective-permute-done.refs_0_), channel_id=1, source_target_pairs={{8,0},{9,1},{10,2},{11,3},{12,4},{13,5},{14,6},{15,7},{16,8},{17,9... | collective-permute-start | bytes 393224 | tf_op jit(solution)/shard_map/weight_y/ppermute | solution.py:417
  30.5 3.8 %copy-start = (bf16[10,256,256]{2,1,0:T(8,128)(2,1)}, bf16[10,256,256]{2,1,0:T(8,128)(2,1)S(1)}, u32[]{:S(2)}) copy-start(bf16[10,256,256]{2,1,0:T(8,128)(2,1)S(1)} %collective-permute-done.1.other_ref.key_hbm) | copy-start | bytes 3932164
  34.3 36.4 %all-to-all-start = ((bf16[16,256,256]{2,1,0:T(8,128)(2,1)}), bf16[16,256,256]{2,1,0:T(8,128)(2,1)S(1)}, u32[]{:S(2)}, u32[]{:S(2)}) async-start(bf16[16,256,256]{2,1,0:T(8,128)(2,1)} %squares.1), calls=%async_computation | async-start | bytes 4194304 | tf_op jit(solution)/shard_map/plane/all_to_all | solution.py:80
  40.3 31.4 %copy-start.1 = (bf16[4,128,512]{2,1,0:T(8,128)(2,1)}, bf16[4,128,512]{2,1,0:T(8,128)(2,1)S(1)}, u32[]{:S(2)}) copy-start(bf16[4,128,512]{2,1,0:T(8,128)(2,1)S(1)} %weight_y.1.refs_0_.weight_0) | copy-start | bytes 1572868
  40.3 15.8 %collective-permute-start.6 = (bf16[4,128,512]{2,1,0:T(8,128)(2,1)S(1)}, bf16[4,128,512]{2,1,0:T(8,128)(2,1)S(1)}, u32[]{:S(2)}, u32[]{:S(2)}) collective-permute-start(bf16[4,128,512]{2,1,0:T(8,128)(2,1)S(1)} %weight_y.1.refs_0_.weight_0), channel_id=1, source_target_pairs={{71,0},{0,1},{1,2},{2,3},{3,4},{4,5},{5,6},{6,7},{79,8},{8,9},{9,1... | collective-permute-start | bytes 1572872 | tf_op jit(solution)/shard_map/weight_z1/ppermute | solution.py:427
  42.2 14.8 %collective-permute-start.5 = (bf16[4,128,512]{2,1,0:T(8,128)(2,1)S(1)}, bf16[4,128,512]{2,1,0:T(8,128)(2,1)S(1)}, u32[]{:S(2)}, u32[]{:S(2)}) collective-permute-start(bf16[4,128,512]{2,1,0:T(8,128)(2,1)S(1)} %weight_y.1.refs_0_.weight_0), channel_id=1, source_target_pairs={{1,0},{2,1},{3,2},{4,3},{5,4},{6,5},{7,6},{64,7},{9,8},{10,9},{11,... | collective-permute-start | bytes 1572872 | tf_op jit(solution)/shard_map/weight_z1/ppermute | solution.py:426
  56.1 15.5 %copy-start.2 = (bf16[4,128,512]{2,1,0:T(8,128)(2,1)}, bf16[4,128,512]{2,1,0:T(8,128)(2,1)S(1)}, u32[]{:S(2)}) copy-start(bf16[4,128,512]{2,1,0:T(8,128)(2,1)S(1)} %collective-permute-done.6.refs_2_.weight_3) | copy-start | bytes 1572868
  57.0 8.0 %copy-start.3 = (bf16[4,128,512]{2,1,0:T(8,128)(2,1)}, bf16[4,128,512]{2,1,0:T(8,128)(2,1)S(1)}, u32[]{:S(2)}) copy-start(bf16[4,128,512]{2,1,0:T(8,128)(2,1)S(1)} %collective-permute-done.5.refs_1_.weight_1) | copy-start | bytes 1572868
  60.0 18.9 %collective-permute-start.7 = (bf16[4,128,512]{2,1,0:T(8,128)(2,1)S(1)}, bf16[4,128,512]{2,1,0:T(8,128)(2,1)}, u32[]{:S(2)}, u32[]{:S(2)}) collective-permute-start(bf16[4,128,512]{2,1,0:T(8,128)(2,1)S(1)} %weight_y.1.refs_0_.weight_0), channel_id=1, source_target_pairs={{2,0},{71,1},{4,2},{1,3},{6,4},{3,5},{64,6},{5,7},{10,8},{79,9},{1... | collective-permute-start | bytes 1572872 | tf_op jit(solution)/shard_map/weight_z1/ppermute | solution.py:430
  65.0 21.0 %collective-permute-start.8 = (bf16[6,256,256]{2,1,0:T(8,128)(2,1)}, bf16[6,256,256]{2,1,0:T(8,128)(2,1)}, u32[]{:S(2)}, u32[]{:S(2)}) collective-permute-start(bf16[6,256,256]{2,1,0:T(8,128)(2,1)} %weight_z1.1), channel_id=1, source_target_pairs={{0,32},{1,33},{2,34},{3,35},{4,36},{5,37},{6,38},{7,39},{8,40},{9,... | collective-permute-start | bytes 2359304 | tf_op jit(solution)/shard_map/back_early/ppermute | solution.py:432
  71.7 20.3 %all-to-all-start.1 = ((bf16[16,16,256]{2,1,0:T(8,128)(2,1)}), bf16[16,16,256]{2,1,0:T(8,128)(2,1)S(1)}, u32[]{:S(2)}, u32[]{:S(2)}) async-start(bf16[16,16,256]{2,1,0:T(8,128)(2,1)} %split.1), calls=%async_computation.1 | async-start | bytes 262144 | tf_op jit(solution)/shard_map/ring_z/all_to_all | solution.py:80
  81.1 4.9 %collective-permute-start.9 = (bf16[2,256,256]{2,1,0:T(8,128)(2,1)S(1)}, bf16[2,256,256]{2,1,0:T(8,128)(2,1)S(1)}, u32[]{:S(2)}, u32[]{:S(2)}) collective-permute-start(bf16[2,256,256]{2,1,0:T(8,128)(2,1)S(1)} %back_late.1), channel_id=1, source_target_pairs={{0,32},{1,33},{2,34},{3,35},{4,36},{5,37},{6,38},{7,39},{8,40},{9,... | collective-permute-start | bytes 786440 | tf_op jit(solution)/shard_map/back_late/ppermute | solution.py:438
  86.0 0.7 copy-start.5
  86.7 5.2 %copy-start.4 = (s32[512]{0:T(512)S(1)}, s32[512]{0:T(512)}, u32[]{:S(2)}) copy-start(s32[512]{0:T(512)} %param.9) | copy-start | bytes 6148
